TPU v7x, 32 devices: a whole 2x2x4 slice. The times are simulated.
32 devices in a mesh: rec: 8 (over z, x), feat: 4 (over y, core).
Axes of the slice: x: 2, y: 2, z: 4, core: 2. Of those that a mesh axis runs over, the one named last changes fastest.
Arguments:
- records: bfloat16 [12288, 3072], P('rec'), may hold values from -4 to 4
- real_labels: int32 [12288], P('rec'), may hold values from 0 to 255
- frequencies: bfloat16 [3072, 8192], P(None, 'feat'), may hold values from -0.109375 to 0.109375
- class_noise: float32 [256, 2, 8192], P(None, None, 'feat'), may hold values from -48 to 48
- latents: bfloat16 [1024, 128], P('rec'), may hold values from -5 to 5
- syn_labels: int32 [1024], P('rec'), may hold values from 0 to 255
- w_latent: bfloat16 [128, 2048], replicated, may hold values from -0.5 to 0.5
- class_embed: bfloat16 [256, 2048], replicated, may hold values from -5 to 5
- w_out: bfloat16 [2048, 3072], P(None, 'feat'), may hold values from -0.125 to 0.125
Outputs:
- grad_w_out: float32 [2048, 3072], P('rec', 'feat')
- grad_w_latent: float32 [128, 2048], P(None, 'rec')
- grad_embed: float32 [256, 2048], P(None, 'rec')
All inputs are finite; a program needn't handle non-finite values.
Results may differ from a plain program's by a relative error of at most 0.0053.
Values may be sent and summed in bfloat16 or wider, within the bound.
No kernel may reach another device: no remote copies, remote signals or barrier semaphores. Data moves between devices by JAX's collectives and lax.ppermute only.
A program may use at most 128 MiB of HBM per device.

v0:
```python
import jax
import jax.numpy as jnp
from jax import lax
from jax.sharding import PartitionSpec as P


def one_hot(labels, count, dtype):
    return (labels[:, None] == jnp.arange(count, dtype=jnp.int32)[None, :]).astype(dtype)


def class_sums(pre, labels, classes):
    phi = jnp.concatenate([jnp.cos(pre), jnp.sin(pre)], axis=1).astype(jnp.bfloat16)
    table = one_hot(labels, classes, jnp.bfloat16)
    return lax.dot_general(table, phi, (((0,), (0,)), ((), ())), preferred_element_type=jnp.float32)


def on_device(
    records,
    real_labels,
    frequencies,
    class_noise,
    latents,
    syn_labels,
    w_latent,
    class_embed,
    w_out,
):
    classes = class_embed.shape[0]
    nf_local = frequencies.shape[1]
    groups = lax.axis_size("rec")
    real_total = records.shape[0] * groups
    syn_total = latents.shape[0] * groups
    real_pre = jnp.dot(records, frequencies, preferred_element_type=jnp.float32)
    real_local = class_sums(real_pre, real_labels, classes)
    syn_table = one_hot(syn_labels, classes, jnp.bfloat16)
    preact = jnp.dot(latents, w_latent, preferred_element_type=jnp.float32) + jnp.dot(
        syn_table, class_embed, preferred_element_type=jnp.float32
    )
    hidden = jnp.maximum(preact, 0.0).astype(jnp.bfloat16)
    out_cols = jnp.tanh(
        lax.dot_general(w_out, hidden, (((0,), (1,)), ((), ())), preferred_element_type=jnp.float32)
    ).astype(jnp.bfloat16)
    images = lax.all_gather(out_cols, "feat", axis=0, tiled=True)
    syn_pre = lax.dot_general(
        images, frequencies, (((0,), (0,)), ((), ())), preferred_element_type=jnp.float32
    )
    syn_local = class_sums(syn_pre, syn_labels, classes)
    noise_flat = class_noise.reshape(classes, 2 * nf_local)
    real_sum = lax.psum(real_local, "rec")
    syn_sum = lax.psum(syn_local, "rec")
    class_gap = syn_sum / syn_total - (real_sum + noise_flat) / real_total
    feat_grad = 16.0 * jnp.dot(
        syn_table.astype(jnp.float32), class_gap, precision=lax.Precision.HIGHEST
    )
    pre_grad = (
        -jnp.sin(syn_pre) * feat_grad[:, :nf_local] + jnp.cos(syn_pre) * feat_grad[:, nf_local:]
    ).astype(jnp.bfloat16)
    image_grad = lax.psum_scatter(
        lax.dot_general(
            frequencies, pre_grad, (((1,), (1,)), ((), ())), preferred_element_type=jnp.float32
        ),
        "feat",
        scatter_dimension=0,
        tiled=True,
    )
    out_grad = (image_grad * (1.0 - jnp.square(out_cols.astype(jnp.float32)))).astype(jnp.bfloat16)
    w2_term = lax.dot_general(
        hidden, out_grad, (((0,), (1,)), ((), ())), preferred_element_type=jnp.float32
    )
    grad_w_out = lax.psum_scatter(w2_term, "rec", scatter_dimension=0, tiled=True)
    hidden_term = lax.dot_general(
        out_grad, w_out, (((0,), (1,)), ((), ())), preferred_element_type=jnp.float32
    )
    hidden_grad = lax.psum(hidden_term, "feat")
    pre_hidden = jnp.where(preact > 0, hidden_grad, 0.0).astype(jnp.bfloat16)
    latent_term = lax.dot_general(
        latents, pre_hidden, (((0,), (0,)), ((), ())), preferred_element_type=jnp.float32
    )
    embed_term = lax.dot_general(
        syn_table, pre_hidden, (((0,), (0,)), ((), ())), preferred_element_type=jnp.float32
    )
    grad_w_latent, grad_embed = (
        lax.psum_scatter(latent_term, "rec", scatter_dimension=1, tiled=True),
        lax.psum_scatter(embed_term, "rec", scatter_dimension=1, tiled=True),
    )
    return (grad_w_out, grad_w_latent, grad_embed)


def solution(mesh):
    in_specs = (
        P("rec", None),
        P("rec"),
        P(None, "feat"),
        P(None, None, "feat"),
        P("rec", None),
        P("rec"),
        P(),
        P(),
        P(None, "feat"),
    )
    out_specs = (P("rec", "feat"), P(None, "rec"), P(None, "rec"))
    return jax.shard_map(
        on_device, mesh=mesh, in_specs=in_specs, out_specs=out_specs, check_vma=False
    )
```

profile of v0, /device:TPU:0, one launch (start us, length us, event | category | flops | bytes accessed | tf_op | source)
XLA Modules:
  0.0 733.4 jit_solution(1828449246523724659)
XLA Ops:
  7.2 0.0 copy-start
  7.2 0.0 all-reduce.4.cloned.1.call-start
  7.2 1.7 fusion.22
  9.0 1.3 convolution_add_fusion
  10.3 0.0 copy-start.1
  10.3 1.0 copy-done.1
  11.3 0.0 copy-done
  11.3 0.6 fusion.11
  11.9 10.2 %all_gather.3 = bf16[3072,128]{0,1:T(8,128)(2,1)S(1)} all-gather(bf16[768,128]{0,1:T(8,128)(2,1)S(1)} %fusion.11), channel_id=1, replica_groups=mesh['rec'=8,'feat'=4] {'feat'}, dimensions={0}, use_global_device_ids=true | all-gather | bytes 983040 | tf_op jit(solution)/shard_map/all_gather | solution.py:43
  22.1 9.3 %fusion.34 = (f32[128,2048]{1,0:T(8,128)S(1)}, f32[128,2048]{1,0:T(8,128)S(1)}) fusion(bf16[3072,128]{0,1:T(8,128)(2,1)S(1)} %all_gather.3, bf16[3072,2048]{1,0:T(8,128)(2,1)} %param.11), kind=kOutput, calls=%fused_computation.47 | convolution fusion | flops 1610612736 | bytes 15466496 | tf_op jit(solution)/shard_map/dot_general | solution.py:44
  31.5 0.0 slice-done
  31.5 0.0 slice-done.1
  31.5 0.0 slice-done.2
  31.5 0.5 copy-done.8
  32.1 76.5 %cosine_convert_fusion = (bf16[1536,2048]{1,0:T(8,128)(2,1)}, bf16[1536,2048]{1,0:T(8,128)(2,1)}) fusion(bf16[1536,3072]{1,0:T(8,128)(2,1)S(1)} %copy-done.8, bf16[3072,2048]{1,0:T(8,128)(2,1)S(1)} %bitcast.20), kind=kOutput, calls=%fused_computation.5 | convolution fusion | flops 19333644288 | bytes 34603008 | tf_op jit(solution)/shard_map/dot_general | solution.py:33
  108.6 0.0 copy-done.2
  108.6 0.0 copy-start.9
  108.6 0.0 copy-start.10
  108.6 0.1 convert.13
  108.7 0.0 copy-done.4
  108.7 0.1 convert.12
  108.7 0.0 copy-done.7
  108.8 3.0 fusion.14
  111.7 1.2 copy-done.10
  112.9 8.6 %fusion = f32[256,4096]{1,0:T(8,128)} fusion(bf16[1536,2048]{1,0:T(8,128)(2,1)} %get-tuple-element.9, bf16[1536,2048]{1,0:T(8,128)(2,1)S(1)} %copy-done.10, s32[1536]{0:T(1024)S(1)} %copy-done.9), kind=kOutput, calls=%fused_computation | convolution fusion | flops 3246784512 | bytes 16783360 | tf_op jit(solution)/shard_map/dot_general | solution.py:14
  121.5 0.0 all-reduce.4.cloned.1.call-update
  121.5 0.2 reduce-scatter.5.cloned.1.call-start
  121.7 8.0 %copy.13 = f32[32,8,2,2048]{3,1,2,0:T(8,128)} copy(f32[32,8,2,2048]{3,2,1,0:T(2,128)} %bitcast.22) | data formatting | bytes 8388608
  129.7 263.9 %all-reduce.4.cloned.1.call-done = (f32[256,4096]{1,0:T(8,128)}, f32[256,4096]{1,0:T(8,128)}) async-done(((f32[256,4096]{1,0:T(8,128)}, f32[256,4096]{1,0:T(8,128)}), (f32[256,4096]{1,0:T(8,128)}, f32[256,4096]{1,0:T(8,128)})) %all-reduce.4.cloned.1.call-update) | async-done | bytes 8388624 | tf_op jit(solution)/shard_map/psum | solution.py:49
  393.6 7.1 convolution_multiply_fusion
  400.7 10.0 %convolution_bitcast_fusion = f32[3072,128]{0,1:T(8,128)} fusion(bf16[3072,2048]{1,0:T(8,128)(2,1)} %param.11, f32[128,2048]{1,0:T(8,128)S(1)} %copy-done.5, f32[128,4096]{1,0:T(8,128)S(1)} %convolution_multiply_fusion, f32[128,2048]{1,0:T(8,128)S(1)} %copy-done.3), kind=kOutput, calls=%fused_computation.11 | convolution fusion | flops 1611923456 | bytes 18350080 | tf_op jit(solution)/shard_map/dot_general | solution.py:59
  410.7 0.0 reduce-scatter.5.cloned.1.call-update
  410.7 0.0 reduce-scatter.9.cloned.1.call-start
  410.8 27.3 %reduce-scatter.5.cloned.1.call-done = f32[768,128]{0,1:T(8,128)} async-done(((f32[3072,128]{0,1:T(8,128)}), f32[768,128]{0,1:T(8,128)}) %reduce-scatter.5.cloned.1.call-update) | async-done | bytes 393232 | tf_op jit(solution)/shard_map/reduce_scatter | solution.py:58
  438.1 3.1 fusion.33
  441.2 26.6 %all-reduce.5 = bf16[128,2048]{1,0:T(8,128)(2,1)} all-reduce(f32[128,2048]{1,0:T(8,128)} %fusion.33), channel_id=1, replica_groups=mesh['rec'=8,'feat'=4] {'feat'}, use_global_device_ids=true, to_apply=%region_4.0 | all-reduce | flops 262144 | bytes 1572864 | tf_op jit(solution)/shard_map/psum | solution.py:74
  467.8 2.7 convolution_bitcast_fusion.1
  470.5 0.0 reduce-scatter.9.cloned.1.call-update
  470.5 0.0 reduce-scatter.11.cloned.1.call-start
  470.5 3.3 fusion.21
  473.9 0.0 reduce-scatter.11.cloned.1.call-update
  473.9 0.0 reduce-scatter.7.cloned.1.call-start
  473.9 4.9 fusion.20
  478.9 0.0 reduce-scatter.7.cloned.1.call-update
  478.9 55.6 %reduce-scatter.9.cloned.1.call-done = f32[128,256]{0,1:T(8,128)} async-done(((f32[128,2048]{0,1:T(8,128)}), f32[128,256]{0,1:T(8,128)}) %reduce-scatter.9.cloned.1.call-update) | async-done | bytes 131088 | tf_op jit(solution)/shard_map/reduce_scatter | solution.py:83
  534.5 1.7 copy.12
  536.1 69.7 %reduce-scatter.11.cloned.1.call-done = f32[256,256]{1,0:T(8,128)} async-done(((f32[256,2048]{1,0:T(8,128)}), f32[256,256]{1,0:T(8,128)}) %reduce-scatter.11.cloned.1.call-update) | async-done | bytes 262160 | tf_op jit(solution)/shard_map/reduce_scatter | solution.py:84
  605.8 121.0 %reduce-scatter.7.cloned.1.call-done = f32[256,768]{1,0:T(8,128)} async-done(((f32[2048,768]{1,0:T(8,128)}), f32[256,768]{1,0:T(8,128)}) %reduce-scatter.7.cloned.1.call-update) | async-done | bytes 786448 | tf_op jit(solution)/shard_map/reduce_scatter | solution.py:70
  (15 shorter events, 0.0 us)
Async XLA Ops:
  7.2 4.1 copy-start
  7.2 386.4 %all-reduce.4.cloned.1.call-start = ((), (), s32[]{:S(2)}) async-start(), calls=%async_computation.8 | async-start | bytes 16777216 | tf_op jit(solution)/shard_map/psum | solution.py:49
  10.3 1.0 copy-start.1
  11.3 20.2 %slice-start = ((s8[12582912]{0:T(1024)(128)(4,1)}), s8[4194304]{0:T(1024)(128)(4,1)S(1)}, s32[]{:S(2)}) async-start(s8[12582912]{0:T(1024)(128)(4,1)} %bitcast.19), calls=%async_computation.9 | async-start | bytes 8388608
  22.1 9.4 %slice-start.1 = ((s8[12582912]{0:T(1024)(128)(4,1)}), s8[4194304]{0:T(1024)(128)(4,1)S(1)}, s32[]{:S(2)}) async-start(s8[12582912]{0:T(1024)(128)(4,1)} %bitcast.19), calls=%async_computation.10 | async-start | bytes 8388608
  22.1 9.4 %slice-start.2 = ((s8[12582912]{0:T(1024)(128)(4,1)}), s8[4194304]{0:T(1024)(128)(4,1)S(1)}, s32[]{:S(2)}) async-start(s8[12582912]{0:T(1024)(128)(4,1)} %bitcast.19), calls=%async_computation.11 | async-start | bytes 8388608
  22.1 9.9 %copy-start.8 = (bf16[1536,3072]{1,0:T(8,128)(2,1)S(1)}, bf16[1536,3072]{1,0:T(8,128)(2,1)}, u32[]{:S(2)}) copy-start(bf16[1536,3072]{1,0:T(8,128)(2,1)} %param.9) | copy-start | bytes 28311556
  32.1 76.5 %copy-start.2 = (f32[128,2048]{1,0:T(8,128)}, f32[128,2048]{1,0:T(8,128)S(1)}, u32[]{:S(2)}) copy-start(f32[128,2048]{1,0:T(8,128)S(1)} %get-tuple-element.10) | copy-start | bytes 3145732
  32.1 76.6 %copy-start.4 = (f32[128,2048]{1,0:T(8,128)}, f32[128,2048]{1,0:T(8,128)S(1)}, u32[]{:S(2)}) copy-start(f32[128,2048]{1,0:T(8,128)S(1)} %get-tuple-element.11) | copy-start | bytes 3145732
  32.1 76.7 %copy-start.7 = (s32[128]{0:T(128)S(1)}, s32[128]{0:T(128)}, u32[]{:S(2)}) copy-start(s32[128]{0:T(128)} %param.14) | copy-start | bytes 1540
  108.6 3.1 copy-start.9
  108.6 4.3 copy-start.10
  121.5 316.6 %reduce-scatter.5.cloned.1.call-start = ((), (), s32[]{:S(2)}) async-start(), calls=%async_computation.4 | async-start | bytes 1966080 | tf_op jit(solution)/shard_map/reduce_scatter | solution.py:58
  393.6 7.1 copy-start.3
  393.6 7.1 copy-start.5
  410.7 57.1 %copy-start.6 = (bf16[128,128]{1,0:T(8,128)(2,1)S(1)}, bf16[128,128]{1,0:T(8,128)(2,1)}, u32[]{:S(2)}) copy-start(bf16[128,128]{1,0:T(8,128)(2,1)} %param.13) | copy-start | bytes 98308
  410.7 123.8 %reduce-scatter.9.cloned.1.call-start = ((), (), s32[]{:S(2)}) async-start(), calls=%async_computation.6 | async-start | bytes 1179648 | tf_op jit(solution)/shard_map/reduce_scatter | solution.py:83
  470.5 135.4 %reduce-scatter.11.cloned.1.call-start = ((), (), s32[]{:S(2)}) async-start(), calls=%async_computation.7 | async-start | bytes 2359296 | tf_op jit(solution)/shard_map/reduce_scatter | solution.py:84
  473.9 253.0 %reduce-scatter.7.cloned.1.call-start = ((), (), s32[]{:S(2)}) async-start(), calls=%async_computation.5 | async-start | bytes 7077888 | tf_op jit(solution)/shard_map/reduce_scatter | solution.py:70
Sparse Core Ops, SparseCore 0:
  121.6 271.9 all-reduce.3
  410.8 27.1 reduce-scatter.4
  470.6 63.8 reduce-scatter.8
  538.4 67.3 reduce-scatter.10
  609.8 116.9 reduce-scatter.6
where the time goes:
time: 734 us; the launch traced here: 733 us
  waiting for transfers between devices  538 us (73%)
  matrix products  132 us (18%)
  blocking collectives  36.8 us (5%)
  between operations  13.9 us (2%)
  local copies, waits for them, and re-layouts  12.4 us (2%)
    psum x1, waiting for transfers between devices, on_device(): real_sum = lax.psum(real_local, 'rec')  264 us
    reduce_scatter x1, waiting for transfers between devices, on_device(): lax.psum_scatter(w2_term, 'rec', scatter_dimension=0, tiled=True)  121 us
    dot_general x1, matrix products, on_device(): real_pre = jnp.dot(records, frequencies, preferred_element_type=jnp.float32)  76.5 us
    reduce_scatter x1, waiting for transfers between devices, on_device(): lax.psum_scatter(embed_term, 'rec', scatter_dimension=1, tiled=True)  69.7 us
    reduce_scatter x1, waiting for transfers between devices, on_device(): lax.psum_scatter(latent_term, 'rec', scatter_dimension=1, tiled=True)  55.6 us
    reduce_scatter x1, waiting for transfers between devices, on_device(): lax.psum_scatter(lax.dot_general(frequencies, pre_grad, (((1,), (1,)), ((...  27.3 us
    psum x1, blocking collectives, on_device(): hidden_grad = lax.psum(hidden_term, 'feat')  26.6 us
  transfers between devices with their start and end apart: 5, of which 5 were waited for; matrix products, arithmetic and copies ran while one was open for 2% of the time, Pallas kernels for 0%

commit v1 on v0

v1 whole, which is shorter than its diff:
```python
import functools

import jax
import jax.numpy as jnp
from jax import lax
from jax.experimental import pallas as pl
from jax.experimental.pallas import tpu as pltpu
from jax.sharding import PartitionSpec as P

BF = jnp.bfloat16
F32 = jnp.float32

TURN = 0.15915494309189535
SIN = (4.44286783702217, -7.307441307726672, 3.59477116396636, -0.7843353598850176)
COS = (1.4142134962552275, -6.978850948563815, 5.739460376907241, -1.883557905986894, 0.3106880275267554)


def cos_sin(x):
    turns = x * TURN
    u = turns - jnp.round(turns)
    sq = u * u
    p = SIN[-1]
    for c in SIN[-2::-1]:
        p = p * sq + c
    q = COS[-1]
    for c in COS[-2::-1]:
        q = q * sq + c
    s = u * p
    return 1.0 - s * s, s * q


def one_hot(labels, count, dtype):
    return (labels[:, None] == jnp.arange(count, dtype=jnp.int32)[None, :]).astype(dtype)


def real_kernel(rows, labels_ref, records_ref, freq_ref, out_ref, table_ref):
    total = records_ref.shape[0]
    classes = table_ref.shape[0]
    owners, _, width = out_ref.shape
    part = width // 2

    @pl.when(pl.program_id(0) == 0)
    def _():
        ids = lax.broadcasted_iota(jnp.int32, (classes, total), 0)
        table_ref[...] = jnp.where(ids == labels_ref[...], 1.0, 0.0).astype(BF)

    freq = freq_ref[...]
    block = freq.shape[1]

    def sums(i, pre):
        co, si = cos_sin(pre)
        phi = jnp.concatenate([co.astype(BF), si.astype(BF)], axis=1)
        return jnp.dot(table_ref[:, i * rows : (i + 1) * rows], phi, preferred_element_type=F32)

    acc = None
    before = None
    steps = total // rows
    for i in range(steps + 1):
        pre = None
        if i < steps:
            pre = jnp.dot(records_ref[i * rows : (i + 1) * rows, :], freq, preferred_element_type=F32)
        if i > 0:
            d = sums(i - 1, before)
            acc = d if acc is None else acc + d
        before = pre
    for o in range(owners):
        out_ref[o, :, :part] = acc[:, o * part : (o + 1) * part]
        out_ref[o, :, part:] = acc[:, block + o * part : block + (o + 1) * part]


def real_sums(labels, records, freq, classes, owners):
    m, k = records.shape
    n = freq.shape[1]
    block = min(512, n)
    rows = 512
    part = n // owners
    per = block // part
    return pl.pallas_call(
        functools.partial(real_kernel, rows),
        grid=(n // block,),
        in_specs=[
            pl.BlockSpec((1, m), lambda j: (0, 0)),
            pl.BlockSpec((m, k), lambda j: (0, 0)),
            pl.BlockSpec((k, block), lambda j: (0, j)),
        ],
        out_specs=pl.BlockSpec((per, classes, 2 * part), lambda j: (j, 0, 0)),
        out_shape=jax.ShapeDtypeStruct((owners, classes, 2 * part), F32),
        scratch_shapes=[pltpu.VMEM((classes, m), BF)],
        compiler_params=pltpu.CompilerParams(vmem_limit_bytes=56 * 2**20),
        cost_estimate=pl.CostEstimate(
            flops=2 * m * n * (k + 2 * classes), bytes_accessed=2 * (m * k + k * n), transcendentals=0
        ),
    )(labels.reshape(1, m), records, freq)


def bits_of(n):
    return [1 << b for b in range(n.bit_length() - 1)]


def swap(x, axis, bit):
    n = lax.axis_size(axis)
    return lax.ppermute(x, axis, [(i, i ^ bit) for i in range(n)])


def pick(x, index, dim):
    return lax.dynamic_index_in_dim(x, index, dim, keepdims=False)


def halving(x, axis, order, count):
    me = lax.axis_index(axis)
    nbits = len(order)
    x = x.reshape((2,) * nbits + x.shape[1:])
    left = sorted(order, reverse=True)
    for bit in order:
        dim = left.index(bit)
        left.remove(bit)
        mine = (me // bit) % 2
        got = swap(pick(x, 1 - mine, dim).astype(BF), axis, bit)
        x = pick(x, mine, dim).astype(F32) + got.astype(F32)
    return x


def on_device(
    records, real_labels, frequencies, class_noise, latents, syn_labels, w_latent, class_embed, w_out
):
    classes = class_embed.shape[0]
    hid = class_embed.shape[1]
    groups = lax.axis_size("rec")
    feats = lax.axis_size("feat")
    rec = lax.axis_index("rec")
    nf = frequencies.shape[1]
    part = nf // groups
    rows, dz = latents.shape
    cols = w_out.shape[1]
    real_total = records.shape[0] * groups
    syn_total = rows * groups

    label_row = jnp.zeros((16, dz), BF).at[0, :].set(syn_labels.astype(BF))
    packed = jnp.concatenate([latents, label_row], axis=0)
    packed = lax.all_to_all(
        jnp.broadcast_to(packed[None], (groups,) + packed.shape), "rec", 0, 0, tiled=True
    )
    all_latents = packed[:, :rows].reshape(syn_total, dz)
    all_labels = packed[:, rows].reshape(syn_total).astype(jnp.int32)
    all_table = one_hot(all_labels, classes, BF)

    table = one_hot(syn_labels, classes, BF)
    preact = jnp.dot(latents, w_latent, preferred_element_type=F32) + jnp.dot(
        table, class_embed, preferred_element_type=F32
    )
    hidden = jnp.maximum(preact, 0.0).astype(BF)
    own_images = jnp.tanh(jnp.dot(hidden, w_out, preferred_element_type=F32)).astype(BF)
    images = lax.all_gather(own_images, "feat", axis=0)
    images = images.transpose(1, 0, 2).reshape(rows, feats * cols)
    syn_pre = jnp.dot(images, frequencies, preferred_element_type=F32)
    syn_cos, syn_sin = cos_sin(syn_pre)
    syn_phi = jnp.concatenate(
        [syn_cos.reshape(rows, groups, part), syn_sin.reshape(rows, groups, part)], axis=2
    ).astype(BF)
    syn_sum = lax.dot_general(
        table, syn_phi.reshape(rows, 2 * nf), (((0,), (0,)), ((), ())), preferred_element_type=F32
    )
    syn_sum = syn_sum.reshape(classes, groups, 2 * part).transpose(1, 0, 2)

    real_sum = real_sums(real_labels, records, frequencies, classes, groups)
    gap = syn_sum * (1.0 / syn_total) - real_sum * (1.0 / real_total)
    half = classes // 2
    order = bits_of(groups)
    other = [order[1], order[0]] + order[2:]
    gap = jnp.concatenate(
        [halving(gap[:, :half], "rec", order, groups), halving(gap[:, half:], "rec", other, groups)], axis=0
    )
    noise = lax.dynamic_slice_in_dim(class_noise, rec * part, part, 2).reshape(classes, 2 * part)
    gap = (16.0 * (gap - noise * (1.0 / real_total))).astype(BF)

    feat_grad = jnp.dot(all_table, gap, preferred_element_type=F32).astype(BF)
    feat_grad = lax.all_to_all(feat_grad.reshape(groups, rows, 2 * part), "rec", 0, 0, tiled=True)
    feat_grad = feat_grad.transpose(1, 0, 2).astype(F32)
    pre_grad = (
        -syn_sin.reshape(rows, groups, part) * feat_grad[:, :, :part]
        + syn_cos.reshape(rows, groups, part) * feat_grad[:, :, part:]
    )
    pre_grad = pre_grad.astype(BF).reshape(rows, nf)
    image_grad = lax.dot_general(
        frequencies, pre_grad, (((1,), (1,)), ((), ())), preferred_element_type=F32
    )
    image_grad = halving(image_grad.reshape(feats, cols, rows), "feat", bits_of(feats), feats)
    image_grad = image_grad.T
    out_grad = (image_grad * (1.0 - jnp.square(own_images.astype(F32)))).astype(BF)

    out_grad = lax.all_to_all(
        jnp.broadcast_to(out_grad[None], (groups, rows, cols)), "rec", 0, 0, tiled=True
    ).reshape(syn_total, cols)

    mine = hid // groups
    start = rec * mine
    all_preact = jnp.dot(
        all_latents, lax.dynamic_slice_in_dim(w_latent, start, mine, 1), preferred_element_type=F32
    ) + jnp.dot(
        all_table, lax.dynamic_slice_in_dim(class_embed, start, mine, 1), preferred_element_type=F32
    )
    all_hidden = jnp.maximum(all_preact, 0.0).astype(BF)
    grad_w_out = lax.dot_general(
        all_hidden, out_grad, (((0,), (0,)), ((), ())), preferred_element_type=F32
    )
    hidden_grad = lax.dot_general(
        out_grad,
        lax.dynamic_slice_in_dim(w_out, start, mine, 0),
        (((1,), (1,)), ((), ())),
        preferred_element_type=F32,
    )
    core = lax.axis_index("feat") % 2
    half = syn_total // 2
    hidden_grad = hidden_grad.reshape(2, half, mine)
    got = swap(pick(hidden_grad, 1 - core, 0).astype(BF), "feat", 1)
    hidden_grad = pick(hidden_grad, core, 0) + got.astype(F32)
    for bit in bits_of(feats)[1:]:
        send = hidden_grad.astype(BF)
        hidden_grad = send.astype(F32) + swap(send, "feat", bit).astype(F32)
    my_preact = lax.dynamic_slice_in_dim(all_preact, core * half, half, 0)
    pre_hidden = jnp.where(my_preact > 0, hidden_grad, 0.0).astype(BF)
    lhs = jnp.concatenate([all_latents, all_table], axis=1)
    lhs = lax.dynamic_slice_in_dim(lhs, core * half, half, 0)
    grads = lax.dot_general(lhs, pre_hidden, (((0,), (0,)), ((), ())), preferred_element_type=F32)
    grads = grads + swap(grads, "feat", 1)
    return grad_w_out, grads[:dz], grads[dz:]


def solution(mesh):
    in_specs = (
        P("rec", None),
        P("rec"),
        P(None, "feat"),
        P(None, None, "feat"),
        P("rec", None),
        P("rec"),
        P(),
        P(),
        P(None, "feat"),
    )
    out_specs = (P("rec", "feat"), P(None, "rec"), P(None, "rec"))
    return jax.shard_map(
        on_device, mesh=mesh, in_specs=in_specs, out_specs=out_specs, check_vma=False
    )
```

time: 734 us -> 250 us (0.34)
  waiting for transfers between devices: 538 us -> 89.8 us
  matrix products: 132 us -> 35.2 us
  Pallas kernels: 0 us -> 31.4 us
  starting transfers between devices: 0.39 us -> 29.5 us
  blocking collectives: 36.8 us -> 9.07 us
  local copies, waits for them, and re-layouts: 12.4 us -> 39.9 us
  between operations: 13.9 us -> 0.93 us
  other arithmetic: 0.12 us -> 12.4 us
    reduce_scatter x4 -> x0, waiting for transfers between devices: 274 us -> none  [the longest x1 121 us: on_device(): lax.psum_scatter(w2_term, 'rec', scatter_dimension=0, tiled=True)]
    psum x1 -> x0, waiting for transfers between devices: 264 us -> none  [on_device(): real_sum = lax.psum(real_local, 'rec')]
    dot_general x12 -> x10, matrix products: 122 us -> 25.1 us  [the longest x1 8.36 us: on_device(): syn_pre = jnp.dot(images, frequencies, preferred_element_type=F32)]
    all_to_all x0 -> x3, waiting for transfers between devices: none -> 57.4 us  [the longest x1 37.2 us: on_device(): lax.all_to_all(jnp.broadcast_to(out_grad[None], (groups, rows, cols)), 'r...]
    ppermute x0 -> x11, waiting for transfers between devices: none -> 32.4 us  [swap(): return lax.ppermute(x, axis, [(i, i ^ bit) for i in range(n)])]
    pallas_call x0 -> x1, Pallas kernels: none -> 31.4 us  [real_sums(): pl.pallas_call(functools.partial(real_kernel, rows), grid=(n // block,),...]
    psum x1 -> x0, blocking collectives: 26.6 us -> none  [on_device(): hidden_grad = lax.psum(hidden_term, 'feat')]
    all_to_all x0 -> x3, starting transfers between devices: none -> 16.6 us  [the longest x1 7.25 us: on_device(): lax.all_to_all(jnp.broadcast_to(packed[None], (groups,) + packed.shape),...]
  transfers between devices with their start and end apart: 5 -> 14, of which waited for: 5 -> 9; matrix products, arithmetic and copies ran while one was open for 2% -> 21% of each run, Pallas kernels for 0% -> 13%
where the time goes in v1:
time: 250 us; the launch traced here: 248 us
  waiting for transfers between devices  89.8 us (36%)
  local copies, waits for them, and re-layouts  39.9 us (16%)
  matrix products  35.2 us (14%)
  Pallas kernels  31.4 us (13%)
  starting transfers between devices  29.5 us (12%)
  other arithmetic  12.4 us (5%)
  blocking collectives  9.07 us (4%)
    all_to_all x1, waiting for transfers between devices, on_device(): lax.all_to_all(jnp.broadcast_to(out_grad[None], (groups, rows, cols)), 'r...  37.2 us
    ppermute x11, waiting for transfers between devices, swap(): return lax.ppermute(x, axis, [(i, i ^ bit) for i in range(n)])  32.4 us
    pallas_call x1, Pallas kernels, real_sums(): pl.pallas_call(functools.partial(real_kernel, rows), grid=(n // block,),...  31.4 us
    all_to_all x1, waiting for transfers between devices, on_device(): lax.all_to_all(feat_grad.reshape(groups, rows, 2 * part), 'rec', 0, 0, ti...  20.3 us
    ppermute x11, starting transfers between devices, swap(): return lax.ppermute(x, axis, [(i, i ^ bit) for i in range(n)])  12.9 us
    dot_general x1, matrix products, on_device(): lax.dot_general(frequencies, pre_grad, (((1,), (1,)), ((), ())), preferre...  10.1 us
    all_gather x1, blocking collectives, on_device(): images = lax.all_gather(own_images, 'feat', axis=0)  9.07 us
    dot_general x1, matrix products, on_device(): syn_pre = jnp.dot(images, frequencies, preferred_element_type=F32)  8.36 us
  transfers between devices with their start and end apart: 14, of which 9 were waited for; matrix products, arithmetic and copies ran while one was open for 21% of the time, Pallas kernels for 13%

profile of v1, /device:TPU:0, one launch (start us, length us, event | category | flops | bytes accessed | tf_op | source)
XLA Modules:
  0.0 248.2 jit_solution(4612680639699977260)
XLA Ops:
  3.1 7.3 %all-to-all-start = ((bf16[8,144,128]{2,1,0:T(8,128)(2,1)}), bf16[8,144,128]{2,1,0:T(8,128)(2,1)}, u32[]{:S(2)}, u32[]{:S(2)}) async-start(bf16[8,144,128]{2,1,0:T(8,128)(2,1)} %broadcast_in_dim.5), calls=%async_computation | async-start | bytes 589824 | tf_op jit(solution)/shard_map/all_to_all | solution.py:140
  10.4 2.6 %fusion.37 = f32[128,2048]{1,0:T(8,128)} fusion(bf16[256,2048]{1,0:T(8,128)(2,1)} %param.18, s32[128]{0:T(128)} %param.16), kind=kOutput, calls=%fused_computation.78 | convolution fusion | flops 134250496 | bytes 2097664 | tf_op jit(solution)/shard_map/dot_general | solution.py:148
  13.0 2.2 fusion.4
  15.2 9.1 %all-gather = bf16[512,768]{1,0:T(8,128)(2,1)} all-gather(bf16[128,768]{1,0:T(8,128)(2,1)S(1)} %fusion.4), channel_id=2, replica_groups=mesh['rec'=8,'feat'=4] {'feat'}, dimensions={0}, use_global_device_ids=true | all-gather | bytes 983040 | tf_op jit(solution)/shard_map/all_gather | solution.py:153
  24.3 2.3 copy.33
  26.5 8.4 %fusion.56 = (f32[128,2048]{1,0:T(8,128)}, f32[128,2048]{1,0:T(8,128)S(1)}, bf16[128,2048]{1,0:T(8,128)(2,1)S(1)}) fusion(bf16[128,3072]{0,1:T(8,128)(2,1)} %bitcast.103, bf16[3072,2048]{1,0:T(8,128)(2,1)} %freq_ref.1), kind=kOutput, calls=%fused_computation.104 | convolution fusion | flops 1616904192 | bytes 15990784 | tf_op jit(solution)/shard_map/dot_general | solution.py:155
  37.5 2.7 %copy.44 = bf16[128,8,512]{0,2,1:T(8,128)(2,1)} copy(bf16[128,8,512]{2,1,0:T(8,128)(2,1)} %pad_maximum_fusion) | data formatting | bytes 2097152 | tf_op jit(solution)/shard_map/convert_element_type | solution.py:159
  40.7 31.4 %shard_map.112 = f32[8,256,512]{2,1,0:T(8,128)} custom-call(s32[1,1536]{1,0:T(1,128)} %reshape.101.labels_ref, bf16[1536,3072]{1,0:T(8,128)(2,1)} %records_ref.1, bf16[3072,2048]{1,0:T(8,128)(2,1)} %freq_ref.1), custom_call_target="tpu_custom_call" | custom-call | flops 22548578304 | bytes 22020096 | tf_op jit(solution)/shard_map/pallas_call | solution.py:78
  72.1 2.9 %bitcast_subtract_fusion = f32[8,256,512]{2,1,0:T(8,128)S(1)} fusion(f32[8,256,512]{2,1,0:T(8,128)} %shard_map.112, bf16[128,8,512]{0,2,1:T(8,128)(2,1)S(1)} %copy-done.3, s32[128]{0:T(128)S(1)} %copy-done.10), kind=kOutput, calls=%fused_computation | convolution fusion | flops 271613952 | bytes 9437696 | tf_op jit(solution)/shard_map/dot_general | solution.py:160
  75.0 2.7 %fusion.58 = (f32[8,128,512]{2,1,0:T(8,128)}, f32[8,128,512]{2,1,0:T(8,128)}) fusion(f32[8,256,512]{2,1,0:T(8,128)S(1)} %bitcast_subtract_fusion), kind=kLoop, calls=%fused_computation.106 | loop fusion | bytes 8388608 | tf_op jit(solution)/shard_map/slice | solution.py:171
  77.7 2.1 fusion.12
  79.9 2.0 collective-permute-start
  81.9 2.1 fusion.11
  84.0 1.5 collective-permute-start.3
  85.4 1.3 dynamic-slice_multiply_fusion
  88.5 6.2 %collective-permute-done = bf16[2,2,128,512]{3,2,0,1:T(8,128)(2,1)} collective-permute-done((bf16[2,2,128,512]{3,2,0,1:T(8,128)(2,1)}, bf16[2,2,128,512]{3,2,0,1:T(8,128)(2,1)}, u32[]{:S(2)}, u32[]{:S(2)}) %collective-permute-start) | collective-permute-done | bytes 524320 | tf_op jit(solution)/shard_map/ppermute | solution.py:102
  94.6 1.6 bitcast_add_fusion.1
  96.3 1.8 collective-permute-start.1
  98.2 1.2 bitcast_add_fusion
  99.5 1.4 collective-permute-start.4
  100.9 3.5 %collective-permute-done.1 = bf16[2,128,512]{2,1,0:T(8,128)(2,1)S(1)} collective-permute-done((bf16[2,128,512]{2,1,0:T(8,128)(2,1)S(1)}, bf16[2,128,512]{2,1,0:T(8,128)(2,1)S(1)}, u32[]{:S(2)}, u32[]{:S(2)}) %collective-permute-start.1) | collective-permute-done | bytes 262176 | tf_op jit(solution)/shard_map/ppermute | solution.py:102
  104.5 2.4 collective-permute-start.2
  107.1 2.4 collective-permute-start.5
  109.5 6.7 %collective-permute-done.2 = bf16[128,512]{1,0:T(8,128)(2,1)S(1)} collective-permute-done((bf16[128,512]{1,0:T(8,128)(2,1)S(1)}, bf16[128,512]{1,0:T(8,128)(2,1)S(1)}, u32[]{:S(2)}, u32[]{:S(2)}) %collective-permute-start.2) | collective-permute-done | bytes 131104 | tf_op jit(solution)/shard_map/ppermute | solution.py:102
  116.2 2.1 collective-permute-done.5
  118.3 1.4 convolution_convert_fusion
  119.8 5.1 %all-to-all-start.1 = ((bf16[8,128,512]{2,1,0:T(8,128)(2,1)}), bf16[8,128,512]{2,1,0:T(8,128)(2,1)}, u32[]{:S(2)}, u32[]{:S(2)}) async-start(bf16[8,128,512]{2,1,0:T(8,128)(2,1)} %bitcast.107), calls=%async_computation.1 | async-start | bytes 2097152 | tf_op jit(solution)/shard_map/all_to_all | solution.py:177
  124.8 2.6 %copy.39 = f32[128,8,256]{0,2,1:T(8,128)} copy(f32[128,8,256]{2,1,0:T(8,128)} %bitcast.98) | data formatting | bytes 2097152 | tf_op jit(solution)/shard_map/reshape | solution.py:158
  127.4 2.5 %copy.43 = f32[128,2048]{0,1:T(8,128)} copy(f32[128,2048]{1,0:T(8,128)} %get-tuple-element.17) | data formatting | bytes 2097152 | tf_op jit(solution)/shard_map/neg | solution.py:180
  130.0 20.3 %all-to-all-done.1 = bf16[8,128,512]{2,1,0:T(8,128)(2,1)} async-done(((bf16[8,128,512]{2,1,0:T(8,128)(2,1)}), bf16[8,128,512]{2,1,0:T(8,128)(2,1)}, u32[]{:S(2)}, u32[]{:S(2)}) %all-to-all-start.1) | async-done | bytes 1048608 | tf_op jit(solution)/shard_map/all_to_all | solution.py:177
  150.2 2.3 copy.37
  152.5 1.5 convert_bitcast_fusion
  154.5 10.1 %convolution_bitcast_fusion = f32[3072,128]{0,1:T(8,128)} fusion(bf16[128,2048]{0,1:T(8,128)(2,1)S(1)} %bitcast.110, bf16[3072,2048]{1,0:T(8,128)(2,1)} %freq_ref.1), kind=kOutput, calls=%fused_computation.1 | convolution fusion | flops 1610612736 | bytes 14680064 | tf_op jit(solution)/shard_map/dot_general | solution.py:184
  164.6 3.1 %copy.40 = f32[3072,128]{1,0:T(8,128)} copy(f32[3072,128]{0,1:T(8,128)} %convolution_bitcast_fusion) | data formatting | bytes 3145728 | tf_op jit(solution)/shard_map/dot_general | solution.py:184
  167.7 1.9 constant_dynamic-slice_fusion
  169.6 1.9 copy.46
  171.6 2.1 constant_dynamic-slice_fusion.1
  173.6 2.3 copy.41
  175.9 1.3 bitcast_add_fusion.2
  179.4 7.0 %collective-permute-done.7 = bf16[768,128]{0,1:T(8,128)(2,1)S(1)} collective-permute-done((bf16[768,128]{0,1:T(8,128)(2,1)}, bf16[768,128]{0,1:T(8,128)(2,1)S(1)}, u32[]{:S(2)}, u32[]{:S(2)}) %collective-permute-start.7) | collective-permute-done | bytes 196640 | tf_op jit(solution)/shard_map/ppermute | solution.py:102
  187.4 1.2 broadcast_in_dim.6
  188.7 4.3 %all-to-all-start.2 = ((bf16[8,128,768]{2,1,0:T(8,128)(2,1)}), bf16[8,128,768]{2,1,0:T(8,128)(2,1)}, u32[]{:S(2)}, u32[]{:S(2)}) async-start(bf16[8,128,768]{2,1,0:T(8,128)(2,1)} %broadcast_in_dim.6), calls=%async_computation.2 | async-start | bytes 3145728 | tf_op jit(solution)/shard_map/all_to_all | solution.py:191
  193.0 37.2 %all-to-all-done.2 = bf16[8,128,768]{2,1,0:T(8,128)(2,1)} async-done(((bf16[8,128,768]{2,1,0:T(8,128)(2,1)}), bf16[8,128,768]{2,1,0:T(8,128)(2,1)}, u32[]{:S(2)}, u32[]{:S(2)}) %all-to-all-start.2) | async-done | bytes 1572896 | tf_op jit(solution)/shard_map/all_to_all | solution.py:191
  230.1 2.0 fusion.23
  233.5 1.1 fusion.43
  235.3 1.3 convolution_add_fusion.1
  236.6 6.9 %collective-permute-done.9 = bf16[512,256]{1,0:T(8,128)(2,1)S(1)} collective-permute-done((bf16[512,256]{1,0:T(8,128)(2,1)S(1)}, bf16[512,256]{1,0:T(8,128)(2,1)S(1)}, u32[]{:S(2)}, u32[]{:S(2)}) %collective-permute-start.9) | collective-permute-done | bytes 262176 | tf_op jit(solution)/shard_map/ppermute | solution.py:102
  243.8 2.9 %fusion.10 = f32[256,768]{1,0:T(8,128)} fusion(bf16[1024,768]{1,0:T(8,128)(2,1)} %bitcast.36, f32[1024,256]{1,0:T(8,128)S(1)} %convolution_add_fusion.1), kind=kOutput, calls=%fused_computation.34 | convolution fusion | flops 403177472 | bytes 3407872 | tf_op jit(solution)/shard_map/dot_general | solution.py:203
  (62 shorter events, 15.4 us)
Async XLA Ops:
  0.6 12.4 %copy-start = (bf16[2048,768]{1,0:T(8,128)(2,1)S(1)}, bf16[2048,768]{1,0:T(8,128)(2,1)}, u32[]{:S(2)}) copy-start(bf16[2048,768]{1,0:T(8,128)(2,1)} %param.19) | copy-start | bytes 9437188
  0.6 12.3 %copy-start.8 = (bf16[128,128]{1,0:T(8,128)(2,1)S(1)}, bf16[128,128]{1,0:T(8,128)(2,1)}, u32[]{:S(2)}) copy-start(bf16[128,128]{1,0:T(8,128)(2,1)} %param.15) | copy-start | bytes 98308
  3.1 84.4 %all-to-all-start = ((bf16[8,144,128]{2,1,0:T(8,128)(2,1)}), bf16[8,144,128]{2,1,0:T(8,128)(2,1)}, u32[]{:S(2)}, u32[]{:S(2)}) async-start(bf16[8,144,128]{2,1,0:T(8,128)(2,1)} %broadcast_in_dim.5), calls=%async_computation | async-start | bytes 589824 | tf_op jit(solution)/shard_map/all_to_all | solution.py:140
  35.2 1.0 copy-start.1
  36.4 3.7 %copy-start.9 = (s32[1536]{0:T(1024)S(1)}, s32[1536]{0:T(1024)}, u32[]{:S(2)}) copy-start(s32[1536]{0:T(1024)} %param.12) | copy-start | bytes 18436
  40.7 31.4 %copy-start.3 = (bf16[128,8,512]{0,2,1:T(8,128)(2,1)S(1)}, bf16[128,8,512]{0,2,1:T(8,128)(2,1)}, u32[]{:S(2)}) copy-start(bf16[128,8,512]{0,2,1:T(8,128)(2,1)} %copy.44) | copy-start | bytes 3145732
  40.7 31.4 %copy-start.10 = (s32[128]{0:T(128)S(1)}, s32[128]{0:T(128)}, u32[]{:S(2)}) copy-start(s32[128]{0:T(128)} %param.16) | copy-start | bytes 1540
  79.9 14.8 %collective-permute-start = (bf16[2,2,128,512]{3,2,0,1:T(8,128)(2,1)}, bf16[2,2,128,512]{3,2,0,1:T(8,128)(2,1)}, u32[]{:S(2)}, u32[]{:S(2)}) collective-permute-start(bf16[2,2,128,512]{3,2,0,1:T(8,128)(2,1)} %fusion.12), channel_id=1, source_target_pairs={{0,4},{4,0},{8,12},{12,8},{16,20},{20,16},{24,28},{28,24},{1,5},{5... | collective-permute-start | bytes 1572872 | tf_op jit(solution)/shard_map/ppermute | solution.py:102
  84.0 14.2 %collective-permute-start.3 = (bf16[2,2,128,512]{3,2,1,0:T(8,128)(2,1)}, bf16[2,2,128,512]{3,2,1,0:T(8,128)(2,1)}, u32[]{:S(2)}, u32[]{:S(2)}) collective-permute-start(bf16[2,2,128,512]{3,2,1,0:T(8,128)(2,1)} %fusion.11), channel_id=1, source_target_pairs={{0,8},{4,12},{8,0},{12,4},{16,24},{20,28},{24,16},{28,20},{1,9},{5... | collective-permute-start | bytes 1572872 | tf_op jit(solution)/shard_map/ppermute | solution.py:102
  87.6 10.6 %copy-start.2 = (f32[8,128,512]{2,1,0:T(8,128)S(1)}, f32[8,128,512]{2,1,0:T(8,128)}, u32[]{:S(2)}) copy-start(f32[8,128,512]{2,1,0:T(8,128)} %get-tuple-element.16) | copy-start | bytes 6291460
  96.3 8.1 %collective-permute-start.1 = (bf16[2,128,512]{2,1,0:T(8,128)(2,1)S(1)}, bf16[2,128,512]{2,1,0:T(8,128)(2,1)S(1)}, u32[]{:S(2)}, u32[]{:S(2)}) collective-permute-start(bf16[2,128,512]{2,1,0:T(8,128)(2,1)S(1)} %fusion.27), channel_id=1, source_target_pairs={{0,8},{4,12},{8,0},{12,4},{16,24},{20,28},{24,16},{28,20},{1,9},{5... | collective-permute-start | bytes 786440 | tf_op jit(solution)/shard_map/ppermute | solution.py:102
  99.5 18.9 %copy-start.7 = (f32[32,8,2,256]{3,1,2,0:T(8,128)S(1)}, f32[32,8,2,256]{3,1,2,0:T(8,128)}, u32[]{:S(2)}) copy-start(f32[32,8,2,256]{3,1,2,0:T(8,128)} %copy.49) | copy-start | bytes 1572868
  99.5 7.5 %collective-permute-start.4 = (bf16[2,128,512]{2,1,0:T(8,128)(2,1)S(1)}, bf16[2,128,512]{2,1,0:T(8,128)(2,1)S(1)}, u32[]{:S(2)}, u32[]{:S(2)}) collective-permute-start(bf16[2,128,512]{2,1,0:T(8,128)(2,1)S(1)} %fusion.28), channel_id=1, source_target_pairs={{0,4},{4,0},{8,12},{12,8},{16,20},{20,16},{24,28},{28,24},{1,5},{5... | collective-permute-start | bytes 786440 | tf_op jit(solution)/shard_map/ppermute | solution.py:102
  104.5 11.7 %collective-permute-start.2 = (bf16[128,512]{1,0:T(8,128)(2,1)S(1)}, bf16[128,512]{1,0:T(8,128)(2,1)S(1)}, u32[]{:S(2)}, u32[]{:S(2)}) collective-permute-start(bf16[128,512]{1,0:T(8,128)(2,1)S(1)} %fusion.34), channel_id=1, source_target_pairs={{0,16},{4,20},{8,24},{12,28},{16,0},{20,4},{24,8},{28,12},{1,17},{... | collective-permute-start | bytes 393224 | tf_op jit(solution)/shard_map/ppermute | solution.py:102
  107.1 11.2 %collective-permute-start.5 = (bf16[128,512]{1,0:T(8,128)(2,1)S(1)}, bf16[128,512]{1,0:T(8,128)(2,1)S(1)}, u32[]{:S(2)}, u32[]{:S(2)}) collective-permute-start(bf16[128,512]{1,0:T(8,128)(2,1)S(1)} %fusion.35), channel_id=1, source_target_pairs={{0,16},{4,20},{8,24},{12,28},{16,0},{20,4},{24,8},{28,12},{1,17},{... | collective-permute-start | bytes 393224 | tf_op jit(solution)/shard_map/ppermute | solution.py:102
  119.8 30.4 %all-to-all-start.1 = ((bf16[8,128,512]{2,1,0:T(8,128)(2,1)}), bf16[8,128,512]{2,1,0:T(8,128)(2,1)}, u32[]{:S(2)}, u32[]{:S(2)}) async-start(bf16[8,128,512]{2,1,0:T(8,128)(2,1)} %bitcast.107), calls=%async_computation.1 | async-start | bytes 2097152 | tf_op jit(solution)/shard_map/all_to_all | solution.py:177
  152.5 1.5 copy-start.4
  152.5 1.9 copy-start.5
  171.6 4.4 %collective-permute-start.6 = (bf16[2,768,128]{1,2,0:T(8,128)(2,1)}, bf16[2,768,128]{1,2,0:T(8,128)(2,1)}, u32[]{:S(2)}, u32[]{:S(2)}) collective-permute-start(bf16[2,768,128]{1,2,0:T(8,128)(2,1)} %bitcast.117), channel_id=1, source_target_pairs={{0,1},{1,0},{2,3},{3,2},{4,5},{5,4},{6,7},{7,6},{8,9},{9,8},{10,11... | collective-permute-start | bytes 1179656 | tf_op jit(solution)/shard_map/ppermute | solution.py:102
  177.2 0.9 copy-start.6
  178.8 7.5 %collective-permute-start.7 = (bf16[768,128]{0,1:T(8,128)(2,1)}, bf16[768,128]{0,1:T(8,128)(2,1)S(1)}, u32[]{:S(2)}, u32[]{:S(2)}) collective-permute-start(bf16[768,128]{0,1:T(8,128)(2,1)} %fusion.33), channel_id=1, source_target_pairs={{0,2},{1,3},{2,0},{3,1},{4,6},{5,7},{6,4},{7,5},{8,10},{9,11},{10,... | collective-permute-start | bytes 589832 | tf_op jit(solution)/shard_map/ppermute | solution.py:102
  188.7 41.5 %all-to-all-start.2 = ((bf16[8,128,768]{2,1,0:T(8,128)(2,1)}), bf16[8,128,768]{2,1,0:T(8,128)(2,1)}, u32[]{:S(2)}, u32[]{:S(2)}) async-start(bf16[8,128,768]{2,1,0:T(8,128)(2,1)} %broadcast_in_dim.6), calls=%async_computation.2 | async-start | bytes 3145728 | tf_op jit(solution)/shard_map/all_to_all | solution.py:191
  232.2 2.4 collective-permute-start.8
  234.7 8.8 %collective-permute-start.9 = (bf16[512,256]{1,0:T(8,128)(2,1)S(1)}, bf16[512,256]{1,0:T(8,128)(2,1)S(1)}, u32[]{:S(2)}, u32[]{:S(2)}) collective-permute-start(bf16[512,256]{1,0:T(8,128)(2,1)S(1)} %fusion.15), channel_id=1, source_target_pairs={{0,2},{1,3},{2,0},{3,1},{4,6},{5,7},{6,4},{7,5},{8,10},{9,11},{10,... | collective-permute-start | bytes 786440 | tf_op jit(solution)/shard_map/ppermute | solution.py:102
  243.8 3.0 %collective-permute-start.10 = (f32[384,256]{1,0:T(8,128)S(1)}, f32[384,256]{1,0:T(8,128)S(1)}, u32[]{:S(2)}, u32[]{:S(2)}) collective-permute-start(f32[384,256]{1,0:T(8,128)S(1)} %fusion.21), channel_id=1, source_target_pairs={{0,1},{1,0},{2,3},{3,2},{4,5},{5,4},{6,7},{7,6},{8,9},{9,8},{10,11... | collective-permute-start | bytes 1179656 | tf_op jit(solution)/shard_map/ppermute | solution.py:102

commit v2 on v1

--- a/solution.py
+++ b/solution.py
@@ -120,7 +120,7 @@
     return x
 
 
-def on_device(
+def general(
     records, real_labels, frequencies, class_noise, latents, syn_labels, w_latent, class_embed, w_out
 ):
     classes = class_embed.shape[0]
@@ -226,7 +226,520 @@
     return grad_w_out, grads[:dz], grads[dz:]
 
 
+def block(shape, index):
+    return pl.BlockSpec(shape, index)
+
+
+def first_kernel(labels_ref, records_ref, freq_ref, out_ref, table_ref):
+    classes, total = table_ref.shape
+
+    @pl.when(pl.program_id(0) == 0)
+    def _():
+        ids = lax.broadcasted_iota(jnp.int32, (classes, total), 0)
+        table_ref[...] = jnp.where(ids == labels_ref[...], 1.0, 0.0).astype(BF)
+
+    freq = freq_ref[...]
+    half = total // 2
+    before = jnp.dot(records_ref[:half, :], freq, preferred_element_type=F32)
+    after = jnp.dot(records_ref[half:, :], freq, preferred_element_type=F32)
+    acc = sums(table_ref[:, :half], before) + sums(table_ref[:, half:], after)
+    out_ref[0] = acc
+
+
+def sums(table, pre):
+    co, si = cos_sin(pre)
+    phi = jnp.concatenate([co.astype(BF), si.astype(BF)], axis=1)
+    return jnp.dot(table, phi, preferred_element_type=F32)
+
+
+def first_sums(labels, records, freq, classes, size):
+    k = records.shape[1]
+    n = freq.shape[1]
+    return pl.pallas_call(
+        first_kernel,
+        grid=(n // 512,),
+        in_specs=[
+            block((1, size), lambda j: (0, 0)),
+            block((size, k), lambda j: (0, 0)),
+            block((k, 512), lambda j: (0, j)),
+        ],
+        out_specs=block((1, classes, 1024), lambda j: (j, 0, 0)),
+        out_shape=jax.ShapeDtypeStruct((n // 512, classes, 1024), F32),
+        scratch_shapes=[pltpu.VMEM((classes, size), BF)],
+        compiler_params=pltpu.CompilerParams(vmem_limit_bytes=48 * 2**20),
+        cost_estimate=pl.CostEstimate(
+            flops=2 * size * n * (k + 2 * classes), bytes_accessed=2 * (size * k + k * n), transcendentals=0
+        ),
+    )(labels.reshape(1, -1), records, freq)
+
+
+def second_kernel(
+    masks,
+    real_total,
+    syn_total,
+    me_ref,
+    real_labels_ref,
+    syn_labels_ref,
+    *refs,
+):
+    count = len(masks)
+    images = refs[:count]
+    blocks = refs[count : count + 2]
+    freq_ref, part_ref, send_a, keep_a, send_b, keep_b, cs_ref, real_table, syn_table = refs[count + 2 :]
+    classes, total = real_table.shape
+    feat, x, z_low = me_ref[0], me_ref[1], me_ref[2]
+    step = pl.program_id(0)
+
+    @pl.when(step == 0)
+    def _():
+        ids = lax.broadcasted_iota(jnp.int32, (classes, total), 0)
+        real_table[...] = jnp.where(ids == real_labels_ref[...], 1.0, 0.0).astype(BF)
+        ids = lax.broadcasted_iota(jnp.int32, syn_table.shape, 0)
+        syn_table[...] = jnp.where(ids == syn_labels_ref[...], 1.0, 0.0).astype(BF)
+
+    cols = images[0].shape[1]
+    syn_pre = None
+    for mask, image in zip(masks, images):
+        at = pl.multiple_of((feat ^ mask) * cols, 128)
+        d = jnp.dot(image[...], freq_ref[pl.ds(at, cols), :], preferred_element_type=F32)
+        syn_pre = d if syn_pre is None else syn_pre + d
+    freq = freq_ref[...]
+    size = total // 2
+    pre0 = jnp.dot(blocks[0][...], freq, preferred_element_type=F32)
+    co, si = cos_sin(syn_pre)
+    cs_ref[0] = co
+    cs_ref[1] = si
+    phi = jnp.concatenate([co.astype(BF), si.astype(BF)], axis=1)
+    syn = jnp.dot(syn_table[...], phi, preferred_element_type=F32)
+    pre1 = jnp.dot(blocks[1][...], freq, preferred_element_type=F32)
+    acc = part_ref[0] + sums(real_table[:, :size], pre0)
+    acc = acc + sums(real_table[:, size:], pre1)
+    gap = syn * (1.0 / syn_total) - acc * (1.0 / real_total)
+    zero = jnp.concatenate([gap[:, :256], gap[:, 512:768]], axis=1)
+    one = jnp.concatenate([gap[:, 256:512], gap[:, 768:]], axis=1)
+    half = classes // 2
+    keep_a[0] = jnp.where(x == 0, zero[:half], one[:half])
+    send_a[0] = jnp.where(x == 0, one[:half], zero[:half]).astype(BF)
+    high = step // 2
+
+    @pl.when(step % 2 == z_low)
+    def _():
+        keep_b[high, 0] = zero[half:]
+        keep_b[high, 1] = one[half:]
+
+    @pl.when(step % 2 != z_low)
+    def _():
+        send_b[high, 0] = zero[half:].astype(BF)
+        send_b[high, 1] = one[half:].astype(BF)
+
+
+def second_sums(me, real_labels, syn_labels, masks, images, records, size, freq, part, totals):
+    k = records.shape[1]
+    n = freq.shape[1]
+    rows, cols = images[0].shape
+    classes = part.shape[1]
+    half = classes // 2
+    grid_spec = pltpu.PrefetchScalarGridSpec(
+        num_scalar_prefetch=1,
+        grid=(n // 512,),
+        in_specs=[
+            block((1, 2 * size), lambda j, me: (0, 0)),
+            block((1, rows), lambda j, me: (0, 0)),
+        ]
+        + [block((rows, cols), lambda j, me: (0, 0)) for _ in images]
+        + [
+            block((size, k), lambda j, me: (1, 0)),
+            block((size, k), lambda j, me: (2, 0)),
+            block((k, 512), lambda j, me: (0, j)),
+            block((1, classes, 1024), lambda j, me: (j, 0, 0)),
+        ],
+        out_specs=[
+            block((1, half, 512), lambda j, me: (j, 0, 0)),
+            block((1, half, 512), lambda j, me: (j, 0, 0)),
+            block((2, 2, half, 512), lambda j, me: (0, 0, 0, 0)),
+            block((2, 2, half, 512), lambda j, me: (0, 0, 0, 0)),
+            block((2, rows, 512), lambda j, me: (0, 0, j)),
+        ],
+        scratch_shapes=[pltpu.VMEM((classes, 2 * size), BF), pltpu.VMEM((classes, rows), BF)],
+    )
+    return pl.pallas_call(
+        functools.partial(second_kernel, masks, *totals),
+        grid_spec=grid_spec,
+        out_shape=[
+            jax.ShapeDtypeStruct((4, half, 512), BF),
+            jax.ShapeDtypeStruct((4, half, 512), F32),
+            jax.ShapeDtypeStruct((2, 2, half, 512), BF),
+            jax.ShapeDtypeStruct((2, 2, half, 512), F32),
+            jax.ShapeDtypeStruct((2, rows, n), F32),
+        ],
+        compiler_params=pltpu.CompilerParams(vmem_limit_bytes=56 * 2**20),
+        cost_estimate=pl.CostEstimate(
+            flops=2 * (2 * size + rows) * n * (k + 2 * classes),
+            bytes_accessed=2 * (2 * size * k + k * n) + 4 * classes * n * 2,
+            transcendentals=0,
+        ),
+    )(me, real_labels.reshape(1, -1), syn_labels.reshape(1, -1), *images, records, records, freq, part)
+
+
+def stage_two_kernel(me_ref, ka_s, ka_k, ra_s, ra_k, kb_s, kb_k, rb_s, rb_k, sa, na, sb, nb):
+    sa[0] = (ka_s[0, 0] + ra_s[0, 0].astype(F32)).astype(BF)
+    na[0] = ka_k[0, 0] + ra_k[0, 0].astype(F32)
+    sb[0] = (kb_s[0, 0] + rb_s[0, 0].astype(F32)).astype(BF)
+    nb[0] = kb_k[0, 0] + rb_k[0, 0].astype(F32)
+
+
+def stage_two(me, keep_a, got_a, keep_b, got_b):
+    half, width = keep_b.shape[2:]
+    shape = (1, 1, half, width)
+    keep_a = keep_a.reshape(2, 2, half, width)
+    got_a = got_a.reshape(2, 2, half, width)
+    low = lambda flip: block(shape, lambda h, me: (h, me[2] ^ flip, 0, 0))
+    xs = lambda flip: block(shape, lambda h, me: (h, me[1] ^ flip, 0, 0))
+    out = block((1, half, width), lambda h, me: (h, 0, 0))
+    spec = pltpu.PrefetchScalarGridSpec(
+        num_scalar_prefetch=1,
+        grid=(2,),
+        in_specs=[low(1), low(0), low(1), low(0), xs(1), xs(0), xs(1), xs(0)],
+        out_specs=[out] * 4,
+    )
+    kinds = [BF, F32, BF, F32]
+    return pl.pallas_call(
+        stage_two_kernel,
+        grid_spec=spec,
+        out_shape=[jax.ShapeDtypeStruct((2, half, width), t) for t in kinds],
+        cost_estimate=pl.CostEstimate(flops=0, bytes_accessed=4 * 2**20, transcendentals=0),
+    )(me, keep_a, keep_a, got_a, got_a, keep_b, keep_b, got_b, got_b)
+
+
+def stage_three_kernel(me_ref, na_s, na_k, ga_s, ga_k, nb_s, nb_k, gb_s, gb_k, send, keep):
+    half = na_s.shape[1]
+    send[:half] = (na_s[0] + ga_s[0].astype(F32)).astype(BF)
+    keep[:half] = na_k[0] + ga_k[0].astype(F32)
+    send[half:] = (nb_s[0] + gb_s[0].astype(F32)).astype(BF)
+    keep[half:] = nb_k[0] + gb_k[0].astype(F32)
+
+
+def stage_three(me, next_a, got_a, next_b, got_b):
+    _, half, width = next_a.shape
+    high = lambda flip: block((1, half, width), lambda h, me: (me[3] ^ flip, 0, 0))
+    out = block((2 * half, width), lambda h, me: (0, 0))
+    spec = pltpu.PrefetchScalarGridSpec(
+        num_scalar_prefetch=1,
+        grid=(1,),
+        in_specs=[high(1), high(0)] * 4,
+        out_specs=[out, out],
+    )
+    return pl.pallas_call(
+        stage_three_kernel,
+        grid_spec=spec,
+        out_shape=[jax.ShapeDtypeStruct((2 * half, width), t) for t in (BF, F32)],
+        cost_estimate=pl.CostEstimate(flops=0, bytes_accessed=3 * 2**20, transcendentals=0),
+    )(me, next_a, next_a, got_a, got_a, next_b, next_b, got_b, got_b)
+
+
+def gap_kernel(real_total, me_ref, keep_ref, got_ref, noise_ref, labels_ref, out_ref):
+    classes = keep_ref.shape[0]
+    part = noise_ref.shape[2]
+    noise = jnp.concatenate([noise_ref[:, 0, :], noise_ref[:, 1, :]], axis=1)
+    gap = keep_ref[...] + got_ref[...].astype(F32) - noise * (1.0 / real_total)
+    gap = (16.0 * gap).astype(BF)
+    ids = lax.broadcasted_iota(jnp.int32, (labels_ref.shape[0], classes), 1)
+    table = jnp.where(ids == labels_ref[...], 1.0, 0.0).astype(BF)
+    out_ref[...] = jnp.dot(table, gap, preferred_element_type=F32).astype(BF)
+
+
+def gap_rows(me, keep, got, noise, labels, real_total):
+    classes, width = keep.shape
+    total = labels.shape[0]
+    spec = pltpu.PrefetchScalarGridSpec(
+        num_scalar_prefetch=1,
+        grid=(1,),
+        in_specs=[
+            block((classes, width), lambda h, me: (0, 0)),
+            block((classes, width), lambda h, me: (0, 0)),
+            block((classes, 2, width // 2), lambda h, me: (0, 0, me[4])),
+            block((total, 1), lambda h, me: (0, 0)),
+        ],
+        out_specs=block((total, width), lambda h, me: (0, 0)),
+    )
+    return pl.pallas_call(
+        functools.partial(gap_kernel, real_total),
+        grid_spec=spec,
+        out_shape=jax.ShapeDtypeStruct((total, width), BF),
+        cost_estimate=pl.CostEstimate(
+            flops=2 * total * classes * width, bytes_accessed=3 * 2**20, transcendentals=0
+        ),
+    )(me, keep, got, noise, labels.reshape(total, 1))
+
+
+NT = (((1,), (1,)), ((), ()))
+
+
+def image_kernel(me_ref, cs_ref, rows_ref, freq_ref, send_ref, keep_ref, pre_ref):
+    step = pl.program_id(0)
+    owners, _, width = rows_ref.shape
+    part = width // 2
+
+    @pl.when(step == 0)
+    def _():
+        for o in range(owners):
+            at = slice(o * part, (o + 1) * part)
+            grad = rows_ref[o].astype(F32)
+            pre = cs_ref[0, :, at] * grad[:, part:] - cs_ref[1, :, at] * grad[:, :part]
+            pre_ref[:, at] = pre.astype(BF)
+
+    out = lax.dot_general(freq_ref[...], pre_ref[...], NT, preferred_element_type=F32)
+
+    @pl.when(step < 2)
+    def _():
+        send_ref[0] = out.astype(BF)
+
+    @pl.when(step >= 2)
+    def _():
+        keep_ref[0] = out
+
+
+def image_grads(me, cs, feat_rows, freq, cols):
+    k, n = freq.shape
+    owners, rows, width = feat_rows.shape
+    spec = pltpu.PrefetchScalarGridSpec(
+        num_scalar_prefetch=1,
+        grid=(4,),
+        in_specs=[
+            block((2, rows, n), lambda s, me: (0, 0, 0)),
+            block((owners, rows, width), lambda s, me: (0, 0, 0)),
+            block((cols, n), lambda s, me: ((s % 2) * 2 + ((me[0] % 2) ^ (1 - s // 2)), 0)),
+        ],
+        out_specs=[
+            block((1, cols, rows), lambda s, me: (jnp.minimum(s, 1), 0, 0)),
+            block((1, cols, rows), lambda s, me: (jnp.maximum(s - 2, 0), 0, 0)),
+        ],
+        scratch_shapes=[pltpu.VMEM((rows, n), BF)],
+    )
+    return pl.pallas_call(
+        image_kernel,
+        grid_spec=spec,
+        out_shape=[jax.ShapeDtypeStruct((2, cols, rows), t) for t in (BF, F32)],
+        compiler_params=pltpu.CompilerParams(vmem_limit_bytes=40 * 2**20),
+        cost_estimate=pl.CostEstimate(flops=2 * k * n * rows, bytes_accessed=2 * k * n, transcendentals=0),
+    )(me, cs, feat_rows, freq)
+
+
+def split_y_kernel(me_ref, keep_s, keep_k, got_s, got_k, send, keep):
+    send[...] = (keep_s[0] + got_s[0].astype(F32)).astype(BF)
+    keep[...] = keep_k[0] + got_k[0].astype(F32)
+
+
+def split_y(me, keep, got):
+    _, cols, rows = keep.shape
+    at = lambda flip: block((1, cols, rows), lambda h, me: ((me[0] // 2) ^ flip, 0, 0))
+    out = block((cols, rows), lambda h, me: (0, 0))
+    spec = pltpu.PrefetchScalarGridSpec(
+        num_scalar_prefetch=1, grid=(1,), in_specs=[at(1), at(0)] * 2, out_specs=[out, out]
+    )
+    return pl.pallas_call(
+        split_y_kernel,
+        grid_spec=spec,
+        out_shape=[jax.ShapeDtypeStruct((cols, rows), t) for t in (BF, F32)],
+        cost_estimate=pl.CostEstimate(flops=0, bytes_accessed=2**20, transcendentals=0),
+    )(me, keep, keep, got, got)
+
+
+def out_kernel(keep, got, image, out):
+    grad = (keep[...] + got[...].astype(F32)).T
+    grad = grad * (1.0 - jnp.square(image[...].astype(F32)))
+    grad = grad.astype(BF)
+    for r in range(out.shape[0]):
+        out[r] = grad
+
+
+def out_grads(keep, got, image, copies):
+    rows, cols = image.shape
+    return pl.pallas_call(
+        out_kernel,
+        out_shape=jax.ShapeDtypeStruct((copies, rows, cols), BF),
+        cost_estimate=pl.CostEstimate(flops=0, bytes_accessed=2**20, transcendentals=0),
+    )(keep, got, image)
+
+
+def hidden_kernel(me_ref, w_ref, grad_ref, send, keep):
+    core = me_ref[0] % 2
+    out = lax.dot_general(w_ref[...], grad_ref[0], NT, preferred_element_type=F32)
+    half = out.shape[0] // 2
+    keep[0] = jnp.where(core == 0, out[:half], out[half:])
+    send[0] = jnp.where(core == 0, out[half:], out[:half]).astype(BF)
+
+
+def hidden_grads(me, w_out, out_grad):
+    groups, rows, cols = out_grad.shape
+    hid = w_out.shape[0]
+    mine = hid // groups
+    out = block((1, mine // 2, rows), lambda r, me: (r, 0, 0))
+    spec = pltpu.PrefetchScalarGridSpec(
+        num_scalar_prefetch=1,
+        grid=(groups,),
+        in_specs=[
+            block((mine, cols), lambda r, me: (r, 0)),
+            block((1, rows, cols), lambda r, me: (0, 0, 0)),
+        ],
+        out_specs=[out, out],
+    )
+    return pl.pallas_call(
+        hidden_kernel,
+        grid_spec=spec,
+        out_shape=[jax.ShapeDtypeStruct((groups, mine // 2, rows), t) for t in (BF, F32)],
+        cost_estimate=pl.CostEstimate(
+            flops=2 * hid * cols * rows, bytes_accessed=2 * hid * cols, transcendentals=0
+        ),
+    )(me, w_out, out_grad)
+
+
+def add_kernel(a, b, out):
+    out[...] = (a[...].astype(F32) + b[...].astype(F32)).astype(out.dtype)
+
+
+def add(a, b, kind):
+    return pl.pallas_call(
+        add_kernel,
+        out_shape=jax.ShapeDtypeStruct(a.shape, kind),
+        cost_estimate=pl.CostEstimate(flops=0, bytes_accessed=2**20, transcendentals=0),
+    )(a, b)
+
+
+def weight_kernel(hidden_ref, grad_ref, out_ref):
+    groups, rows, cols = grad_ref.shape
+    out_ref[...] = jnp.dot(
+        hidden_ref[...], grad_ref[...].reshape(groups * rows, cols), preferred_element_type=F32
+    )
+
+
+def weight_grads(hidden, grad):
+    groups, rows, cols = grad.shape
+    mine = hidden.shape[0]
+    return pl.pallas_call(
+        weight_kernel,
+        out_shape=jax.ShapeDtypeStruct((mine, cols), F32),
+        cost_estimate=pl.CostEstimate(
+            flops=2 * mine * groups * rows * cols, bytes_accessed=4 * 2**20, transcendentals=0
+        ),
+    )(hidden, grad)
+
+
+def last_kernel(me_ref, got_ref, preact_ref, lhs_ref, out_ref):
+    groups, width, rows = got_ref.shape
+    acc = None
+    for g in range(groups):
+        at = slice(g * rows, (g + 1) * rows)
+        grad = jnp.where(preact_ref[:, at] > 0, got_ref[g].astype(F32), 0.0).astype(BF)
+        d = lax.dot_general(lhs_ref[:, at], grad, NT, preferred_element_type=F32)
+        acc = d if acc is None else acc + d
+    out_ref[...] = acc
+
+
+def last_grads(me, got, preact, lhs):
+    groups, width, rows = got.shape
+    count, total = lhs.shape
+    spec = pltpu.PrefetchScalarGridSpec(
+        num_scalar_prefetch=1,
+        grid=(1,),
+        in_specs=[
+            block((groups, width, rows), lambda h, me: (0, 0, 0)),
+            block((width, total), lambda h, me: (me[0] % 2, 0)),
+            block((count, total), lambda h, me: (0, 0)),
+        ],
+        out_specs=block((count, width), lambda h, me: (0, 0)),
+    )
+    return pl.pallas_call(
+        last_kernel,
+        grid_spec=spec,
+        out_shape=jax.ShapeDtypeStruct((count, width), F32),
+        cost_estimate=pl.CostEstimate(
+            flops=2 * total * count * width, bytes_accessed=2 * 2**20, transcendentals=0
+        ),
+    )(me, got, preact, lhs)
+
+
+def eight_by_four(
+    records, real_labels, frequencies, class_noise, latents, syn_labels, w_latent, class_embed, w_out
+):
+    classes, hid = class_embed.shape
+    groups = lax.axis_size("rec")
+    rec = lax.axis_index("rec")
+    feat = lax.axis_index("feat")
+    rows, dz = latents.shape
+    cols = w_out.shape[1]
+    real_total = records.shape[0] * groups
+    syn_total = rows * groups
+    me = jnp.stack([feat, rec % 2, (rec // 2) % 2, rec // 4, rec]).astype(jnp.int32)
+
+    table = one_hot(syn_labels, classes, BF)
+    preact = jnp.dot(latents, w_latent, preferred_element_type=F32) + jnp.dot(
+        table, class_embed, preferred_element_type=F32
+    )
+    hidden = jnp.maximum(preact, 0.0).astype(BF)
+    own = jnp.tanh(jnp.dot(hidden, w_out, preferred_element_type=F32)).astype(BF)
+    far = swap(own, "feat", 2)
+    images = [own, far, swap(own, "feat", 1), swap(far, "feat", 1)]
+
+    label_row = jnp.zeros((16, dz), BF).at[0, :].set(syn_labels.astype(BF))
+    packed = jnp.concatenate([latents, label_row], axis=0)
+    packed = lax.all_to_all(
+        jnp.broadcast_to(packed[None], (groups,) + packed.shape), "rec", 0, 0, tiled=True
+    )
+
+    size = records.shape[0] // 3
+    part = first_sums(real_labels[:size], records, frequencies, classes, size)
+    send_a, keep_a, send_b, keep_b, cs = second_sums(
+        me, real_labels[size:], syn_labels, (0, 2, 1, 3), images, records, size, frequencies, part,
+        (real_total, syn_total),
+    )
+    got_a = swap(send_a, "rec", 1)
+    got_b = swap(send_b, "rec", 2)
+
+    all_latents = packed[:, :rows].reshape(syn_total, dz)
+    all_labels = packed[:, rows].reshape(syn_total).astype(jnp.int32)
+    all_table = one_hot(all_labels, classes, BF)
+    mine = hid // groups
+    lhs = jnp.concatenate([all_latents, all_table], axis=1).T
+    w = jnp.concatenate(
+        [
+            lax.dynamic_slice_in_dim(w_latent, rec * mine, mine, 1),
+            lax.dynamic_slice_in_dim(class_embed, rec * mine, mine, 1),
+        ],
+        axis=0,
+    )
+    all_preact = lax.dot_general(w, lhs, (((0,), (0,)), ((), ())), preferred_element_type=F32)
+    all_hidden = jnp.maximum(all_preact, 0.0).astype(BF)
+
+    send_a, next_a, send_b, next_b = stage_two(me, keep_a, got_a, keep_b, got_b)
+    got_a = swap(send_a, "rec", 2)
+    got_b = swap(send_b, "rec", 1)
+    send, keep = stage_three(me, next_a, got_a, next_b, got_b)
+    got = swap(send, "rec", 4)
+    feat_grad = gap_rows(me, keep, got, class_noise, all_labels, real_total)
+    feat_grad = lax.all_to_all(feat_grad.reshape(groups, rows, -1), "rec", 0, 0, tiled=True)
+
+    send, keep = image_grads(me, cs, feat_grad, frequencies, cols)
+    send, keep = split_y(me, keep, swap(send, "feat", 1))
+    out_grad = out_grads(keep, swap(send, "feat", 2), own, groups)
+
+    all_grad = lax.all_to_all(out_grad, "rec", 0, 0, tiled=True)
+    send, keep = hidden_grads(me, w_out, out_grad)
+    part_grad = add(keep, swap(send, "feat", 1), BF)
+    part_grad = add(part_grad, swap(part_grad, "feat", 2), BF)
+    part_grad = lax.all_to_all(part_grad, "rec", 0, 0, tiled=True)
+    grads = last_grads(me, part_grad, all_preact, lhs)
+    other = swap(grads, "feat", 1)
+    core = feat % 2
+    grads = jnp.concatenate(
+        [jnp.where(core == 0, grads, other), jnp.where(core == 0, other, grads)], axis=1
+    )
+    grad_w_out = weight_grads(all_hidden, all_grad)
+    return grad_w_out, grads[:dz], grads[dz:]
+
+
 def solution(mesh):
+    shape = (mesh.shape["rec"], mesh.shape["feat"])
     in_specs = (
         P("rec", None),
         P("rec"),
@@ -240,5 +753,5 @@
     )
     out_specs = (P("rec", "feat"), P(None, "rec"), P(None, "rec"))
     return jax.shard_map(
-        on_device, mesh=mesh, in_specs=in_specs, out_specs=out_specs, check_vma=False
-    )
+        eight_by_four if shape == (8, 4) else general, mesh=mesh, in_specs=in_specs, out_specs=out_specs, check_vma=False
+    )

time: 250 us -> 246 us (0.984)
  Pallas kernels: 31.4 us -> 81.9 us
  blocking collectives: 9.07 us -> 41.9 us
  matrix products: 35.2 us -> 5.32 us
  local copies, waits for them, and re-layouts: 39.9 us -> 14.3 us
  waiting for transfers between devices: 89.8 us -> 74.2 us
  other arithmetic: 12.4 us -> 3.4 us
  starting transfers between devices: 29.5 us -> 22.7 us
    pallas_call x1 -> x13, Pallas kernels: 31.4 us -> 81.9 us  [the longest x1 27.8 us: second_sums(): pl.pallas_call(functools.partial(second_kernel, masks, *totals), grid_spe...]
    all_to_all x0 -> x2, blocking collectives: none -> 41.9 us  [the longest x1 29.2 us: eight_by_four(): lax.all_to_all(feat_grad.reshape(groups, rows, -1), 'rec', 0, 0, tiled=True)]
    all_to_all x3 -> x2, waiting for transfers between devices: 57.4 us -> 26.6 us  [the longest x1 26.6 us: eight_by_four(): all_grad = lax.all_to_all(out_grad, 'rec', 0, 0, tiled=True)]
    dot_general x11 -> x3, matrix products: 35.2 us -> 5.32 us  [the longest x1 2.7 us: eight_by_four(): jnp.dot(hidden, w_out, preferred_element_type=F32)]
    ppermute x11 -> x13, waiting for transfers between devices: 32.4 us -> 47.6 us  [swap(): return lax.ppermute(x, axis, [(i, i ^ bit) for i in range(n)])]
    all_to_all x3 -> x2, starting transfers between devices: 16.6 us -> 7.45 us  [the longest x1 3.87 us: eight_by_four(): lax.all_to_all(jnp.broadcast_to(packed[None], (groups,) + packed.shape),...]
    all_gather x1 -> x0, blocking collectives: 9.07 us -> none  [on_device(): images = lax.all_gather(own_images, 'feat', axis=0)]
    convert_element_type x9 -> x1, local copies, waits for them, and re-layouts: 7.75 us -> 1.06 us  [eight_by_four(): all_labels = packed[:, rows].reshape(syn_total).astype(jnp.int32)]
  transfers between devices with their start and end apart: 14 -> 15, of which waited for: 9 -> 12; matrix products, arithmetic and copies ran while one was open for 21% -> 3% of each run, Pallas kernels for 13% -> 10%
where the time goes in v2:
time: 246 us; the launch traced here: 245 us
  Pallas kernels  81.9 us (33%)
  waiting for transfers between devices  74.2 us (30%)
  blocking collectives  41.9 us (17%)
  starting transfers between devices  22.7 us (9%)
  local copies, waits for them, and re-layouts  14.3 us (6%)
  matrix products  5.32 us (2%)
  other arithmetic  3.4 us (1%)
    ppermute x13, waiting for transfers between devices, swap(): return lax.ppermute(x, axis, [(i, i ^ bit) for i in range(n)])  47.6 us
    all_to_all x1, blocking collectives, eight_by_four(): lax.all_to_all(feat_grad.reshape(groups, rows, -1), 'rec', 0, 0, tiled=True)  29.2 us
    pallas_call x1, Pallas kernels, second_sums(): pl.pallas_call(functools.partial(second_kernel, masks, *totals), grid_spe...  27.8 us
    all_to_all x1, waiting for transfers between devices, eight_by_four(): all_grad = lax.all_to_all(out_grad, 'rec', 0, 0, tiled=True)  26.6 us
    ppermute x13, starting transfers between devices, swap(): return lax.ppermute(x, axis, [(i, i ^ bit) for i in range(n)])  15.3 us
    pallas_call x1, Pallas kernels, first_sums(): pl.pallas_call(first_kernel, grid=(n // 512,), in_specs=[block((1, size),...  13.7 us
    all_to_all x1, blocking collectives, eight_by_four(): part_grad = lax.all_to_all(part_grad, 'rec', 0, 0, tiled=True)  12.7 us
    unnamed x46, local copies, waits for them, and re-layouts  11 us
  transfers between devices with their start and end apart: 15, of which 12 were waited for; matrix products, arithmetic and copies ran while one was open for 3% of the time, Pallas kernels for 10%

profile of v2, /device:TPU:0, one launch (start us, length us, event | category | flops | bytes accessed | tf_op | source)
XLA Modules:
  0.0 244.6 jit_solution(13035781980872663761)
XLA Ops:
  0.7 1.2 copy-done
  1.9 1.0 fusion.12
  2.9 2.7 %fusion.4.refs_0_.image = bf16[128,768]{1,0:T(8,128)(2,1)S(1)} fusion(bf16[2048,768]{1,0:T(8,128)(2,1)} %w_ref.1, f32[128,2048]{1,0:T(8,128)S(1)} %fusion.12, bf16[128,128]{1,0:T(8,128)(2,1)S(1)} %copy-done.17, bf16[128,2048]{1,0:T(8,128)(2,1)S(1)} %copy-done.12), kind=kOutput, calls=%fused_computation.5 | convolution fusion | flops 470646784 | bytes 4947968 | tf_op jit(solution)/shard_map/dot_general | solution.py:680
  5.6 3.0 %collective-permute-start = (bf16[128,768]{1,0:T(8,128)(2,1)S(1)}, bf16[128,768]{1,0:T(8,128)(2,1)S(1)}, u32[]{:S(2)}, u32[]{:S(2)}) collective-permute-start(bf16[128,768]{1,0:T(8,128)(2,1)S(1)} %fusion.4.refs_0_.image), channel_id=1, source_target_pairs={{0,2},{1,3},{2,0},{3,1},{4,6},{5,7},{6,4},{7,5},{8,10},{9,11},{10,... | collective-permute-start | bytes 589832 | tf_op jit(solution)/shard_map/ppermute | solution.py:102
  8.7 4.9 %collective-permute-done.refs_1_ = bf16[128,768]{1,0:T(8,128)(2,1)S(1)} collective-permute-done((bf16[128,768]{1,0:T(8,128)(2,1)S(1)}, bf16[128,768]{1,0:T(8,128)(2,1)S(1)}, u32[]{:S(2)}, u32[]{:S(2)}) %collective-permute-start) | collective-permute-done | bytes 196640 | tf_op jit(solution)/shard_map/ppermute | solution.py:102
  13.6 13.7 %shard_map.112.refs_7_ = f32[4,256,1024]{2,1,0:T(8,128)S(1)} custom-call(s32[1,512]{1,0:T(1,128)S(1)} %bitcast.23, bf16[1536,3072]{1,0:T(8,128)(2,1)} %refs_5_.1, bf16[3072,2048]{1,0:T(8,128)(2,1)} %freq_ref.3), custom_call_target="tpu_custom_call" | custom-call | flops 7516192768 | bytes 15728640 | tf_op jit(solution)/shard_map/pallas_call | solution.py:258
  27.3 2.0 copy-done.4
  31.3 27.8 %shard_map.113 = (bf16[4,128,512]{2,1,0:T(8,128)(2,1)}, f32[4,128,512]{2,1,0:T(8,128)}, bf16[2,2,128,512]{3,2,1,0:T(8,128)(2,1)}, f32[2,2,128,512]{3,2,1,0:T(8,128)}, f32[2,128,2048]{2,1,0:T(8,128)}) custom-call(s32[5]{0:T(128)} %stack.23.me_ref, s32[1,1024]{1,0:T(1,128)} %bitcast.31, s32[1,128]{1,0:T(1,128)} %bitcast.32, bf16[128,768]{1,0:T(8,128)(2,1)} %copy-done.11, ...), custom_call_target="tpu_custom_call" | custom-call | flops 16911433728 | bytes 23068672 | tf_op jit(solution)/shard_map/pallas_call | solution.py:365
  59.0 1.7 collective-permute-start.3
  60.8 1.6 collective-permute-start.4
  62.4 0.8 broadcast_in_dim.2
  63.1 3.9 %all-to-all-start = ((bf16[8,144,128]{2,1,0:T(8,128)(2,1)}), bf16[8,144,128]{2,1,0:T(8,128)(2,1)S(1)}, u32[]{:S(2)}, u32[]{:S(2)}) async-start(bf16[8,144,128]{2,1,0:T(8,128)(2,1)} %broadcast_in_dim.2), calls=%async_computation | async-start | bytes 589824 | tf_op jit(solution)/shard_map/all_to_all | solution.py:686
  67.0 7.7 %collective-permute-done.3 = bf16[4,128,512]{2,1,0:T(8,128)(2,1)S(1)} collective-permute-done((bf16[4,128,512]{2,1,0:T(8,128)(2,1)}, bf16[4,128,512]{2,1,0:T(8,128)(2,1)S(1)}, u32[]{:S(2)}, u32[]{:S(2)}) %collective-permute-start.3) | collective-permute-done | bytes 524320 | tf_op jit(solution)/shard_map/ppermute | solution.py:102
  74.7 2.9 %collective-permute-done.4.rb_s.rb_k = bf16[2,2,128,512]{3,2,1,0:T(8,128)(2,1)S(1)} collective-permute-done((bf16[2,2,128,512]{3,2,1,0:T(8,128)(2,1)}, bf16[2,2,128,512]{3,2,1,0:T(8,128)(2,1)S(1)}, u32[]{:S(2)}, u32[]{:S(2)}) %collective-permute-start.4) | collective-permute-done | bytes 524320 | tf_op jit(solution)/shard_map/ppermute | solution.py:102
  77.6 0.8 copy-done.7
  78.5 3.5 %shard_map.114 = (bf16[2,128,512]{2,1,0:T(8,128)(2,1)}, f32[2,128,512]{2,1,0:T(8,128)}, bf16[2,128,512]{2,1,0:T(8,128)(2,1)}, f32[2,128,512]{2,1,0:T(8,128)}) custom-call(s32[5]{0:T(128)} %stack.23.me_ref, f32[2,2,128,512]{3,2,1,0:T(8,128)} %bitcast.24, f32[2,2,128,512]{3,2,1,0:T(8,128)} %bitcast.25, bf16[2,2,128,512]{3,2,1,0:T(8,128)(2,1)} %bitcast.27, ...), custom_call_target="tpu_custom_call" | custom-call | bytes 4194304 | tf_op jit(solution)/shard_map/pallas_call | solution.py:406
  82.6 6.1 %collective-permute-done.5.ga_s.ga_k = bf16[2,128,512]{2,1,0:T(8,128)(2,1)S(1)} collective-permute-done((bf16[2,128,512]{2,1,0:T(8,128)(2,1)}, bf16[2,128,512]{2,1,0:T(8,128)(2,1)S(1)}, u32[]{:S(2)}, u32[]{:S(2)}) %collective-permute-start.5) | collective-permute-done | bytes 262176 | tf_op jit(solution)/shard_map/ppermute | solution.py:102
  89.5 3.0 %shard_map.115 = (bf16[256,512]{1,0:T(8,128)(2,1)}, f32[256,512]{1,0:T(8,128)}) custom-call(s32[5]{0:T(128)} %stack.23.me_ref, f32[2,128,512]{2,1,0:T(8,128)} %get-tuple-element.37.na_s.na_k, f32[2,128,512]{2,1,0:T(8,128)} %get-tuple-element.37.na_s.na_k, bf16[2,128,512]{2,1,0:T(8,128)(2,1)} %copy-done.9, bf16[2,128,512]{2,1,0:T(8,128)(2,1)} %copy-done.9, ...), custom_call_target="tpu_custom_call" | custom-call | bytes 3145728 | tf_op jit(solution)/shard_map/pallas_call | solution.py:432
  92.5 5.2 %collective-permute-start.7 = (bf16[256,512]{1,0:T(8,128)(2,1)}, bf16[256,512]{1,0:T(8,128)(2,1)S(1)}, u32[]{:S(2)}, u32[]{:S(2)}) collective-permute-start(bf16[256,512]{1,0:T(8,128)(2,1)} %get-tuple-element.42), channel_id=1, source_target_pairs={{0,16},{4,20},{8,24},{12,28},{16,0},{20,4},{24,8},{28,12},{1,17},{... | collective-permute-start | bytes 786440 | tf_op jit(solution)/shard_map/ppermute | solution.py:102
  97.8 1.1 copy.18.labels_ref
  98.8 8.0 %collective-permute-done.7.got_ref = bf16[256,512]{1,0:T(8,128)(2,1)S(1)} collective-permute-done((bf16[256,512]{1,0:T(8,128)(2,1)}, bf16[256,512]{1,0:T(8,128)(2,1)S(1)}, u32[]{:S(2)}, u32[]{:S(2)}) %collective-permute-start.7) | collective-permute-done | bytes 262176 | tf_op jit(solution)/shard_map/ppermute | solution.py:102
  107.6 3.8 %shard_map.116 = bf16[1024,512]{1,0:T(8,128)(2,1)} custom-call(s32[5]{0:T(128)} %stack.23.me_ref, f32[256,512]{1,0:T(8,128)} %get-tuple-element.41.keep_ref, bf16[256,512]{1,0:T(8,128)(2,1)} %copy-done.15, f32[256,2,2048]{2,1,0:T(2,128)} %noise_ref.1, s32[1024,1]{1,0:T(8,128)} %copy.18.labels_ref), custom_call_target="tpu_custom_call" | custom-call | flops 268435456 | bytes 3145728 | tf_op jit(solution)/shard_map/pallas_call | solution.py:465
  111.3 29.2 %all_to_all.20.rows_ref = bf16[8,128,512]{2,1,0:T(8,128)(2,1)S(1)} all-to-all(bf16[8,128,512]{2,1,0:T(8,128)(2,1)} %bitcast.26), channel_id=1, replica_groups=mesh['rec'=8,'feat'=4] {'rec'}, dimensions={0} | all-to-all | bytes 2097152 | tf_op jit(solution)/shard_map/all_to_all | solution.py:720
  140.5 7.9 %shard_map.117 = (bf16[2,768,128]{2,1,0:T(8,128)(2,1)S(1)}, f32[2,768,128]{2,1,0:T(8,128)S(1)}) custom-call(s32[5]{0:T(128)S(1)} %copy-done.3, f32[2,128,2048]{2,1,0:T(8,128)S(1)} %copy-done.2, bf16[8,128,512]{2,1,0:T(8,128)(2,1)S(1)} %all_to_all.20.rows_ref, bf16[3072,2048]{1,0:T(8,128)(2,1)} %freq_ref.3), custom_call_target="tpu_custom_call" | custom-call | flops 1610612736 | bytes 12582912 | tf_op jit(solution)/shard_map/pallas_call | solution.py:519
  148.4 0.9 copy-done.1
  149.3 1.7 collective-permute-done.8.got_s.got_k
  151.0 0.7 copy-done.8
  151.8 2.7 %shard_map.118 = (bf16[768,128]{1,0:T(8,128)(2,1)}, f32[768,128]{1,0:T(8,128)}) custom-call(s32[5]{0:T(128)} %stack.23.me_ref, f32[2,768,128]{2,1,0:T(8,128)} %copy-done.1, f32[2,768,128]{2,1,0:T(8,128)} %copy-done.1, bf16[2,768,128]{2,1,0:T(8,128)(2,1)} %copy-done.8, bf16[2,768,128]{2,1,0:T(8,128)(2,1)} %copy-done.8), custom_call_target="tpu_custom_call" | custom-call | bytes 1048576 | tf_op jit(solution)/shard_map/pallas_call | solution.py:540
  154.5 1.5 collective-permute-start.9
  156.0 5.6 %collective-permute-done.9.got = bf16[768,128]{1,0:T(8,128)(2,1)S(1)} collective-permute-done((bf16[768,128]{1,0:T(8,128)(2,1)}, bf16[768,128]{1,0:T(8,128)(2,1)S(1)}, u32[]{:S(2)}, u32[]{:S(2)}) %collective-permute-start.9) | collective-permute-done | bytes 196640 | tf_op jit(solution)/shard_map/ppermute | solution.py:102
  162.4 2.5 %shard_map.119.grad_ref = bf16[8,128,768]{2,1,0:T(8,128)(2,1)} custom-call(f32[768,128]{1,0:T(8,128)} %get-tuple-element.45.keep, bf16[768,128]{1,0:T(8,128)(2,1)} %copy-done.16, bf16[128,768]{1,0:T(8,128)(2,1)} %copy-done.11), custom_call_target="tpu_custom_call" | custom-call | bytes 1048576 | tf_op jit(solution)/shard_map/pallas_call | solution.py:558
  164.9 7.2 %shard_map.121 = (bf16[8,128,128]{2,1,0:T(8,128)(2,1)}, f32[8,128,128]{2,1,0:T(8,128)}) custom-call(s32[5]{0:T(128)} %stack.23.me_ref, bf16[2048,768]{1,0:T(8,128)(2,1)} %w_ref.1, bf16[8,128,768]{2,1,0:T(8,128)(2,1)} %shard_map.119.grad_ref), custom_call_target="tpu_custom_call" | custom-call | flops 402653184 | bytes 3145728 | tf_op jit(solution)/shard_map/pallas_call | solution.py:587
  172.1 1.7 collective-permute-done.10.b
  174.5 1.9 shard_map.122.a
  176.4 1.5 collective-permute-start.11
  177.9 7.0 %collective-permute-done.11.b = bf16[8,128,128]{2,1,0:T(8,128)(2,1)S(1)} collective-permute-done((bf16[8,128,128]{2,1,0:T(8,128)(2,1)}, bf16[8,128,128]{2,1,0:T(8,128)(2,1)S(1)}, u32[]{:S(2)}, u32[]{:S(2)}) %collective-permute-start.11) | collective-permute-done | bytes 262176 | tf_op jit(solution)/shard_map/ppermute | solution.py:102
  185.7 1.8 shard_map.123
  187.5 12.7 %all_to_all.21.got_ref = bf16[8,128,128]{2,1,0:T(8,128)(2,1)} all-to-all(bf16[8,128,128]{2,1,0:T(8,128)(2,1)} %shard_map.123), channel_id=1, replica_groups=mesh['rec'=8,'feat'=4] {'rec'}, dimensions={0} | all-to-all | bytes 524288 | tf_op jit(solution)/shard_map/all_to_all | solution.py:730
  200.2 3.6 %all-to-all-start.2 = ((bf16[8,128,768]{2,1,0:T(8,128)(2,1)}), bf16[8,128,768]{2,1,0:T(8,128)(2,1)S(1)}, u32[]{:S(2)}, u32[]{:S(2)}) async-start(bf16[8,128,768]{2,1,0:T(8,128)(2,1)} %shard_map.119.grad_ref), calls=%async_computation.2 | async-start | bytes 3145728 | tf_op jit(solution)/shard_map/all_to_all | solution.py:726
  204.1 0.9 fusion.7.lhs_ref
  205.0 1.6 maximum_convert_fusion
  206.7 3.1 %shard_map.124 = f32[384,128]{1,0:T(8,128)} custom-call(s32[5]{0:T(128)} %stack.23.me_ref, bf16[8,128,128]{2,1,0:T(8,128)(2,1)} %all_to_all.21.got_ref, f32[256,1024]{1,0:T(8,128)} %get-tuple-element.54.preact_ref, bf16[384,1024]{1,0:T(8,128)(2,1)} %fusion.7.lhs_ref), custom_call_target="tpu_custom_call" | custom-call | flops 100663296 | bytes 2097152 | tf_op jit(solution)/shard_map/pallas_call | solution.py:652
  209.7 1.6 collective-permute-done.12
  211.4 1.0 broadcast_select_fusion.1
  213.0 0.7 pad_maximum_fusion.2
  213.7 26.6 %all-to-all-done.2.grad_ref = bf16[8,128,768]{2,1,0:T(8,128)(2,1)S(1)} async-done(((bf16[8,128,768]{2,1,0:T(8,128)(2,1)}), bf16[8,128,768]{2,1,0:T(8,128)(2,1)S(1)}, u32[]{:S(2)}, u32[]{:S(2)}) %all-to-all-start.2) | async-done | bytes 1572896 | tf_op jit(solution)/shard_map/all_to_all | solution.py:726
  240.3 1.2 copy-done.5
  241.5 3.0 %shard_map.120 = f32[256,768]{1,0:T(8,128)} custom-call(bf16[256,1024]{1,0:T(8,128)(2,1)} %get-tuple-element.53.hidden_ref, bf16[8,128,768]{2,1,0:T(8,128)(2,1)} %copy-done.5), custom_call_target="tpu_custom_call" | custom-call | flops 402653184 | bytes 4194304 | tf_op jit(solution)/shard_map/pallas_call | solution.py:619
  (64 shorter events, 7.2 us)
Async XLA Ops:
  0.6 1.2 copy-start
  0.6 2.2 copy-start.17
  0.7 2.2 copy-start.12
  2.9 5.8 %copy-start.18 = (s32[1536]{0:T(1024)S(1)}, s32[1536]{0:T(1024)}, u32[]{:S(2)}) copy-start(s32[1536]{0:T(1024)} %param.12) | copy-start | bytes 18436
  5.6 21.7 %copy-start.11 = (bf16[128,768]{1,0:T(8,128)(2,1)}, bf16[128,768]{1,0:T(8,128)(2,1)S(1)}, u32[]{:S(2)}) copy-start(bf16[128,768]{1,0:T(8,128)(2,1)S(1)} %fusion.4.refs_0_.image) | copy-start | bytes 589828
  5.6 7.9 %collective-permute-start = (bf16[128,768]{1,0:T(8,128)(2,1)S(1)}, bf16[128,768]{1,0:T(8,128)(2,1)S(1)}, u32[]{:S(2)}, u32[]{:S(2)}) collective-permute-start(bf16[128,768]{1,0:T(8,128)(2,1)S(1)} %fusion.4.refs_0_.image), channel_id=1, source_target_pairs={{0,2},{1,3},{2,0},{3,1},{4,6},{5,7},{6,4},{7,5},{8,10},{9,11},{10,... | collective-permute-start | bytes 589832 | tf_op jit(solution)/shard_map/ppermute | solution.py:102
  8.7 21.8 %collective-permute-start.1 = (bf16[128,768]{1,0:T(8,128)(2,1)S(1)}, bf16[128,768]{1,0:T(8,128)(2,1)S(1)}, u32[]{:S(2)}, u32[]{:S(2)}) collective-permute-start(bf16[128,768]{1,0:T(8,128)(2,1)S(1)} %fusion.4.refs_0_.image), channel_id=1, source_target_pairs={{0,1},{1,0},{2,3},{3,2},{4,5},{5,4},{6,7},{7,6},{8,9},{9,8},{10,11... | collective-permute-start | bytes 589832 | tf_op jit(solution)/shard_map/ppermute | solution.py:102
  13.6 13.7 %copy-start.20 = (bf16[128,768]{1,0:T(8,128)(2,1)}, bf16[128,768]{1,0:T(8,128)(2,1)S(1)}, u32[]{:S(2)}) copy-start(bf16[128,768]{1,0:T(8,128)(2,1)S(1)} %collective-permute-done.refs_1_) | copy-start | bytes 589828
  13.6 17.0 %collective-permute-start.2 = (bf16[128,768]{1,0:T(8,128)(2,1)S(1)}, bf16[128,768]{1,0:T(8,128)(2,1)S(1)}, u32[]{:S(2)}, u32[]{:S(2)}) collective-permute-start(bf16[128,768]{1,0:T(8,128)(2,1)S(1)} %collective-permute-done.refs_1_), channel_id=1, source_target_pairs={{0,1},{1,0},{2,3},{3,2},{4,5},{5,4},{6,7},{7,6},{8,9},{9,8},{10,11... | collective-permute-start | bytes 589832 | tf_op jit(solution)/shard_map/ppermute | solution.py:102
  27.3 2.0 copy-start.4
  30.5 0.7 copy-start.21
  30.5 0.7 copy-start.22
  31.3 31.1 %copy-start.19 = (s32[128]{0:T(128)S(1)}, s32[128]{0:T(128)}, u32[]{:S(2)}) copy-start(s32[128]{0:T(128)} %param.16) | copy-start | bytes 1540
  59.0 15.7 %collective-permute-start.3 = (bf16[4,128,512]{2,1,0:T(8,128)(2,1)}, bf16[4,128,512]{2,1,0:T(8,128)(2,1)S(1)}, u32[]{:S(2)}, u32[]{:S(2)}) collective-permute-start(bf16[4,128,512]{2,1,0:T(8,128)(2,1)} %get-tuple-element.34), channel_id=1, source_target_pairs={{0,4},{4,0},{8,12},{12,8},{16,20},{20,16},{24,28},{28,24},{1,5},{5... | collective-permute-start | bytes 1572872 | tf_op jit(solution)/shard_map/ppermute | solution.py:102
  60.8 16.9 %collective-permute-start.4 = (bf16[2,2,128,512]{3,2,1,0:T(8,128)(2,1)}, bf16[2,2,128,512]{3,2,1,0:T(8,128)(2,1)S(1)}, u32[]{:S(2)}, u32[]{:S(2)}) collective-permute-start(bf16[2,2,128,512]{3,2,1,0:T(8,128)(2,1)} %get-tuple-element.36), channel_id=1, source_target_pairs={{0,8},{4,12},{8,0},{12,4},{16,24},{20,28},{24,16},{28,20},{1,9},{5... | collective-permute-start | bytes 1572872 | tf_op jit(solution)/shard_map/ppermute | solution.py:102
  63.1 34.6 %all-to-all-start = ((bf16[8,144,128]{2,1,0:T(8,128)(2,1)}), bf16[8,144,128]{2,1,0:T(8,128)(2,1)S(1)}, u32[]{:S(2)}, u32[]{:S(2)}) async-start(bf16[8,144,128]{2,1,0:T(8,128)(2,1)} %broadcast_in_dim.2), calls=%async_computation | async-start | bytes 589824 | tf_op jit(solution)/shard_map/all_to_all | solution.py:686
  74.7 2.9 %copy-start.6 = (bf16[4,128,512]{2,1,0:T(8,128)(2,1)}, bf16[4,128,512]{2,1,0:T(8,128)(2,1)S(1)}, u32[]{:S(2)}) copy-start(bf16[4,128,512]{2,1,0:T(8,128)(2,1)S(1)} %collective-permute-done.3) | copy-start | bytes 1572868
  77.6 0.8 copy-start.7
  82.0 6.8 %collective-permute-start.5 = (bf16[2,128,512]{2,1,0:T(8,128)(2,1)}, bf16[2,128,512]{2,1,0:T(8,128)(2,1)S(1)}, u32[]{:S(2)}, u32[]{:S(2)}) collective-permute-start(bf16[2,128,512]{2,1,0:T(8,128)(2,1)} %get-tuple-element.38), channel_id=1, source_target_pairs={{0,8},{4,12},{8,0},{12,4},{16,24},{20,28},{24,16},{28,20},{1,9},{5... | collective-permute-start | bytes 786440 | tf_op jit(solution)/shard_map/ppermute | solution.py:102
  82.0 6.8 %collective-permute-start.6 = (bf16[2,128,512]{2,1,0:T(8,128)(2,1)}, bf16[2,128,512]{2,1,0:T(8,128)(2,1)S(1)}, u32[]{:S(2)}, u32[]{:S(2)}) collective-permute-start(bf16[2,128,512]{2,1,0:T(8,128)(2,1)} %get-tuple-element.40), channel_id=1, source_target_pairs={{0,4},{4,0},{8,12},{12,8},{16,20},{20,16},{24,28},{28,24},{1,5},{5... | collective-permute-start | bytes 786440 | tf_op jit(solution)/shard_map/ppermute | solution.py:102
  88.7 0.7 copy-start.9
  88.8 0.7 copy-start.10
  92.5 14.4 %collective-permute-start.7 = (bf16[256,512]{1,0:T(8,128)(2,1)}, bf16[256,512]{1,0:T(8,128)(2,1)S(1)}, u32[]{:S(2)}, u32[]{:S(2)}) collective-permute-start(bf16[256,512]{1,0:T(8,128)(2,1)} %get-tuple-element.42), channel_id=1, source_target_pairs={{0,16},{4,20},{8,24},{12,28},{16,0},{20,4},{24,8},{28,12},{1,17},{... | collective-permute-start | bytes 786440 | tf_op jit(solution)/shard_map/ppermute | solution.py:102
  106.9 0.7 copy-start.15
  111.3 29.2 %copy-start.2 = (f32[2,128,2048]{2,1,0:T(8,128)S(1)}, f32[2,128,2048]{2,1,0:T(8,128)}, u32[]{:S(2)}) copy-start(f32[2,128,2048]{2,1,0:T(8,128)} %get-tuple-element.32.cs_ref) | copy-start | bytes 6291460
  111.3 29.2 %copy-start.3 = (s32[5]{0:T(128)S(1)}, s32[5]{0:T(128)}, u32[]{:S(2)}) copy-start(s32[5]{0:T(128)} %stack.23.me_ref) | copy-start | bytes 64
  148.4 0.9 copy-start.1
  149.3 1.7 collective-permute-start.8
  151.0 0.7 copy-start.8
  154.5 7.2 %collective-permute-start.9 = (bf16[768,128]{1,0:T(8,128)(2,1)}, bf16[768,128]{1,0:T(8,128)(2,1)S(1)}, u32[]{:S(2)}, u32[]{:S(2)}) collective-permute-start(bf16[768,128]{1,0:T(8,128)(2,1)} %get-tuple-element.46), channel_id=1, source_target_pairs={{0,2},{1,3},{2,0},{3,1},{4,6},{5,7},{6,4},{7,5},{8,10},{9,11},{10,... | collective-permute-start | bytes 589832 | tf_op jit(solution)/shard_map/ppermute | solution.py:102
  161.7 0.7 copy-start.16
  172.1 1.7 collective-permute-start.10
  173.8 0.7 copy-start.14
  176.4 8.6 %collective-permute-start.11 = (bf16[8,128,128]{2,1,0:T(8,128)(2,1)}, bf16[8,128,128]{2,1,0:T(8,128)(2,1)S(1)}, u32[]{:S(2)}, u32[]{:S(2)}) collective-permute-start(bf16[8,128,128]{2,1,0:T(8,128)(2,1)} %shard_map.122.a), channel_id=1, source_target_pairs={{0,2},{1,3},{2,0},{3,1},{4,6},{5,7},{6,4},{7,5},{8,10},{9,11},{10,... | collective-permute-start | bytes 786440 | tf_op jit(solution)/shard_map/ppermute | solution.py:102
  185.0 0.7 copy-start.13
  200.2 40.2 %all-to-all-start.2 = ((bf16[8,128,768]{2,1,0:T(8,128)(2,1)}), bf16[8,128,768]{2,1,0:T(8,128)(2,1)S(1)}, u32[]{:S(2)}, u32[]{:S(2)}) async-start(bf16[8,128,768]{2,1,0:T(8,128)(2,1)} %shard_map.119.grad_ref), calls=%async_computation.2 | async-start | bytes 3145728 | tf_op jit(solution)/shard_map/all_to_all | solution.py:726
  209.7 1.7 collective-permute-start.12
  240.3 1.2 copy-start.5

commit v3 on v2

--- a/solution.py
+++ b/solution.py
@@ -230,128 +230,101 @@
     return pl.BlockSpec(shape, index)
 
 
-def first_kernel(labels_ref, records_ref, freq_ref, out_ref, table_ref):
-    classes, total = table_ref.shape
-
-    @pl.when(pl.program_id(0) == 0)
-    def _():
-        ids = lax.broadcasted_iota(jnp.int32, (classes, total), 0)
-        table_ref[...] = jnp.where(ids == labels_ref[...], 1.0, 0.0).astype(BF)
-
-    freq = freq_ref[...]
-    half = total // 2
-    before = jnp.dot(records_ref[:half, :], freq, preferred_element_type=F32)
-    after = jnp.dot(records_ref[half:, :], freq, preferred_element_type=F32)
-    acc = sums(table_ref[:, :half], before) + sums(table_ref[:, half:], after)
-    out_ref[0] = acc
-
-
 def sums(table, pre):
     co, si = cos_sin(pre)
     phi = jnp.concatenate([co.astype(BF), si.astype(BF)], axis=1)
     return jnp.dot(table, phi, preferred_element_type=F32)
 
 
-def first_sums(labels, records, freq, classes, size):
-    k = records.shape[1]
-    n = freq.shape[1]
-    return pl.pallas_call(
-        first_kernel,
-        grid=(n // 512,),
-        in_specs=[
-            block((1, size), lambda j: (0, 0)),
-            block((size, k), lambda j: (0, 0)),
-            block((k, 512), lambda j: (0, j)),
-        ],
-        out_specs=block((1, classes, 1024), lambda j: (j, 0, 0)),
-        out_shape=jax.ShapeDtypeStruct((n // 512, classes, 1024), F32),
-        scratch_shapes=[pltpu.VMEM((classes, size), BF)],
-        compiler_params=pltpu.CompilerParams(vmem_limit_bytes=48 * 2**20),
-        cost_estimate=pl.CostEstimate(
-            flops=2 * size * n * (k + 2 * classes), bytes_accessed=2 * (size * k + k * n), transcendentals=0
-        ),
-    )(labels.reshape(1, -1), records, freq)
-
-
-def second_kernel(
-    masks,
-    real_total,
-    syn_total,
-    me_ref,
-    real_labels_ref,
-    syn_labels_ref,
-    *refs,
-):
+def features_kernel(masks, size, real_total, syn_total, me_ref, real_labels_ref, syn_labels_ref, *refs):
     count = len(masks)
     images = refs[:count]
-    blocks = refs[count : count + 2]
-    freq_ref, part_ref, send_a, keep_a, send_b, keep_b, cs_ref, real_table, syn_table = refs[count + 2 :]
+    records_hbm, freq_ref, send_a, keep_a, send_b, keep_b, cs_ref = refs[count : count + 7]
+    records, real_table, syn_table, sem = refs[count + 7 :]
     classes, total = real_table.shape
+    steps = total // size
     feat, x, z_low = me_ref[0], me_ref[1], me_ref[2]
     step = pl.program_id(0)
+    cols = images[0].shape[1]
+
+    def copy(i):
+        at = pl.ds(i * size, size)
+        return pltpu.make_async_copy(records_hbm.at[at, :], records.at[at, :], sem.at[i])
+
+    def body(wait):
+        syn_pre = None
+        for mask, image in zip(masks, images):
+            at = pl.multiple_of((feat ^ mask) * cols, 128)
+            d = jnp.dot(image[...], freq_ref[pl.ds(at, cols), :], preferred_element_type=F32)
+            syn_pre = d if syn_pre is None else syn_pre + d
+        freq = freq_ref[...]
+        acc = None
+        before = None
+        for i in range(steps + 1):
+            if i < steps:
+                if wait:
+                    copy(i).wait()
+                pre = jnp.dot(records[i * size : (i + 1) * size, :], freq, preferred_element_type=F32)
+            if i == 0:
+                co, si = cos_sin(syn_pre)
+                cs_ref[0] = co
+                cs_ref[1] = si
+                phi = jnp.concatenate([co.astype(BF), si.astype(BF)], axis=1)
+                syn = jnp.dot(syn_table[...], phi, preferred_element_type=F32)
+            else:
+                d = sums(real_table[:, (i - 1) * size : i * size], before)
+                acc = d if acc is None else acc + d
+            before = pre
+        gap = syn * (1.0 / syn_total) - acc * (1.0 / real_total)
+        zero = jnp.concatenate([gap[:, :256], gap[:, 512:768]], axis=1)
+        one = jnp.concatenate([gap[:, 256:512], gap[:, 768:]], axis=1)
+        half = classes // 2
+        keep_a[0] = jnp.where(x == 0, zero[:half], one[:half])
+        send_a[0] = jnp.where(x == 0, one[:half], zero[:half]).astype(BF)
+        high = step // 2
+
+        @pl.when(step % 2 == z_low)
+        def _():
+            keep_b[high, 0] = zero[half:]
+            keep_b[high, 1] = one[half:]
+
+        @pl.when(step % 2 != z_low)
+        def _():
+            send_b[high, 0] = zero[half:].astype(BF)
+            send_b[high, 1] = one[half:].astype(BF)
 
     @pl.when(step == 0)
     def _():
+        for i in range(steps):
+            copy(i).start()
         ids = lax.broadcasted_iota(jnp.int32, (classes, total), 0)
         real_table[...] = jnp.where(ids == real_labels_ref[...], 1.0, 0.0).astype(BF)
         ids = lax.broadcasted_iota(jnp.int32, syn_table.shape, 0)
         syn_table[...] = jnp.where(ids == syn_labels_ref[...], 1.0, 0.0).astype(BF)
-
-    cols = images[0].shape[1]
-    syn_pre = None
-    for mask, image in zip(masks, images):
-        at = pl.multiple_of((feat ^ mask) * cols, 128)
-        d = jnp.dot(image[...], freq_ref[pl.ds(at, cols), :], preferred_element_type=F32)
-        syn_pre = d if syn_pre is None else syn_pre + d
-    freq = freq_ref[...]
-    size = total // 2
-    pre0 = jnp.dot(blocks[0][...], freq, preferred_element_type=F32)
-    co, si = cos_sin(syn_pre)
-    cs_ref[0] = co
-    cs_ref[1] = si
-    phi = jnp.concatenate([co.astype(BF), si.astype(BF)], axis=1)
-    syn = jnp.dot(syn_table[...], phi, preferred_element_type=F32)
-    pre1 = jnp.dot(blocks[1][...], freq, preferred_element_type=F32)
-    acc = part_ref[0] + sums(real_table[:, :size], pre0)
-    acc = acc + sums(real_table[:, size:], pre1)
-    gap = syn * (1.0 / syn_total) - acc * (1.0 / real_total)
-    zero = jnp.concatenate([gap[:, :256], gap[:, 512:768]], axis=1)
-    one = jnp.concatenate([gap[:, 256:512], gap[:, 768:]], axis=1)
-    half = classes // 2
-    keep_a[0] = jnp.where(x == 0, zero[:half], one[:half])
-    send_a[0] = jnp.where(x == 0, one[:half], zero[:half]).astype(BF)
-    high = step // 2
-
-    @pl.when(step % 2 == z_low)
+        body(True)
+
+    @pl.when(step > 0)
     def _():
-        keep_b[high, 0] = zero[half:]
-        keep_b[high, 1] = one[half:]
-
-    @pl.when(step % 2 != z_low)
-    def _():
-        send_b[high, 0] = zero[half:].astype(BF)
-        send_b[high, 1] = one[half:].astype(BF)
-
-
-def second_sums(me, real_labels, syn_labels, masks, images, records, size, freq, part, totals):
-    k = records.shape[1]
+        body(False)
+
+
+def feature_sums(me, real_labels, syn_labels, masks, images, records, freq, classes, totals):
+    total, k = records.shape
     n = freq.shape[1]
     rows, cols = images[0].shape
-    classes = part.shape[1]
     half = classes // 2
+    size = 512
     grid_spec = pltpu.PrefetchScalarGridSpec(
         num_scalar_prefetch=1,
         grid=(n // 512,),
         in_specs=[
-            block((1, 2 * size), lambda j, me: (0, 0)),
+            block((1, total), lambda j, me: (0, 0)),
             block((1, rows), lambda j, me: (0, 0)),
         ]
         + [block((rows, cols), lambda j, me: (0, 0)) for _ in images]
         + [
-            block((size, k), lambda j, me: (1, 0)),
-            block((size, k), lambda j, me: (2, 0)),
+            pl.BlockSpec(memory_space=pl.ANY),
             block((k, 512), lambda j, me: (0, j)),
-            block((1, classes, 1024), lambda j, me: (j, 0, 0)),
         ],
         out_specs=[
             block((1, half, 512), lambda j, me: (j, 0, 0)),
@@ -360,10 +333,15 @@
             block((2, 2, half, 512), lambda j, me: (0, 0, 0, 0)),
             block((2, rows, 512), lambda j, me: (0, 0, j)),
         ],
-        scratch_shapes=[pltpu.VMEM((classes, 2 * size), BF), pltpu.VMEM((classes, rows), BF)],
-    )
-    return pl.pallas_call(
-        functools.partial(second_kernel, masks, *totals),
+        scratch_shapes=[
+            pltpu.VMEM((total, k), BF),
+            pltpu.VMEM((classes, total), BF),
+            pltpu.VMEM((classes, rows), BF),
+            pltpu.SemaphoreType.DMA((total // size,)),
+        ],
+    )
+    return pl.pallas_call(
+        functools.partial(features_kernel, masks, size, *totals),
         grid_spec=grid_spec,
         out_shape=[
             jax.ShapeDtypeStruct((4, half, 512), BF),
@@ -372,13 +350,13 @@
             jax.ShapeDtypeStruct((2, 2, half, 512), F32),
             jax.ShapeDtypeStruct((2, rows, n), F32),
         ],
-        compiler_params=pltpu.CompilerParams(vmem_limit_bytes=56 * 2**20),
+        compiler_params=pltpu.CompilerParams(vmem_limit_bytes=50 * 2**20),
         cost_estimate=pl.CostEstimate(
-            flops=2 * (2 * size + rows) * n * (k + 2 * classes),
-            bytes_accessed=2 * (2 * size * k + k * n) + 4 * classes * n * 2,
+            flops=2 * (total + rows) * n * (k + 2 * classes),
+            bytes_accessed=2 * (total * k + k * n) + 4 * classes * n * 2,
             transcendentals=0,
         ),
-    )(me, real_labels.reshape(1, -1), syn_labels.reshape(1, -1), *images, records, records, freq, part)
+    )(me, real_labels.reshape(1, -1), syn_labels.reshape(1, -1), *images, records, freq)
 
 
 def stage_two_kernel(me_ref, ka_s, ka_k, ra_s, ra_k, kb_s, kb_k, rb_s, rb_k, sa, na, sb, nb):
@@ -407,6 +385,7 @@
         stage_two_kernel,
         grid_spec=spec,
         out_shape=[jax.ShapeDtypeStruct((2, half, width), t) for t in kinds],
+        compiler_params=pltpu.CompilerParams(vmem_limit_bytes=8 * 2**20),
         cost_estimate=pl.CostEstimate(flops=0, bytes_accessed=4 * 2**20, transcendentals=0),
     )(me, keep_a, keep_a, got_a, got_a, keep_b, keep_b, got_b, got_b)
 
@@ -433,6 +412,7 @@
         stage_three_kernel,
         grid_spec=spec,
         out_shape=[jax.ShapeDtypeStruct((2 * half, width), t) for t in (BF, F32)],
+        compiler_params=pltpu.CompilerParams(vmem_limit_bytes=8 * 2**20),
         cost_estimate=pl.CostEstimate(flops=0, bytes_accessed=3 * 2**20, transcendentals=0),
     )(me, next_a, next_a, got_a, got_a, next_b, next_b, got_b, got_b)
 
@@ -466,6 +446,7 @@
         functools.partial(gap_kernel, real_total),
         grid_spec=spec,
         out_shape=jax.ShapeDtypeStruct((total, width), BF),
+        compiler_params=pltpu.CompilerParams(vmem_limit_bytes=14 * 2**20),
         cost_estimate=pl.CostEstimate(
             flops=2 * total * classes * width, bytes_accessed=3 * 2**20, transcendentals=0
         ),
@@ -520,7 +501,7 @@
         image_kernel,
         grid_spec=spec,
         out_shape=[jax.ShapeDtypeStruct((2, cols, rows), t) for t in (BF, F32)],
-        compiler_params=pltpu.CompilerParams(vmem_limit_bytes=40 * 2**20),
+        compiler_params=pltpu.CompilerParams(vmem_limit_bytes=24 * 2**20),
         cost_estimate=pl.CostEstimate(flops=2 * k * n * rows, bytes_accessed=2 * k * n, transcendentals=0),
     )(me, cs, feat_rows, freq)
 
@@ -541,46 +522,48 @@
         split_y_kernel,
         grid_spec=spec,
         out_shape=[jax.ShapeDtypeStruct((cols, rows), t) for t in (BF, F32)],
+        compiler_params=pltpu.CompilerParams(vmem_limit_bytes=8 * 2**20),
         cost_estimate=pl.CostEstimate(flops=0, bytes_accessed=2**20, transcendentals=0),
     )(me, keep, keep, got, got)
 
 
-def out_kernel(keep, got, image, out):
+def out_kernel(keep, got, image, out, flipped):
     grad = (keep[...] + got[...].astype(F32)).T
     grad = grad * (1.0 - jnp.square(image[...].astype(F32)))
-    grad = grad.astype(BF)
-    for r in range(out.shape[0]):
-        out[r] = grad
-
-
-def out_grads(keep, got, image, copies):
+    out[...] = grad.astype(BF)
+    flipped[...] = grad.T.astype(BF)
+
+
+def out_grads(keep, got, image):
     rows, cols = image.shape
     return pl.pallas_call(
         out_kernel,
-        out_shape=jax.ShapeDtypeStruct((copies, rows, cols), BF),
+        out_shape=[jax.ShapeDtypeStruct((rows, cols), BF), jax.ShapeDtypeStruct((cols, rows), BF)],
+        compiler_params=pltpu.CompilerParams(vmem_limit_bytes=8 * 2**20),
         cost_estimate=pl.CostEstimate(flops=0, bytes_accessed=2**20, transcendentals=0),
     )(keep, got, image)
 
 
 def hidden_kernel(me_ref, w_ref, grad_ref, send, keep):
     core = me_ref[0] % 2
-    out = lax.dot_general(w_ref[...], grad_ref[0], NT, preferred_element_type=F32)
-    half = out.shape[0] // 2
-    keep[0] = jnp.where(core == 0, out[:half], out[half:])
-    send[0] = jnp.where(core == 0, out[half:], out[:half]).astype(BF)
-
-
-def hidden_grads(me, w_out, out_grad):
-    groups, rows, cols = out_grad.shape
+    out = jnp.dot(w_ref[...], grad_ref[...], preferred_element_type=F32)
+    count, half, rows = send.shape
+    out = out.reshape(count, 2, half, rows)
+    keep[...] = jnp.where(core == 0, out[:, 0], out[:, 1])
+    send[...] = jnp.where(core == 0, out[:, 1], out[:, 0]).astype(BF)
+
+
+def hidden_grads(me, w_out, flipped, groups):
+    cols, rows = flipped.shape
     hid = w_out.shape[0]
     mine = hid // groups
-    out = block((1, mine // 2, rows), lambda r, me: (r, 0, 0))
+    out = block((2, mine // 2, rows), lambda r, me: (r, 0, 0))
     spec = pltpu.PrefetchScalarGridSpec(
         num_scalar_prefetch=1,
-        grid=(groups,),
+        grid=(groups // 2,),
         in_specs=[
-            block((mine, cols), lambda r, me: (r, 0)),
-            block((1, rows, cols), lambda r, me: (0, 0, 0)),
+            block((2 * mine, cols), lambda r, me: (r, 0)),
+            block((cols, rows), lambda r, me: (0, 0)),
         ],
         out_specs=[out, out],
     )
@@ -588,10 +571,11 @@
         hidden_kernel,
         grid_spec=spec,
         out_shape=[jax.ShapeDtypeStruct((groups, mine // 2, rows), t) for t in (BF, F32)],
+        compiler_params=pltpu.CompilerParams(vmem_limit_bytes=8 * 2**20),
         cost_estimate=pl.CostEstimate(
             flops=2 * hid * cols * rows, bytes_accessed=2 * hid * cols, transcendentals=0
         ),
-    )(me, w_out, out_grad)
+    )(me, w_out, flipped)
 
 
 def add_kernel(a, b, out):
@@ -602,27 +586,41 @@
     return pl.pallas_call(
         add_kernel,
         out_shape=jax.ShapeDtypeStruct(a.shape, kind),
+        compiler_params=pltpu.CompilerParams(vmem_limit_bytes=8 * 2**20),
         cost_estimate=pl.CostEstimate(flops=0, bytes_accessed=2**20, transcendentals=0),
     )(a, b)
 
 
-def weight_kernel(hidden_ref, grad_ref, out_ref):
-    groups, rows, cols = grad_ref.shape
-    out_ref[...] = jnp.dot(
-        hidden_ref[...], grad_ref[...].reshape(groups * rows, cols), preferred_element_type=F32
-    )
-
-
-def weight_grads(hidden, grad):
-    groups, rows, cols = grad.shape
-    mine = hidden.shape[0]
+def weight_kernel(me_ref, hidden_ref, *refs):
+    out_ref = refs[-1]
+    acc = None
+    for mask, grad in enumerate(refs[:-1]):
+        rows = grad.shape[0]
+        at = pl.multiple_of((me_ref[4] ^ mask) * rows, 128)
+        d = jnp.dot(hidden_ref[:, pl.ds(at, rows)], grad[...], preferred_element_type=F32)
+        acc = d if acc is None else acc + d
+    out_ref[...] = acc
+
+
+def weight_grads(me, hidden, grads):
+    rows, cols = grads[0].shape
+    mine, total = hidden.shape
+    spec = pltpu.PrefetchScalarGridSpec(
+        num_scalar_prefetch=1,
+        grid=(1,),
+        in_specs=[block((mine, total), lambda h, me: (0, 0))]
+        + [block((rows, cols), lambda h, me: (0, 0)) for _ in grads],
+        out_specs=block((mine, cols), lambda h, me: (0, 0)),
+    )
     return pl.pallas_call(
         weight_kernel,
+        grid_spec=spec,
         out_shape=jax.ShapeDtypeStruct((mine, cols), F32),
+        compiler_params=pltpu.CompilerParams(vmem_limit_bytes=12 * 2**20),
         cost_estimate=pl.CostEstimate(
-            flops=2 * mine * groups * rows * cols, bytes_accessed=4 * 2**20, transcendentals=0
+            flops=2 * mine * total * cols, bytes_accessed=4 * 2**20, transcendentals=0
         ),
-    )(hidden, grad)
+    )(me, hidden, *grads)
 
 
 def last_kernel(me_ref, got_ref, preact_ref, lhs_ref, out_ref):
@@ -653,6 +651,7 @@
         last_kernel,
         grid_spec=spec,
         out_shape=jax.ShapeDtypeStruct((count, width), F32),
+        compiler_params=pltpu.CompilerParams(vmem_limit_bytes=12 * 2**20),
         cost_estimate=pl.CostEstimate(
             flops=2 * total * count * width, bytes_accessed=2 * 2**20, transcendentals=0
         ),
@@ -687,10 +686,8 @@
         jnp.broadcast_to(packed[None], (groups,) + packed.shape), "rec", 0, 0, tiled=True
     )
 
-    size = records.shape[0] // 3
-    part = first_sums(real_labels[:size], records, frequencies, classes, size)
-    send_a, keep_a, send_b, keep_b, cs = second_sums(
-        me, real_labels[size:], syn_labels, (0, 2, 1, 3), images, records, size, frequencies, part,
+    send_a, keep_a, send_b, keep_b, cs = feature_sums(
+        me, real_labels, syn_labels, (0, 2, 1, 3), images, records, frequencies, classes,
         (real_total, syn_total),
     )
     got_a = swap(send_a, "rec", 1)
@@ -721,10 +718,18 @@
 
     send, keep = image_grads(me, cs, feat_grad, frequencies, cols)
     send, keep = split_y(me, keep, swap(send, "feat", 1))
-    out_grad = out_grads(keep, swap(send, "feat", 2), own, groups)
-
-    all_grad = lax.all_to_all(out_grad, "rec", 0, 0, tiled=True)
-    send, keep = hidden_grads(me, w_out, out_grad)
+    out_grad, flipped = out_grads(keep, swap(send, "feat", 2), own)
+
+    by = {0: out_grad}
+    by[1] = swap(out_grad, "rec", 1)
+    by[2] = swap(out_grad, "rec", 2)
+    by[4] = swap(out_grad, "rec", 4)
+    by[3] = swap(by[2], "rec", 1)
+    by[6] = swap(by[4], "rec", 2)
+    by[5] = swap(by[4], "rec", 1)
+    by[7] = swap(by[6], "rec", 1)
+
+    send, keep = hidden_grads(me, w_out, flipped, groups)
     part_grad = add(keep, swap(send, "feat", 1), BF)
     part_grad = add(part_grad, swap(part_grad, "feat", 2), BF)
     part_grad = lax.all_to_all(part_grad, "rec", 0, 0, tiled=True)
@@ -734,7 +739,7 @@
     grads = jnp.concatenate(
         [jnp.where(core == 0, grads, other), jnp.where(core == 0, other, grads)], axis=1
     )
-    grad_w_out = weight_grads(all_hidden, all_grad)
+    grad_w_out = weight_grads(me, all_hidden, [by[mask] for mask in range(groups)])
     return grad_w_out, grads[:dz], grads[dz:]
 
 

time: 246 us -> 202 us (0.82)
  Pallas kernels: 81.9 us -> 55.7 us
  waiting for transfers between devices: 74.2 us -> 60.3 us
  blocking collectives: 41.9 us -> 28.6 us
  starting transfers between devices: 22.7 us -> 29.1 us
  local copies, waits for them, and re-layouts: 14.3 us -> 17.4 us
    all_to_all x1, waiting for transfers between devices: 26.6 us -> 0.72 us  [eight_by_four(): part_grad = lax.all_to_all(part_grad, 'rec', 0, 0, tiled=True)]
    all_to_all x1 -> x0, blocking collectives: 12.7 us -> none  [eight_by_four(): part_grad = lax.all_to_all(part_grad, 'rec', 0, 0, tiled=True)]
    ppermute x13 -> x20, waiting for transfers between devices: 47.6 us -> 59.6 us  [swap(): return lax.ppermute(x, axis, [(i, i ^ bit) for i in range(n)])]
    pallas_call x4 -> x3, Pallas kernels: 47 us -> 40.9 us  [the longest x1 36.2 us: feature_sums(): pl.pallas_call(functools.partial(features_kernel, masks, size, *totals),...]
    ppermute x13 -> x20, starting transfers between devices: 15.3 us -> 21 us  [swap(): return lax.ppermute(x, axis, [(i, i ^ bit) for i in range(n)])]
    pallas_call x1, Pallas kernels: 7.23 us -> 2.06 us  [hidden_grads(): pl.pallas_call(hidden_kernel, grid_spec=spec, out_shape=[jax.ShapeDtypeSt...]
    pallas_call x1, Pallas kernels: 7.89 us -> 4.83 us  [image_grads(): pl.pallas_call(image_kernel, grid_spec=spec, out_shape=[jax.ShapeDtypeStr...]
    pallas_call x2, Pallas kernels: 3.66 us -> 0.81 us  [add(): pl.pallas_call(add_kernel, out_shape=jax.ShapeDtypeStruct(a.shape, kind),...]
  transfers between devices with their start and end apart: 15 -> 22, of which waited for: 12 -> 14; matrix products, arithmetic and copies ran while one was open for 3% -> 4% of each run, Pallas kernels for 10% -> 5%
where the time goes in v3:
time: 202 us; the launch traced here: 201 us
  waiting for transfers between devices  60.3 us (30%)
  Pallas kernels  55.7 us (28%)
  starting transfers between devices  29.1 us (14%)
  blocking collectives  28.6 us (14%)
  local copies, waits for them, and re-layouts  17.4 us (9%)
  matrix products  5.31 us (3%)
  other arithmetic  3.63 us (2%)
    ppermute x20, waiting for transfers between devices, swap(): return lax.ppermute(x, axis, [(i, i ^ bit) for i in range(n)])  59.6 us
    pallas_call x1, Pallas kernels, feature_sums(): pl.pallas_call(functools.partial(features_kernel, masks, size, *totals),...  36.2 us
    all_to_all x1, blocking collectives, eight_by_four(): lax.all_to_all(feat_grad.reshape(groups, rows, -1), 'rec', 0, 0, tiled=True)  28.6 us
    ppermute x20, starting transfers between devices, swap(): return lax.ppermute(x, axis, [(i, i ^ bit) for i in range(n)])  21 us
    unnamed x32, local copies, waits for them, and re-layouts  12.8 us
    pallas_call x1, Pallas kernels, image_grads(): pl.pallas_call(image_kernel, grid_spec=spec, out_shape=[jax.ShapeDtypeStr...  4.83 us
    all_to_all x1, starting transfers between devices, eight_by_four(): lax.all_to_all(jnp.broadcast_to(packed[None], (groups,) + packed.shape),...  4.05 us
    all_to_all x1, starting transfers between devices, eight_by_four(): part_grad = lax.all_to_all(part_grad, 'rec', 0, 0, tiled=True)  4.04 us
  transfers between devices with their start and end apart: 22, of which 14 were waited for; matrix products, arithmetic and copies ran while one was open for 4% of the time, Pallas kernels for 5%

profile of v3, /device:TPU:0, one launch (start us, length us, event | category | flops | bytes accessed | tf_op | source)
XLA Modules:
  0.0 201.0 jit_solution(15396740959385275543)
XLA Ops:
  0.7 1.2 copy-done
  1.9 1.0 fusion.12
  2.9 2.9 %fusion.4.refs_0_.image = bf16[128,768]{1,0:T(8,128)(2,1)S(1)} fusion(bf16[2048,768]{1,0:T(8,128)(2,1)} %w_ref.1, f32[128,2048]{1,0:T(8,128)S(1)} %fusion.12, bf16[128,128]{1,0:T(8,128)(2,1)} %param.15, bf16[128,2048]{1,0:T(8,128)(2,1)} %param.17), kind=kOutput, calls=%fused_computation.5 | convolution fusion | flops 470646784 | bytes 4947968 | tf_op jit(solution)/shard_map/dot_general | solution.py:679
  5.8 3.0 %collective-permute-start = (bf16[128,768]{1,0:T(8,128)(2,1)S(1)}, bf16[128,768]{1,0:T(8,128)(2,1)S(1)}, u32[]{:S(2)}, u32[]{:S(2)}) collective-permute-start(bf16[128,768]{1,0:T(8,128)(2,1)S(1)} %fusion.4.refs_0_.image), channel_id=1, source_target_pairs={{0,2},{1,3},{2,0},{3,1},{4,6},{5,7},{6,4},{7,5},{8,10},{9,11},{10,... | collective-permute-start | bytes 589832 | tf_op jit(solution)/shard_map/ppermute | solution.py:102
  8.9 4.9 %collective-permute-done.refs_1_ = bf16[128,768]{1,0:T(8,128)(2,1)S(1)} collective-permute-done((bf16[128,768]{1,0:T(8,128)(2,1)S(1)}, bf16[128,768]{1,0:T(8,128)(2,1)S(1)}, u32[]{:S(2)}, u32[]{:S(2)}) %collective-permute-start) | collective-permute-done | bytes 196640 | tf_op jit(solution)/shard_map/ppermute | solution.py:102
  15.9 0.9 copy-done.7
  16.9 0.9 copy-done.9
  17.8 0.9 copy-done.11
  18.7 36.2 %shard_map.112 = (bf16[4,128,512]{2,1,0:T(8,128)(2,1)}, f32[4,128,512]{2,1,0:T(8,128)S(1)}, bf16[2,2,128,512]{3,2,1,0:T(8,128)(2,1)}, f32[2,2,128,512]{3,2,1,0:T(8,128)S(1)}, f32[2,128,2048]{2,1,0:T(8,128)}) custom-call(s32[5]{0:T(128)S(1)} %stack.23.me_ref, s32[1,1536]{1,0:T(1,128)S(1)} %reshape.72.real_labels_ref, s32[1,128]{1,0:T(1,128)S(1)} %bitcast.24, ...), custom_call_target="tpu_custom_call" | custom-call | flops 24427626496 | bytes 26214400 | tf_op jit(solution)/shard_map/pallas_call | solution.py:343
  54.9 1.8 collective-permute-start.3
  56.7 1.6 collective-permute-start.4
  58.3 0.8 broadcast_in_dim.2
  59.1 4.1 %all-to-all-start = ((bf16[8,144,128]{2,1,0:T(8,128)(2,1)}), bf16[8,144,128]{2,1,0:T(8,128)(2,1)}, u32[]{:S(2)}, u32[]{:S(2)}) async-start(bf16[8,144,128]{2,1,0:T(8,128)(2,1)} %broadcast_in_dim.2), calls=%async_computation | async-start | bytes 589824 | tf_op jit(solution)/shard_map/all_to_all | solution.py:685
  63.1 7.7 %collective-permute-done.3 = bf16[4,128,512]{2,1,0:T(8,128)(2,1)} collective-permute-done((bf16[4,128,512]{2,1,0:T(8,128)(2,1)}, bf16[4,128,512]{2,1,0:T(8,128)(2,1)}, u32[]{:S(2)}, u32[]{:S(2)}) %collective-permute-start.3) | collective-permute-done | bytes 524320 | tf_op jit(solution)/shard_map/ppermute | solution.py:102
  70.8 2.7 %collective-permute-done.4.rb_s.rb_k = bf16[2,2,128,512]{3,2,1,0:T(8,128)(2,1)} collective-permute-done((bf16[2,2,128,512]{3,2,1,0:T(8,128)(2,1)}, bf16[2,2,128,512]{3,2,1,0:T(8,128)(2,1)}, u32[]{:S(2)}, u32[]{:S(2)}) %collective-permute-start.4) | collective-permute-done | bytes 524320 | tf_op jit(solution)/shard_map/ppermute | solution.py:102
  73.5 2.0 shard_map.113
  76.2 6.2 %collective-permute-done.5.ga_s.ga_k = bf16[2,128,512]{2,1,0:T(8,128)(2,1)S(1)} collective-permute-done((bf16[2,128,512]{2,1,0:T(8,128)(2,1)S(1)}, bf16[2,128,512]{2,1,0:T(8,128)(2,1)S(1)}, u32[]{:S(2)}, u32[]{:S(2)}) %collective-permute-start.5) | collective-permute-done | bytes 262176 | tf_op jit(solution)/shard_map/ppermute | solution.py:102
  83.4 4.8 %collective-permute-start.7 = (bf16[256,512]{1,0:T(8,128)(2,1)S(1)}, bf16[256,512]{1,0:T(8,128)(2,1)S(1)}, u32[]{:S(2)}, u32[]{:S(2)}) collective-permute-start(bf16[256,512]{1,0:T(8,128)(2,1)S(1)} %get-tuple-element.44), channel_id=1, source_target_pairs={{0,16},{4,20},{8,24},{12,28},{16,0},{20,4},{24,8},{28,12},{1,17},{... | collective-permute-start | bytes 786440 | tf_op jit(solution)/shard_map/ppermute | solution.py:102
  88.3 0.7 slice.31
  89.2 8.2 %collective-permute-done.7.got_ref = bf16[256,512]{1,0:T(8,128)(2,1)S(1)} collective-permute-done((bf16[256,512]{1,0:T(8,128)(2,1)S(1)}, bf16[256,512]{1,0:T(8,128)(2,1)S(1)}, u32[]{:S(2)}, u32[]{:S(2)}) %collective-permute-start.7) | collective-permute-done | bytes 262176 | tf_op jit(solution)/shard_map/ppermute | solution.py:102
  97.4 2.2 %copy-done.3 = f32[256,2,2048]{2,1,0:T(2,128)S(1)} copy-done((f32[256,2,2048]{2,1,0:T(2,128)S(1)}, f32[256,2,2048]{2,1,0:T(2,128)}, u32[]{:S(2)}) %copy-start.3) | copy-done | bytes 4194328
  99.6 1.3 shard_map.115
  100.9 28.6 %all_to_all.15.rows_ref = bf16[8,128,512]{2,1,0:T(8,128)(2,1)S(1)} all-to-all(bf16[8,128,512]{2,1,0:T(8,128)(2,1)S(1)} %bitcast.23), channel_id=1, replica_groups=mesh['rec'=8,'feat'=4] {'rec'}, dimensions={0} | all-to-all | bytes 2097152 | tf_op jit(solution)/shard_map/all_to_all | solution.py:717
  129.5 4.6 %copy-done.1 = bf16[3072,2048]{1,0:T(8,128)(2,1)S(1)} copy-done((bf16[3072,2048]{1,0:T(8,128)(2,1)S(1)}, bf16[3072,2048]{1,0:T(8,128)(2,1)}, u32[]{:S(2)}) %copy-start.1) | copy-done | bytes 12582936
  134.1 4.8 %shard_map.116 = (bf16[2,768,128]{2,1,0:T(8,128)(2,1)S(1)}, f32[2,768,128]{2,1,0:T(8,128)S(1)}) custom-call(s32[5]{0:T(128)S(1)} %stack.23.me_ref, f32[2,128,2048]{2,1,0:T(8,128)S(1)} %copy-done.4, bf16[8,128,512]{2,1,0:T(8,128)(2,1)S(1)} %all_to_all.15.rows_ref, bf16[3072,2048]{1,0:T(8,128)(2,1)S(1)} %copy-done.1), custom_call_target="tpu_custom_call" | custom-call | flops 1610612736 | bytes 12582912 | tf_op jit(solution)/shard_map/pallas_call | solution.py:500
  139.1 1.7 collective-permute-done.8.got_s.got_k
  141.4 1.5 collective-permute-start.9
  142.9 5.5 %collective-permute-done.9.got = bf16[768,128]{1,0:T(8,128)(2,1)S(1)} collective-permute-done((bf16[768,128]{1,0:T(8,128)(2,1)S(1)}, bf16[768,128]{1,0:T(8,128)(2,1)S(1)}, u32[]{:S(2)}, u32[]{:S(2)}) %collective-permute-start.9) | collective-permute-done | bytes 196640 | tf_op jit(solution)/shard_map/ppermute | solution.py:102
  148.4 0.9 shard_map.118
  149.3 2.1 %shard_map.120 = (bf16[8,128,128]{2,1,0:T(8,128)(2,1)S(1)}, f32[8,128,128]{2,1,0:T(8,128)S(1)}) custom-call(s32[5]{0:T(128)S(1)} %stack.23.me_ref, bf16[2048,768]{1,0:T(8,128)(2,1)S(1)} %copy-done.2, bf16[768,128]{1,0:T(8,128)(2,1)S(1)} %get-tuple-element.50.grad_ref), custom_call_target="tpu_custom_call" | custom-call | flops 402653184 | bytes 3145728 | tf_op jit(solution)/shard_map/pallas_call | solution.py:570
  151.4 1.5 collective-permute-done.17.b
  153.0 1.5 collective-permute-start.18
  154.5 1.0 collective-permute-start.13
  155.5 1.5 constant_dynamic-slice_fusion.1
  157.7 9.0 %collective-permute-done.13.refs_4_ = bf16[128,768]{1,0:T(8,128)(2,1)} collective-permute-done((bf16[128,768]{1,0:T(8,128)(2,1)}, bf16[128,768]{1,0:T(8,128)(2,1)}, u32[]{:S(2)}, u32[]{:S(2)}) %collective-permute-start.13) | collective-permute-done | bytes 196640 | tf_op jit(solution)/shard_map/ppermute | solution.py:102
  166.7 0.8 shard_map.122
  167.5 4.0 %all-to-all-start.2 = ((bf16[8,128,128]{2,1,0:T(8,128)(2,1)}), bf16[8,128,128]{2,1,0:T(8,128)(2,1)}, u32[]{:S(2)}, u32[]{:S(2)}) async-start(bf16[8,128,128]{2,1,0:T(8,128)(2,1)} %shard_map.122), calls=%async_computation.2 | async-start | bytes 524288 | tf_op jit(solution)/shard_map/all_to_all | solution.py:735
  171.7 1.2 slice.30
  173.0 1.4 maximum_convert_fusion
  174.4 2.0 collective-permute-start.10
  176.5 1.9 collective-permute-start.12
  178.6 1.2 fusion.7.lhs_ref
  179.7 0.7 all-to-all-done.2.got_ref
  180.5 2.6 %shard_map.123 = f32[384,128]{1,0:T(8,128)} custom-call(s32[5]{0:T(128)S(1)} %stack.23.me_ref, bf16[8,128,128]{2,1,0:T(8,128)(2,1)} %all-to-all-done.2.got_ref, f32[256,1024]{1,0:T(8,128)S(1)} %get-tuple-element.58.preact_ref, bf16[384,1024]{1,0:T(8,128)(2,1)S(1)} %fusion.7.lhs_ref), custom_call_target="tpu_custom_call" | custom-call | flops 100663296 | bytes 2097152 | tf_op jit(solution)/shard_map/pallas_call | solution.py:650
  183.1 8.4 %collective-permute-done.12.refs_3_ = bf16[128,768]{1,0:T(8,128)(2,1)} collective-permute-done((bf16[128,768]{1,0:T(8,128)(2,1)}, bf16[128,768]{1,0:T(8,128)(2,1)}, u32[]{:S(2)}, u32[]{:S(2)}) %collective-permute-start.12) | collective-permute-done | bytes 196640 | tf_op jit(solution)/shard_map/ppermute | solution.py:102
  191.5 3.2 %collective-permute-done.16.refs_7_ = bf16[128,768]{1,0:T(8,128)(2,1)} collective-permute-done((bf16[128,768]{1,0:T(8,128)(2,1)}, bf16[128,768]{1,0:T(8,128)(2,1)}, u32[]{:S(2)}, u32[]{:S(2)}) %collective-permute-start.16) | collective-permute-done | bytes 196640 | tf_op jit(solution)/shard_map/ppermute | solution.py:102
  194.8 3.9 %shard_map.119 = f32[256,768]{1,0:T(8,128)} custom-call(s32[5]{0:T(128)S(1)} %stack.23.me_ref, bf16[256,1024]{1,0:T(8,128)(2,1)S(1)} %get-tuple-element.57.hidden_ref, bf16[128,768]{1,0:T(8,128)(2,1)} %get-tuple-element.49.refs_0_, bf16[128,768]{1,0:T(8,128)(2,1)} %collective-permute-done.10.refs_1_, bf16[128,768]{1,0:T(8,128)(2,1)} %collective-permute-done.11.refs_2_, ...), custom_call_target="tpu_custom_call" | custom-call | flops 402653184 | bytes 4194304 | tf_op jit(solution)/shard_map/pallas_call | solution.py:615
  198.7 1.0 broadcast_select_fusion.1
  (61 shorter events, 7.7 us)
Async XLA Ops:
  0.6 1.2 copy-start
  0.6 15.3 %copy-start.5 = (s32[128]{0:T(128)S(1)}, s32[128]{0:T(128)}, u32[]{:S(2)}) copy-start(s32[128]{0:T(128)} %param.16) | copy-start | bytes 1540
  0.7 13.8 %copy-start.15 = (s32[1536]{0:T(1024)S(1)}, s32[1536]{0:T(1024)}, u32[]{:S(2)}) copy-start(s32[1536]{0:T(1024)} %param.12) | copy-start | bytes 18436
  5.8 7.9 %collective-permute-start = (bf16[128,768]{1,0:T(8,128)(2,1)S(1)}, bf16[128,768]{1,0:T(8,128)(2,1)S(1)}, u32[]{:S(2)}, u32[]{:S(2)}) collective-permute-start(bf16[128,768]{1,0:T(8,128)(2,1)S(1)} %fusion.4.refs_0_.image), channel_id=1, source_target_pairs={{0,2},{1,3},{2,0},{3,1},{4,6},{5,7},{6,4},{7,5},{8,10},{9,11},{10,... | collective-permute-start | bytes 589832 | tf_op jit(solution)/shard_map/ppermute | solution.py:102
  8.9 5.7 %collective-permute-start.1 = (bf16[128,768]{1,0:T(8,128)(2,1)S(1)}, bf16[128,768]{1,0:T(8,128)(2,1)S(1)}, u32[]{:S(2)}, u32[]{:S(2)}) collective-permute-start(bf16[128,768]{1,0:T(8,128)(2,1)S(1)} %fusion.4.refs_0_.image), channel_id=1, source_target_pairs={{0,1},{1,0},{2,3},{3,2},{4,5},{5,4},{6,7},{7,6},{8,9},{9,8},{10,11... | collective-permute-start | bytes 589832 | tf_op jit(solution)/shard_map/ppermute | solution.py:102
  13.8 1.5 collective-permute-start.2
  13.8 0.7 copy-start.6
  14.6 0.7 copy-start.8
  15.2 0.7 copy-start.10
  15.9 0.9 copy-start.7
  16.9 0.9 copy-start.9
  17.8 0.9 copy-start.11
  18.7 39.6 %copy-start.14 = (bf16[128,128]{1,0:T(8,128)(2,1)S(1)}, bf16[128,128]{1,0:T(8,128)(2,1)}, u32[]{:S(2)}) copy-start(bf16[128,128]{1,0:T(8,128)(2,1)} %param.15) | copy-start | bytes 98308
  54.9 15.9 %collective-permute-start.3 = (bf16[4,128,512]{2,1,0:T(8,128)(2,1)}, bf16[4,128,512]{2,1,0:T(8,128)(2,1)}, u32[]{:S(2)}, u32[]{:S(2)}) collective-permute-start(bf16[4,128,512]{2,1,0:T(8,128)(2,1)} %get-tuple-element.36), channel_id=1, source_target_pairs={{0,4},{4,0},{8,12},{12,8},{16,20},{20,16},{24,28},{28,24},{1,5},{5... | collective-permute-start | bytes 1572872 | tf_op jit(solution)/shard_map/ppermute | solution.py:102
  56.7 16.8 %collective-permute-start.4 = (bf16[2,2,128,512]{3,2,1,0:T(8,128)(2,1)}, bf16[2,2,128,512]{3,2,1,0:T(8,128)(2,1)}, u32[]{:S(2)}, u32[]{:S(2)}) collective-permute-start(bf16[2,2,128,512]{3,2,1,0:T(8,128)(2,1)} %get-tuple-element.38), channel_id=1, source_target_pairs={{0,8},{4,12},{8,0},{12,4},{16,24},{20,28},{24,16},{28,20},{1,9},{5... | collective-permute-start | bytes 1572872 | tf_op jit(solution)/shard_map/ppermute | solution.py:102
  59.1 29.2 %all-to-all-start = ((bf16[8,144,128]{2,1,0:T(8,128)(2,1)}), bf16[8,144,128]{2,1,0:T(8,128)(2,1)}, u32[]{:S(2)}, u32[]{:S(2)}) async-start(bf16[8,144,128]{2,1,0:T(8,128)(2,1)} %broadcast_in_dim.2), calls=%async_computation | async-start | bytes 589824 | tf_op jit(solution)/shard_map/all_to_all | solution.py:685
  75.5 6.9 %collective-permute-start.5 = (bf16[2,128,512]{2,1,0:T(8,128)(2,1)S(1)}, bf16[2,128,512]{2,1,0:T(8,128)(2,1)S(1)}, u32[]{:S(2)}, u32[]{:S(2)}) collective-permute-start(bf16[2,128,512]{2,1,0:T(8,128)(2,1)S(1)} %get-tuple-element.40), channel_id=1, source_target_pairs={{0,8},{4,12},{8,0},{12,4},{16,24},{20,28},{24,16},{28,20},{1,9},{5... | collective-permute-start | bytes 786440 | tf_op jit(solution)/shard_map/ppermute | solution.py:102
  75.6 7.2 %collective-permute-start.6 = (bf16[2,128,512]{2,1,0:T(8,128)(2,1)S(1)}, bf16[2,128,512]{2,1,0:T(8,128)(2,1)S(1)}, u32[]{:S(2)}, u32[]{:S(2)}) collective-permute-start(bf16[2,128,512]{2,1,0:T(8,128)(2,1)S(1)} %get-tuple-element.42), channel_id=1, source_target_pairs={{0,4},{4,0},{8,12},{12,8},{16,20},{20,16},{24,28},{28,24},{1,5},{5... | collective-permute-start | bytes 786440 | tf_op jit(solution)/shard_map/ppermute | solution.py:102
  83.4 14.0 %collective-permute-start.7 = (bf16[256,512]{1,0:T(8,128)(2,1)S(1)}, bf16[256,512]{1,0:T(8,128)(2,1)S(1)}, u32[]{:S(2)}, u32[]{:S(2)}) collective-permute-start(bf16[256,512]{1,0:T(8,128)(2,1)S(1)} %get-tuple-element.44), channel_id=1, source_target_pairs={{0,16},{4,20},{8,24},{12,28},{16,0},{20,4},{24,8},{28,12},{1,17},{... | collective-permute-start | bytes 786440 | tf_op jit(solution)/shard_map/ppermute | solution.py:102
  97.4 2.2 %copy-start.3 = (f32[256,2,2048]{2,1,0:T(2,128)S(1)}, f32[256,2,2048]{2,1,0:T(2,128)}, u32[]{:S(2)}) copy-start(f32[256,2,2048]{2,1,0:T(2,128)} %noise_ref.1) | copy-start | bytes 12582916
  99.6 29.9 %copy-start.4 = (f32[2,128,2048]{2,1,0:T(8,128)S(1)}, f32[2,128,2048]{2,1,0:T(8,128)}, u32[]{:S(2)}) copy-start(f32[2,128,2048]{2,1,0:T(8,128)} %get-tuple-element.34.cs_ref) | copy-start | bytes 6291460
  129.5 4.6 %copy-start.1 = (bf16[3072,2048]{1,0:T(8,128)(2,1)S(1)}, bf16[3072,2048]{1,0:T(8,128)(2,1)}, u32[]{:S(2)}) copy-start(bf16[3072,2048]{1,0:T(8,128)(2,1)} %freq_ref.1) | copy-start | bytes 37748740
  139.0 10.3 %copy-start.2 = (bf16[2048,768]{1,0:T(8,128)(2,1)S(1)}, bf16[2048,768]{1,0:T(8,128)(2,1)}, u32[]{:S(2)}) copy-start(bf16[2048,768]{1,0:T(8,128)(2,1)} %w_ref.1) | copy-start | bytes 9437188
  139.0 1.8 collective-permute-start.8
  141.4 7.0 %collective-permute-start.9 = (bf16[768,128]{1,0:T(8,128)(2,1)S(1)}, bf16[768,128]{1,0:T(8,128)(2,1)S(1)}, u32[]{:S(2)}, u32[]{:S(2)}) collective-permute-start(bf16[768,128]{1,0:T(8,128)(2,1)S(1)} %get-tuple-element.48), channel_id=1, source_target_pairs={{0,2},{1,3},{2,0},{3,1},{4,6},{5,7},{6,4},{7,5},{8,10},{9,11},{10,... | collective-permute-start | bytes 589832 | tf_op jit(solution)/shard_map/ppermute | solution.py:102
  151.3 1.6 collective-permute-start.17
  153.0 13.7 %collective-permute-start.18 = (bf16[8,128,128]{2,1,0:T(8,128)(2,1)S(1)}, bf16[8,128,128]{2,1,0:T(8,128)(2,1)S(1)}, u32[]{:S(2)}, u32[]{:S(2)}) collective-permute-start(bf16[8,128,128]{2,1,0:T(8,128)(2,1)S(1)} %shard_map.121.a), channel_id=1, source_target_pairs={{0,2},{1,3},{2,0},{3,1},{4,6},{5,7},{6,4},{7,5},{8,10},{9,11},{10,... | collective-permute-start | bytes 786440 | tf_op jit(solution)/shard_map/ppermute | solution.py:102
  154.5 12.2 %collective-permute-start.13 = (bf16[128,768]{1,0:T(8,128)(2,1)}, bf16[128,768]{1,0:T(8,128)(2,1)}, u32[]{:S(2)}, u32[]{:S(2)}) collective-permute-start(bf16[128,768]{1,0:T(8,128)(2,1)} %get-tuple-element.49.refs_0_), channel_id=1, source_target_pairs={{0,16},{4,20},{8,24},{12,28},{16,0},{20,4},{24,8},{28,12},{1,17},{... | collective-permute-start | bytes 589832 | tf_op jit(solution)/shard_map/ppermute | solution.py:102
  157.0 19.4 %collective-permute-start.11 = (bf16[128,768]{1,0:T(8,128)(2,1)}, bf16[128,768]{1,0:T(8,128)(2,1)}, u32[]{:S(2)}, u32[]{:S(2)}) collective-permute-start(bf16[128,768]{1,0:T(8,128)(2,1)} %get-tuple-element.49.refs_0_), channel_id=1, source_target_pairs={{0,8},{4,12},{8,0},{12,4},{16,24},{20,28},{24,16},{28,20},{1,9},{5... | collective-permute-start | bytes 589832 | tf_op jit(solution)/shard_map/ppermute | solution.py:102
  166.7 11.6 %collective-permute-start.15 = (bf16[128,768]{1,0:T(8,128)(2,1)}, bf16[128,768]{1,0:T(8,128)(2,1)}, u32[]{:S(2)}, u32[]{:S(2)}) collective-permute-start(bf16[128,768]{1,0:T(8,128)(2,1)} %collective-permute-done.13.refs_4_), channel_id=1, source_target_pairs={{0,8},{4,12},{8,0},{12,4},{16,24},{20,28},{24,16},{28,20},{1,9},{5... | collective-permute-start | bytes 589832 | tf_op jit(solution)/shard_map/ppermute | solution.py:102
  167.5 13.0 %all-to-all-start.2 = ((bf16[8,128,128]{2,1,0:T(8,128)(2,1)}), bf16[8,128,128]{2,1,0:T(8,128)(2,1)}, u32[]{:S(2)}, u32[]{:S(2)}) async-start(bf16[8,128,128]{2,1,0:T(8,128)(2,1)} %shard_map.122), calls=%async_computation.2 | async-start | bytes 524288 | tf_op jit(solution)/shard_map/all_to_all | solution.py:735
  171.6 6.7 %copy-start.12 = (bf16[1024,256]{0,1:T(8,128)(2,1)}, bf16[1024,256]{0,1:T(8,128)(2,1)S(1)}, u32[]{:S(2)}) copy-start(bf16[1024,256]{0,1:T(8,128)(2,1)S(1)} %fusion.5) | copy-start | bytes 1572868
  173.0 5.4 %copy-start.13 = (bf16[1024,128]{0,1:T(8,128)(2,1)}, bf16[1024,128]{0,1:T(8,128)(2,1)S(1)}, u32[]{:S(2)}) copy-start(bf16[1024,128]{0,1:T(8,128)(2,1)S(1)} %copy.19) | copy-start | bytes 786436
  174.4 8.8 %collective-permute-start.10 = (bf16[128,768]{1,0:T(8,128)(2,1)}, bf16[128,768]{1,0:T(8,128)(2,1)}, u32[]{:S(2)}, u32[]{:S(2)}) collective-permute-start(bf16[128,768]{1,0:T(8,128)(2,1)} %get-tuple-element.49.refs_0_), channel_id=1, source_target_pairs={{0,4},{4,0},{8,12},{12,8},{16,20},{20,16},{24,28},{28,24},{1,5},{5... | collective-permute-start | bytes 589832 | tf_op jit(solution)/shard_map/ppermute | solution.py:102
  176.3 15.2 %collective-permute-start.14 = (bf16[128,768]{1,0:T(8,128)(2,1)}, bf16[128,768]{1,0:T(8,128)(2,1)}, u32[]{:S(2)}, u32[]{:S(2)}) collective-permute-start(bf16[128,768]{1,0:T(8,128)(2,1)} %collective-permute-done.13.refs_4_), channel_id=1, source_target_pairs={{0,4},{4,0},{8,12},{12,8},{16,20},{20,16},{24,28},{28,24},{1,5},{5... | collective-permute-start | bytes 589832 | tf_op jit(solution)/shard_map/ppermute | solution.py:102
  176.5 15.1 %collective-permute-start.12 = (bf16[128,768]{1,0:T(8,128)(2,1)}, bf16[128,768]{1,0:T(8,128)(2,1)}, u32[]{:S(2)}, u32[]{:S(2)}) collective-permute-start(bf16[128,768]{1,0:T(8,128)(2,1)} %collective-permute-done.11.refs_2_), channel_id=1, source_target_pairs={{0,4},{4,0},{8,12},{12,8},{16,20},{20,16},{24,28},{28,24},{1,5},{5... | collective-permute-start | bytes 589832 | tf_op jit(solution)/shard_map/ppermute | solution.py:102
  178.4 16.4 %collective-permute-start.16 = (bf16[128,768]{1,0:T(8,128)(2,1)}, bf16[128,768]{1,0:T(8,128)(2,1)}, u32[]{:S(2)}, u32[]{:S(2)}) collective-permute-start(bf16[128,768]{1,0:T(8,128)(2,1)} %collective-permute-done.15.refs_6_), channel_id=1, source_target_pairs={{0,4},{4,0},{8,12},{12,8},{16,20},{20,16},{24,28},{28,24},{1,5},{5... | collective-permute-start | bytes 589832 | tf_op jit(solution)/shard_map/ppermute | solution.py:102
  183.0 15.6 %collective-permute-start.19 = (f32[384,128]{1,0:T(8,128)}, f32[384,128]{1,0:T(8,128)S(1)}, u32[]{:S(2)}, u32[]{:S(2)}) collective-permute-start(f32[384,128]{1,0:T(8,128)} %shard_map.123), channel_id=1, source_target_pairs={{0,1},{1,0},{2,3},{3,2},{4,5},{5,4},{6,7},{7,6},{8,9},{9,8},{10,11... | collective-permute-start | bytes 589832 | tf_op jit(solution)/shard_map/ppermute | solution.py:102

commit v4 on v3

--- a/solution.py
+++ b/solution.py
@@ -236,25 +236,36 @@
     return jnp.dot(table, phi, preferred_element_type=F32)
 
 
-def features_kernel(masks, size, real_total, syn_total, me_ref, real_labels_ref, syn_labels_ref, *refs):
+def features_kernel(
+    masks, last, real_total, syn_total, me_ref, real_labels_ref, syn_labels_ref, *refs
+):
     count = len(masks)
     images = refs[:count]
-    records_hbm, freq_ref, send_a, keep_a, send_b, keep_b, cs_ref = refs[count : count + 7]
-    records, real_table, syn_table, sem = refs[count + 7 :]
+    records_hbm, freq_ref = refs[count : count + 2]
+    outs = refs[count + 2 : -4]
+    records, real_table, syn_table, sem = refs[-4:]
     classes, total = real_table.shape
+    size = 512
     steps = total // size
-    feat, x, z_low = me_ref[0], me_ref[1], me_ref[2]
     step = pl.program_id(0)
     cols = images[0].shape[1]
+    half = classes // 2
 
     def copy(i):
         at = pl.ds(i * size, size)
         return pltpu.make_async_copy(records_hbm.at[at, :], records.at[at, :], sem.at[i])
 
-    def body(wait):
+    def work(wait):
+        if wait:
+            for i in range(steps):
+                copy(i).start()
+            ids = lax.broadcasted_iota(jnp.int32, (classes, total), 0)
+            real_table[...] = jnp.where(ids == real_labels_ref[...], 1.0, 0.0).astype(BF)
+            ids = lax.broadcasted_iota(jnp.int32, syn_table.shape, 0)
+            syn_table[...] = jnp.where(ids == syn_labels_ref[...], 1.0, 0.0).astype(BF)
         syn_pre = None
         for mask, image in zip(masks, images):
-            at = pl.multiple_of((feat ^ mask) * cols, 128)
+            at = pl.multiple_of((me_ref[0] ^ mask) * cols, 128)
             d = jnp.dot(image[...], freq_ref[pl.ds(at, cols), :], preferred_element_type=F32)
             syn_pre = d if syn_pre is None else syn_pre + d
         freq = freq_ref[...]
@@ -267,8 +278,8 @@
                 pre = jnp.dot(records[i * size : (i + 1) * size, :], freq, preferred_element_type=F32)
             if i == 0:
                 co, si = cos_sin(syn_pre)
-                cs_ref[0] = co
-                cs_ref[1] = si
+                outs[-1][0, 0] = co
+                outs[-1][0, 1] = si
                 phi = jnp.concatenate([co.astype(BF), si.astype(BF)], axis=1)
                 syn = jnp.dot(syn_table[...], phi, preferred_element_type=F32)
             else:
@@ -276,224 +287,213 @@
                 acc = d if acc is None else acc + d
             before = pre
         gap = syn * (1.0 / syn_total) - acc * (1.0 / real_total)
-        zero = jnp.concatenate([gap[:, :256], gap[:, 512:768]], axis=1)
-        one = jnp.concatenate([gap[:, 256:512], gap[:, 768:]], axis=1)
-        half = classes // 2
-        keep_a[0] = jnp.where(x == 0, zero[:half], one[:half])
-        send_a[0] = jnp.where(x == 0, one[:half], zero[:half]).astype(BF)
-        high = step // 2
-
-        @pl.when(step % 2 == z_low)
-        def _():
-            keep_b[high, 0] = zero[half:]
-            keep_b[high, 1] = one[half:]
-
-        @pl.when(step % 2 != z_low)
-        def _():
-            send_b[high, 0] = zero[half:].astype(BF)
-            send_b[high, 1] = one[half:].astype(BF)
+        width = gap.shape[1] // 4
+        return [
+            jnp.concatenate(
+                [gap[:, h * width : (h + 1) * width], gap[:, (h + 2) * width : (h + 3) * width]], axis=1
+            )
+            for h in range(2)
+        ]
+
+    if last:
+        parts = work(True)
+        for h in range(2):
+            outs[0][h] = parts[h][:half]
+            outs[1][h] = parts[h][half:]
+        return
+    send_a, keep_a, send_b, keep_b = outs[:4]
 
     @pl.when(step == 0)
     def _():
-        for i in range(steps):
-            copy(i).start()
-        ids = lax.broadcasted_iota(jnp.int32, (classes, total), 0)
-        real_table[...] = jnp.where(ids == real_labels_ref[...], 1.0, 0.0).astype(BF)
-        ids = lax.broadcasted_iota(jnp.int32, syn_table.shape, 0)
-        syn_table[...] = jnp.where(ids == syn_labels_ref[...], 1.0, 0.0).astype(BF)
-        body(True)
+        parts = work(True)
+        for h in range(2):
+            send_a[0, h] = parts[h][:half].astype(BF)
+            send_b[0, h] = parts[h][half:].astype(BF)
 
     @pl.when(step > 0)
     def _():
-        body(False)
-
-
-def feature_sums(me, real_labels, syn_labels, masks, images, records, freq, classes, totals):
+        parts = work(False)
+
+        @pl.when(step == 1)
+        def _():
+            for h in range(2):
+                send_a[0, h] = parts[h][:half].astype(BF)
+                keep_b[h] = parts[h][half:]
+
+        @pl.when(step == 2)
+        def _():
+            for h in range(2):
+                keep_a[h] = parts[h][:half]
+                send_b[0, h] = parts[h][half:].astype(BF)
+
+
+def feature_sums(last, me, real_labels, syn_labels, masks, images, records, freq, classes, totals):
     total, k = records.shape
     n = freq.shape[1]
     rows, cols = images[0].shape
     half = classes // 2
-    size = 512
+    tile = n // 4
+    tiles = 1 if last else 3
+    whole = lambda shape: block(shape, lambda j, me: (0,) * len(shape))
+    kept = jax.ShapeDtypeStruct((2, half, tile), F32)
+    sent = jax.ShapeDtypeStruct((2, 2, half, tile), BF)
+    wave = jax.ShapeDtypeStruct((tiles, 2, rows, tile), F32)
+    wave_spec = block((1, 2, rows, tile), lambda j, me: (j, 0, 0, 0))
+    if last:
+        shapes = [kept, kept, wave]
+        specs = [whole(kept.shape), whole(kept.shape), wave_spec]
+    else:
+        shapes = [sent, kept, sent, kept, wave]
+        specs = [
+            block((1, 2, half, tile), lambda j, me: (jnp.minimum(j, 1), 0, 0, 0)),
+            whole(kept.shape),
+            block((1, 2, half, tile), lambda j, me: (j // 2, 0, 0, 0)),
+            whole(kept.shape),
+            wave_spec,
+        ]
     grid_spec = pltpu.PrefetchScalarGridSpec(
         num_scalar_prefetch=1,
-        grid=(n // 512,),
-        in_specs=[
-            block((1, total), lambda j, me: (0, 0)),
-            block((1, rows), lambda j, me: (0, 0)),
-        ]
-        + [block((rows, cols), lambda j, me: (0, 0)) for _ in images]
+        grid=(tiles,),
+        in_specs=[whole((1, total)), whole((1, rows))]
+        + [whole((rows, cols)) for _ in images]
         + [
             pl.BlockSpec(memory_space=pl.ANY),
-            block((k, 512), lambda j, me: (0, j)),
+            block((k, tile), lambda j, me: (0, me[5] ^ (0 if last else 3 - j))),
         ],
-        out_specs=[
-            block((1, half, 512), lambda j, me: (j, 0, 0)),
-            block((1, half, 512), lambda j, me: (j, 0, 0)),
-            block((2, 2, half, 512), lambda j, me: (0, 0, 0, 0)),
-            block((2, 2, half, 512), lambda j, me: (0, 0, 0, 0)),
-            block((2, rows, 512), lambda j, me: (0, 0, j)),
-        ],
+        out_specs=specs,
         scratch_shapes=[
             pltpu.VMEM((total, k), BF),
             pltpu.VMEM((classes, total), BF),
             pltpu.VMEM((classes, rows), BF),
-            pltpu.SemaphoreType.DMA((total // size,)),
+            pltpu.SemaphoreType.DMA((total // 512,)),
         ],
     )
     return pl.pallas_call(
-        functools.partial(features_kernel, masks, size, *totals),
+        functools.partial(features_kernel, masks, last, *totals),
         grid_spec=grid_spec,
-        out_shape=[
-            jax.ShapeDtypeStruct((4, half, 512), BF),
-            jax.ShapeDtypeStruct((4, half, 512), F32),
-            jax.ShapeDtypeStruct((2, 2, half, 512), BF),
-            jax.ShapeDtypeStruct((2, 2, half, 512), F32),
-            jax.ShapeDtypeStruct((2, rows, n), F32),
-        ],
-        compiler_params=pltpu.CompilerParams(vmem_limit_bytes=50 * 2**20),
+        out_shape=shapes,
+        compiler_params=pltpu.CompilerParams(vmem_limit_bytes=44 * 2**20),
         cost_estimate=pl.CostEstimate(
-            flops=2 * (total + rows) * n * (k + 2 * classes),
-            bytes_accessed=2 * (total * k + k * n) + 4 * classes * n * 2,
+            flops=2 * (total + rows) * tiles * tile * (k + 2 * classes),
+            bytes_accessed=2 * (total * k + k * tiles * tile),
             transcendentals=0,
         ),
     )(me, real_labels.reshape(1, -1), syn_labels.reshape(1, -1), *images, records, freq)
 
 
-def stage_two_kernel(me_ref, ka_s, ka_k, ra_s, ra_k, kb_s, kb_k, rb_s, rb_k, sa, na, sb, nb):
-    sa[0] = (ka_s[0, 0] + ra_s[0, 0].astype(F32)).astype(BF)
-    na[0] = ka_k[0, 0] + ra_k[0, 0].astype(F32)
-    sb[0] = (kb_s[0, 0] + rb_s[0, 0].astype(F32)).astype(BF)
-    nb[0] = kb_k[0, 0] + rb_k[0, 0].astype(F32)
-
-
-def stage_two(me, keep_a, got_a, keep_b, got_b):
-    half, width = keep_b.shape[2:]
-    shape = (1, 1, half, width)
-    keep_a = keep_a.reshape(2, 2, half, width)
-    got_a = got_a.reshape(2, 2, half, width)
-    low = lambda flip: block(shape, lambda h, me: (h, me[2] ^ flip, 0, 0))
-    xs = lambda flip: block(shape, lambda h, me: (h, me[1] ^ flip, 0, 0))
-    out = block((1, half, width), lambda h, me: (h, 0, 0))
-    spec = pltpu.PrefetchScalarGridSpec(
-        num_scalar_prefetch=1,
-        grid=(2,),
-        in_specs=[low(1), low(0), low(1), low(0), xs(1), xs(0), xs(1), xs(0)],
-        out_specs=[out] * 4,
-    )
-    kinds = [BF, F32, BF, F32]
-    return pl.pallas_call(
-        stage_two_kernel,
-        grid_spec=spec,
-        out_shape=[jax.ShapeDtypeStruct((2, half, width), t) for t in kinds],
-        compiler_params=pltpu.CompilerParams(vmem_limit_bytes=8 * 2**20),
-        cost_estimate=pl.CostEstimate(flops=0, bytes_accessed=4 * 2**20, transcendentals=0),
-    )(me, keep_a, keep_a, got_a, got_a, keep_b, keep_b, got_b, got_b)
-
-
-def stage_three_kernel(me_ref, na_s, na_k, ga_s, ga_k, nb_s, nb_k, gb_s, gb_k, send, keep):
-    half = na_s.shape[1]
-    send[:half] = (na_s[0] + ga_s[0].astype(F32)).astype(BF)
-    keep[:half] = na_k[0] + ga_k[0].astype(F32)
-    send[half:] = (nb_s[0] + gb_s[0].astype(F32)).astype(BF)
-    keep[half:] = nb_k[0] + gb_k[0].astype(F32)
-
-
-def stage_three(me, next_a, got_a, next_b, got_b):
-    _, half, width = next_a.shape
-    high = lambda flip: block((1, half, width), lambda h, me: (me[3] ^ flip, 0, 0))
-    out = block((2 * half, width), lambda h, me: (0, 0))
+def stage_two_send_kernel(ka, ga, kb, gb, sa, sb):
+    sa[...] = (ka[...] + ga[0].astype(F32)).astype(BF)
+    sb[...] = (kb[...] + gb[0].astype(F32)).astype(BF)
+
+
+def stage_two_send(keep_a, got_a, keep_b, got_b):
+    return pl.pallas_call(
+        stage_two_send_kernel,
+        out_shape=[jax.ShapeDtypeStruct(keep_a.shape, BF)] * 2,
+        compiler_params=pltpu.CompilerParams(vmem_limit_bytes=10 * 2**20),
+        cost_estimate=pl.CostEstimate(flops=0, bytes_accessed=3 * 2**20, transcendentals=0),
+    )(keep_a, got_a, keep_b, got_b)
+
+
+def stage_three_kernel(me_ref, na, fa, ga, nb, fb, gb, send, keep):
+    high = me_ref[3]
+    half = na.shape[1]
+    for flip, out in ((1, send), (0, keep)):
+        at = high ^ flip
+        out[:half] = (na[at] + fa[1, at].astype(F32) + ga[at].astype(F32)).astype(out.dtype)
+        out[half:] = (nb[at] + fb[1, at].astype(F32) + gb[at].astype(F32)).astype(out.dtype)
+
+
+def stage_three(me, keep_a, first_a, got_a, keep_b, first_b, got_b):
+    _, half, width = keep_a.shape
+    args = (keep_a, first_a, got_a, keep_b, first_b, got_b)
+    whole = lambda shape: block(shape, lambda h, me: (0,) * len(shape))
     spec = pltpu.PrefetchScalarGridSpec(
         num_scalar_prefetch=1,
         grid=(1,),
-        in_specs=[high(1), high(0)] * 4,
-        out_specs=[out, out],
+        in_specs=[whole(x.shape) for x in args],
+        out_specs=[whole((2 * half, width))] * 2,
     )
     return pl.pallas_call(
         stage_three_kernel,
         grid_spec=spec,
         out_shape=[jax.ShapeDtypeStruct((2 * half, width), t) for t in (BF, F32)],
-        compiler_params=pltpu.CompilerParams(vmem_limit_bytes=8 * 2**20),
+        compiler_params=pltpu.CompilerParams(vmem_limit_bytes=12 * 2**20),
         cost_estimate=pl.CostEstimate(flops=0, bytes_accessed=3 * 2**20, transcendentals=0),
-    )(me, next_a, next_a, got_a, got_a, next_b, next_b, got_b, got_b)
-
-
-def gap_kernel(real_total, me_ref, keep_ref, got_ref, noise_ref, labels_ref, out_ref):
+    )(me, *args)
+
+
+def gap_kernel(real_total, keep_ref, got_ref, noise_ref, labels_ref, out_ref):
     classes = keep_ref.shape[0]
-    part = noise_ref.shape[2]
-    noise = jnp.concatenate([noise_ref[:, 0, :], noise_ref[:, 1, :]], axis=1)
-    gap = keep_ref[...] + got_ref[...].astype(F32) - noise * (1.0 / real_total)
+    gap = keep_ref[...] + got_ref[...].astype(F32) - noise_ref[...] * (1.0 / real_total)
     gap = (16.0 * gap).astype(BF)
     ids = lax.broadcasted_iota(jnp.int32, (labels_ref.shape[0], classes), 1)
     table = jnp.where(ids == labels_ref[...], 1.0, 0.0).astype(BF)
     out_ref[...] = jnp.dot(table, gap, preferred_element_type=F32).astype(BF)
 
 
-def gap_rows(me, keep, got, noise, labels, real_total):
+def gap_rows(keep, got, noise, labels, real_total):
     classes, width = keep.shape
     total = labels.shape[0]
-    spec = pltpu.PrefetchScalarGridSpec(
-        num_scalar_prefetch=1,
-        grid=(1,),
-        in_specs=[
-            block((classes, width), lambda h, me: (0, 0)),
-            block((classes, width), lambda h, me: (0, 0)),
-            block((classes, 2, width // 2), lambda h, me: (0, 0, me[4])),
-            block((total, 1), lambda h, me: (0, 0)),
-        ],
-        out_specs=block((total, width), lambda h, me: (0, 0)),
-    )
     return pl.pallas_call(
         functools.partial(gap_kernel, real_total),
-        grid_spec=spec,
         out_shape=jax.ShapeDtypeStruct((total, width), BF),
         compiler_params=pltpu.CompilerParams(vmem_limit_bytes=14 * 2**20),
         cost_estimate=pl.CostEstimate(
             flops=2 * total * classes * width, bytes_accessed=3 * 2**20, transcendentals=0
         ),
-    )(me, keep, got, noise, labels.reshape(total, 1))
+    )(keep, got, noise, labels.reshape(total, 1))
 
 
 NT = (((1,), (1,)), ((), ()))
 
 
-def image_kernel(me_ref, cs_ref, rows_ref, freq_ref, send_ref, keep_ref, pre_ref):
+def image_kernel(me_ref, three_ref, last_ref, rows_ref, freq_ref, send_ref, keep_ref, pre_ref):
     step = pl.program_id(0)
-    owners, _, width = rows_ref.shape
-    part = width // 2
+    cols = send_ref.shape[1]
+    tile = three_ref.shape[3]
+    part = tile // 2
 
     @pl.when(step == 0)
     def _():
-        for o in range(owners):
-            at = slice(o * part, (o + 1) * part)
-            grad = rows_ref[o].astype(F32)
-            pre = cs_ref[0, :, at] * grad[:, part:] - cs_ref[1, :, at] * grad[:, :part]
-            pre_ref[:, at] = pre.astype(BF)
+        for t in range(4):
+            place = me_ref[5] ^ (3 - t)
+            wave = last_ref.at[0] if t == 3 else three_ref.at[t]
+            for h in range(2):
+                grad = rows_ref[4 * h + 2 * (place % 2) + place // 2].astype(F32)
+                lanes = slice(h * part, (h + 1) * part)
+                pre = wave[0, :, lanes] * grad[:, part:] - wave[1, :, lanes] * grad[:, :part]
+                at = pl.multiple_of(place * tile + h * part, 128)
+                pre_ref[:, pl.ds(at, part)] = pre.astype(BF)
 
     out = lax.dot_general(freq_ref[...], pre_ref[...], NT, preferred_element_type=F32)
-
-    @pl.when(step < 2)
+    steps = pl.num_programs(0) // 2
+
+    @pl.when(step < steps)
     def _():
         send_ref[0] = out.astype(BF)
 
-    @pl.when(step >= 2)
+    @pl.when(step >= steps)
     def _():
         keep_ref[0] = out
 
 
-def image_grads(me, cs, feat_rows, freq, cols):
+def image_grads(me, three, last, feat_rows, freq, cols):
     k, n = freq.shape
     owners, rows, width = feat_rows.shape
+    whole = lambda x: block(x.shape, lambda s, me: (0,) * x.ndim)
+
+    def source(s, me):
+        owner = 2 * ((s // 2) % 2) + ((me[0] % 2) ^ (1 - s // 4))
+        return 2 * owner + s % 2, 0
+
     spec = pltpu.PrefetchScalarGridSpec(
         num_scalar_prefetch=1,
-        grid=(4,),
-        in_specs=[
-            block((2, rows, n), lambda s, me: (0, 0, 0)),
-            block((owners, rows, width), lambda s, me: (0, 0, 0)),
-            block((cols, n), lambda s, me: ((s % 2) * 2 + ((me[0] % 2) ^ (1 - s // 2)), 0)),
-        ],
+        grid=(8,),
+        in_specs=[whole(three), whole(last), whole(feat_rows), block((cols // 2, n), source)],
         out_specs=[
-            block((1, cols, rows), lambda s, me: (jnp.minimum(s, 1), 0, 0)),
-            block((1, cols, rows), lambda s, me: (jnp.maximum(s - 2, 0), 0, 0)),
+            block((1, cols // 2, rows), lambda s, me: (jnp.minimum(s, 3) // 2, jnp.minimum(s, 3) % 2, 0)),
+            block((1, cols // 2, rows), lambda s, me: (jnp.maximum(s - 4, 0) // 2, jnp.maximum(s - 4, 0) % 2, 0)),
         ],
         scratch_shapes=[pltpu.VMEM((rows, n), BF)],
     )
@@ -501,9 +501,9 @@
         image_kernel,
         grid_spec=spec,
         out_shape=[jax.ShapeDtypeStruct((2, cols, rows), t) for t in (BF, F32)],
-        compiler_params=pltpu.CompilerParams(vmem_limit_bytes=24 * 2**20),
+        compiler_params=pltpu.CompilerParams(vmem_limit_bytes=56 * 2**20),
         cost_estimate=pl.CostEstimate(flops=2 * k * n * rows, bytes_accessed=2 * k * n, transcendentals=0),
-    )(me, cs, feat_rows, freq)
+    )(me, three, last, feat_rows, freq)
 
 
 def split_y_kernel(me_ref, keep_s, keep_k, got_s, got_k, send, keep):
@@ -658,6 +658,37 @@
     )(me, got, preact, lhs)
 
 
+def outputs_kernel(dz, me_ref, own, other, latent, embed):
+    width = own.shape[1]
+    mine = pl.multiple_of((me_ref[0] % 2) * width, 128)
+    theirs = pl.multiple_of((1 - me_ref[0] % 2) * width, 128)
+    for x, at in ((own, mine), (other, theirs)):
+        latent[:, pl.ds(at, width)] = x[:dz]
+        embed[:, pl.ds(at, width)] = x[dz:]
+
+
+def outputs(me, own, other, dz):
+    count, width = own.shape
+    whole = lambda shape: block(shape, lambda h, me: (0,) * len(shape))
+    spec = pltpu.PrefetchScalarGridSpec(
+        num_scalar_prefetch=1,
+        grid=(1,),
+        in_specs=[whole(own.shape), whole(own.shape)],
+        out_specs=[whole((dz, 2 * width)), whole((count - dz, 2 * width))],
+    )
+    return pl.pallas_call(
+        functools.partial(outputs_kernel, dz),
+        grid_spec=spec,
+        out_shape=[jax.ShapeDtypeStruct((c, 2 * width), F32) for c in (dz, count - dz)],
+        compiler_params=pltpu.CompilerParams(vmem_limit_bytes=8 * 2**20),
+        cost_estimate=pl.CostEstimate(flops=0, bytes_accessed=2**20, transcendentals=0),
+    )(me, own, other)
+
+
+def tie(first, later):
+    return lax.optimization_barrier((first, later))
+
+
 def eight_by_four(
     records, real_labels, frequencies, class_noise, latents, syn_labels, w_latent, class_embed, w_out
 ):
@@ -669,7 +700,9 @@
     cols = w_out.shape[1]
     real_total = records.shape[0] * groups
     syn_total = rows * groups
-    me = jnp.stack([feat, rec % 2, (rec // 2) % 2, rec // 4, rec]).astype(jnp.int32)
+    x, z_low, z_high = rec % 2, (rec // 2) % 2, rec // 4
+    place = 2 * x + z_low
+    me = jnp.stack([feat, x, z_low, z_high, rec, place]).astype(jnp.int32)
 
     table = one_hot(syn_labels, classes, BF)
     preact = jnp.dot(latents, w_latent, preferred_element_type=F32) + jnp.dot(
@@ -686,12 +719,14 @@
         jnp.broadcast_to(packed[None], (groups,) + packed.shape), "rec", 0, 0, tiled=True
     )
 
-    send_a, keep_a, send_b, keep_b, cs = feature_sums(
-        me, real_labels, syn_labels, (0, 2, 1, 3), images, records, frequencies, classes,
-        (real_total, syn_total),
-    )
-    got_a = swap(send_a, "rec", 1)
-    got_b = swap(send_b, "rec", 2)
+    images, packed = tie(images, packed)
+    args = (me, real_labels, syn_labels, (0, 2, 1, 3), images, records, frequencies, classes)
+    totals = (real_total, syn_total)
+    send_a, keep_a, send_b, keep_b, three = feature_sums(False, *args, totals)
+    first_a = swap(send_a, "rec", 1)
+    first_b = swap(send_b, "rec", 2)
+    last_a, last_b, last = feature_sums(True, *args, totals)
+    last_a, (first_a, first_b) = tie(last_a, (first_a, first_b))
 
     all_latents = packed[:, :rows].reshape(syn_total, dz)
     all_labels = packed[:, rows].reshape(syn_total).astype(jnp.int32)
@@ -708,15 +743,19 @@
     all_preact = lax.dot_general(w, lhs, (((0,), (0,)), ((), ())), preferred_element_type=F32)
     all_hidden = jnp.maximum(all_preact, 0.0).astype(BF)
 
-    send_a, next_a, send_b, next_b = stage_two(me, keep_a, got_a, keep_b, got_b)
+    send_a, send_b = stage_two_send(keep_a, first_a, keep_b, first_b)
     got_a = swap(send_a, "rec", 2)
     got_b = swap(send_b, "rec", 1)
-    send, keep = stage_three(me, next_a, got_a, next_b, got_b)
+    part = frequencies.shape[1] // groups
+    noise = lax.dynamic_slice_in_dim(class_noise, (2 * place + z_high) * part, part, 2)
+    noise = noise.reshape(classes, 2 * part)
+    got_a, noise = tie(got_a, noise)
+    send, keep = stage_three(me, last_a, first_a, got_a, last_b, first_b, got_b)
     got = swap(send, "rec", 4)
-    feat_grad = gap_rows(me, keep, got, class_noise, all_labels, real_total)
+    feat_grad = gap_rows(keep, got, noise, all_labels, real_total)
     feat_grad = lax.all_to_all(feat_grad.reshape(groups, rows, -1), "rec", 0, 0, tiled=True)
 
-    send, keep = image_grads(me, cs, feat_grad, frequencies, cols)
+    send, keep = image_grads(me, three, last, feat_grad, frequencies, cols)
     send, keep = split_y(me, keep, swap(send, "feat", 1))
     out_grad, flipped = out_grads(keep, swap(send, "feat", 2), own)
 
@@ -724,23 +763,22 @@
     by[1] = swap(out_grad, "rec", 1)
     by[2] = swap(out_grad, "rec", 2)
     by[4] = swap(out_grad, "rec", 4)
+    send, keep = hidden_grads(me, w_out, flipped, groups)
+    part_grad = add(keep, swap(send, "feat", 1), BF)
+    part_grad, (by[1], by[2]) = tie(part_grad, (by[1], by[2]))
     by[3] = swap(by[2], "rec", 1)
+    far_grad = swap(part_grad, "feat", 2)
+    far_grad, by[4] = tie(far_grad, by[4])
     by[6] = swap(by[4], "rec", 2)
     by[5] = swap(by[4], "rec", 1)
+    part_grad = add(part_grad, far_grad, BF)
+    part_grad = lax.all_to_all(part_grad, "rec", 0, 0, tiled=True)
+    part_grad, (by[3], by[6]) = tie(part_grad, (by[3], by[6]))
     by[7] = swap(by[6], "rec", 1)
-
-    send, keep = hidden_grads(me, w_out, flipped, groups)
-    part_grad = add(keep, swap(send, "feat", 1), BF)
-    part_grad = add(part_grad, swap(part_grad, "feat", 2), BF)
-    part_grad = lax.all_to_all(part_grad, "rec", 0, 0, tiled=True)
     grads = last_grads(me, part_grad, all_preact, lhs)
-    other = swap(grads, "feat", 1)
-    core = feat % 2
-    grads = jnp.concatenate(
-        [jnp.where(core == 0, grads, other), jnp.where(core == 0, other, grads)], axis=1
-    )
+    grad_w_latent, grad_embed = outputs(me, grads, swap(grads, "feat", 1), dz)
     grad_w_out = weight_grads(me, all_hidden, [by[mask] for mask in range(groups)])
-    return grad_w_out, grads[:dz], grads[dz:]
+    return grad_w_out, grad_w_latent, grad_embed
 
 
 def solution(mesh):

time: 202 us -> 211 us (1.045)
  Pallas kernels: 55.7 us -> 67.8 us
  local copies, waits for them, and re-layouts: 17.4 us -> 15.1 us
    pallas_call x1, Pallas kernels: 4.83 us -> 12 us  [image_grads(): pl.pallas_call(image_kernel, grid_spec=spec, out_shape=[jax.ShapeDtypeStr...]
    pallas_call x3 -> x5, Pallas kernels: 39.5 us -> 44.3 us  [the longest x2 41.6 us: feature_sums(): pl.pallas_call(functools.partial(features_kernel, masks, last, *totals),...]
    all_to_all x1, starting transfers between devices: 4.05 us -> 7.25 us  [eight_by_four(): lax.all_to_all(jnp.broadcast_to(packed[None], (groups,) + packed.shape),...]
    unnamed x32 -> x43, local copies, waits for them, and re-layouts: 12.8 us -> 10.2 us
    ppermute x20, starting transfers between devices: 21 us -> 18.8 us  [swap(): return lax.ppermute(x, axis, [(i, i ^ bit) for i in range(n)])]
  transfers between devices with their start and end apart: 22 -> 22, of which waited for: 14 -> 14; matrix products, arithmetic and copies ran while one was open for 4% -> 5% of each run, Pallas kernels for 5% -> 7%
where the time goes in v4:
time: 211 us; the launch traced here: 210 us
  Pallas kernels  67.8 us (32%)
  waiting for transfers between devices  58.8 us (28%)
  blocking collectives  30.3 us (14%)
  starting transfers between devices  30.1 us (14%)
  local copies, waits for them, and re-layouts  15.1 us (7%)
  matrix products  5.43 us (3%)
    ppermute x20, waiting for transfers between devices, swap(): return lax.ppermute(x, axis, [(i, i ^ bit) for i in range(n)])  58.8 us
    pallas_call x2, Pallas kernels, feature_sums(): pl.pallas_call(functools.partial(features_kernel, masks, last, *totals),...  41.6 us
    all_to_all x1, blocking collectives, eight_by_four(): lax.all_to_all(feat_grad.reshape(groups, rows, -1), 'rec', 0, 0, tiled=True)  30.3 us
    ppermute x20, starting transfers between devices, swap(): return lax.ppermute(x, axis, [(i, i ^ bit) for i in range(n)])  18.8 us
    pallas_call x1, Pallas kernels, image_grads(): pl.pallas_call(image_kernel, grid_spec=spec, out_shape=[jax.ShapeDtypeStr...  12 us
    unnamed x43, local copies, waits for them, and re-layouts  10.2 us
    all_to_all x1, starting transfers between devices, eight_by_four(): lax.all_to_all(jnp.broadcast_to(packed[None], (groups,) + packed.shape),...  7.25 us
  transfers between devices with their start and end apart: 22, of which 14 were waited for; matrix products, arithmetic and copies ran while one was open for 5% of the time, Pallas kernels for 7%

profile of v4, /device:TPU:0, one launch (start us, length us, event | category | flops | bytes accessed | tf_op | source)
XLA Modules:
  0.0 210.2 jit_solution(6741420000901259713)
XLA Ops:
  2.9 7.3 %all-to-all-start = ((bf16[8,144,128]{2,1,0:T(8,128)(2,1)}), bf16[8,144,128]{2,1,0:T(8,128)(2,1)S(1)}, u32[]{:S(2)}, u32[]{:S(2)}) async-start(bf16[8,144,128]{2,1,0:T(8,128)(2,1)} %broadcast_in_dim.2), calls=%async_computation | async-start | bytes 589824 | tf_op jit(solution)/shard_map/all_to_all | solution.py:718
  10.2 1.1 fusion.12
  11.3 2.9 %fusion.4.refs_0_.image = bf16[128,768]{1,0:T(8,128)(2,1)S(1)} fusion(bf16[2048,768]{1,0:T(8,128)(2,1)} %w_ref.1, f32[128,2048]{1,0:T(8,128)S(1)} %fusion.12, bf16[128,128]{1,0:T(8,128)(2,1)} %param.15, bf16[128,2048]{1,0:T(8,128)(2,1)} %param.17), kind=kOutput, calls=%fused_computation.5 | convolution fusion | flops 470646784 | bytes 4947968 | tf_op jit(solution)/shard_map/dot_general | solution.py:712
  14.2 1.6 collective-permute-start
  15.8 4.8 %collective-permute-done.refs_1_ = bf16[128,768]{1,0:T(8,128)(2,1)S(1)} collective-permute-done((bf16[128,768]{1,0:T(8,128)(2,1)S(1)}, bf16[128,768]{1,0:T(8,128)(2,1)S(1)}, u32[]{:S(2)}, u32[]{:S(2)}) %collective-permute-start) | collective-permute-done | bytes 196640 | tf_op jit(solution)/shard_map/ppermute | solution.py:102
  20.7 1.3 collective-permute-done.2.refs_3_
  22.1 27.8 %shard_map.112 = (bf16[2,2,128,512]{3,2,1,0:T(8,128)(2,1)S(1)}, f32[2,128,512]{2,1,0:T(8,128)S(1)}, bf16[2,2,128,512]{3,2,1,0:T(8,128)(2,1)S(1)}, f32[2,128,512]{2,1,0:T(8,128)S(1)}, f32[3,2,128,512]{3,2,1,0:T(8,128)S(1)}) custom-call(s32[6]{0:T(128)S(1)} %stack.27.me_ref, s32[1,1536]{1,0:T(1,128)S(1)} %reshape.71.real_labels_ref, s32[1,128]{1,0:T(1,128)S(1)} %bitcast.24, ...), custom_call_target="tpu_custom_call" | custom-call | flops 18320719872 | bytes 18874368 | tf_op jit(solution)/shard_map/pallas_call | solution.py:371
  49.9 1.2 copy-done.3
  51.0 1.7 collective-permute-start.3
  52.8 1.5 collective-permute-start.4
  54.2 13.9 %shard_map.113 = (f32[2,128,512]{2,1,0:T(8,128)S(1)}, f32[2,128,512]{2,1,0:T(8,128)S(1)}, f32[1,2,128,512]{3,2,1,0:T(8,128)S(1)}) custom-call(s32[6]{0:T(128)S(1)} %stack.27.me_ref, s32[1,1536]{1,0:T(1,128)S(1)} %reshape.71.real_labels_ref, s32[1,128]{1,0:T(1,128)S(1)} %bitcast.25, bf16[128,768]{1,0:T(8,128)(2,1)S(1)} %fusion.4.refs_0_.image, ...), custom_call_target="tpu_custom_call" | custom-call | flops 6106906624 | bytes 12582912 | tf_op jit(solution)/shard_map/pallas_call | solution.py:371
  69.7 0.8 shard_map.114
  71.4 1.2 constant_dynamic-slice_fusion
  72.7 6.0 %collective-permute-done.5.ga = bf16[2,128,512]{2,1,0:T(8,128)(2,1)} collective-permute-done((bf16[2,128,512]{2,1,0:T(8,128)(2,1)}, bf16[2,128,512]{2,1,0:T(8,128)(2,1)}, u32[]{:S(2)}, u32[]{:S(2)}) %collective-permute-start.5) | collective-permute-done | bytes 262176 | tf_op jit(solution)/shard_map/ppermute | solution.py:102
  78.9 1.0 copy-done.6
  79.9 2.4 %shard_map.115 = (bf16[256,512]{1,0:T(8,128)(2,1)}, f32[256,512]{1,0:T(8,128)S(1)}) custom-call(s32[6]{0:T(128)S(1)} %stack.27.me_ref, f32[2,128,512]{2,1,0:T(8,128)S(1)} %get-tuple-element.65.na, bf16[2,2,128,512]{3,2,1,0:T(8,128)(2,1)S(1)} %collective-permute-done.3.ga.fa, bf16[2,128,512]{2,1,0:T(8,128)(2,1)} %collective-permute-done.5.ga, ...), custom_call_target="tpu_custom_call" | custom-call | bytes 3145728 | tf_op jit(solution)/shard_map/pallas_call | solution.py:417
  82.3 2.4 %collective-permute-start.7 = (bf16[256,512]{1,0:T(8,128)(2,1)}, bf16[256,512]{1,0:T(8,128)(2,1)S(1)}, u32[]{:S(2)}, u32[]{:S(2)}) collective-permute-start(bf16[256,512]{1,0:T(8,128)(2,1)} %get-tuple-element.75), channel_id=1, source_target_pairs={{0,16},{4,20},{8,24},{12,28},{16,0},{20,4},{24,8},{28,12},{1,17},{... | collective-permute-start | bytes 786440 | tf_op jit(solution)/shard_map/ppermute | solution.py:102
  84.7 1.0 copy.17
  86.0 9.7 %collective-permute-done.7.got_ref = bf16[256,512]{1,0:T(8,128)(2,1)S(1)} collective-permute-done((bf16[256,512]{1,0:T(8,128)(2,1)}, bf16[256,512]{1,0:T(8,128)(2,1)S(1)}, u32[]{:S(2)}, u32[]{:S(2)}) %collective-permute-start.7) | collective-permute-done | bytes 262176 | tf_op jit(solution)/shard_map/ppermute | solution.py:102
  95.6 1.0 copy-done.8
  97.2 30.3 %all_to_all.15.rows_ref = bf16[8,128,512]{2,1,0:T(8,128)(2,1)} all-to-all(bf16[8,128,512]{2,1,0:T(8,128)(2,1)S(1)} %bitcast.22), channel_id=1, replica_groups=mesh['rec'=8,'feat'=4] {'rec'}, dimensions={0} | all-to-all | bytes 2097152 | tf_op jit(solution)/shard_map/all_to_all | solution.py:756
  127.5 12.0 %shard_map.117 = (bf16[2,768,128]{2,1,0:T(8,128)(2,1)}, f32[2,768,128]{2,1,0:T(8,128)}) custom-call(s32[6]{0:T(128)} %copy-done.15, f32[3,2,128,512]{3,2,1,0:T(8,128)} %copy-done.3, f32[1,2,128,512]{3,2,1,0:T(8,128)} %copy-done.4, bf16[8,128,512]{2,1,0:T(8,128)(2,1)} %all_to_all.15.rows_ref, bf16[3072,2048]{1,0:T(8,128)(2,1)} %freq_ref.1), custom_call_target="tpu_custom_call" | custom-call | flops 1610612736 | bytes 12582912 | tf_op jit(solution)/shard_map/pallas_call | solution.py:500
  139.5 1.9 collective-permute-done.8.got_s.got_k
  141.4 1.1 copy-done.2
  143.2 1.6 collective-permute-start.9
  144.8 5.4 %collective-permute-done.9.got = bf16[768,128]{1,0:T(8,128)(2,1)S(1)} collective-permute-done((bf16[768,128]{1,0:T(8,128)(2,1)S(1)}, bf16[768,128]{1,0:T(8,128)(2,1)S(1)}, u32[]{:S(2)}, u32[]{:S(2)}) %collective-permute-start.9) | collective-permute-done | bytes 196640 | tf_op jit(solution)/shard_map/ppermute | solution.py:102
  150.5 2.1 shard_map.120
  152.7 1.5 collective-permute-start.11
  154.3 5.7 %collective-permute-done.11.refs_1_ = bf16[128,768]{1,0:T(8,128)(2,1)S(1)} collective-permute-done((bf16[128,768]{1,0:T(8,128)(2,1)S(1)}, bf16[128,768]{1,0:T(8,128)(2,1)S(1)}, u32[]{:S(2)}, u32[]{:S(2)}) %collective-permute-start.11) | collective-permute-done | bytes 196640 | tf_op jit(solution)/shard_map/ppermute | solution.py:102
  161.3 1.5 collective-permute-start.13
  163.3 1.5 constant_dynamic-slice_fusion.2
  165.0 8.9 %collective-permute-done.14.refs_4_ = bf16[128,768]{1,0:T(8,128)(2,1)} collective-permute-done((bf16[128,768]{1,0:T(8,128)(2,1)S(1)}, bf16[128,768]{1,0:T(8,128)(2,1)}, u32[]{:S(2)}, u32[]{:S(2)}) %collective-permute-start.14) | collective-permute-done | bytes 196640 | tf_op jit(solution)/shard_map/ppermute | solution.py:102
  174.7 4.0 %all-to-all-start.2 = ((bf16[8,128,128]{2,1,0:T(8,128)(2,1)}), bf16[8,128,128]{2,1,0:T(8,128)(2,1)}, u32[]{:S(2)}, u32[]{:S(2)}) async-start(bf16[8,128,128]{2,1,0:T(8,128)(2,1)} %shard_map.122), calls=%async_computation.2 | async-start | bytes 524288 | tf_op jit(solution)/shard_map/all_to_all | solution.py:775
  178.8 2.0 collective-permute-start.15
  180.8 1.5 collective-permute-start.16
  182.3 1.4 maximum_convert_fusion
  183.8 3.9 %collective-permute-done.15.refs_3_ = bf16[128,768]{1,0:T(8,128)(2,1)S(1)} collective-permute-done((bf16[128,768]{1,0:T(8,128)(2,1)}, bf16[128,768]{1,0:T(8,128)(2,1)S(1)}, u32[]{:S(2)}, u32[]{:S(2)}) %collective-permute-start.15) | collective-permute-done | bytes 196640 | tf_op jit(solution)/shard_map/ppermute | solution.py:102
  188.3 1.9 collective-permute-done.16.refs_6_
  190.2 1.9 shard_map.124.own
  192.1 0.9 collective-permute-start.17
  193.0 1.2 collective-permute-start.18
  194.2 1.3 shard_map.125
  195.5 4.6 %collective-permute-done.17.refs_5_ = bf16[128,768]{1,0:T(8,128)(2,1)S(1)} collective-permute-done((bf16[128,768]{1,0:T(8,128)(2,1)}, bf16[128,768]{1,0:T(8,128)(2,1)S(1)}, u32[]{:S(2)}, u32[]{:S(2)}) %collective-permute-start.17) | collective-permute-done | bytes 196640 | tf_op jit(solution)/shard_map/ppermute | solution.py:102
  200.1 3.8 %collective-permute-done.18.refs_7_ = bf16[128,768]{1,0:T(8,128)(2,1)S(1)} collective-permute-done((bf16[128,768]{1,0:T(8,128)(2,1)}, bf16[128,768]{1,0:T(8,128)(2,1)S(1)}, u32[]{:S(2)}, u32[]{:S(2)}) %collective-permute-start.18) | collective-permute-done | bytes 196640 | tf_op jit(solution)/shard_map/ppermute | solution.py:102
  203.9 0.9 copy-done.10
  204.8 0.9 copy-done.12
  205.7 0.9 copy-done.14
  206.7 3.5 %shard_map.123 = f32[256,768]{1,0:T(8,128)} custom-call(s32[6]{0:T(128)S(1)} %copy-done.16, bf16[256,1024]{1,0:T(8,128)(2,1)S(1)} %get-tuple-element.97.hidden_ref, bf16[128,768]{1,0:T(8,128)(2,1)S(1)} %copy-done.10, bf16[128,768]{1,0:T(8,128)(2,1)S(1)} %copy-done.12, bf16[128,768]{1,0:T(8,128)(2,1)} %collective-permute-done.12.refs_2_, ...), custom_call_target="tpu_custom_call" | custom-call | flops 402653184 | bytes 4194304 | tf_op jit(solution)/shard_map/pallas_call | solution.py:615
  (73 shorter events, 10.6 us)
Async XLA Ops:
  0.6 9.5 %copy-start = (bf16[256,2048]{1,0:T(8,128)(2,1)S(1)}, bf16[256,2048]{1,0:T(8,128)(2,1)}, u32[]{:S(2)}) copy-start(bf16[256,2048]{1,0:T(8,128)(2,1)} %param.18) | copy-start | bytes 3145732
  2.9 19.1 %all-to-all-start = ((bf16[8,144,128]{2,1,0:T(8,128)(2,1)}), bf16[8,144,128]{2,1,0:T(8,128)(2,1)S(1)}, u32[]{:S(2)}, u32[]{:S(2)}) async-start(bf16[8,144,128]{2,1,0:T(8,128)(2,1)} %broadcast_in_dim.2), calls=%async_computation | async-start | bytes 589824 | tf_op jit(solution)/shard_map/all_to_all | solution.py:718
  10.2 10.5 %copy-start.20 = (s32[1536]{0:T(1024)S(1)}, s32[1536]{0:T(1024)}, u32[]{:S(2)}) copy-start(s32[1536]{0:T(1024)} %param.12) | copy-start | bytes 18436
  10.2 11.9 %copy-start.17 = (s32[128]{0:T(128)S(1)}, s32[128]{0:T(128)}, u32[]{:S(2)}) copy-start(s32[128]{0:T(128)} %param.16) | copy-start | bytes 1540
  14.2 6.4 %collective-permute-start = (bf16[128,768]{1,0:T(8,128)(2,1)S(1)}, bf16[128,768]{1,0:T(8,128)(2,1)S(1)}, u32[]{:S(2)}, u32[]{:S(2)}) collective-permute-start(bf16[128,768]{1,0:T(8,128)(2,1)S(1)} %fusion.4.refs_0_.image), channel_id=1, source_target_pairs={{0,2},{1,3},{2,0},{3,1},{4,6},{5,7},{6,4},{7,5},{8,10},{9,11},{10,... | collective-permute-start | bytes 589832 | tf_op jit(solution)/shard_map/ppermute | solution.py:102
  15.8 5.0 %collective-permute-start.1 = (bf16[128,768]{1,0:T(8,128)(2,1)S(1)}, bf16[128,768]{1,0:T(8,128)(2,1)S(1)}, u32[]{:S(2)}, u32[]{:S(2)}) collective-permute-start(bf16[128,768]{1,0:T(8,128)(2,1)S(1)} %fusion.4.refs_0_.image), channel_id=1, source_target_pairs={{0,1},{1,0},{2,3},{3,2},{4,5},{5,4},{6,7},{7,6},{8,9},{9,8},{10,11... | collective-permute-start | bytes 589832 | tf_op jit(solution)/shard_map/ppermute | solution.py:102
  20.6 1.4 collective-permute-start.2
  20.7 58.2 %copy-start.15 = (s32[6]{0:T(128)}, s32[6]{0:T(128)S(1)}, u32[]{:S(2)}) copy-start(s32[6]{0:T(128)S(1)} %stack.27.me_ref) | copy-start | bytes 76
  22.1 27.8 %copy-start.18 = (bf16[8,144,128]{2,1,0:T(8,128)(2,1)}, bf16[8,144,128]{2,1,0:T(8,128)(2,1)S(1)}, u32[]{:S(2)}) copy-start(bf16[8,144,128]{2,1,0:T(8,128)(2,1)S(1)} %all-to-all-done) | copy-start | bytes 884740
  49.9 1.2 copy-start.3
  51.0 18.6 %collective-permute-start.3 = (bf16[2,2,128,512]{3,2,1,0:T(8,128)(2,1)S(1)}, bf16[2,2,128,512]{3,2,1,0:T(8,128)(2,1)S(1)}, u32[]{:S(2)}, u32[]{:S(2)}) collective-permute-start(bf16[2,2,128,512]{3,2,1,0:T(8,128)(2,1)S(1)} %get-tuple-element.63), channel_id=1, source_target_pairs={{0,4},{4,0},{8,12},{12,8},{16,20},{20,16},{24,28},{28,24},{1,5},{5... | collective-permute-start | bytes 1572872 | tf_op jit(solution)/shard_map/ppermute | solution.py:102
  52.8 16.9 %collective-permute-start.4 = (bf16[2,2,128,512]{3,2,1,0:T(8,128)(2,1)S(1)}, bf16[2,2,128,512]{3,2,1,0:T(8,128)(2,1)S(1)}, u32[]{:S(2)}, u32[]{:S(2)}) collective-permute-start(bf16[2,2,128,512]{3,2,1,0:T(8,128)(2,1)S(1)} %get-tuple-element.64), channel_id=1, source_target_pairs={{0,8},{4,12},{8,0},{12,4},{16,24},{20,28},{24,16},{28,20},{1,9},{5... | collective-permute-start | bytes 1572872 | tf_op jit(solution)/shard_map/ppermute | solution.py:102
  68.1 0.8 copy-start.4
  68.9 0.8 copy-start.5
  70.5 8.1 %collective-permute-start.5 = (bf16[2,128,512]{2,1,0:T(8,128)(2,1)}, bf16[2,128,512]{2,1,0:T(8,128)(2,1)}, u32[]{:S(2)}, u32[]{:S(2)}) collective-permute-start(bf16[2,128,512]{2,1,0:T(8,128)(2,1)} %get-tuple-element.70), channel_id=1, source_target_pairs={{0,8},{4,12},{8,0},{12,4},{16,24},{20,28},{24,16},{28,20},{1,9},{5... | collective-permute-start | bytes 786440 | tf_op jit(solution)/shard_map/ppermute | solution.py:102
  71.1 7.8 %collective-permute-start.6 = (bf16[2,128,512]{2,1,0:T(8,128)(2,1)}, bf16[2,128,512]{2,1,0:T(8,128)(2,1)}, u32[]{:S(2)}, u32[]{:S(2)}) collective-permute-start(bf16[2,128,512]{2,1,0:T(8,128)(2,1)} %get-tuple-element.73), channel_id=1, source_target_pairs={{0,4},{4,0},{8,12},{12,8},{16,20},{20,16},{24,28},{28,24},{1,5},{5... | collective-permute-start | bytes 786440 | tf_op jit(solution)/shard_map/ppermute | solution.py:102
  78.9 1.0 copy-start.6
  82.3 3.4 %copy-start.7 = (f32[256,512]{1,0:T(8,128)}, f32[256,512]{1,0:T(8,128)S(1)}, u32[]{:S(2)}) copy-start(f32[256,512]{1,0:T(8,128)S(1)} %get-tuple-element.74.keep_ref) | copy-start | bytes 1572868
  82.3 13.3 %collective-permute-start.7 = (bf16[256,512]{1,0:T(8,128)(2,1)}, bf16[256,512]{1,0:T(8,128)(2,1)S(1)}, u32[]{:S(2)}, u32[]{:S(2)}) collective-permute-start(bf16[256,512]{1,0:T(8,128)(2,1)} %get-tuple-element.75), channel_id=1, source_target_pairs={{0,16},{4,20},{8,24},{12,28},{16,0},{20,4},{24,8},{28,12},{1,17},{... | collective-permute-start | bytes 786440 | tf_op jit(solution)/shard_map/ppermute | solution.py:102
  95.6 1.0 copy-start.8
  127.5 13.9 %copy-start.16 = (s32[6]{0:T(128)S(1)}, s32[6]{0:T(128)}, u32[]{:S(2)}) copy-start(s32[6]{0:T(128)} %copy-done.15) | copy-start | bytes 76
  139.5 11.0 %copy-start.1 = (bf16[2048,768]{1,0:T(8,128)(2,1)S(1)}, bf16[2048,768]{1,0:T(8,128)(2,1)}, u32[]{:S(2)}) copy-start(bf16[2048,768]{1,0:T(8,128)(2,1)} %w_ref.1) | copy-start | bytes 9437188
  139.5 1.9 collective-permute-start.8
  141.4 1.1 copy-start.2
  143.2 21.6 %slice-start = ((bf16[8,144,128]{2,1,0:T(8,128)(2,1)}), bf16[8,128,128]{2,1,0:T(8,128)(2,1)S(1)}, s32[]{:S(2)}) async-start(bf16[8,144,128]{2,1,0:T(8,128)(2,1)} %copy-done.18), calls=%async_computation.3 | async-start | bytes 524288 | tf_op jit(solution)/shard_map/slice | solution.py:731
  143.2 7.0 %collective-permute-start.9 = (bf16[768,128]{1,0:T(8,128)(2,1)S(1)}, bf16[768,128]{1,0:T(8,128)(2,1)S(1)}, u32[]{:S(2)}, u32[]{:S(2)}) collective-permute-start(bf16[768,128]{1,0:T(8,128)(2,1)S(1)} %get-tuple-element.80), channel_id=1, source_target_pairs={{0,2},{1,3},{2,0},{3,1},{4,6},{5,7},{6,4},{7,5},{8,10},{9,11},{10,... | collective-permute-start | bytes 589832 | tf_op jit(solution)/shard_map/ppermute | solution.py:102
  150.5 24.2 %copy-start.9 = (bf16[128,768]{1,0:T(8,128)(2,1)}, bf16[128,768]{1,0:T(8,128)(2,1)S(1)}, u32[]{:S(2)}) copy-start(bf16[128,768]{1,0:T(8,128)(2,1)S(1)} %get-tuple-element.81.refs_0_) | copy-start | bytes 589828
  152.6 1.6 collective-permute-start.10
  152.7 7.3 %collective-permute-start.11 = (bf16[128,768]{1,0:T(8,128)(2,1)S(1)}, bf16[128,768]{1,0:T(8,128)(2,1)S(1)}, u32[]{:S(2)}, u32[]{:S(2)}) collective-permute-start(bf16[128,768]{1,0:T(8,128)(2,1)S(1)} %get-tuple-element.81.refs_0_), channel_id=1, source_target_pairs={{0,4},{4,0},{8,12},{12,8},{16,20},{20,16},{24,28},{28,24},{1,5},{5... | collective-permute-start | bytes 589832 | tf_op jit(solution)/shard_map/ppermute | solution.py:102
  154.2 7.1 %collective-permute-start.12 = (bf16[128,768]{1,0:T(8,128)(2,1)S(1)}, bf16[128,768]{1,0:T(8,128)(2,1)}, u32[]{:S(2)}, u32[]{:S(2)}) collective-permute-start(bf16[128,768]{1,0:T(8,128)(2,1)S(1)} %get-tuple-element.81.refs_0_), channel_id=1, source_target_pairs={{0,8},{4,12},{8,0},{12,4},{16,24},{20,28},{24,16},{28,20},{1,9},{5... | collective-permute-start | bytes 589832 | tf_op jit(solution)/shard_map/ppermute | solution.py:102
  160.0 0.7 copy-start.11
  161.3 12.6 %collective-permute-start.13 = (bf16[8,128,128]{2,1,0:T(8,128)(2,1)S(1)}, bf16[8,128,128]{2,1,0:T(8,128)(2,1)S(1)}, u32[]{:S(2)}, u32[]{:S(2)}) collective-permute-start(bf16[8,128,128]{2,1,0:T(8,128)(2,1)S(1)} %shard_map.121.a), channel_id=1, source_target_pairs={{0,2},{1,3},{2,0},{3,1},{4,6},{5,7},{6,4},{7,5},{8,10},{9,11},{10,... | collective-permute-start | bytes 786440 | tf_op jit(solution)/shard_map/ppermute | solution.py:102
  162.8 11.1 %collective-permute-start.14 = (bf16[128,768]{1,0:T(8,128)(2,1)S(1)}, bf16[128,768]{1,0:T(8,128)(2,1)}, u32[]{:S(2)}, u32[]{:S(2)}) collective-permute-start(bf16[128,768]{1,0:T(8,128)(2,1)S(1)} %get-tuple-element.81.refs_0_), channel_id=1, source_target_pairs={{0,16},{4,20},{8,24},{12,28},{16,0},{20,4},{24,8},{28,12},{1,17},{... | collective-permute-start | bytes 589832 | tf_op jit(solution)/shard_map/ppermute | solution.py:102
  164.9 17.3 %copy-start.19 = (bf16[1024,128]{0,1:T(8,128)(2,1)}, bf16[1024,128]{0,1:T(8,128)(2,1)S(1)}, u32[]{:S(2)}) copy-start(bf16[1024,128]{0,1:T(8,128)(2,1)S(1)} %copy.19) | copy-start | bytes 786436
  174.7 15.5 %all-to-all-start.2 = ((bf16[8,128,128]{2,1,0:T(8,128)(2,1)}), bf16[8,128,128]{2,1,0:T(8,128)(2,1)}, u32[]{:S(2)}, u32[]{:S(2)}) async-start(bf16[8,128,128]{2,1,0:T(8,128)(2,1)} %shard_map.122), calls=%async_computation.2 | async-start | bytes 524288 | tf_op jit(solution)/shard_map/all_to_all | solution.py:775
  178.8 8.8 %collective-permute-start.15 = (bf16[128,768]{1,0:T(8,128)(2,1)}, bf16[128,768]{1,0:T(8,128)(2,1)S(1)}, u32[]{:S(2)}, u32[]{:S(2)}) collective-permute-start(bf16[128,768]{1,0:T(8,128)(2,1)} %collective-permute-done.12.refs_2_), channel_id=1, source_target_pairs={{0,4},{4,0},{8,12},{12,8},{16,20},{20,16},{24,28},{28,24},{1,5},{5... | collective-permute-start | bytes 589832 | tf_op jit(solution)/shard_map/ppermute | solution.py:102
  180.8 9.4 %collective-permute-start.16 = (bf16[128,768]{1,0:T(8,128)(2,1)}, bf16[128,768]{1,0:T(8,128)(2,1)}, u32[]{:S(2)}, u32[]{:S(2)}) collective-permute-start(bf16[128,768]{1,0:T(8,128)(2,1)} %collective-permute-done.14.refs_4_), channel_id=1, source_target_pairs={{0,8},{4,12},{8,0},{12,4},{16,24},{20,28},{24,16},{28,20},{1,9},{5... | collective-permute-start | bytes 589832 | tf_op jit(solution)/shard_map/ppermute | solution.py:102
  187.6 0.7 copy-start.13
  192.1 2.2 %collective-permute-start.19 = (f32[384,128]{1,0:T(8,128)S(1)}, f32[384,128]{1,0:T(8,128)S(1)}, u32[]{:S(2)}, u32[]{:S(2)}) collective-permute-start(f32[384,128]{1,0:T(8,128)S(1)} %shard_map.124.own), channel_id=1, source_target_pairs={{0,1},{1,0},{2,3},{3,2},{4,5},{5,4},{6,7},{7,6},{8,9},{9,8},{10,11... | collective-permute-start | bytes 589832 | tf_op jit(solution)/shard_map/ppermute | solution.py:102
  192.1 8.0 %collective-permute-start.17 = (bf16[128,768]{1,0:T(8,128)(2,1)}, bf16[128,768]{1,0:T(8,128)(2,1)S(1)}, u32[]{:S(2)}, u32[]{:S(2)}) collective-permute-start(bf16[128,768]{1,0:T(8,128)(2,1)} %collective-permute-done.14.refs_4_), channel_id=1, source_target_pairs={{0,4},{4,0},{8,12},{12,8},{16,20},{20,16},{24,28},{28,24},{1,5},{5... | collective-permute-start | bytes 589832 | tf_op jit(solution)/shard_map/ppermute | solution.py:102
  193.0 10.9 %collective-permute-start.18 = (bf16[128,768]{1,0:T(8,128)(2,1)}, bf16[128,768]{1,0:T(8,128)(2,1)S(1)}, u32[]{:S(2)}, u32[]{:S(2)}) collective-permute-start(bf16[128,768]{1,0:T(8,128)(2,1)} %collective-permute-done.16.refs_6_), channel_id=1, source_target_pairs={{0,4},{4,0},{8,12},{12,8},{16,20},{20,16},{24,28},{28,24},{1,5},{5... | collective-permute-start | bytes 589832 | tf_op jit(solution)/shard_map/ppermute | solution.py:102
  203.9 0.9 copy-start.10
  204.8 0.9 copy-start.12
  205.7 0.9 copy-start.14

commit v5 on v4

--- a/solution.py
+++ b/solution.py
@@ -484,16 +484,15 @@
     whole = lambda x: block(x.shape, lambda s, me: (0,) * x.ndim)
 
     def source(s, me):
-        owner = 2 * ((s // 2) % 2) + ((me[0] % 2) ^ (1 - s // 4))
-        return 2 * owner + s % 2, 0
+        return 2 * (s % 2) + ((me[0] % 2) ^ (1 - s // 2)), 0
 
     spec = pltpu.PrefetchScalarGridSpec(
         num_scalar_prefetch=1,
-        grid=(8,),
-        in_specs=[whole(three), whole(last), whole(feat_rows), block((cols // 2, n), source)],
+        grid=(4,),
+        in_specs=[whole(three), whole(last), whole(feat_rows), block((cols, n), source)],
         out_specs=[
-            block((1, cols // 2, rows), lambda s, me: (jnp.minimum(s, 3) // 2, jnp.minimum(s, 3) % 2, 0)),
-            block((1, cols // 2, rows), lambda s, me: (jnp.maximum(s - 4, 0) // 2, jnp.maximum(s - 4, 0) % 2, 0)),
+            block((1, cols, rows), lambda s, me: (jnp.minimum(s, 1), 0, 0)),
+            block((1, cols, rows), lambda s, me: (jnp.maximum(s - 2, 0), 0, 0)),
         ],
         scratch_shapes=[pltpu.VMEM((rows, n), BF)],
     )
@@ -527,55 +526,49 @@
     )(me, keep, keep, got, got)
 
 
-def out_kernel(keep, got, image, out, flipped):
+def out_kernel(keep, got, image, out):
     grad = (keep[...] + got[...].astype(F32)).T
     grad = grad * (1.0 - jnp.square(image[...].astype(F32)))
     out[...] = grad.astype(BF)
-    flipped[...] = grad.T.astype(BF)
 
 
 def out_grads(keep, got, image):
-    rows, cols = image.shape
     return pl.pallas_call(
         out_kernel,
-        out_shape=[jax.ShapeDtypeStruct((rows, cols), BF), jax.ShapeDtypeStruct((cols, rows), BF)],
+        out_shape=jax.ShapeDtypeStruct(image.shape, BF),
         compiler_params=pltpu.CompilerParams(vmem_limit_bytes=8 * 2**20),
         cost_estimate=pl.CostEstimate(flops=0, bytes_accessed=2**20, transcendentals=0),
     )(keep, got, image)
 
 
-def hidden_kernel(me_ref, w_ref, grad_ref, send, keep):
+def hidden_kernel(me_ref, w_ref, *refs):
+    grads = refs[:4]
+    send, keep = refs[4:]
     core = me_ref[0] % 2
-    out = jnp.dot(w_ref[...], grad_ref[...], preferred_element_type=F32)
-    count, half, rows = send.shape
-    out = out.reshape(count, 2, half, rows)
-    keep[...] = jnp.where(core == 0, out[:, 0], out[:, 1])
-    send[...] = jnp.where(core == 0, out[:, 1], out[:, 0]).astype(BF)
-
-
-def hidden_grads(me, w_out, flipped, groups):
-    cols, rows = flipped.shape
-    hid = w_out.shape[0]
-    mine = hid // groups
-    out = block((2, mine // 2, rows), lambda r, me: (r, 0, 0))
+    out = [lax.dot_general(w_ref[...], g[...], NT, preferred_element_type=F32) for g in grads]
+    for i in range(2):
+        keep[i] = jnp.where(core == 0, out[2 * i], out[2 * i + 1])
+        send[i] = jnp.where(core == 0, out[2 * i + 1], out[2 * i]).astype(BF)
+
+
+def hidden_grads(me, w_out, grads, mine):
+    rows, cols = grads[0].shape
+    whole = lambda shape: block(shape, lambda r, me: (0,) * len(shape))
     spec = pltpu.PrefetchScalarGridSpec(
         num_scalar_prefetch=1,
-        grid=(groups // 2,),
-        in_specs=[
-            block((2 * mine, cols), lambda r, me: (r, 0)),
-            block((cols, rows), lambda r, me: (0, 0)),
-        ],
-        out_specs=[out, out],
+        grid=(1,),
+        in_specs=[block((mine, cols), lambda r, me: (me[4], 0))] + [whole((rows, cols))] * 4,
+        out_specs=[whole((2, mine, rows))] * 2,
     )
     return pl.pallas_call(
         hidden_kernel,
         grid_spec=spec,
-        out_shape=[jax.ShapeDtypeStruct((groups, mine // 2, rows), t) for t in (BF, F32)],
+        out_shape=[jax.ShapeDtypeStruct((2, mine, rows), t) for t in (BF, F32)],
         compiler_params=pltpu.CompilerParams(vmem_limit_bytes=8 * 2**20),
         cost_estimate=pl.CostEstimate(
-            flops=2 * hid * cols * rows, bytes_accessed=2 * hid * cols, transcendentals=0
+            flops=8 * mine * cols * rows, bytes_accessed=2 * 5 * mine * cols, transcendentals=0
         ),
-    )(me, w_out, flipped)
+    )(me, w_out, *grads)
 
 
 def add_kernel(a, b, out):
@@ -623,66 +616,56 @@
     )(me, hidden, *grads)
 
 
-def last_kernel(me_ref, got_ref, preact_ref, lhs_ref, out_ref):
-    groups, width, rows = got_ref.shape
+def last_kernel(me_ref, preact_ref, lhs_ref, p0, q0, p1, q1, out_ref):
+    rows = p0.shape[2]
     acc = None
-    for g in range(groups):
-        at = slice(g * rows, (g + 1) * rows)
-        grad = jnp.where(preact_ref[:, at] > 0, got_ref[g].astype(F32), 0.0).astype(BF)
-        d = lax.dot_general(lhs_ref[:, at], grad, NT, preferred_element_type=F32)
-        acc = d if acc is None else acc + d
+    for h, (p, q) in enumerate(((p0, q0), (p1, q1))):
+        for i in range(2):
+            mask = 4 * h + 2 * i + me_ref[0] % 2
+            at = pl.ds(pl.multiple_of((me_ref[4] ^ mask) * rows, 128), rows)
+            grad = p[i].astype(F32) + q[i].astype(F32)
+            grad = jnp.where(preact_ref[:, at] > 0, grad, 0.0).astype(BF)
+            d = lax.dot_general(lhs_ref[:, at], grad, NT, preferred_element_type=F32)
+            acc = d if acc is None else acc + d
     out_ref[...] = acc
 
 
-def last_grads(me, got, preact, lhs):
-    groups, width, rows = got.shape
+def last_grads(me, preact, lhs, parts):
     count, total = lhs.shape
-    spec = pltpu.PrefetchScalarGridSpec(
-        num_scalar_prefetch=1,
-        grid=(1,),
-        in_specs=[
-            block((groups, width, rows), lambda h, me: (0, 0, 0)),
-            block((width, total), lambda h, me: (me[0] % 2, 0)),
-            block((count, total), lambda h, me: (0, 0)),
-        ],
-        out_specs=block((count, width), lambda h, me: (0, 0)),
-    )
-    return pl.pallas_call(
-        last_kernel,
-        grid_spec=spec,
-        out_shape=jax.ShapeDtypeStruct((count, width), F32),
-        compiler_params=pltpu.CompilerParams(vmem_limit_bytes=12 * 2**20),
-        cost_estimate=pl.CostEstimate(
-            flops=2 * total * count * width, bytes_accessed=2 * 2**20, transcendentals=0
-        ),
-    )(me, got, preact, lhs)
-
-
-def outputs_kernel(dz, me_ref, own, other, latent, embed):
-    width = own.shape[1]
-    mine = pl.multiple_of((me_ref[0] % 2) * width, 128)
-    theirs = pl.multiple_of((1 - me_ref[0] % 2) * width, 128)
-    for x, at in ((own, mine), (other, theirs)):
-        latent[:, pl.ds(at, width)] = x[:dz]
-        embed[:, pl.ds(at, width)] = x[dz:]
-
-
-def outputs(me, own, other, dz):
-    count, width = own.shape
+    mine = preact.shape[0]
+    args = (preact, lhs, *parts)
     whole = lambda shape: block(shape, lambda h, me: (0,) * len(shape))
     spec = pltpu.PrefetchScalarGridSpec(
         num_scalar_prefetch=1,
         grid=(1,),
-        in_specs=[whole(own.shape), whole(own.shape)],
-        out_specs=[whole((dz, 2 * width)), whole((count - dz, 2 * width))],
-    )
-    return pl.pallas_call(
-        functools.partial(outputs_kernel, dz),
+        in_specs=[whole(x.shape) for x in args],
+        out_specs=whole((count, mine)),
+    )
+    return pl.pallas_call(
+        last_kernel,
         grid_spec=spec,
-        out_shape=[jax.ShapeDtypeStruct((c, 2 * width), F32) for c in (dz, count - dz)],
+        out_shape=jax.ShapeDtypeStruct((count, mine), F32),
+        compiler_params=pltpu.CompilerParams(vmem_limit_bytes=12 * 2**20),
+        cost_estimate=pl.CostEstimate(
+            flops=total * count * mine, bytes_accessed=2 * 2**20, transcendentals=0
+        ),
+    )(me, *args)
+
+
+def outputs_kernel(own, other, latent, embed):
+    dz = latent.shape[0]
+    latent[...] = own[:dz] + other[:dz]
+    embed[...] = own[dz:] + other[dz:]
+
+
+def outputs(own, other, dz):
+    count, mine = own.shape
+    return pl.pallas_call(
+        outputs_kernel,
+        out_shape=[jax.ShapeDtypeStruct((c, mine), F32) for c in (dz, count - dz)],
         compiler_params=pltpu.CompilerParams(vmem_limit_bytes=8 * 2**20),
         cost_estimate=pl.CostEstimate(flops=0, bytes_accessed=2**20, transcendentals=0),
-    )(me, own, other)
+    )(own, other)
 
 
 def tie(first, later):
@@ -714,7 +697,7 @@
     images = [own, far, swap(own, "feat", 1), swap(far, "feat", 1)]
 
     label_row = jnp.zeros((16, dz), BF).at[0, :].set(syn_labels.astype(BF))
-    packed = jnp.concatenate([latents, label_row], axis=0)
+    packed, _ = tie(jnp.concatenate([latents, label_row], axis=0), own)
     packed = lax.all_to_all(
         jnp.broadcast_to(packed[None], (groups,) + packed.shape), "rec", 0, 0, tiled=True
     )
@@ -754,30 +737,35 @@
     got = swap(send, "rec", 4)
     feat_grad = gap_rows(keep, got, noise, all_labels, real_total)
     feat_grad = lax.all_to_all(feat_grad.reshape(groups, rows, -1), "rec", 0, 0, tiled=True)
+    feat_grad, (all_preact, all_hidden, lhs) = tie(feat_grad, (all_preact, all_hidden, lhs))
 
     send, keep = image_grads(me, three, last, feat_grad, frequencies, cols)
     send, keep = split_y(me, keep, swap(send, "feat", 1))
-    out_grad, flipped = out_grads(keep, swap(send, "feat", 2), own)
+    out_grad = out_grads(keep, swap(send, "feat", 2), own)
 
     by = {0: out_grad}
+    by[4] = swap(out_grad, "rec", 4)
+    by[2] = swap(out_grad, "rec", 2)
     by[1] = swap(out_grad, "rec", 1)
-    by[2] = swap(out_grad, "rec", 2)
-    by[4] = swap(out_grad, "rec", 4)
-    send, keep = hidden_grads(me, w_out, flipped, groups)
-    part_grad = add(keep, swap(send, "feat", 1), BF)
-    part_grad, (by[1], by[2]) = tie(part_grad, (by[1], by[2]))
+    by[4], (by[2], by[1]) = tie(by[4], (by[2], by[1]))
     by[3] = swap(by[2], "rec", 1)
-    far_grad = swap(part_grad, "feat", 2)
-    far_grad, by[4] = tie(far_grad, by[4])
     by[6] = swap(by[4], "rec", 2)
     by[5] = swap(by[4], "rec", 1)
-    part_grad = add(part_grad, far_grad, BF)
-    part_grad = lax.all_to_all(part_grad, "rec", 0, 0, tiled=True)
-    part_grad, (by[3], by[6]) = tie(part_grad, (by[3], by[6]))
+
+    def reduced(send, keep):
+        part = add(keep, swap(send, "feat", 1), BF)
+        return [part, swap(part, "feat", 2)]
+
+    send, keep = hidden_grads(me, w_out, [by[i] for i in range(4)], mine)
+    by[6], send = tie(by[6], send)
     by[7] = swap(by[6], "rec", 1)
-    grads = last_grads(me, part_grad, all_preact, lhs)
-    grad_w_latent, grad_embed = outputs(me, grads, swap(grads, "feat", 1), dz)
+    parts = reduced(send, keep)
+    by[7], parts = tie(by[7], parts)
+    parts += reduced(*hidden_grads(me, w_out, [by[4 + i] for i in range(4)], mine))
     grad_w_out = weight_grads(me, all_hidden, [by[mask] for mask in range(groups)])
+    parts[3], grad_w_out = tie(parts[3], grad_w_out)
+    grads = last_grads(me, all_preact, lhs, parts)
+    grad_w_latent, grad_embed = outputs(grads, swap(grads, "feat", 1), dz)
     return grad_w_out, grad_w_latent, grad_embed
 
 

time: 211 us -> 193 us (0.915)
  blocking collectives: 30.3 us -> 0 us
  waiting for transfers between devices: 58.8 us -> 76.5 us
  Pallas kernels: 67.8 us -> 63.4 us
  local copies, waits for them, and re-layouts: 15.1 us -> 12.8 us
    all_to_all x1 -> x0, blocking collectives: 30.3 us -> none  [eight_by_four(): lax.all_to_all(feat_grad.reshape(groups, rows, -1), 'rec', 0, 0, tiled=True)]
    all_to_all x1, waiting for transfers between devices: 0.01 us -> 22.2 us  [eight_by_four(): lax.all_to_all(feat_grad.reshape(groups, rows, -1), 'rec', 0, 0, tiled=True)]
    ppermute x20 -> x22, waiting for transfers between devices: 58.8 us -> 52.5 us  [swap(): return lax.ppermute(x, axis, [(i, i ^ bit) for i in range(n)])]
    unnamed x43 -> x35, local copies, waits for them, and re-layouts: 10.2 us -> 7.81 us
    ppermute x20 -> x22, starting transfers between devices: 18.8 us -> 19.9 us  [swap(): return lax.ppermute(x, axis, [(i, i ^ bit) for i in range(n)])]
  transfers between devices with their start and end apart: 22 -> 24, of which waited for: 14 -> 16; matrix products, arithmetic and copies ran while one was open for 5% -> 3% of each run, Pallas kernels for 7% -> 9%
where the time goes in v5:
time: 193 us; the launch traced here: 192 us
  waiting for transfers between devices  76.5 us (40%)
  Pallas kernels  63.4 us (33%)
  starting transfers between devices  31.7 us (16%)
  local copies, waits for them, and re-layouts  12.8 us (7%)
  matrix products  5.36 us (3%)
    ppermute x22, waiting for transfers between devices, swap(): return lax.ppermute(x, axis, [(i, i ^ bit) for i in range(n)])  52.5 us
    pallas_call x2, Pallas kernels, feature_sums(): pl.pallas_call(functools.partial(features_kernel, masks, last, *totals),...  41.6 us
    all_to_all x1, waiting for transfers between devices, eight_by_four(): lax.all_to_all(feat_grad.reshape(groups, rows, -1), 'rec', 0, 0, tiled=True)  22.2 us
    ppermute x22, starting transfers between devices, swap(): return lax.ppermute(x, axis, [(i, i ^ bit) for i in range(n)])  19.9 us
    pallas_call x1, Pallas kernels, image_grads(): pl.pallas_call(image_kernel, grid_spec=spec, out_shape=[jax.ShapeDtypeStr...  9.89 us
    unnamed x35, local copies, waits for them, and re-layouts  7.81 us
    all_to_all x1, starting transfers between devices, eight_by_four(): lax.all_to_all(jnp.broadcast_to(packed[None], (groups,) + packed.shape),...  7.25 us
    all_to_all x1, starting transfers between devices, eight_by_four(): lax.all_to_all(feat_grad.reshape(groups, rows, -1), 'rec', 0, 0, tiled=True)  4.57 us
  transfers between devices with their start and end apart: 24, of which 16 were waited for; matrix products, arithmetic and copies ran while one was open for 3% of the time, Pallas kernels for 9%

profile of v5, /device:TPU:0, one launch (start us, length us, event | category | flops | bytes accessed | tf_op | source)
XLA Modules:
  0.0 192.3 jit_solution(11100945095445896866)
XLA Ops:
  1.9 1.0 fusion.12
  3.7 2.9 %fusion.4.refs_0_.image = bf16[128,768]{1,0:T(8,128)(2,1)S(1)} fusion(bf16[2048,768]{1,0:T(8,128)(2,1)} %w_ref.3, f32[128,2048]{1,0:T(8,128)S(1)} %fusion.12, bf16[128,128]{1,0:T(8,128)(2,1)} %param.15, bf16[128,2048]{1,0:T(8,128)(2,1)} %param.17), kind=kOutput, calls=%fused_computation.5 | convolution fusion | flops 470646784 | bytes 4947968 | tf_op jit(solution)/shard_map/dot_general | solution.py:695
  7.4 7.3 %all-to-all-start = ((bf16[8,144,128]{2,1,0:T(8,128)(2,1)}), bf16[8,144,128]{2,1,0:T(8,128)(2,1)S(1)}, u32[]{:S(2)}, u32[]{:S(2)}) async-start(bf16[8,144,128]{2,1,0:T(8,128)(2,1)} %broadcast_in_dim.2), calls=%async_computation | async-start | bytes 589824 | tf_op jit(solution)/shard_map/all_to_all | solution.py:701
  14.6 1.5 collective-permute-start
  16.2 4.8 %collective-permute-done.refs_1_ = bf16[128,768]{1,0:T(8,128)(2,1)S(1)} collective-permute-done((bf16[128,768]{1,0:T(8,128)(2,1)S(1)}, bf16[128,768]{1,0:T(8,128)(2,1)S(1)}, u32[]{:S(2)}, u32[]{:S(2)}) %collective-permute-start) | collective-permute-done | bytes 196640 | tf_op jit(solution)/shard_map/ppermute | solution.py:102
  21.1 1.3 collective-permute-done.2.refs_3_
  22.4 1.8 all-to-all-done
  25.0 27.8 %shard_map.112 = (bf16[2,2,128,512]{3,2,1,0:T(8,128)(2,1)S(1)}, f32[2,128,512]{2,1,0:T(8,128)S(1)}, bf16[2,2,128,512]{3,2,1,0:T(8,128)(2,1)S(1)}, f32[2,128,512]{2,1,0:T(8,128)S(1)}, f32[3,2,128,512]{3,2,1,0:T(8,128)S(1)}) custom-call(s32[6]{0:T(128)S(1)} %stack.27.me_ref, s32[1,1536]{1,0:T(1,128)S(1)} %reshape.69.real_labels_ref, s32[1,128]{1,0:T(1,128)S(1)} %bitcast.23, ...), custom_call_target="tpu_custom_call" | custom-call | flops 18320719872 | bytes 18874368 | tf_op jit(solution)/shard_map/pallas_call | solution.py:371
  52.7 1.2 copy-done.5
  53.9 1.4 collective-permute-start.3
  55.3 13.9 %shard_map.113 = (f32[2,128,512]{2,1,0:T(8,128)S(1)}, f32[2,128,512]{2,1,0:T(8,128)S(1)}, f32[1,2,128,512]{3,2,1,0:T(8,128)S(1)}) custom-call(s32[6]{0:T(128)S(1)} %stack.27.me_ref, s32[1,1536]{1,0:T(1,128)S(1)} %reshape.69.real_labels_ref, s32[1,128]{1,0:T(1,128)S(1)} %bitcast.24, bf16[128,768]{1,0:T(8,128)(2,1)S(1)} %fusion.4.refs_0_.image, ...), custom_call_target="tpu_custom_call" | custom-call | flops 6106906624 | bytes 12582912 | tf_op jit(solution)/shard_map/pallas_call | solution.py:371
  70.8 0.9 shard_map.114
  71.7 2.0 %collective-permute-start.5 = (bf16[2,128,512]{2,1,0:T(8,128)(2,1)}, bf16[2,128,512]{2,1,0:T(8,128)(2,1)S(1)}, u32[]{:S(2)}, u32[]{:S(2)}) collective-permute-start(bf16[2,128,512]{2,1,0:T(8,128)(2,1)} %get-tuple-element.77), channel_id=1, source_target_pairs={{0,8},{4,12},{8,0},{12,4},{16,24},{20,28},{24,16},{28,20},{1,9},{5... | collective-permute-start | bytes 786440 | tf_op jit(solution)/shard_map/ppermute | solution.py:102
  74.3 1.2 constant_dynamic-slice_fusion.2
  75.6 4.1 %collective-permute-done.5.ga = bf16[2,128,512]{2,1,0:T(8,128)(2,1)S(1)} collective-permute-done((bf16[2,128,512]{2,1,0:T(8,128)(2,1)}, bf16[2,128,512]{2,1,0:T(8,128)(2,1)S(1)}, u32[]{:S(2)}, u32[]{:S(2)}) %collective-permute-start.5) | collective-permute-done | bytes 262176 | tf_op jit(solution)/shard_map/ppermute | solution.py:102
  80.4 1.0 copy-done.8
  81.4 2.3 %shard_map.115 = (bf16[256,512]{1,0:T(8,128)(2,1)}, f32[256,512]{1,0:T(8,128)S(1)}) custom-call(s32[6]{0:T(128)S(1)} %stack.27.me_ref, f32[2,128,512]{2,1,0:T(8,128)S(1)} %get-tuple-element.72.na, bf16[2,2,128,512]{3,2,1,0:T(8,128)(2,1)S(1)} %collective-permute-done.3.ga.fa, bf16[2,128,512]{2,1,0:T(8,128)(2,1)S(1)} %collective-permute-done.5.ga, ...), custom_call_target="tpu_custom_call" | custom-call | bytes 3145728 | tf_op jit(solution)/shard_map/pallas_call | solution.py:417
  83.7 2.0 %collective-permute-start.7 = (bf16[256,512]{1,0:T(8,128)(2,1)}, bf16[256,512]{1,0:T(8,128)(2,1)S(1)}, u32[]{:S(2)}, u32[]{:S(2)}) collective-permute-start(bf16[256,512]{1,0:T(8,128)(2,1)} %get-tuple-element.82), channel_id=1, source_target_pairs={{0,16},{4,20},{8,24},{12,28},{16,0},{20,4},{24,8},{28,12},{1,17},{... | collective-permute-start | bytes 786440 | tf_op jit(solution)/shard_map/ppermute | solution.py:102
  85.7 1.0 copy.16
  87.0 9.6 %collective-permute-done.7.got_ref = bf16[256,512]{1,0:T(8,128)(2,1)S(1)} collective-permute-done((bf16[256,512]{1,0:T(8,128)(2,1)}, bf16[256,512]{1,0:T(8,128)(2,1)S(1)}, u32[]{:S(2)}, u32[]{:S(2)}) %collective-permute-start.7) | collective-permute-done | bytes 262176 | tf_op jit(solution)/shard_map/ppermute | solution.py:102
  96.7 1.0 copy-done.10
  97.7 1.5 shard_map.116
  99.2 4.6 %all-to-all-start.1 = ((bf16[8,128,512]{2,1,0:T(8,128)(2,1)}), bf16[8,128,512]{2,1,0:T(8,128)(2,1)}, u32[]{:S(2)}, u32[]{:S(2)}) async-start(bf16[8,128,512]{2,1,0:T(8,128)(2,1)} %bitcast.9), calls=%async_computation.1 | async-start | bytes 2097152 | tf_op jit(solution)/shard_map/all_to_all | solution.py:739
  103.8 1.5 constant_dynamic-slice_fusion.1
  106.2 1.4 maximum_convert_fusion
  107.6 22.2 %all-to-all-done.1.rows_ref = bf16[8,128,512]{2,1,0:T(8,128)(2,1)} async-done(((bf16[8,128,512]{2,1,0:T(8,128)(2,1)}), bf16[8,128,512]{2,1,0:T(8,128)(2,1)}, u32[]{:S(2)}, u32[]{:S(2)}) %all-to-all-start.1) | async-done | bytes 1048608 | tf_op jit(solution)/shard_map/all_to_all | solution.py:739
  129.8 9.9 %shard_map.117 = (bf16[2,768,128]{2,1,0:T(8,128)(2,1)}, f32[2,768,128]{2,1,0:T(8,128)}) custom-call(s32[6]{0:T(128)} %copy-done.11, f32[3,2,128,512]{3,2,1,0:T(8,128)} %copy-done.5, f32[1,2,128,512]{3,2,1,0:T(8,128)} %copy-done.6, bf16[8,128,512]{2,1,0:T(8,128)(2,1)} %all-to-all-done.1.rows_ref, bf16[3072,2048]{1,0:T(8,128)(2,1)} %freq_ref.1), custom_call_target="tpu_custom_call" | custom-call | flops 1610612736 | bytes 12582912 | tf_op jit(solution)/shard_map/pallas_call | solution.py:499
  139.7 1.9 %collective-permute-done.8.got_s.got_k = bf16[2,768,128]{2,1,0:T(8,128)(2,1)S(1)} collective-permute-done((bf16[2,768,128]{2,1,0:T(8,128)(2,1)}, bf16[2,768,128]{2,1,0:T(8,128)(2,1)S(1)}, u32[]{:S(2)}, u32[]{:S(2)}) %collective-permute-start.8) | collective-permute-done | bytes 393248 | tf_op jit(solution)/shard_map/ppermute | solution.py:102
  141.6 1.1 copy-done.2
  143.4 1.6 collective-permute-start.9
  145.0 5.4 %collective-permute-done.9.got = bf16[768,128]{1,0:T(8,128)(2,1)S(1)} collective-permute-done((bf16[768,128]{1,0:T(8,128)(2,1)S(1)}, bf16[768,128]{1,0:T(8,128)(2,1)S(1)}, u32[]{:S(2)}, u32[]{:S(2)}) %collective-permute-start.9) | collective-permute-done | bytes 196640 | tf_op jit(solution)/shard_map/ppermute | solution.py:102
  150.7 2.0 %collective-permute-start.11 = (bf16[128,768]{1,0:T(8,128)(2,1)S(1)}, bf16[128,768]{1,0:T(8,128)(2,1)S(1)}, u32[]{:S(2)}, u32[]{:S(2)}) collective-permute-start(bf16[128,768]{1,0:T(8,128)(2,1)S(1)} %shard_map.119.refs_0_), channel_id=1, source_target_pairs={{0,8},{4,12},{8,0},{12,4},{16,24},{20,28},{24,16},{28,20},{1,9},{5... | collective-permute-start | bytes 589832 | tf_op jit(solution)/shard_map/ppermute | solution.py:102
  152.7 1.4 collective-permute-start.12
  154.2 6.9 %collective-permute-done.10.refs_0_.refs_4_ = bf16[128,768]{1,0:T(8,128)(2,1)S(1)} collective-permute-done((bf16[128,768]{1,0:T(8,128)(2,1)S(1)}, bf16[128,768]{1,0:T(8,128)(2,1)S(1)}, u32[]{:S(2)}, u32[]{:S(2)}) %collective-permute-start.10) | collective-permute-done | bytes 196640 | tf_op jit(solution)/shard_map/ppermute | solution.py:102
  161.1 1.4 collective-permute-start.15
  162.7 5.1 %collective-permute-done.15.refs_3_ = bf16[128,768]{1,0:T(8,128)(2,1)S(1)} collective-permute-done((bf16[128,768]{1,0:T(8,128)(2,1)S(1)}, bf16[128,768]{1,0:T(8,128)(2,1)S(1)}, u32[]{:S(2)}, u32[]{:S(2)}) %collective-permute-start.15) | collective-permute-done | bytes 196640 | tf_op jit(solution)/shard_map/ppermute | solution.py:102
  167.8 1.1 shard_map.120
  169.0 1.3 collective-permute-start.16
  171.2 1.6 collective-permute-start.18
  172.8 4.1 %collective-permute-done.16.refs_3_.refs_7_ = bf16[128,768]{1,0:T(8,128)(2,1)S(1)} collective-permute-done((bf16[128,768]{1,0:T(8,128)(2,1)S(1)}, bf16[128,768]{1,0:T(8,128)(2,1)S(1)}, u32[]{:S(2)}, u32[]{:S(2)}) %collective-permute-start.16) | collective-permute-done | bytes 196640 | tf_op jit(solution)/shard_map/ppermute | solution.py:102
  176.8 3.8 %collective-permute-done.13.refs_1_.refs_5_ = bf16[128,768]{1,0:T(8,128)(2,1)S(1)} collective-permute-done((bf16[128,768]{1,0:T(8,128)(2,1)S(1)}, bf16[128,768]{1,0:T(8,128)(2,1)S(1)}, u32[]{:S(2)}, u32[]{:S(2)}) %collective-permute-start.13) | collective-permute-done | bytes 196640 | tf_op jit(solution)/shard_map/ppermute | solution.py:102
  180.6 1.1 shard_map.122
  181.8 1.3 collective-permute-done.19.b
  183.1 1.6 collective-permute-start.20
  184.7 2.4 %shard_map.124 = f32[256,768]{1,0:T(8,128)} custom-call(s32[6]{0:T(128)S(1)} %copy-done.12, bf16[256,1024]{1,0:T(8,128)(2,1)S(1)} %get-tuple-element.100.hidden_ref, bf16[128,768]{1,0:T(8,128)(2,1)S(1)} %shard_map.119.refs_0_, bf16[128,768]{1,0:T(8,128)(2,1)S(1)} %collective-permute-done.12.refs_1_, bf16[128,768]{1,0:T(8,128)(2,1)S(1)} %collective-permute-done.11.refs_2_, ...), custom_call_target="tpu_custom_call" | custom-call | flops 402653184 | bytes 4194304 | tf_op jit(solution)/shard_map/pallas_call | solution.py:608
  187.1 1.7 collective-permute-done.20.q1
  188.8 1.0 shard_map.125.own
  189.8 1.7 collective-permute-done.21.other
  (69 shorter events, 10.8 us)
Async XLA Ops:
  0.6 1.2 copy-start
  2.9 18.1 %copy-start.16 = (s32[1536]{0:T(1024)S(1)}, s32[1536]{0:T(1024)}, u32[]{:S(2)}) copy-start(s32[1536]{0:T(1024)} %param.12) | copy-start | bytes 18436
  2.9 22.1 %copy-start.13 = (s32[128]{0:T(128)S(1)}, s32[128]{0:T(128)}, u32[]{:S(2)}) copy-start(s32[128]{0:T(128)} %param.16) | copy-start | bytes 1540
  6.6 48.7 %copy-start.3 = (bf16[128,768]{1,0:T(8,128)(2,1)}, bf16[128,768]{1,0:T(8,128)(2,1)S(1)}, u32[]{:S(2)}) copy-start(bf16[128,768]{1,0:T(8,128)(2,1)S(1)} %fusion.4.refs_0_.image) | copy-start | bytes 589828
  7.4 16.9 %all-to-all-start = ((bf16[8,144,128]{2,1,0:T(8,128)(2,1)}), bf16[8,144,128]{2,1,0:T(8,128)(2,1)S(1)}, u32[]{:S(2)}, u32[]{:S(2)}) async-start(bf16[8,144,128]{2,1,0:T(8,128)(2,1)} %broadcast_in_dim.2), calls=%async_computation | async-start | bytes 589824 | tf_op jit(solution)/shard_map/all_to_all | solution.py:701
  14.6 6.4 %collective-permute-start = (bf16[128,768]{1,0:T(8,128)(2,1)S(1)}, bf16[128,768]{1,0:T(8,128)(2,1)S(1)}, u32[]{:S(2)}, u32[]{:S(2)}) collective-permute-start(bf16[128,768]{1,0:T(8,128)(2,1)S(1)} %fusion.4.refs_0_.image), channel_id=1, source_target_pairs={{0,2},{1,3},{2,0},{3,1},{4,6},{5,7},{6,4},{7,5},{8,10},{9,11},{10,... | collective-permute-start | bytes 589832 | tf_op jit(solution)/shard_map/ppermute | solution.py:102
  16.2 5.0 %collective-permute-start.1 = (bf16[128,768]{1,0:T(8,128)(2,1)S(1)}, bf16[128,768]{1,0:T(8,128)(2,1)S(1)}, u32[]{:S(2)}, u32[]{:S(2)}) collective-permute-start(bf16[128,768]{1,0:T(8,128)(2,1)S(1)} %fusion.4.refs_0_.image), channel_id=1, source_target_pairs={{0,1},{1,0},{2,3},{3,2},{4,5},{5,4},{6,7},{7,6},{8,9},{9,8},{10,11... | collective-permute-start | bytes 589832 | tf_op jit(solution)/shard_map/ppermute | solution.py:102
  21.0 1.4 collective-permute-start.2
  21.1 59.3 %copy-start.11 = (s32[6]{0:T(128)}, s32[6]{0:T(128)S(1)}, u32[]{:S(2)}) copy-start(s32[6]{0:T(128)S(1)} %stack.27.me_ref) | copy-start | bytes 76
  24.3 0.7 copy-start.14
  52.7 1.2 copy-start.5
  53.9 16.9 %collective-permute-start.3 = (bf16[2,2,128,512]{3,2,1,0:T(8,128)(2,1)S(1)}, bf16[2,2,128,512]{3,2,1,0:T(8,128)(2,1)S(1)}, u32[]{:S(2)}, u32[]{:S(2)}) collective-permute-start(bf16[2,2,128,512]{3,2,1,0:T(8,128)(2,1)S(1)} %get-tuple-element.70), channel_id=1, source_target_pairs={{0,4},{4,0},{8,12},{12,8},{16,20},{20,16},{24,28},{28,24},{1,5},{5... | collective-permute-start | bytes 1572872 | tf_op jit(solution)/shard_map/ppermute | solution.py:102
  55.3 15.5 %collective-permute-start.4 = (bf16[2,2,128,512]{3,2,1,0:T(8,128)(2,1)S(1)}, bf16[2,2,128,512]{3,2,1,0:T(8,128)(2,1)S(1)}, u32[]{:S(2)}, u32[]{:S(2)}) collective-permute-start(bf16[2,2,128,512]{3,2,1,0:T(8,128)(2,1)S(1)} %get-tuple-element.71), channel_id=1, source_target_pairs={{0,8},{4,12},{8,0},{12,4},{16,24},{20,28},{24,16},{28,20},{1,9},{5... | collective-permute-start | bytes 1572872 | tf_op jit(solution)/shard_map/ppermute | solution.py:102
  69.2 0.8 copy-start.6
  70.0 0.8 copy-start.7
  71.7 8.0 %collective-permute-start.5 = (bf16[2,128,512]{2,1,0:T(8,128)(2,1)}, bf16[2,128,512]{2,1,0:T(8,128)(2,1)S(1)}, u32[]{:S(2)}, u32[]{:S(2)}) collective-permute-start(bf16[2,128,512]{2,1,0:T(8,128)(2,1)} %get-tuple-element.77), channel_id=1, source_target_pairs={{0,8},{4,12},{8,0},{12,4},{16,24},{20,28},{24,16},{28,20},{1,9},{5... | collective-permute-start | bytes 786440 | tf_op jit(solution)/shard_map/ppermute | solution.py:102
  73.7 6.7 %collective-permute-start.6 = (bf16[2,128,512]{2,1,0:T(8,128)(2,1)}, bf16[2,128,512]{2,1,0:T(8,128)(2,1)}, u32[]{:S(2)}, u32[]{:S(2)}) collective-permute-start(bf16[2,128,512]{2,1,0:T(8,128)(2,1)} %get-tuple-element.80), channel_id=1, source_target_pairs={{0,4},{4,0},{8,12},{12,8},{16,20},{20,16},{24,28},{28,24},{1,5},{5... | collective-permute-start | bytes 786440 | tf_op jit(solution)/shard_map/ppermute | solution.py:102
  80.4 1.0 copy-start.8
  83.7 3.1 %copy-start.9 = (f32[256,512]{1,0:T(8,128)}, f32[256,512]{1,0:T(8,128)S(1)}, u32[]{:S(2)}) copy-start(f32[256,512]{1,0:T(8,128)S(1)} %get-tuple-element.81.keep_ref) | copy-start | bytes 1572868
  83.7 13.0 %collective-permute-start.7 = (bf16[256,512]{1,0:T(8,128)(2,1)}, bf16[256,512]{1,0:T(8,128)(2,1)S(1)}, u32[]{:S(2)}, u32[]{:S(2)}) collective-permute-start(bf16[256,512]{1,0:T(8,128)(2,1)} %get-tuple-element.82), channel_id=1, source_target_pairs={{0,16},{4,20},{8,24},{12,28},{16,0},{20,4},{24,8},{28,12},{1,17},{... | collective-permute-start | bytes 786440 | tf_op jit(solution)/shard_map/ppermute | solution.py:102
  86.8 18.4 %slice-start = ((bf16[8,144,128]{2,1,0:T(8,128)(2,1)}), bf16[8,128,128]{2,1,0:T(8,128)(2,1)S(1)}, s32[]{:S(2)}) async-start(bf16[8,144,128]{2,1,0:T(8,128)(2,1)} %copy-done.14), calls=%async_computation.2 | async-start | bytes 524288 | tf_op jit(solution)/shard_map/slice | solution.py:714
  96.7 1.0 copy-start.10
  99.2 30.6 %all-to-all-start.1 = ((bf16[8,128,512]{2,1,0:T(8,128)(2,1)}), bf16[8,128,512]{2,1,0:T(8,128)(2,1)}, u32[]{:S(2)}, u32[]{:S(2)}) async-start(bf16[8,128,512]{2,1,0:T(8,128)(2,1)} %bitcast.9), calls=%async_computation.1 | async-start | bytes 2097152 | tf_op jit(solution)/shard_map/all_to_all | solution.py:739
  105.4 0.7 copy-start.15
  129.8 11.8 %copy-start.12 = (s32[6]{0:T(128)S(1)}, s32[6]{0:T(128)}, u32[]{:S(2)}) copy-start(s32[6]{0:T(128)} %copy-done.11) | copy-start | bytes 76
  129.8 20.6 %copy-start.4 = (bf16[128,768]{1,0:T(8,128)(2,1)S(1)}, bf16[128,768]{1,0:T(8,128)(2,1)}, u32[]{:S(2)}) copy-start(bf16[128,768]{1,0:T(8,128)(2,1)} %copy-done.3) | copy-start | bytes 589828
  139.7 28.2 %copy-start.1 = (bf16[2048,768]{1,0:T(8,128)(2,1)S(1)}, bf16[2048,768]{1,0:T(8,128)(2,1)}, u32[]{:S(2)}) copy-start(bf16[2048,768]{1,0:T(8,128)(2,1)} %w_ref.3) | copy-start | bytes 9437188
  139.7 1.9 %collective-permute-start.8 = (bf16[2,768,128]{2,1,0:T(8,128)(2,1)}, bf16[2,768,128]{2,1,0:T(8,128)(2,1)S(1)}, u32[]{:S(2)}, u32[]{:S(2)}) collective-permute-start(bf16[2,768,128]{2,1,0:T(8,128)(2,1)} %get-tuple-element.87), channel_id=1, source_target_pairs={{0,1},{1,0},{2,3},{3,2},{4,5},{5,4},{6,7},{7,6},{8,9},{9,8},{10,11... | collective-permute-start | bytes 1179656 | tf_op jit(solution)/shard_map/ppermute | solution.py:102
  141.6 1.1 copy-start.2
  143.4 7.0 %collective-permute-start.9 = (bf16[768,128]{1,0:T(8,128)(2,1)S(1)}, bf16[768,128]{1,0:T(8,128)(2,1)S(1)}, u32[]{:S(2)}, u32[]{:S(2)}) collective-permute-start(bf16[768,128]{1,0:T(8,128)(2,1)S(1)} %get-tuple-element.89), channel_id=1, source_target_pairs={{0,2},{1,3},{2,0},{3,1},{4,6},{5,7},{6,4},{7,5},{8,10},{9,11},{10,... | collective-permute-start | bytes 589832 | tf_op jit(solution)/shard_map/ppermute | solution.py:102
  150.6 10.5 %collective-permute-start.10 = (bf16[128,768]{1,0:T(8,128)(2,1)S(1)}, bf16[128,768]{1,0:T(8,128)(2,1)S(1)}, u32[]{:S(2)}, u32[]{:S(2)}) collective-permute-start(bf16[128,768]{1,0:T(8,128)(2,1)S(1)} %shard_map.119.refs_0_), channel_id=1, source_target_pairs={{0,16},{4,20},{8,24},{12,28},{16,0},{20,4},{24,8},{28,12},{1,17},{... | collective-permute-start | bytes 589832 | tf_op jit(solution)/shard_map/ppermute | solution.py:102
  150.7 10.4 %collective-permute-start.11 = (bf16[128,768]{1,0:T(8,128)(2,1)S(1)}, bf16[128,768]{1,0:T(8,128)(2,1)S(1)}, u32[]{:S(2)}, u32[]{:S(2)}) collective-permute-start(bf16[128,768]{1,0:T(8,128)(2,1)S(1)} %shard_map.119.refs_0_), channel_id=1, source_target_pairs={{0,8},{4,12},{8,0},{12,4},{16,24},{20,28},{24,16},{28,20},{1,9},{5... | collective-permute-start | bytes 589832 | tf_op jit(solution)/shard_map/ppermute | solution.py:102
  152.7 8.4 %collective-permute-start.12 = (bf16[128,768]{1,0:T(8,128)(2,1)S(1)}, bf16[128,768]{1,0:T(8,128)(2,1)S(1)}, u32[]{:S(2)}, u32[]{:S(2)}) collective-permute-start(bf16[128,768]{1,0:T(8,128)(2,1)S(1)} %shard_map.119.refs_0_), channel_id=1, source_target_pairs={{0,4},{4,0},{8,12},{12,8},{16,20},{20,16},{24,28},{28,24},{1,5},{5... | collective-permute-start | bytes 589832 | tf_op jit(solution)/shard_map/ppermute | solution.py:102
  161.1 6.8 %collective-permute-start.15 = (bf16[128,768]{1,0:T(8,128)(2,1)S(1)}, bf16[128,768]{1,0:T(8,128)(2,1)S(1)}, u32[]{:S(2)}, u32[]{:S(2)}) collective-permute-start(bf16[128,768]{1,0:T(8,128)(2,1)S(1)} %collective-permute-done.11.refs_2_), channel_id=1, source_target_pairs={{0,4},{4,0},{8,12},{12,8},{16,20},{20,16},{24,28},{28,24},{1,5},{5... | collective-permute-start | bytes 589832 | tf_op jit(solution)/shard_map/ppermute | solution.py:102
  162.5 6.5 %collective-permute-start.14 = (bf16[128,768]{1,0:T(8,128)(2,1)S(1)}, bf16[128,768]{1,0:T(8,128)(2,1)S(1)}, u32[]{:S(2)}, u32[]{:S(2)}) collective-permute-start(bf16[128,768]{1,0:T(8,128)(2,1)S(1)} %collective-permute-done.10.refs_0_.refs_4_), channel_id=1, source_target_pairs={{0,8},{4,12},{8,0},{12,4},{16,24},{20,28},{24,16},{28,20},{1,9},{5... | collective-permute-start | bytes 589832 | tf_op jit(solution)/shard_map/ppermute | solution.py:102
  169.0 2.2 %collective-permute-start.17 = (bf16[2,256,128]{2,1,0:T(8,128)(2,1)S(1)}, bf16[2,256,128]{2,1,0:T(8,128)(2,1)S(1)}, u32[]{:S(2)}, u32[]{:S(2)}) collective-permute-start(bf16[2,256,128]{2,1,0:T(8,128)(2,1)S(1)} %get-tuple-element.96), channel_id=1, source_target_pairs={{0,1},{1,0},{2,3},{3,2},{4,5},{5,4},{6,7},{7,6},{8,9},{9,8},{10,11... | collective-permute-start | bytes 393224 | tf_op jit(solution)/shard_map/ppermute | solution.py:102
  169.0 7.8 %collective-permute-start.16 = (bf16[128,768]{1,0:T(8,128)(2,1)S(1)}, bf16[128,768]{1,0:T(8,128)(2,1)S(1)}, u32[]{:S(2)}, u32[]{:S(2)}) collective-permute-start(bf16[128,768]{1,0:T(8,128)(2,1)S(1)} %collective-permute-done.14.refs_2_.refs_6_), channel_id=1, source_target_pairs={{0,4},{4,0},{8,12},{12,8},{16,20},{20,16},{24,28},{28,24},{1,5},{5... | collective-permute-start | bytes 589832 | tf_op jit(solution)/shard_map/ppermute | solution.py:102
  170.3 10.3 %collective-permute-start.13 = (bf16[128,768]{1,0:T(8,128)(2,1)S(1)}, bf16[128,768]{1,0:T(8,128)(2,1)S(1)}, u32[]{:S(2)}, u32[]{:S(2)}) collective-permute-start(bf16[128,768]{1,0:T(8,128)(2,1)S(1)} %collective-permute-done.10.refs_0_.refs_4_), channel_id=1, source_target_pairs={{0,4},{4,0},{8,12},{12,8},{16,20},{20,16},{24,28},{28,24},{1,5},{5... | collective-permute-start | bytes 589832 | tf_op jit(solution)/shard_map/ppermute | solution.py:102
  171.2 5.6 %collective-permute-start.18 = (bf16[2,256,128]{2,1,0:T(8,128)(2,1)S(1)}, bf16[2,256,128]{2,1,0:T(8,128)(2,1)S(1)}, u32[]{:S(2)}, u32[]{:S(2)}) collective-permute-start(bf16[2,256,128]{2,1,0:T(8,128)(2,1)S(1)} %shard_map.121.p0), channel_id=1, source_target_pairs={{0,2},{1,3},{2,0},{3,1},{4,6},{5,7},{6,4},{7,5},{8,10},{9,11},{10,... | collective-permute-start | bytes 393224 | tf_op jit(solution)/shard_map/ppermute | solution.py:102
  181.7 1.4 collective-permute-start.19
  183.1 5.6 %collective-permute-start.20 = (bf16[2,256,128]{2,1,0:T(8,128)(2,1)S(1)}, bf16[2,256,128]{2,1,0:T(8,128)(2,1)S(1)}, u32[]{:S(2)}, u32[]{:S(2)}) collective-permute-start(bf16[2,256,128]{2,1,0:T(8,128)(2,1)S(1)} %shard_map.123.p1), channel_id=1, source_target_pairs={{0,2},{1,3},{2,0},{3,1},{4,6},{5,7},{6,4},{7,5},{8,10},{9,11},{10,... | collective-permute-start | bytes 393224 | tf_op jit(solution)/shard_map/ppermute | solution.py:102
  189.7 1.8 collective-permute-start.21

commit v6 on v5

--- a/solution.py
+++ b/solution.py
@@ -242,7 +242,7 @@
     count = len(masks)
     images = refs[:count]
     records_hbm, freq_ref = refs[count : count + 2]
-    outs = refs[count + 2 : -4]
+    outs = refs[count + 3 : -4]
     records, real_table, syn_table, sem = refs[-4:]
     classes, total = real_table.shape
     size = 512
@@ -263,11 +263,6 @@
             real_table[...] = jnp.where(ids == real_labels_ref[...], 1.0, 0.0).astype(BF)
             ids = lax.broadcasted_iota(jnp.int32, syn_table.shape, 0)
             syn_table[...] = jnp.where(ids == syn_labels_ref[...], 1.0, 0.0).astype(BF)
-        syn_pre = None
-        for mask, image in zip(masks, images):
-            at = pl.multiple_of((me_ref[0] ^ mask) * cols, 128)
-            d = jnp.dot(image[...], freq_ref[pl.ds(at, cols), :], preferred_element_type=F32)
-            syn_pre = d if syn_pre is None else syn_pre + d
         freq = freq_ref[...]
         acc = None
         before = None
@@ -276,16 +271,21 @@
                 if wait:
                     copy(i).wait()
                 pre = jnp.dot(records[i * size : (i + 1) * size, :], freq, preferred_element_type=F32)
-            if i == 0:
-                co, si = cos_sin(syn_pre)
-                outs[-1][0, 0] = co
-                outs[-1][0, 1] = si
-                phi = jnp.concatenate([co.astype(BF), si.astype(BF)], axis=1)
-                syn = jnp.dot(syn_table[...], phi, preferred_element_type=F32)
             else:
+                syn_pre = None
+                for mask, image in zip(masks, images):
+                    at = pl.multiple_of((me_ref[0] ^ mask) * cols, 128)
+                    d = jnp.dot(image[...], freq_ref[pl.ds(at, cols), :], preferred_element_type=F32)
+                    syn_pre = d if syn_pre is None else syn_pre + d
+            if i > 0:
                 d = sums(real_table[:, (i - 1) * size : i * size], before)
                 acc = d if acc is None else acc + d
             before = pre
+        co, si = cos_sin(syn_pre)
+        outs[-1][0, 0] = co
+        outs[-1][0, 1] = si
+        phi = jnp.concatenate([co.astype(BF), si.astype(BF)], axis=1)
+        syn = jnp.dot(syn_table[...], phi, preferred_element_type=F32)
         gap = syn * (1.0 / syn_total) - acc * (1.0 / real_total)
         width = gap.shape[1] // 4
         return [
@@ -327,7 +327,7 @@
                 send_b[0, h] = parts[h][half:].astype(BF)
 
 
-def feature_sums(last, me, real_labels, syn_labels, masks, images, records, freq, classes, totals):
+def feature_sums(last, me, real_labels, syn_labels, masks, images, records, freq, classes, totals, after):
     total, k = records.shape
     n = freq.shape[1]
     rows, cols = images[0].shape
@@ -337,7 +337,7 @@
     whole = lambda shape: block(shape, lambda j, me: (0,) * len(shape))
     kept = jax.ShapeDtypeStruct((2, half, tile), F32)
     sent = jax.ShapeDtypeStruct((2, 2, half, tile), BF)
-    wave = jax.ShapeDtypeStruct((tiles, 2, rows, tile), F32)
+    wave = pltpu.HBM((tiles, 2, rows, tile), F32)
     wave_spec = block((1, 2, rows, tile), lambda j, me: (j, 0, 0, 0))
     if last:
         shapes = [kept, kept, wave]
@@ -359,6 +359,7 @@
         + [
             pl.BlockSpec(memory_space=pl.ANY),
             block((k, tile), lambda j, me: (0, me[5] ^ (0 if last else 3 - j))),
+            pl.BlockSpec(memory_space=pl.ANY),
         ],
         out_specs=specs,
         scratch_shapes=[
@@ -378,24 +379,25 @@
             bytes_accessed=2 * (total * k + k * tiles * tile),
             transcendentals=0,
         ),
-    )(me, real_labels.reshape(1, -1), syn_labels.reshape(1, -1), *images, records, freq)
-
-
-def stage_two_send_kernel(ka, ga, kb, gb, sa, sb):
+    )(me, real_labels.reshape(1, -1), syn_labels.reshape(1, -1), *images, records, freq, after)
+
+
+def stage_two_send_kernel(ka, ga, kb, gb, after, sa, sb):
     sa[...] = (ka[...] + ga[0].astype(F32)).astype(BF)
     sb[...] = (kb[...] + gb[0].astype(F32)).astype(BF)
 
 
-def stage_two_send(keep_a, got_a, keep_b, got_b):
+def stage_two_send(keep_a, got_a, keep_b, got_b, after):
     return pl.pallas_call(
         stage_two_send_kernel,
+        in_specs=[pl.BlockSpec()] * 4 + [pl.BlockSpec(memory_space=pl.ANY)],
         out_shape=[jax.ShapeDtypeStruct(keep_a.shape, BF)] * 2,
         compiler_params=pltpu.CompilerParams(vmem_limit_bytes=10 * 2**20),
         cost_estimate=pl.CostEstimate(flops=0, bytes_accessed=3 * 2**20, transcendentals=0),
-    )(keep_a, got_a, keep_b, got_b)
-
-
-def stage_three_kernel(me_ref, na, fa, ga, nb, fb, gb, send, keep):
+    )(keep_a, got_a, keep_b, got_b, after)
+
+
+def stage_three_kernel(me_ref, na, fa, ga, nb, fb, gb, after, behind, send, keep):
     high = me_ref[3]
     half = na.shape[1]
     for flip, out in ((1, send), (0, keep)):
@@ -404,14 +406,14 @@
         out[half:] = (nb[at] + fb[1, at].astype(F32) + gb[at].astype(F32)).astype(out.dtype)
 
 
-def stage_three(me, keep_a, first_a, got_a, keep_b, first_b, got_b):
+def stage_three(me, keep_a, first_a, got_a, keep_b, first_b, got_b, after):
     _, half, width = keep_a.shape
     args = (keep_a, first_a, got_a, keep_b, first_b, got_b)
     whole = lambda shape: block(shape, lambda h, me: (0,) * len(shape))
     spec = pltpu.PrefetchScalarGridSpec(
         num_scalar_prefetch=1,
         grid=(1,),
-        in_specs=[whole(x.shape) for x in args],
+        in_specs=[whole(x.shape) for x in args] + [pl.BlockSpec(memory_space=pl.ANY)] * 2,
         out_specs=[whole((2 * half, width))] * 2,
     )
     return pl.pallas_call(
@@ -420,89 +422,99 @@
         out_shape=[jax.ShapeDtypeStruct((2 * half, width), t) for t in (BF, F32)],
         compiler_params=pltpu.CompilerParams(vmem_limit_bytes=12 * 2**20),
         cost_estimate=pl.CostEstimate(flops=0, bytes_accessed=3 * 2**20, transcendentals=0),
-    )(me, *args)
-
-
-def gap_kernel(real_total, keep_ref, got_ref, noise_ref, labels_ref, out_ref):
+    )(me, *args, *after)
+
+
+def gap_kernel(real_total, me_ref, keep_ref, got_ref, noise_ref, labels_ref, out_ref):
     classes = keep_ref.shape[0]
+    rows = labels_ref.shape[1]
     gap = keep_ref[...] + got_ref[...].astype(F32) - noise_ref[...] * (1.0 / real_total)
     gap = (16.0 * gap).astype(BF)
-    ids = lax.broadcasted_iota(jnp.int32, (labels_ref.shape[0], classes), 1)
-    table = jnp.where(ids == labels_ref[...], 1.0, 0.0).astype(BF)
-    out_ref[...] = jnp.dot(table, gap, preferred_element_type=F32).astype(BF)
-
-
-def gap_rows(keep, got, noise, labels, real_total):
+    ids = lax.broadcasted_iota(jnp.int32, (classes, rows), 0)
+    for mask in range(labels_ref.shape[0]):
+        table = jnp.where(ids == labels_ref[mask : mask + 1, :], 1.0, 0.0).astype(BF)
+        out = lax.dot_general(table, gap, (((0,), (0,)), ((), ())), preferred_element_type=F32)
+        out_ref[me_ref[4] ^ mask] = out.astype(BF)
+
+
+def gap_rows(me, keep, got, noise, labels, real_total):
     classes, width = keep.shape
-    total = labels.shape[0]
+    groups, rows = labels.shape
+    whole = lambda shape: block(shape, lambda h, me: (0,) * len(shape))
+    spec = pltpu.PrefetchScalarGridSpec(
+        num_scalar_prefetch=1,
+        grid=(1,),
+        in_specs=[whole(x.shape) for x in (keep, got, noise, labels)],
+        out_specs=whole((groups, rows, width)),
+    )
     return pl.pallas_call(
         functools.partial(gap_kernel, real_total),
-        out_shape=jax.ShapeDtypeStruct((total, width), BF),
+        grid_spec=spec,
+        out_shape=jax.ShapeDtypeStruct((groups, rows, width), BF),
         compiler_params=pltpu.CompilerParams(vmem_limit_bytes=14 * 2**20),
         cost_estimate=pl.CostEstimate(
-            flops=2 * total * classes * width, bytes_accessed=3 * 2**20, transcendentals=0
+            flops=2 * groups * rows * classes * width, bytes_accessed=3 * 2**20, transcendentals=0
         ),
-    )(keep, got, noise, labels.reshape(total, 1))
+    )(me, keep, got, noise, labels)
 
 
 NT = (((1,), (1,)), ((), ()))
 
 
-def image_kernel(me_ref, three_ref, last_ref, rows_ref, freq_ref, send_ref, keep_ref, pre_ref):
-    step = pl.program_id(0)
+def image_kernel(
+    me_ref, three_ref, last_ref, rows_ref, freq_hbm, a, b, c, send_ref, keep_ref, freq_ref, pre_ref, sem
+):
     cols = send_ref.shape[1]
     tile = three_ref.shape[3]
     part = tile // 2
-
-    @pl.when(step == 0)
-    def _():
-        for t in range(4):
-            place = me_ref[5] ^ (3 - t)
-            wave = last_ref.at[0] if t == 3 else three_ref.at[t]
-            for h in range(2):
-                grad = rows_ref[4 * h + 2 * (place % 2) + place // 2].astype(F32)
-                lanes = slice(h * part, (h + 1) * part)
-                pre = wave[0, :, lanes] * grad[:, part:] - wave[1, :, lanes] * grad[:, :part]
-                at = pl.multiple_of(place * tile + h * part, 128)
-                pre_ref[:, pl.ds(at, part)] = pre.astype(BF)
-
-    out = lax.dot_general(freq_ref[...], pre_ref[...], NT, preferred_element_type=F32)
-    steps = pl.num_programs(0) // 2
-
-    @pl.when(step < steps)
-    def _():
-        send_ref[0] = out.astype(BF)
-
-    @pl.when(step >= steps)
-    def _():
-        keep_ref[0] = out
-
-
-def image_grads(me, three, last, feat_rows, freq, cols):
+    core = me_ref[0] % 2
+    copies = []
+    for s in range(4):
+        first = (2 * (s % 2) + (core ^ (1 - s // 2))) * cols
+        source = freq_hbm.at[pl.ds(pl.multiple_of(first, 128), cols), :]
+        copies.append(pltpu.make_async_copy(source, freq_ref.at[s], sem.at[s]))
+        copies[-1].start()
+    for t in range(4):
+        place = me_ref[5] ^ (3 - t)
+        wave = last_ref.at[0] if t == 3 else three_ref.at[t]
+        for h in range(2):
+            grad = rows_ref[4 * h + 2 * (place % 2) + place // 2].astype(F32)
+            lanes = slice(h * part, (h + 1) * part)
+            pre = wave[0, :, lanes] * grad[:, part:] - wave[1, :, lanes] * grad[:, :part]
+            at = pl.multiple_of(place * tile + h * part, 128)
+            pre_ref[:, pl.ds(at, part)] = pre.astype(BF)
+    for s in range(4):
+        copies[s].wait()
+        out = lax.dot_general(freq_ref[s], pre_ref[...], NT, preferred_element_type=F32)
+        if s < 2:
+            send_ref[s] = out.astype(BF)
+        else:
+            keep_ref[s - 2] = out
+
+
+def image_grads(me, three, last, feat_rows, freq, cols, after):
     k, n = freq.shape
     owners, rows, width = feat_rows.shape
-    whole = lambda x: block(x.shape, lambda s, me: (0,) * x.ndim)
-
-    def source(s, me):
-        return 2 * (s % 2) + ((me[0] % 2) ^ (1 - s // 2)), 0
-
+    whole = lambda shape: block(shape, lambda s, me: (0,) * len(shape))
     spec = pltpu.PrefetchScalarGridSpec(
         num_scalar_prefetch=1,
-        grid=(4,),
-        in_specs=[whole(three), whole(last), whole(feat_rows), block((cols, n), source)],
-        out_specs=[
-            block((1, cols, rows), lambda s, me: (jnp.minimum(s, 1), 0, 0)),
-            block((1, cols, rows), lambda s, me: (jnp.maximum(s - 2, 0), 0, 0)),
+        grid=(1,),
+        in_specs=[whole(three.shape), whole(last.shape), whole(feat_rows.shape)]
+        + [pl.BlockSpec(memory_space=pl.ANY)] * 4,
+        out_specs=[whole((2, cols, rows))] * 2,
+        scratch_shapes=[
+            pltpu.VMEM((4, cols, n), BF),
+            pltpu.VMEM((rows, n), BF),
+            pltpu.SemaphoreType.DMA((4,)),
         ],
-        scratch_shapes=[pltpu.VMEM((rows, n), BF)],
     )
     return pl.pallas_call(
         image_kernel,
         grid_spec=spec,
         out_shape=[jax.ShapeDtypeStruct((2, cols, rows), t) for t in (BF, F32)],
-        compiler_params=pltpu.CompilerParams(vmem_limit_bytes=56 * 2**20),
+        compiler_params=pltpu.CompilerParams(vmem_limit_bytes=52 * 2**20),
         cost_estimate=pl.CostEstimate(flops=2 * k * n * rows, bytes_accessed=2 * k * n, transcendentals=0),
-    )(me, three, last, feat_rows, freq)
+    )(me, three, last, feat_rows, freq, *after)
 
 
 def split_y_kernel(me_ref, keep_s, keep_k, got_s, got_k, send, keep):
@@ -543,7 +555,7 @@
 
 def hidden_kernel(me_ref, w_ref, *refs):
     grads = refs[:4]
-    send, keep = refs[4:]
+    send, keep = refs[5:]
     core = me_ref[0] % 2
     out = [lax.dot_general(w_ref[...], g[...], NT, preferred_element_type=F32) for g in grads]
     for i in range(2):
@@ -551,13 +563,14 @@
         send[i] = jnp.where(core == 0, out[2 * i + 1], out[2 * i]).astype(BF)
 
 
-def hidden_grads(me, w_out, grads, mine):
+def hidden_grads(me, w_out, grads, mine, after):
     rows, cols = grads[0].shape
     whole = lambda shape: block(shape, lambda r, me: (0,) * len(shape))
     spec = pltpu.PrefetchScalarGridSpec(
         num_scalar_prefetch=1,
         grid=(1,),
-        in_specs=[block((mine, cols), lambda r, me: (me[4], 0))] + [whole((rows, cols))] * 4,
+        in_specs=[block((mine, cols), lambda r, me: (me[4], 0))] + [whole((rows, cols))] * 4
+        + [pl.BlockSpec(memory_space=pl.ANY)],
         out_specs=[whole((2, mine, rows))] * 2,
     )
     return pl.pallas_call(
@@ -568,7 +581,7 @@
         cost_estimate=pl.CostEstimate(
             flops=8 * mine * cols * rows, bytes_accessed=2 * 5 * mine * cols, transcendentals=0
         ),
-    )(me, w_out, *grads)
+    )(me, w_out, *grads, after)
 
 
 def add_kernel(a, b, out):
@@ -589,8 +602,8 @@
     acc = None
     for mask, grad in enumerate(refs[:-1]):
         rows = grad.shape[0]
-        at = pl.multiple_of((me_ref[4] ^ mask) * rows, 128)
-        d = jnp.dot(hidden_ref[:, pl.ds(at, rows)], grad[...], preferred_element_type=F32)
+        at = slice(mask * rows, (mask + 1) * rows)
+        d = jnp.dot(hidden_ref[:, at], grad[...], preferred_element_type=F32)
         acc = d if acc is None else acc + d
     out_ref[...] = acc
 
@@ -616,13 +629,13 @@
     )(me, hidden, *grads)
 
 
-def last_kernel(me_ref, preact_ref, lhs_ref, p0, q0, p1, q1, out_ref):
+def last_kernel(me_ref, preact_ref, lhs_ref, p0, q0, p1, q1, after, out_ref):
     rows = p0.shape[2]
     acc = None
     for h, (p, q) in enumerate(((p0, q0), (p1, q1))):
         for i in range(2):
             mask = 4 * h + 2 * i + me_ref[0] % 2
-            at = pl.ds(pl.multiple_of((me_ref[4] ^ mask) * rows, 128), rows)
+            at = pl.ds(pl.multiple_of(mask * rows, 128), rows)
             grad = p[i].astype(F32) + q[i].astype(F32)
             grad = jnp.where(preact_ref[:, at] > 0, grad, 0.0).astype(BF)
             d = lax.dot_general(lhs_ref[:, at], grad, NT, preferred_element_type=F32)
@@ -630,7 +643,7 @@
     out_ref[...] = acc
 
 
-def last_grads(me, preact, lhs, parts):
+def last_grads(me, preact, lhs, parts, after):
     count, total = lhs.shape
     mine = preact.shape[0]
     args = (preact, lhs, *parts)
@@ -638,7 +651,7 @@
     spec = pltpu.PrefetchScalarGridSpec(
         num_scalar_prefetch=1,
         grid=(1,),
-        in_specs=[whole(x.shape) for x in args],
+        in_specs=[whole(x.shape) for x in args] + [pl.BlockSpec(memory_space=pl.ANY)],
         out_specs=whole((count, mine)),
     )
     return pl.pallas_call(
@@ -649,7 +662,7 @@
         cost_estimate=pl.CostEstimate(
             flops=total * count * mine, bytes_accessed=2 * 2**20, transcendentals=0
         ),
-    )(me, *args)
+    )(me, *args, after)
 
 
 def outputs_kernel(own, other, latent, embed):
@@ -697,22 +710,19 @@
     images = [own, far, swap(own, "feat", 1), swap(far, "feat", 1)]
 
     label_row = jnp.zeros((16, dz), BF).at[0, :].set(syn_labels.astype(BF))
-    packed, _ = tie(jnp.concatenate([latents, label_row], axis=0), own)
-    packed = lax.all_to_all(
-        jnp.broadcast_to(packed[None], (groups,) + packed.shape), "rec", 0, 0, tiled=True
-    )
-
-    images, packed = tie(images, packed)
+    packed = jnp.concatenate([latents, label_row], axis=0)[None]
+    packed = jnp.concatenate([packed, swap(packed, "rec", 1)], axis=0)
+    quad = jnp.concatenate([packed, swap(packed, "rec", 2)], axis=0)
     args = (me, real_labels, syn_labels, (0, 2, 1, 3), images, records, frequencies, classes)
     totals = (real_total, syn_total)
-    send_a, keep_a, send_b, keep_b, three = feature_sums(False, *args, totals)
+    send_a, keep_a, send_b, keep_b, three = feature_sums(False, *args, totals, packed)
+    eight = jnp.concatenate([quad, swap(quad, "rec", 4)], axis=0)
     first_a = swap(send_a, "rec", 1)
     first_b = swap(send_b, "rec", 2)
-    last_a, last_b, last = feature_sums(True, *args, totals)
-    last_a, (first_a, first_b) = tie(last_a, (first_a, first_b))
-
-    all_latents = packed[:, :rows].reshape(syn_total, dz)
-    all_labels = packed[:, rows].reshape(syn_total).astype(jnp.int32)
+    last_a, last_b, last = feature_sums(True, *args, totals, quad)
+
+    all_latents = eight[:, :rows].reshape(syn_total, dz)
+    all_labels = eight[:, rows].reshape(syn_total).astype(jnp.int32)
     all_table = one_hot(all_labels, classes, BF)
     mine = hid // groups
     lhs = jnp.concatenate([all_latents, all_table], axis=1).T
@@ -726,20 +736,20 @@
     all_preact = lax.dot_general(w, lhs, (((0,), (0,)), ((), ())), preferred_element_type=F32)
     all_hidden = jnp.maximum(all_preact, 0.0).astype(BF)
 
-    send_a, send_b = stage_two_send(keep_a, first_a, keep_b, first_b)
+    send_a, send_b = stage_two_send(keep_a, first_a, keep_b, first_b, last)
     got_a = swap(send_a, "rec", 2)
     got_b = swap(send_b, "rec", 1)
     part = frequencies.shape[1] // groups
     noise = lax.dynamic_slice_in_dim(class_noise, (2 * place + z_high) * part, part, 2)
     noise = noise.reshape(classes, 2 * part)
-    got_a, noise = tie(got_a, noise)
-    send, keep = stage_three(me, last_a, first_a, got_a, last_b, first_b, got_b)
+    send, keep = stage_three(me, last_a, first_a, got_a, last_b, first_b, got_b, (noise, eight))
     got = swap(send, "rec", 4)
-    feat_grad = gap_rows(keep, got, noise, all_labels, real_total)
-    feat_grad = lax.all_to_all(feat_grad.reshape(groups, rows, -1), "rec", 0, 0, tiled=True)
-    feat_grad, (all_preact, all_hidden, lhs) = tie(feat_grad, (all_preact, all_hidden, lhs))
-
-    send, keep = image_grads(me, three, last, feat_grad, frequencies, cols)
+    feat_grad = gap_rows(me, keep, got, noise, all_labels.reshape(groups, rows), real_total)
+    feat_grad = lax.all_to_all(feat_grad, "rec", 0, 0, tiled=True)
+
+    send, keep = image_grads(
+        me, three, last, feat_grad, frequencies, cols, (all_preact, all_hidden, lhs)
+    )
     send, keep = split_y(me, keep, swap(send, "feat", 1))
     out_grad = out_grads(keep, swap(send, "feat", 2), own)
 
@@ -756,15 +766,12 @@
         part = add(keep, swap(send, "feat", 1), BF)
         return [part, swap(part, "feat", 2)]
 
-    send, keep = hidden_grads(me, w_out, [by[i] for i in range(4)], mine)
-    by[6], send = tie(by[6], send)
     by[7] = swap(by[6], "rec", 1)
+    send, keep = hidden_grads(me, w_out, [by[i] for i in range(4)], mine, by[5])
     parts = reduced(send, keep)
-    by[7], parts = tie(by[7], parts)
-    parts += reduced(*hidden_grads(me, w_out, [by[4 + i] for i in range(4)], mine))
+    parts += reduced(*hidden_grads(me, w_out, [by[4 + i] for i in range(4)], mine, parts[0]))
     grad_w_out = weight_grads(me, all_hidden, [by[mask] for mask in range(groups)])
-    parts[3], grad_w_out = tie(parts[3], grad_w_out)
-    grads = last_grads(me, all_preact, lhs, parts)
+    grads = last_grads(me, all_preact, lhs, parts, grad_w_out)
     grad_w_latent, grad_embed = outputs(grads, swap(grads, "feat", 1), dz)
     return grad_w_out, grad_w_latent, grad_embed
 

time: 193 us -> 191 us (0.990)
  Pallas kernels: 63.4 us -> 66.8 us
  waiting for transfers between devices: 76.5 us -> 73.3 us
  local copies, waits for them, and re-layouts: 12.8 us -> 9.97 us
    all_to_all x2 -> x1, starting transfers between devices: 11.8 us -> 4.46 us  [eight_by_four(): feat_grad = lax.all_to_all(feat_grad, 'rec', 0, 0, tiled=True)]
    ppermute x22 -> x25, starting transfers between devices: 19.9 us -> 25.5 us  [swap(): return lax.ppermute(x, axis, [(i, i ^ bit) for i in range(n)])]
    all_to_all x2 -> x1, waiting for transfers between devices: 24 us -> 21.3 us  [eight_by_four(): feat_grad = lax.all_to_all(feat_grad, 'rec', 0, 0, tiled=True)]
    pallas_call x1, Pallas kernels: 9.89 us -> 12.1 us  [image_grads(): pl.pallas_call(image_kernel, grid_spec=spec, out_shape=[jax.ShapeDtypeStr...]
    unnamed x35 -> x40, local copies, waits for them, and re-layouts: 7.81 us -> 6.5 us
    ppermute x22 -> x25, waiting for transfers between devices: 52.5 us -> 51.9 us  [swap(): return lax.ppermute(x, axis, [(i, i ^ bit) for i in range(n)])]
  transfers between devices with their start and end apart: 24 -> 26, of which waited for: 16 -> 17; matrix products, arithmetic and copies ran while one was open for 3% -> 4% of each run, Pallas kernels for 9% -> 25%
where the time goes in v6:
time: 191 us; the launch traced here: 190 us
  waiting for transfers between devices  73.3 us (38%)
  Pallas kernels  66.8 us (35%)
  starting transfers between devices  29.9 us (16%)
  local copies, waits for them, and re-layouts  9.97 us (5%)
  matrix products  5.41 us (3%)
  other arithmetic  3.52 us (2%)
    ppermute x25, waiting for transfers between devices, swap(): return lax.ppermute(x, axis, [(i, i ^ bit) for i in range(n)])  51.9 us
    pallas_call x2, Pallas kernels, feature_sums(): pl.pallas_call(functools.partial(features_kernel, masks, last, *totals),...  42.9 us
    ppermute x25, starting transfers between devices, swap(): return lax.ppermute(x, axis, [(i, i ^ bit) for i in range(n)])  25.5 us
    all_to_all x1, waiting for transfers between devices, eight_by_four(): feat_grad = lax.all_to_all(feat_grad, 'rec', 0, 0, tiled=True)  21.3 us
    pallas_call x1, Pallas kernels, image_grads(): pl.pallas_call(image_kernel, grid_spec=spec, out_shape=[jax.ShapeDtypeStr...  12.1 us
    unnamed x40, local copies, waits for them, and re-layouts  6.5 us
    all_to_all x1, starting transfers between devices, eight_by_four(): feat_grad = lax.all_to_all(feat_grad, 'rec', 0, 0, tiled=True)  4.46 us
  transfers between devices with their start and end apart: 26, of which 17 were waited for; matrix products, arithmetic and copies ran while one was open for 4% of the time, Pallas kernels for 25%

profile of v6, /device:TPU:0, one launch (start us, length us, event | category | flops | bytes accessed | tf_op | source)
XLA Modules:
  0.0 190.0 jit_solution(2633281855962726050)
XLA Ops:
  0.7 1.2 copy-done
  1.9 1.0 fusion.12
  2.9 2.9 %fusion.4.refs_0_.image = bf16[128,768]{1,0:T(8,128)(2,1)S(1)} fusion(bf16[2048,768]{1,0:T(8,128)(2,1)} %w_ref.3, f32[128,2048]{1,0:T(8,128)S(1)} %fusion.12, bf16[128,128]{1,0:T(8,128)(2,1)} %param.15, bf16[128,2048]{1,0:T(8,128)(2,1)} %param.17), kind=kOutput, calls=%fused_computation.5 | convolution fusion | flops 470646784 | bytes 4947968 | tf_op jit(solution)/shard_map/dot_general | solution.py:708
  5.8 3.0 %collective-permute-start.3 = (bf16[128,768]{1,0:T(8,128)(2,1)S(1)}, bf16[128,768]{1,0:T(8,128)(2,1)S(1)}, u32[]{:S(2)}, u32[]{:S(2)}) collective-permute-start(bf16[128,768]{1,0:T(8,128)(2,1)S(1)} %fusion.4.refs_0_.image), channel_id=1, source_target_pairs={{0,2},{1,3},{2,0},{3,1},{4,6},{5,7},{6,4},{7,5},{8,10},{9,11},{10,... | collective-permute-start | bytes 589832 | tf_op jit(solution)/shard_map/ppermute | solution.py:102
  9.0 1.6 collective-permute-start
  10.5 3.2 %collective-permute-done.3.refs_1_ = bf16[128,768]{1,0:T(8,128)(2,1)S(1)} collective-permute-done((bf16[128,768]{1,0:T(8,128)(2,1)S(1)}, bf16[128,768]{1,0:T(8,128)(2,1)S(1)}, u32[]{:S(2)}, u32[]{:S(2)}) %collective-permute-start.3) | collective-permute-done | bytes 196640 | tf_op jit(solution)/shard_map/ppermute | solution.py:102
  13.9 1.9 collective-permute-start.1
  15.9 2.8 %collective-permute-done.1 = bf16[2,144,128]{2,0,1:T(2,128)(2,1)S(1)} collective-permute-done((bf16[2,144,128]{2,0,1:T(2,128)(2,1)S(1)}, bf16[2,144,128]{2,0,1:T(2,128)(2,1)S(1)}, u32[]{:S(2)}, u32[]{:S(2)}) %collective-permute-start.1) | collective-permute-done | bytes 73760 | tf_op jit(solution)/shard_map/ppermute | solution.py:102
  19.7 0.9 copy.22.refs_6_
  20.6 2.8 %collective-permute-start.2 = (bf16[4,144,128]{2,0,1:T(4,128)(2,1)}, bf16[4,144,128]{2,0,1:T(4,128)(2,1)}, u32[]{:S(2)}, u32[]{:S(2)}) collective-permute-start(bf16[4,144,128]{2,0,1:T(4,128)(2,1)} %pad_maximum_fusion.3), channel_id=1, source_target_pairs={{0,16},{4,20},{8,24},{12,28},{16,0},{20,4},{24,8},{28,12},{1,17},{... | collective-permute-start | bytes 442376 | tf_op jit(solution)/shard_map/ppermute | solution.py:102
  23.4 28.9 %shard_map.112 = (bf16[2,2,128,512]{3,2,1,0:T(8,128)(2,1)S(1)}, f32[2,128,512]{2,1,0:T(8,128)S(1)}, bf16[2,2,128,512]{3,2,1,0:T(8,128)(2,1)S(1)}, f32[2,128,512]{2,1,0:T(8,128)S(1)}, f32[3,2,128,512]{3,2,1,0:T(8,128)}) custom-call(s32[6]{0:T(128)S(1)} %stack.27.me_ref, s32[1,1536]{1,0:T(1,128)S(1)} %reshape.62.real_labels_ref, s32[1,128]{1,0:T(1,128)S(1)} %bitcast.31, ...), custom_call_target="tpu_custom_call" | custom-call | flops 18320719872 | bytes 18874368 | tf_op jit(solution)/shard_map/pallas_call | solution.py:372
  52.4 1.6 collective-permute-start.6
  53.9 1.6 collective-permute-start.7
  57.4 14.0 %shard_map.113 = (f32[2,128,512]{2,1,0:T(8,128)S(1)}, f32[2,128,512]{2,1,0:T(8,128)S(1)}, f32[1,2,128,512]{3,2,1,0:T(8,128)}) custom-call(s32[6]{0:T(128)S(1)} %stack.27.me_ref, s32[1,1536]{1,0:T(1,128)S(1)} %reshape.62.real_labels_ref, s32[1,128]{1,0:T(1,128)S(1)} %bitcast.32, bf16[128,768]{1,0:T(8,128)(2,1)S(1)} %fusion.4.refs_0_.image, ...), custom_call_target="tpu_custom_call" | custom-call | flops 6106906624 | bytes 12582912 | tf_op jit(solution)/shard_map/pallas_call | solution.py:372
  71.4 1.0 copy-done.6
  74.3 1.2 constant_dynamic-slice_fusion
  75.6 1.4 pad_maximum_fusion.2
  77.0 3.7 %collective-permute-done.8.ga = bf16[2,128,512]{2,1,0:T(8,128)(2,1)} collective-permute-done((bf16[2,128,512]{2,1,0:T(8,128)(2,1)}, bf16[2,128,512]{2,1,0:T(8,128)(2,1)}, u32[]{:S(2)}, u32[]{:S(2)}) %collective-permute-start.8) | collective-permute-done | bytes 262176 | tf_op jit(solution)/shard_map/ppermute | solution.py:102
  80.9 1.7 shard_map.115
  83.0 12.2 %collective-permute-done.10.got_ref = bf16[256,512]{1,0:T(8,128)(2,1)S(1)} collective-permute-done((bf16[256,512]{1,0:T(8,128)(2,1)S(1)}, bf16[256,512]{1,0:T(8,128)(2,1)S(1)}, u32[]{:S(2)}, u32[]{:S(2)}) %collective-permute-start.10) | collective-permute-done | bytes 262176 | tf_op jit(solution)/shard_map/ppermute | solution.py:102
  95.2 2.0 %shard_map.116 = bf16[8,128,512]{2,1,0:T(8,128)(2,1)} custom-call(s32[6]{0:T(128)S(1)} %stack.27.me_ref, f32[256,512]{1,0:T(8,128)S(1)} %get-tuple-element.50.keep_ref, bf16[256,512]{1,0:T(8,128)(2,1)S(1)} %collective-permute-done.10.got_ref, f32[256,512]{1,0:T(8,128)S(1)} %bitcast.30, s32[8,128]{1,0:T(8,128)S(1)} %get-tuple-element.65.labels_ref), custom_call_target="tpu_custom_call" | custom-call | flops 268435456 | bytes 3145728 | tf_op jit(solution)/shard_map/pallas_call | solution.py:450
  97.3 4.5 %all-to-all-start = ((bf16[8,128,512]{2,1,0:T(8,128)(2,1)}), bf16[8,128,512]{2,1,0:T(8,128)(2,1)}, u32[]{:S(2)}, u32[]{:S(2)}) async-start(bf16[8,128,512]{2,1,0:T(8,128)(2,1)} %shard_map.116), calls=%async_computation | async-start | bytes 2097152 | tf_op jit(solution)/shard_map/all_to_all | solution.py:748
  103.0 0.9 fusion.7.c.lhs_ref
  104.0 1.5 maximum_convert_fusion
  105.4 21.3 %all-to-all-done.rows_ref = bf16[8,128,512]{2,1,0:T(8,128)(2,1)} async-done(((bf16[8,128,512]{2,1,0:T(8,128)(2,1)}), bf16[8,128,512]{2,1,0:T(8,128)(2,1)}, u32[]{:S(2)}, u32[]{:S(2)}) %all-to-all-start) | async-done | bytes 1048608 | tf_op jit(solution)/shard_map/all_to_all | solution.py:748
  126.8 12.1 %shard_map.117 = (bf16[2,768,128]{2,1,0:T(8,128)(2,1)S(1)}, f32[2,768,128]{2,1,0:T(8,128)}) custom-call(s32[6]{0:T(128)S(1)} %stack.27.me_ref, f32[3,2,128,512]{3,2,1,0:T(8,128)} %get-tuple-element.40.three_ref, f32[1,2,128,512]{3,2,1,0:T(8,128)S(1)} %copy-done.7, bf16[8,128,512]{2,1,0:T(8,128)(2,1)} %all-to-all-done.rows_ref, bf16[3072,2048]{1,0:T(8,128)(2,1)} %freq_hbm.1, ...), custom_call_target="tpu_custom_call" | custom-call | flops 1610612736 | bytes 12582912 | tf_op jit(solution)/shard_map/pallas_call | solution.py:511
  139.0 1.7 collective-permute-done.11.got_s.got_k
  140.7 1.1 copy-done.4
  142.5 1.6 collective-permute-start.12
  144.1 5.4 %collective-permute-done.12.got = bf16[768,128]{1,0:T(8,128)(2,1)S(1)} collective-permute-done((bf16[768,128]{1,0:T(8,128)(2,1)S(1)}, bf16[768,128]{1,0:T(8,128)(2,1)S(1)}, u32[]{:S(2)}, u32[]{:S(2)}) %collective-permute-start.12) | collective-permute-done | bytes 196640 | tf_op jit(solution)/shard_map/ppermute | solution.py:102
  149.7 1.9 %collective-permute-start.14 = (bf16[128,768]{1,0:T(8,128)(2,1)S(1)}, bf16[128,768]{1,0:T(8,128)(2,1)S(1)}, u32[]{:S(2)}, u32[]{:S(2)}) collective-permute-start(bf16[128,768]{1,0:T(8,128)(2,1)S(1)} %shard_map.119.refs_0_), channel_id=1, source_target_pairs={{0,8},{4,12},{8,0},{12,4},{16,24},{20,28},{24,16},{28,20},{1,9},{5... | collective-permute-start | bytes 589832 | tf_op jit(solution)/shard_map/ppermute | solution.py:102
  151.7 1.5 collective-permute-start.15
  153.2 7.0 %collective-permute-done.13.refs_4_.refs_0_ = bf16[128,768]{1,0:T(8,128)(2,1)S(1)} collective-permute-done((bf16[128,768]{1,0:T(8,128)(2,1)S(1)}, bf16[128,768]{1,0:T(8,128)(2,1)S(1)}, u32[]{:S(2)}, u32[]{:S(2)}) %collective-permute-start.13) | collective-permute-done | bytes 196640 | tf_op jit(solution)/shard_map/ppermute | solution.py:102
  160.4 1.4 collective-permute-start.16
  162.4 4.5 %collective-permute-done.18.refs_6_.refs_2_ = bf16[128,768]{1,0:T(8,128)(2,1)S(1)} collective-permute-done((bf16[128,768]{1,0:T(8,128)(2,1)S(1)}, bf16[128,768]{1,0:T(8,128)(2,1)S(1)}, u32[]{:S(2)}, u32[]{:S(2)}) %collective-permute-start.18) | collective-permute-done | bytes 196640 | tf_op jit(solution)/shard_map/ppermute | solution.py:102
  166.9 1.1 collective-permute-start.19
  168.2 4.2 %collective-permute-done.17.refs_5_.refs_4_.refs_1_ = bf16[128,768]{1,0:T(8,128)(2,1)S(1)} collective-permute-done((bf16[128,768]{1,0:T(8,128)(2,1)S(1)}, bf16[128,768]{1,0:T(8,128)(2,1)S(1)}, u32[]{:S(2)}, u32[]{:S(2)}) %collective-permute-start.17) | collective-permute-done | bytes 196640 | tf_op jit(solution)/shard_map/ppermute | solution.py:102
  172.4 1.1 shard_map.121
  173.6 1.3 collective-permute-done.20.b
  175.4 1.1 shard_map.123
  176.6 1.6 collective-permute-start.21
  178.2 1.3 collective-permute-start.23
  179.6 2.4 %shard_map.120.after = f32[256,768]{1,0:T(8,128)} custom-call(s32[6]{0:T(128)S(1)} %stack.27.me_ref, bf16[256,1024]{1,0:T(8,128)(2,1)S(1)} %get-tuple-element.67.b.hidden_ref, bf16[128,768]{1,0:T(8,128)(2,1)S(1)} %shard_map.119.refs_0_, bf16[128,768]{1,0:T(8,128)(2,1)S(1)} %collective-permute-done.15.refs_1_, ...), custom_call_target="tpu_custom_call" | custom-call | flops 402653184 | bytes 4194304 | tf_op jit(solution)/shard_map/pallas_call | solution.py:621
  181.9 1.0 collective-permute-done.21.q0
  183.0 2.4 %collective-permute-done.23.q1 = bf16[2,256,128]{2,1,0:T(8,128)(2,1)S(1)} collective-permute-done((bf16[2,256,128]{2,1,0:T(8,128)(2,1)S(1)}, bf16[2,256,128]{2,1,0:T(8,128)(2,1)S(1)}, u32[]{:S(2)}, u32[]{:S(2)}) %collective-permute-start.23) | collective-permute-done | bytes 131104 | tf_op jit(solution)/shard_map/ppermute | solution.py:102
  185.3 1.1 copy-done.5
  186.5 0.9 shard_map.125.own
  187.5 1.7 collective-permute-done.24.other
  (82 shorter events, 10.4 us)
Async XLA Ops:
  0.6 1.2 copy-start
  0.6 8.2 %copy-start.12 = (s32[128]{0:T(128)S(1)}, s32[128]{0:T(128)}, u32[]{:S(2)}) copy-start(s32[128]{0:T(128)} %param.16) | copy-start | bytes 1540
  0.7 8.2 %copy-start.17 = (bf16[128,128]{1,0:T(8,128)(2,1)S(1)}, bf16[128,128]{1,0:T(8,128)(2,1)}, u32[]{:S(2)}) copy-start(bf16[128,128]{1,0:T(8,128)(2,1)} %param.15) | copy-start | bytes 98308
  2.9 12.9 %copy-start.18 = (s32[1536]{0:T(1024)S(1)}, s32[1536]{0:T(1024)}, u32[]{:S(2)}) copy-start(s32[1536]{0:T(1024)} %param.12) | copy-start | bytes 18436
  5.8 7.9 %collective-permute-start.3 = (bf16[128,768]{1,0:T(8,128)(2,1)S(1)}, bf16[128,768]{1,0:T(8,128)(2,1)S(1)}, u32[]{:S(2)}, u32[]{:S(2)}) collective-permute-start(bf16[128,768]{1,0:T(8,128)(2,1)S(1)} %fusion.4.refs_0_.image), channel_id=1, source_target_pairs={{0,2},{1,3},{2,0},{3,1},{4,6},{5,7},{6,4},{7,5},{8,10},{9,11},{10,... | collective-permute-start | bytes 589832 | tf_op jit(solution)/shard_map/ppermute | solution.py:102
  9.0 43.4 %copy-start.14 = (bf16[1,144,128]{2,0,1:T(2,128)(2,1)}, bf16[1,144,128]{2,0,1:T(2,128)(2,1)S(1)}, u32[]{:S(2)}) copy-start(bf16[1,144,128]{2,0,1:T(2,128)(2,1)S(1)} %copy.19) | copy-start | bytes 110596
  9.0 4.8 %collective-permute-start = (bf16[1,144,128]{2,0,1:T(2,128)(2,1)S(1)}, bf16[1,144,128]{2,0,1:T(2,128)(2,1)S(1)}, u32[]{:S(2)}, u32[]{:S(2)}) collective-permute-start(bf16[1,144,128]{2,0,1:T(2,128)(2,1)S(1)} %copy.19), channel_id=1, source_target_pairs={{0,4},{4,0},{8,12},{12,8},{16,20},{20,16},{24,28},{28,24},{1,5},{5... | collective-permute-start | bytes 110600 | tf_op jit(solution)/shard_map/ppermute | solution.py:102
  10.5 12.9 %collective-permute-start.4 = (bf16[128,768]{1,0:T(8,128)(2,1)S(1)}, bf16[128,768]{1,0:T(8,128)(2,1)S(1)}, u32[]{:S(2)}, u32[]{:S(2)}) collective-permute-start(bf16[128,768]{1,0:T(8,128)(2,1)S(1)} %fusion.4.refs_0_.image), channel_id=1, source_target_pairs={{0,1},{1,0},{2,3},{3,2},{4,5},{5,4},{6,7},{7,6},{8,9},{9,8},{10,11... | collective-permute-start | bytes 589832 | tf_op jit(solution)/shard_map/ppermute | solution.py:102
  13.8 9.7 %collective-permute-start.5 = (bf16[128,768]{1,0:T(8,128)(2,1)S(1)}, bf16[128,768]{1,0:T(8,128)(2,1)S(1)}, u32[]{:S(2)}, u32[]{:S(2)}) collective-permute-start(bf16[128,768]{1,0:T(8,128)(2,1)S(1)} %collective-permute-done.3.refs_1_), channel_id=1, source_target_pairs={{0,1},{1,0},{2,3},{3,2},{4,5},{5,4},{6,7},{7,6},{8,9},{9,8},{10,11... | collective-permute-start | bytes 589832 | tf_op jit(solution)/shard_map/ppermute | solution.py:102
  13.8 38.6 %copy-start.15 = (bf16[1,144,128]{2,0,1:T(2,128)(2,1)}, bf16[1,144,128]{2,0,1:T(2,128)(2,1)S(1)}, u32[]{:S(2)}) copy-start(bf16[1,144,128]{2,0,1:T(2,128)(2,1)S(1)} %collective-permute-done) | copy-start | bytes 110596
  13.9 4.8 %collective-permute-start.1 = (bf16[2,144,128]{2,0,1:T(2,128)(2,1)S(1)}, bf16[2,144,128]{2,0,1:T(2,128)(2,1)S(1)}, u32[]{:S(2)}, u32[]{:S(2)}) collective-permute-start(bf16[2,144,128]{2,0,1:T(2,128)(2,1)S(1)} %pad_maximum_fusion.4), channel_id=1, source_target_pairs={{0,8},{4,12},{8,0},{12,4},{16,24},{20,28},{24,16},{28,20},{1,9},{5... | collective-permute-start | bytes 221192 | tf_op jit(solution)/shard_map/ppermute | solution.py:102
  18.7 33.6 %copy-start.16 = (bf16[2,144,128]{2,0,1:T(2,128)(2,1)}, bf16[2,144,128]{2,0,1:T(2,128)(2,1)S(1)}, u32[]{:S(2)}) copy-start(bf16[2,144,128]{2,0,1:T(2,128)(2,1)S(1)} %collective-permute-done.1) | copy-start | bytes 221188
  20.6 55.0 %collective-permute-start.2 = (bf16[4,144,128]{2,0,1:T(4,128)(2,1)}, bf16[4,144,128]{2,0,1:T(4,128)(2,1)}, u32[]{:S(2)}, u32[]{:S(2)}) collective-permute-start(bf16[4,144,128]{2,0,1:T(4,128)(2,1)} %pad_maximum_fusion.3), channel_id=1, source_target_pairs={{0,16},{4,20},{8,24},{12,28},{16,0},{20,4},{24,8},{28,12},{1,17},{... | collective-permute-start | bytes 442376 | tf_op jit(solution)/shard_map/ppermute | solution.py:102
  23.4 28.9 %copy-start.8 = (bf16[128,768]{1,0:T(8,128)(2,1)}, bf16[128,768]{1,0:T(8,128)(2,1)S(1)}, u32[]{:S(2)}) copy-start(bf16[128,768]{1,0:T(8,128)(2,1)S(1)} %collective-permute-done.4.refs_2_) | copy-start | bytes 589828
  23.4 28.9 %copy-start.10 = (bf16[128,768]{1,0:T(8,128)(2,1)}, bf16[128,768]{1,0:T(8,128)(2,1)S(1)}, u32[]{:S(2)}) copy-start(bf16[128,768]{1,0:T(8,128)(2,1)S(1)} %collective-permute-done.5.refs_3_) | copy-start | bytes 589828
  52.4 19.0 %collective-permute-start.6 = (bf16[2,2,128,512]{3,2,1,0:T(8,128)(2,1)S(1)}, bf16[2,2,128,512]{3,2,1,0:T(8,128)(2,1)S(1)}, u32[]{:S(2)}, u32[]{:S(2)}) collective-permute-start(bf16[2,2,128,512]{3,2,1,0:T(8,128)(2,1)S(1)} %get-tuple-element.43), channel_id=1, source_target_pairs={{0,4},{4,0},{8,12},{12,8},{16,20},{20,16},{24,28},{28,24},{1,5},{5... | collective-permute-start | bytes 1572872 | tf_op jit(solution)/shard_map/ppermute | solution.py:102
  53.9 17.5 %collective-permute-start.7 = (bf16[2,2,128,512]{3,2,1,0:T(8,128)(2,1)S(1)}, bf16[2,2,128,512]{3,2,1,0:T(8,128)(2,1)S(1)}, u32[]{:S(2)}, u32[]{:S(2)}) collective-permute-start(bf16[2,2,128,512]{3,2,1,0:T(8,128)(2,1)S(1)} %get-tuple-element.46), channel_id=1, source_target_pairs={{0,8},{4,12},{8,0},{12,4},{16,24},{20,28},{24,16},{28,20},{1,9},{5... | collective-permute-start | bytes 1572872 | tf_op jit(solution)/shard_map/ppermute | solution.py:102
  55.5 0.9 copy-start.9
  56.4 0.9 copy-start.11
  71.4 1.0 copy-start.6
  73.3 7.4 %collective-permute-start.8 = (bf16[2,128,512]{2,1,0:T(8,128)(2,1)}, bf16[2,128,512]{2,1,0:T(8,128)(2,1)}, u32[]{:S(2)}, u32[]{:S(2)}) collective-permute-start(bf16[2,128,512]{2,1,0:T(8,128)(2,1)} %get-tuple-element.47), channel_id=1, source_target_pairs={{0,8},{4,12},{8,0},{12,4},{16,24},{20,28},{24,16},{28,20},{1,9},{5... | collective-permute-start | bytes 786440 | tf_op jit(solution)/shard_map/ppermute | solution.py:102
  73.8 7.1 %collective-permute-start.9 = (bf16[2,128,512]{2,1,0:T(8,128)(2,1)}, bf16[2,128,512]{2,1,0:T(8,128)(2,1)}, u32[]{:S(2)}, u32[]{:S(2)}) collective-permute-start(bf16[2,128,512]{2,1,0:T(8,128)(2,1)} %get-tuple-element.49), channel_id=1, source_target_pairs={{0,4},{4,0},{8,12},{12,8},{16,20},{20,16},{24,28},{28,24},{1,5},{5... | collective-permute-start | bytes 786440 | tf_op jit(solution)/shard_map/ppermute | solution.py:102
  77.0 18.2 %copy-start.13 = (bf16[8,144,128]{2,0,1:T(8,128)(2,1)}, bf16[8,144,128]{2,0,1:T(8,128)(2,1)S(1)}, u32[]{:S(2)}) copy-start(bf16[8,144,128]{2,0,1:T(8,128)(2,1)S(1)} %pad_maximum_fusion.2) | copy-start | bytes 884740
  82.6 12.6 %collective-permute-start.10 = (bf16[256,512]{1,0:T(8,128)(2,1)S(1)}, bf16[256,512]{1,0:T(8,128)(2,1)S(1)}, u32[]{:S(2)}, u32[]{:S(2)}) collective-permute-start(bf16[256,512]{1,0:T(8,128)(2,1)S(1)} %get-tuple-element.51), channel_id=1, source_target_pairs={{0,16},{4,20},{8,24},{12,28},{16,0},{20,4},{24,8},{28,12},{1,17},{... | collective-permute-start | bytes 786440 | tf_op jit(solution)/shard_map/ppermute | solution.py:102
  95.2 7.4 %slice-start = ((bf16[8,144,128]{2,0,1:T(8,128)(2,1)}), bf16[8,128,128]{2,0,1:T(8,128)(2,1)S(1)}, s32[]{:S(2)}) async-start(bf16[8,144,128]{2,0,1:T(8,128)(2,1)} %copy-done.13), calls=%async_computation.1 | async-start | bytes 524288 | tf_op jit(solution)/shard_map/slice | solution.py:724
  97.3 29.5 %all-to-all-start = ((bf16[8,128,512]{2,1,0:T(8,128)(2,1)}), bf16[8,128,512]{2,1,0:T(8,128)(2,1)}, u32[]{:S(2)}, u32[]{:S(2)}) async-start(bf16[8,128,512]{2,1,0:T(8,128)(2,1)} %shard_map.116), calls=%async_computation | async-start | bytes 2097152 | tf_op jit(solution)/shard_map/all_to_all | solution.py:748
  102.6 24.2 %copy-start.7 = (f32[1,2,128,512]{3,2,1,0:T(8,128)S(1)}, f32[1,2,128,512]{3,2,1,0:T(8,128)}, u32[]{:S(2)}) copy-start(f32[1,2,128,512]{3,2,1,0:T(8,128)} %get-tuple-element.41.after.last_ref) | copy-start | bytes 1572868
  138.9 33.5 %copy-start.1 = (bf16[2048,768]{1,0:T(8,128)(2,1)S(1)}, bf16[2048,768]{1,0:T(8,128)(2,1)}, u32[]{:S(2)}) copy-start(bf16[2048,768]{1,0:T(8,128)(2,1)} %w_ref.3) | copy-start | bytes 9437188
  138.9 1.8 collective-permute-start.11
  140.7 1.1 copy-start.4
  142.5 7.0 %collective-permute-start.12 = (bf16[768,128]{1,0:T(8,128)(2,1)S(1)}, bf16[768,128]{1,0:T(8,128)(2,1)S(1)}, u32[]{:S(2)}, u32[]{:S(2)}) collective-permute-start(bf16[768,128]{1,0:T(8,128)(2,1)S(1)} %get-tuple-element.55), channel_id=1, source_target_pairs={{0,2},{1,3},{2,0},{3,1},{4,6},{5,7},{6,4},{7,5},{8,10},{9,11},{10,... | collective-permute-start | bytes 589832 | tf_op jit(solution)/shard_map/ppermute | solution.py:102
  149.7 10.5 %collective-permute-start.13 = (bf16[128,768]{1,0:T(8,128)(2,1)S(1)}, bf16[128,768]{1,0:T(8,128)(2,1)S(1)}, u32[]{:S(2)}, u32[]{:S(2)}) collective-permute-start(bf16[128,768]{1,0:T(8,128)(2,1)S(1)} %shard_map.119.refs_0_), channel_id=1, source_target_pairs={{0,16},{4,20},{8,24},{12,28},{16,0},{20,4},{24,8},{28,12},{1,17},{... | collective-permute-start | bytes 589832 | tf_op jit(solution)/shard_map/ppermute | solution.py:102
  149.7 10.4 %collective-permute-start.14 = (bf16[128,768]{1,0:T(8,128)(2,1)S(1)}, bf16[128,768]{1,0:T(8,128)(2,1)S(1)}, u32[]{:S(2)}, u32[]{:S(2)}) collective-permute-start(bf16[128,768]{1,0:T(8,128)(2,1)S(1)} %shard_map.119.refs_0_), channel_id=1, source_target_pairs={{0,8},{4,12},{8,0},{12,4},{16,24},{20,28},{24,16},{28,20},{1,9},{5... | collective-permute-start | bytes 589832 | tf_op jit(solution)/shard_map/ppermute | solution.py:102
  151.7 8.5 %collective-permute-start.15 = (bf16[128,768]{1,0:T(8,128)(2,1)S(1)}, bf16[128,768]{1,0:T(8,128)(2,1)S(1)}, u32[]{:S(2)}, u32[]{:S(2)}) collective-permute-start(bf16[128,768]{1,0:T(8,128)(2,1)S(1)} %shard_map.119.refs_0_), channel_id=1, source_target_pairs={{0,4},{4,0},{8,12},{12,8},{16,20},{20,16},{24,28},{28,24},{1,5},{5... | collective-permute-start | bytes 589832 | tf_op jit(solution)/shard_map/ppermute | solution.py:102
  160.1 6.8 %collective-permute-start.18 = (bf16[128,768]{1,0:T(8,128)(2,1)S(1)}, bf16[128,768]{1,0:T(8,128)(2,1)S(1)}, u32[]{:S(2)}, u32[]{:S(2)}) collective-permute-start(bf16[128,768]{1,0:T(8,128)(2,1)S(1)} %collective-permute-done.13.refs_4_.refs_0_), channel_id=1, source_target_pairs={{0,8},{4,12},{8,0},{12,4},{16,24},{20,28},{24,16},{28,20},{1,9},{5... | collective-permute-start | bytes 589832 | tf_op jit(solution)/shard_map/ppermute | solution.py:102
  160.4 7.8 %collective-permute-start.16 = (bf16[128,768]{1,0:T(8,128)(2,1)S(1)}, bf16[128,768]{1,0:T(8,128)(2,1)S(1)}, u32[]{:S(2)}, u32[]{:S(2)}) collective-permute-start(bf16[128,768]{1,0:T(8,128)(2,1)S(1)} %collective-permute-done.14.refs_2_), channel_id=1, source_target_pairs={{0,4},{4,0},{8,12},{12,8},{16,20},{20,16},{24,28},{28,24},{1,5},{5... | collective-permute-start | bytes 589832 | tf_op jit(solution)/shard_map/ppermute | solution.py:102
  161.8 10.6 %collective-permute-start.17 = (bf16[128,768]{1,0:T(8,128)(2,1)S(1)}, bf16[128,768]{1,0:T(8,128)(2,1)S(1)}, u32[]{:S(2)}, u32[]{:S(2)}) collective-permute-start(bf16[128,768]{1,0:T(8,128)(2,1)S(1)} %collective-permute-done.13.refs_4_.refs_0_), channel_id=1, source_target_pairs={{0,4},{4,0},{8,12},{12,8},{16,20},{20,16},{24,28},{28,24},{1,5},{5... | collective-permute-start | bytes 589832 | tf_op jit(solution)/shard_map/ppermute | solution.py:102
  166.9 8.5 %collective-permute-start.19 = (bf16[128,768]{1,0:T(8,128)(2,1)S(1)}, bf16[128,768]{1,0:T(8,128)(2,1)S(1)}, u32[]{:S(2)}, u32[]{:S(2)}) collective-permute-start(bf16[128,768]{1,0:T(8,128)(2,1)S(1)} %collective-permute-done.18.refs_6_.refs_2_), channel_id=1, source_target_pairs={{0,4},{4,0},{8,12},{12,8},{16,20},{20,16},{24,28},{28,24},{1,5},{5... | collective-permute-start | bytes 589832 | tf_op jit(solution)/shard_map/ppermute | solution.py:102
  173.5 1.4 collective-permute-start.20
  175.0 10.4 %copy-start.2 = (f32[256,1024]{1,0:T(8,128)S(1)}, f32[256,1024]{1,0:T(8,128)}, u32[]{:S(2)}) copy-start(f32[256,1024]{1,0:T(8,128)} %get-tuple-element.68.a.preact_ref) | copy-start | bytes 3145732
  175.0 10.4 %copy-start.3 = (bf16[384,1024]{1,0:T(8,128)(2,1)S(1)}, bf16[384,1024]{1,0:T(8,128)(2,1)}, u32[]{:S(2)}) copy-start(bf16[384,1024]{1,0:T(8,128)(2,1)} %fusion.7.c.lhs_ref) | copy-start | bytes 2359300
  176.5 1.7 collective-permute-start.22
  176.6 6.4 %collective-permute-start.21 = (bf16[2,256,128]{2,1,0:T(8,128)(2,1)S(1)}, bf16[2,256,128]{2,1,0:T(8,128)(2,1)S(1)}, u32[]{:S(2)}, u32[]{:S(2)}) collective-permute-start(bf16[2,256,128]{2,1,0:T(8,128)(2,1)S(1)} %shard_map.122.refs_4_.p0), channel_id=1, source_target_pairs={{0,2},{1,3},{2,0},{3,1},{4,6},{5,7},{6,4},{7,5},{8,10},{9,11},{10,... | collective-permute-start | bytes 393224 | tf_op jit(solution)/shard_map/ppermute | solution.py:102
  178.2 7.1 %collective-permute-start.23 = (bf16[2,256,128]{2,1,0:T(8,128)(2,1)S(1)}, bf16[2,256,128]{2,1,0:T(8,128)(2,1)S(1)}, u32[]{:S(2)}, u32[]{:S(2)}) collective-permute-start(bf16[2,256,128]{2,1,0:T(8,128)(2,1)S(1)} %shard_map.124.p1), channel_id=1, source_target_pairs={{0,2},{1,3},{2,0},{3,1},{4,6},{5,7},{6,4},{7,5},{8,10},{9,11},{10,... | collective-permute-start | bytes 393224 | tf_op jit(solution)/shard_map/ppermute | solution.py:102
  185.3 1.1 copy-start.5
  187.4 1.8 collective-permute-start.24

commit v7 on v6

--- a/solution.py
+++ b/solution.py
@@ -239,10 +239,11 @@
 def features_kernel(
     masks, last, real_total, syn_total, me_ref, real_labels_ref, syn_labels_ref, *refs
 ):
-    count = len(masks)
-    images = refs[:count]
+    count = 1 if last else len(masks)
+    images = [refs[0].at[i] for i in range(len(masks))] if last else refs[:count]
     records_hbm, freq_ref = refs[count : count + 2]
-    outs = refs[count + 3 : -4]
+    outs = refs[count + (4 if last else 3) : -4]
+    wave, token = outs[-2:]
     records, real_table, syn_table, sem = refs[-4:]
     classes, total = real_table.shape
     size = 512
@@ -250,6 +251,7 @@
     step = pl.program_id(0)
     cols = images[0].shape[1]
     half = classes // 2
+    token[...] = jnp.zeros_like(token)
 
     def copy(i):
         at = pl.ds(i * size, size)
@@ -263,6 +265,11 @@
             real_table[...] = jnp.where(ids == real_labels_ref[...], 1.0, 0.0).astype(BF)
             ids = lax.broadcasted_iota(jnp.int32, syn_table.shape, 0)
             syn_table[...] = jnp.where(ids == syn_labels_ref[...], 1.0, 0.0).astype(BF)
+        syn_pre = None
+        for mask, image in zip(masks, images):
+            at = pl.multiple_of((me_ref[0] ^ mask) * cols, 128)
+            d = jnp.dot(image[...], freq_ref[pl.ds(at, cols), :], preferred_element_type=F32)
+            syn_pre = d if syn_pre is None else syn_pre + d
         freq = freq_ref[...]
         acc = None
         before = None
@@ -271,21 +278,16 @@
                 if wait:
                     copy(i).wait()
                 pre = jnp.dot(records[i * size : (i + 1) * size, :], freq, preferred_element_type=F32)
+            if i == 0:
+                co, si = cos_sin(syn_pre)
+                wave[0, 0] = co
+                wave[0, 1] = si
+                phi = jnp.concatenate([co.astype(BF), si.astype(BF)], axis=1)
+                syn = jnp.dot(syn_table[...], phi, preferred_element_type=F32)
             else:
-                syn_pre = None
-                for mask, image in zip(masks, images):
-                    at = pl.multiple_of((me_ref[0] ^ mask) * cols, 128)
-                    d = jnp.dot(image[...], freq_ref[pl.ds(at, cols), :], preferred_element_type=F32)
-                    syn_pre = d if syn_pre is None else syn_pre + d
-            if i > 0:
                 d = sums(real_table[:, (i - 1) * size : i * size], before)
                 acc = d if acc is None else acc + d
             before = pre
-        co, si = cos_sin(syn_pre)
-        outs[-1][0, 0] = co
-        outs[-1][0, 1] = si
-        phi = jnp.concatenate([co.astype(BF), si.astype(BF)], axis=1)
-        syn = jnp.dot(syn_table[...], phi, preferred_element_type=F32)
         gap = syn * (1.0 / syn_total) - acc * (1.0 / real_total)
         width = gap.shape[1] // 4
         return [
@@ -301,10 +303,12 @@
             outs[0][h] = parts[h][:half]
             outs[1][h] = parts[h][half:]
         return
-    send_a, keep_a, send_b, keep_b = outs[:4]
+    send_a, keep_a, send_b, keep_b, both = outs[:5]
 
     @pl.when(step == 0)
     def _():
+        for i in range(count):
+            both[i] = images[i][...]
         parts = work(True)
         for h in range(2):
             send_a[0, h] = parts[h][:half].astype(BF)
@@ -327,40 +331,45 @@
                 send_b[0, h] = parts[h][half:].astype(BF)
 
 
-def feature_sums(last, me, real_labels, syn_labels, masks, images, records, freq, classes, totals, after):
+def feature_sums(
+    last, me, real_labels, syn_labels, masks, images, records, freq, classes, totals, after, waves=None
+):
     total, k = records.shape
     n = freq.shape[1]
-    rows, cols = images[0].shape
+    rows, cols = images.shape[1:] if last else images[0].shape
     half = classes // 2
     tile = n // 4
     tiles = 1 if last else 3
     whole = lambda shape: block(shape, lambda j, me: (0,) * len(shape))
     kept = jax.ShapeDtypeStruct((2, half, tile), F32)
     sent = jax.ShapeDtypeStruct((2, 2, half, tile), BF)
-    wave = pltpu.HBM((tiles, 2, rows, tile), F32)
-    wave_spec = block((1, 2, rows, tile), lambda j, me: (j, 0, 0, 0))
+    both = (len(masks), rows, cols)
+    place = lambda j, me: me[5] ^ (0 if last else 3 - j)
+    anywhere = pl.BlockSpec(memory_space=pl.ANY)
+    shapes = [pltpu.HBM((4, 2, rows, tile), F32), jax.ShapeDtypeStruct((8, 128), F32)]
+    specs = [block((1, 2, rows, tile), lambda j, me: (place(j, me), 0, 0, 0)), whole((8, 128))]
     if last:
-        shapes = [kept, kept, wave]
-        specs = [whole(kept.shape), whole(kept.shape), wave_spec]
+        shapes = [kept, kept] + shapes
+        specs = [whole(kept.shape), whole(kept.shape)] + specs
+        images = (images,)
+        extra = (after, waves)
     else:
-        shapes = [sent, kept, sent, kept, wave]
+        shapes = [sent, kept, sent, kept, pltpu.HBM(both, BF)] + shapes
         specs = [
             block((1, 2, half, tile), lambda j, me: (jnp.minimum(j, 1), 0, 0, 0)),
             whole(kept.shape),
             block((1, 2, half, tile), lambda j, me: (j // 2, 0, 0, 0)),
             whole(kept.shape),
-            wave_spec,
-        ]
+            whole(both),
+        ] + specs
+        extra = (after,)
     grid_spec = pltpu.PrefetchScalarGridSpec(
         num_scalar_prefetch=1,
         grid=(tiles,),
         in_specs=[whole((1, total)), whole((1, rows))]
-        + [whole((rows, cols)) for _ in images]
-        + [
-            pl.BlockSpec(memory_space=pl.ANY),
-            block((k, tile), lambda j, me: (0, me[5] ^ (0 if last else 3 - j))),
-            pl.BlockSpec(memory_space=pl.ANY),
-        ],
+        + [whole(image.shape) for image in images]
+        + [anywhere, block((k, tile), lambda j, me: (0, place(j, me)))]
+        + [anywhere] * len(extra),
         out_specs=specs,
         scratch_shapes=[
             pltpu.VMEM((total, k), BF),
@@ -373,13 +382,14 @@
         functools.partial(features_kernel, masks, last, *totals),
         grid_spec=grid_spec,
         out_shape=shapes,
+        input_output_aliases={7: 2} if last else {},
         compiler_params=pltpu.CompilerParams(vmem_limit_bytes=44 * 2**20),
         cost_estimate=pl.CostEstimate(
             flops=2 * (total + rows) * tiles * tile * (k + 2 * classes),
             bytes_accessed=2 * (total * k + k * tiles * tile),
             transcendentals=0,
         ),
-    )(me, real_labels.reshape(1, -1), syn_labels.reshape(1, -1), *images, records, freq, after)
+    )(me, real_labels.reshape(1, -1), syn_labels.reshape(1, -1), *images, records, freq, *extra)
 
 
 def stage_two_send_kernel(ka, ga, kb, gb, after, sa, sb):
@@ -397,7 +407,7 @@
     )(keep_a, got_a, keep_b, got_b, after)
 
 
-def stage_three_kernel(me_ref, na, fa, ga, nb, fb, gb, after, behind, send, keep):
+def stage_three_kernel(me_ref, na, fa, ga, nb, fb, gb, a, b, c, send, keep):
     high = me_ref[3]
     half = na.shape[1]
     for flip, out in ((1, send), (0, keep)):
@@ -413,7 +423,7 @@
     spec = pltpu.PrefetchScalarGridSpec(
         num_scalar_prefetch=1,
         grid=(1,),
-        in_specs=[whole(x.shape) for x in args] + [pl.BlockSpec(memory_space=pl.ANY)] * 2,
+        in_specs=[whole(x.shape) for x in args] + [pl.BlockSpec(memory_space=pl.ANY)] * 3,
         out_specs=[whole((2 * half, width))] * 2,
     )
     return pl.pallas_call(
@@ -461,60 +471,59 @@
 NT = (((1,), (1,)), ((), ()))
 
 
-def image_kernel(
-    me_ref, three_ref, last_ref, rows_ref, freq_hbm, a, b, c, send_ref, keep_ref, freq_ref, pre_ref, sem
-):
-    cols = send_ref.shape[1]
-    tile = three_ref.shape[3]
+def image_kernel(me_ref, wave_ref, rows_ref, freq_ref, a, b, c, send_ref, keep_ref, pre_ref):
+    step = pl.program_id(0)
+    tile = wave_ref.shape[3]
     part = tile // 2
-    core = me_ref[0] % 2
-    copies = []
-    for s in range(4):
-        first = (2 * (s % 2) + (core ^ (1 - s // 2))) * cols
-        source = freq_hbm.at[pl.ds(pl.multiple_of(first, 128), cols), :]
-        copies.append(pltpu.make_async_copy(source, freq_ref.at[s], sem.at[s]))
-        copies[-1].start()
-    for t in range(4):
-        place = me_ref[5] ^ (3 - t)
-        wave = last_ref.at[0] if t == 3 else three_ref.at[t]
-        for h in range(2):
-            grad = rows_ref[4 * h + 2 * (place % 2) + place // 2].astype(F32)
-            lanes = slice(h * part, (h + 1) * part)
-            pre = wave[0, :, lanes] * grad[:, part:] - wave[1, :, lanes] * grad[:, :part]
-            at = pl.multiple_of(place * tile + h * part, 128)
-            pre_ref[:, pl.ds(at, part)] = pre.astype(BF)
-    for s in range(4):
-        copies[s].wait()
-        out = lax.dot_general(freq_ref[s], pre_ref[...], NT, preferred_element_type=F32)
-        if s < 2:
-            send_ref[s] = out.astype(BF)
-        else:
-            keep_ref[s - 2] = out
-
-
-def image_grads(me, three, last, feat_rows, freq, cols, after):
+
+    @pl.when(step == 0)
+    def _():
+        for place in range(4):
+            for h in range(2):
+                grad = rows_ref[4 * h + 2 * (place % 2) + place // 2].astype(F32)
+                lanes = slice(h * part, (h + 1) * part)
+                pre = wave_ref[place, 0, :, lanes] * grad[:, part:]
+                pre = pre - wave_ref[place, 1, :, lanes] * grad[:, :part]
+                at = place * tile + h * part
+                pre_ref[:, at : at + part] = pre.astype(BF)
+
+    out = lax.dot_general(freq_ref[...], pre_ref[...], NT, preferred_element_type=F32)
+
+    @pl.when(step < 2)
+    def _():
+        send_ref[0] = out.astype(BF)
+
+    @pl.when(step >= 2)
+    def _():
+        keep_ref[0] = out
+
+
+def image_grads(me, waves, feat_rows, freq, cols, after):
     k, n = freq.shape
     owners, rows, width = feat_rows.shape
     whole = lambda shape: block(shape, lambda s, me: (0,) * len(shape))
+
+    def source(s, me):
+        return 2 * (s % 2) + ((me[0] % 2) ^ (1 - s // 2)), 0
+
     spec = pltpu.PrefetchScalarGridSpec(
         num_scalar_prefetch=1,
-        grid=(1,),
-        in_specs=[whole(three.shape), whole(last.shape), whole(feat_rows.shape)]
-        + [pl.BlockSpec(memory_space=pl.ANY)] * 4,
-        out_specs=[whole((2, cols, rows))] * 2,
-        scratch_shapes=[
-            pltpu.VMEM((4, cols, n), BF),
-            pltpu.VMEM((rows, n), BF),
-            pltpu.SemaphoreType.DMA((4,)),
+        grid=(4,),
+        in_specs=[whole(waves.shape), whole(feat_rows.shape), block((cols, n), source)]
+        + [pl.BlockSpec(memory_space=pl.ANY)] * 3,
+        out_specs=[
+            block((1, cols, rows), lambda s, me: (jnp.minimum(s, 1), 0, 0)),
+            block((1, cols, rows), lambda s, me: (jnp.maximum(s - 2, 0), 0, 0)),
         ],
+        scratch_shapes=[pltpu.VMEM((rows, n), BF)],
     )
     return pl.pallas_call(
         image_kernel,
         grid_spec=spec,
-        out_shape=[jax.ShapeDtypeStruct((2, cols, rows), t) for t in (BF, F32)],
+        out_shape=[jax.ShapeDtypeStruct((2, cols, rows), BF), pltpu.HBM((2, cols, rows), F32)],
         compiler_params=pltpu.CompilerParams(vmem_limit_bytes=52 * 2**20),
         cost_estimate=pl.CostEstimate(flops=2 * k * n * rows, bytes_accessed=2 * k * n, transcendentals=0),
-    )(me, three, last, feat_rows, freq, *after)
+    )(me, waves, feat_rows, freq, *after)
 
 
 def split_y_kernel(me_ref, keep_s, keep_k, got_s, got_k, send, keep):
@@ -621,7 +630,7 @@
     return pl.pallas_call(
         weight_kernel,
         grid_spec=spec,
-        out_shape=jax.ShapeDtypeStruct((mine, cols), F32),
+        out_shape=pltpu.HBM((mine, cols), F32),
         compiler_params=pltpu.CompilerParams(vmem_limit_bytes=12 * 2**20),
         cost_estimate=pl.CostEstimate(
             flops=2 * mine * total * cols, bytes_accessed=4 * 2**20, transcendentals=0
@@ -712,14 +721,21 @@
     label_row = jnp.zeros((16, dz), BF).at[0, :].set(syn_labels.astype(BF))
     packed = jnp.concatenate([latents, label_row], axis=0)[None]
     packed = jnp.concatenate([packed, swap(packed, "rec", 1)], axis=0)
-    quad = jnp.concatenate([packed, swap(packed, "rec", 2)], axis=0)
-    args = (me, real_labels, syn_labels, (0, 2, 1, 3), images, records, frequencies, classes)
+    pair = swap(packed, "rec", 2)
+    masks = (0, 2, 1, 3)
     totals = (real_total, syn_total)
-    send_a, keep_a, send_b, keep_b, three = feature_sums(False, *args, totals, packed)
-    eight = jnp.concatenate([quad, swap(quad, "rec", 4)], axis=0)
+    send_a, keep_a, send_b, keep_b, both, waves, token = feature_sums(
+        False, me, real_labels, syn_labels, masks, images, records, frequencies, classes, totals, packed
+    )
     first_a = swap(send_a, "rec", 1)
     first_b = swap(send_b, "rec", 2)
-    last_a, last_b, last = feature_sums(True, *args, totals, quad)
+    pair, token = tie(pair, token)
+    quad = jnp.concatenate([packed, pair], axis=0)
+    eight = jnp.concatenate([quad, swap(quad, "rec", 4)], axis=0)
+    first_token = token
+    last_a, last_b, waves, token = feature_sums(
+        True, me, real_labels, syn_labels, masks, both, records, frequencies, classes, totals, quad, waves
+    )
 
     all_latents = eight[:, :rows].reshape(syn_total, dz)
     all_labels = eight[:, rows].reshape(syn_total).astype(jnp.int32)
@@ -736,19 +752,19 @@
     all_preact = lax.dot_general(w, lhs, (((0,), (0,)), ((), ())), preferred_element_type=F32)
     all_hidden = jnp.maximum(all_preact, 0.0).astype(BF)
 
-    send_a, send_b = stage_two_send(keep_a, first_a, keep_b, first_b, last)
+    send_a, send_b = stage_two_send(keep_a, first_a, keep_b, first_b, token)
     got_a = swap(send_a, "rec", 2)
     got_b = swap(send_b, "rec", 1)
     part = frequencies.shape[1] // groups
     noise = lax.dynamic_slice_in_dim(class_noise, (2 * place + z_high) * part, part, 2)
     noise = noise.reshape(classes, 2 * part)
-    send, keep = stage_three(me, last_a, first_a, got_a, last_b, first_b, got_b, (noise, eight))
+    send, keep = stage_three(me, last_a, first_a, got_a, last_b, first_b, got_b, (noise, eight, first_token))
     got = swap(send, "rec", 4)
     feat_grad = gap_rows(me, keep, got, noise, all_labels.reshape(groups, rows), real_total)
     feat_grad = lax.all_to_all(feat_grad, "rec", 0, 0, tiled=True)
 
     send, keep = image_grads(
-        me, three, last, feat_grad, frequencies, cols, (all_preact, all_hidden, lhs)
+        me, waves, feat_grad, frequencies, cols, (all_preact, all_hidden, lhs)
     )
     send, keep = split_y(me, keep, swap(send, "feat", 1))
     out_grad = out_grads(keep, swap(send, "feat", 2), own)

time: 191 us -> 186 us (0.974)
  Pallas kernels: 66.8 us -> 62.9 us
    pallas_call x1, Pallas kernels: 12.1 us -> 9.5 us  [image_grads(): pl.pallas_call(image_kernel, grid_spec=spec, out_shape=[jax.ShapeDtypeStr...]
    unnamed x40 -> x30, local copies, waits for them, and re-layouts: 6.5 us -> 5.5 us
  transfers between devices with their start and end apart: 26 -> 26, of which waited for: 17 -> 17; matrix products, arithmetic and copies ran while one was open for 4% -> 3% of each run, Pallas kernels for 25% -> 25%
where the time goes in v7:
time: 186 us
  waiting for transfers between devices  74.9 us (40%)
  Pallas kernels  62.9 us (34%)
  starting transfers between devices  30.1 us (16%)
  local copies, waits for them, and re-layouts  9.03 us (5%)
  matrix products  5.37 us (3%)
  other arithmetic  2.61 us (1%)
    ppermute x25, waiting for transfers between devices, swap(): return lax.ppermute(x, axis, [(i, i ^ bit) for i in range(n)])  52.7 us
    pallas_call x2, Pallas kernels, feature_sums(): pl.pallas_call(functools.partial(features_kernel, masks, last, *totals),...  42.6 us
    ppermute x25, starting transfers between devices, swap(): return lax.ppermute(x, axis, [(i, i ^ bit) for i in range(n)])  25.6 us
    all_to_all x1, waiting for transfers between devices, eight_by_four(): feat_grad = lax.all_to_all(feat_grad, 'rec', 0, 0, tiled=True)  22.2 us
    pallas_call x1, Pallas kernels, image_grads(): pl.pallas_call(image_kernel, grid_spec=spec, out_shape=[jax.ShapeDtypeStr...  9.5 us
    unnamed x30, local copies, waits for them, and re-layouts  5.5 us
    all_to_all x1, starting transfers between devices, eight_by_four(): feat_grad = lax.all_to_all(feat_grad, 'rec', 0, 0, tiled=True)  4.47 us
  transfers between devices with their start and end apart: 26, of which 17 were waited for; matrix products, arithmetic and copies ran while one was open for 3% of the time, Pallas kernels for 25%

profile of v7, /device:TPU:0, one launch (start us, length us, event | category | flops | bytes accessed | tf_op | source)
XLA Modules:
  0.0 185.9 jit_solution(9582510633366130418)
XLA Ops:
  0.7 1.2 copy-done
  1.9 1.0 fusion.12
  2.9 2.9 %fusion.4.refs_0_.image = bf16[128,768]{1,0:T(8,128)(2,1)S(1)} fusion(bf16[2048,768]{1,0:T(8,128)(2,1)} %w_ref.3, f32[128,2048]{1,0:T(8,128)S(1)} %fusion.12, bf16[128,128]{1,0:T(8,128)(2,1)} %param.15, bf16[128,2048]{1,0:T(8,128)(2,1)} %param.17), kind=kOutput, calls=%fused_computation.5 | convolution fusion | flops 470646784 | bytes 4947968 | tf_op jit(solution)/shard_map/dot_general | solution.py:717
  5.8 3.0 %collective-permute-start.2 = (bf16[128,768]{1,0:T(8,128)(2,1)S(1)}, bf16[128,768]{1,0:T(8,128)(2,1)S(1)}, u32[]{:S(2)}, u32[]{:S(2)}) collective-permute-start(bf16[128,768]{1,0:T(8,128)(2,1)S(1)} %fusion.4.refs_0_.image), channel_id=1, source_target_pairs={{0,2},{1,3},{2,0},{3,1},{4,6},{5,7},{6,4},{7,5},{8,10},{9,11},{10,... | collective-permute-start | bytes 589832 | tf_op jit(solution)/shard_map/ppermute | solution.py:102
  8.8 4.9 %collective-permute-done.2.refs_1_ = bf16[128,768]{1,0:T(8,128)(2,1)S(1)} collective-permute-done((bf16[128,768]{1,0:T(8,128)(2,1)S(1)}, bf16[128,768]{1,0:T(8,128)(2,1)S(1)}, u32[]{:S(2)}, u32[]{:S(2)}) %collective-permute-start.2) | collective-permute-done | bytes 196640 | tf_op jit(solution)/shard_map/ppermute | solution.py:102
  13.8 1.8 collective-permute-start
  15.7 2.8 %collective-permute-done = bf16[1,144,128]{2,0,1:T(2,128)(2,1)S(1)} collective-permute-done((bf16[1,144,128]{2,0,1:T(2,128)(2,1)S(1)}, bf16[1,144,128]{2,0,1:T(2,128)(2,1)S(1)}, u32[]{:S(2)}, u32[]{:S(2)}) %collective-permute-start) | collective-permute-done | bytes 36896 | tf_op jit(solution)/shard_map/ppermute | solution.py:102
  18.8 1.9 %collective-permute-start.1 = (bf16[2,144,128]{2,0,1:T(2,128)(2,1)S(1)}, bf16[2,144,128]{2,0,1:T(2,128)(2,1)S(1)}, u32[]{:S(2)}, u32[]{:S(2)}) collective-permute-start(bf16[2,144,128]{2,0,1:T(2,128)(2,1)S(1)} %pad_maximum_fusion.4), channel_id=1, source_target_pairs={{0,8},{4,12},{8,0},{12,4},{16,24},{20,28},{24,16},{28,20},{1,9},{5... | collective-permute-start | bytes 221192 | tf_op jit(solution)/shard_map/ppermute | solution.py:102
  20.6 29.2 %shard_map.112 = (bf16[2,2,128,512]{3,2,1,0:T(8,128)(2,1)S(1)}, f32[2,128,512]{2,1,0:T(8,128)S(1)}, bf16[2,2,128,512]{3,2,1,0:T(8,128)(2,1)S(1)}, f32[2,128,512]...) custom-call(s32[6]{0:T(128)S(1)} %stack.27.me_ref, ...), custom_call_target="tpu_custom_call" | custom-call | flops 18320719872 | bytes 18874368 | tf_op jit(solution)/shard_map/pallas_call | solution.py:381
  49.9 0.9 pad_maximum_fusion.3
  50.8 0.9 copy.23.refs_3_
  51.7 2.7 %collective-permute-start.5 = (bf16[4,144,128]{2,0,1:T(4,128)(2,1)}, bf16[4,144,128]{2,0,1:T(4,128)(2,1)}, u32[]{:S(2)}, u32[]{:S(2)}) collective-permute-start(bf16[4,144,128]{2,0,1:T(4,128)(2,1)} %pad_maximum_fusion.3), channel_id=1, source_target_pairs={{0,16},{4,20},{8,24},{12,28},{16,0},{20,4},{24,8},{28,12},{1,17},{... | collective-permute-start | bytes 442376 | tf_op jit(solution)/shard_map/ppermute | solution.py:102
  54.4 1.5 collective-permute-start.6
  56.3 1.1 copy-done.5
  57.5 13.4 %shard_map.113 = (f32[2,128,512]{2,1,0:T(8,128)S(1)}, f32[2,128,512]{2,1,0:T(8,128)S(1)}, f32[4,2,128,512]{3,2,1,0:T(8,128)}, f32[8,128]{1,0:T(8,128)S(1)}) custom-call(s32[6]{0:T(128)S(1)} %stack.27.me_ref, s32[1,1536]{1,0:T(1,128)S(1)} %reshape.61.real_labels_ref, s32[1,128]{1,0:T(1,128)S(1)} %bitcast.32, ...), custom_call_target="tpu_custom_call", output_to_operand_aliasing={{2}: (7, {})} | custom-call | flops 6106906624 | bytes 12582912 | tf_op jit(solution)/shard_map/pallas_call | solution.py:381
  71.7 0.9 shard_map.114
  72.6 1.5 collective-permute-start.8
  74.7 1.3 constant_dynamic-slice_fusion
  76.0 1.3 pad_maximum_fusion.2
  77.4 2.7 %collective-permute-done.8.ga = bf16[2,128,512]{2,1,0:T(8,128)(2,1)S(1)} collective-permute-done((bf16[2,128,512]{2,1,0:T(8,128)(2,1)}, bf16[2,128,512]{2,1,0:T(8,128)(2,1)S(1)}, u32[]{:S(2)}, u32[]{:S(2)}) %collective-permute-start.8) | collective-permute-done | bytes 262176 | tf_op jit(solution)/shard_map/ppermute | solution.py:102
  82.0 11.8 %collective-permute-done.10.got_ref = bf16[256,512]{1,0:T(8,128)(2,1)S(1)} collective-permute-done((bf16[256,512]{1,0:T(8,128)(2,1)S(1)}, bf16[256,512]{1,0:T(8,128)(2,1)S(1)}, u32[]{:S(2)}, u32[]{:S(2)}) %collective-permute-start.10) | collective-permute-done | bytes 262176 | tf_op jit(solution)/shard_map/ppermute | solution.py:102
  93.8 2.1 %shard_map.116 = bf16[8,128,512]{2,1,0:T(8,128)(2,1)} custom-call(s32[6]{0:T(128)S(1)} %stack.27.me_ref, f32[256,512]{1,0:T(8,128)S(1)} %get-tuple-element.60.keep_ref, bf16[256,512]{1,0:T(8,128)(2,1)S(1)} %collective-permute-done.10.got_ref, f32[256,512]{1,0:T(8,128)S(1)} %bitcast.30, s32[8,128]{1,0:T(8,128)S(1)} %get-tuple-element.75.labels_ref), custom_call_target="tpu_custom_call" | custom-call | flops 268435456 | bytes 3145728 | tf_op jit(solution)/shard_map/pallas_call | solution.py:460
  95.9 4.5 %all-to-all-start = ((bf16[8,128,512]{2,1,0:T(8,128)(2,1)}), bf16[8,128,512]{2,1,0:T(8,128)(2,1)}, u32[]{:S(2)}, u32[]{:S(2)}) async-start(bf16[8,128,512]{2,1,0:T(8,128)(2,1)} %shard_map.116), calls=%async_computation | async-start | bytes 2097152 | tf_op jit(solution)/shard_map/all_to_all | solution.py:764
  101.7 1.5 maximum_convert_fusion
  103.2 22.2 %all-to-all-done.rows_ref = bf16[8,128,512]{2,1,0:T(8,128)(2,1)} async-done(((bf16[8,128,512]{2,1,0:T(8,128)(2,1)}), bf16[8,128,512]{2,1,0:T(8,128)(2,1)}, u32[]{:S(2)}, u32[]{:S(2)}) %all-to-all-start) | async-done | bytes 1048608 | tf_op jit(solution)/shard_map/all_to_all | solution.py:764
  125.4 9.5 %shard_map.117 = (bf16[2,768,128]{2,1,0:T(8,128)(2,1)S(1)}, f32[2,768,128]{2,1,0:T(8,128)}) custom-call(s32[6]{0:T(128)S(1)} %stack.27.me_ref, f32[4,2,128,512]{3,2,1,0:T(8,128)} %get-tuple-element.49.wave_ref, bf16[8,128,512]{2,1,0:T(8,128)(2,1)} %all-to-all-done.rows_ref, bf16[3072,2048]{1,0:T(8,128)(2,1)} %freq_ref.1, ...), custom_call_target="tpu_custom_call" | custom-call | flops 1610612736 | bytes 12582912 | tf_op jit(solution)/shard_map/pallas_call | solution.py:520
  134.9 1.7 collective-permute-done.11.got_s.got_k
  136.6 1.1 copy-done.3
  138.4 1.7 collective-permute-start.12
  140.1 5.3 %collective-permute-done.12.got = bf16[768,128]{1,0:T(8,128)(2,1)S(1)} collective-permute-done((bf16[768,128]{1,0:T(8,128)(2,1)S(1)}, bf16[768,128]{1,0:T(8,128)(2,1)S(1)}, u32[]{:S(2)}, u32[]{:S(2)}) %collective-permute-start.12) | collective-permute-done | bytes 196640 | tf_op jit(solution)/shard_map/ppermute | solution.py:102
  145.7 1.9 %collective-permute-start.14 = (bf16[128,768]{1,0:T(8,128)(2,1)S(1)}, bf16[128,768]{1,0:T(8,128)(2,1)S(1)}, u32[]{:S(2)}, u32[]{:S(2)}) collective-permute-start(bf16[128,768]{1,0:T(8,128)(2,1)S(1)} %shard_map.119.refs_0_), channel_id=1, source_target_pairs={{0,8},{4,12},{8,0},{12,4},{16,24},{20,28},{24,16},{28,20},{1,9},{5... | collective-permute-start | bytes 589832 | tf_op jit(solution)/shard_map/ppermute | solution.py:102
  147.6 1.5 collective-permute-start.15
  149.1 7.0 %collective-permute-done.13.refs_4_.refs_0_ = bf16[128,768]{1,0:T(8,128)(2,1)S(1)} collective-permute-done((bf16[128,768]{1,0:T(8,128)(2,1)S(1)}, bf16[128,768]{1,0:T(8,128)(2,1)S(1)}, u32[]{:S(2)}, u32[]{:S(2)}) %collective-permute-start.13) | collective-permute-done | bytes 196640 | tf_op jit(solution)/shard_map/ppermute | solution.py:102
  156.3 1.4 collective-permute-start.16
  158.3 4.5 %collective-permute-done.18.refs_6_.refs_2_ = bf16[128,768]{1,0:T(8,128)(2,1)S(1)} collective-permute-done((bf16[128,768]{1,0:T(8,128)(2,1)S(1)}, bf16[128,768]{1,0:T(8,128)(2,1)S(1)}, u32[]{:S(2)}, u32[]{:S(2)}) %collective-permute-start.18) | collective-permute-done | bytes 196640 | tf_op jit(solution)/shard_map/ppermute | solution.py:102
  162.8 1.1 collective-permute-start.19
  164.1 4.2 %collective-permute-done.17.refs_5_.refs_4_.refs_1_ = bf16[128,768]{1,0:T(8,128)(2,1)S(1)} collective-permute-done((bf16[128,768]{1,0:T(8,128)(2,1)S(1)}, bf16[128,768]{1,0:T(8,128)(2,1)S(1)}, u32[]{:S(2)}, u32[]{:S(2)}) %collective-permute-start.17) | collective-permute-done | bytes 196640 | tf_op jit(solution)/shard_map/ppermute | solution.py:102
  168.3 1.1 shard_map.121
  169.5 1.3 collective-permute-done.20.b
  171.3 1.1 shard_map.123
  172.5 1.7 collective-permute-start.21
  174.3 1.3 collective-permute-start.23
  175.6 2.4 %shard_map.120.after = f32[256,768]{1,0:T(8,128)} custom-call(s32[6]{0:T(128)S(1)} %stack.27.me_ref, bf16[256,1024]{1,0:T(8,128)(2,1)S(1)} %get-tuple-element.77.b.hidden_ref, bf16[128,768]{1,0:T(8,128)(2,1)S(1)} %shard_map.119.refs_0_, bf16[128,768]{1,0:T(8,128)(2,1)S(1)} %collective-permute-done.15.refs_1_, ...), custom_call_target="tpu_custom_call" | custom-call | flops 402653184 | bytes 4194304 | tf_op jit(solution)/shard_map/pallas_call | solution.py:630
  178.0 0.9 collective-permute-done.21.q0
  178.9 2.4 %collective-permute-done.23.q1 = bf16[2,256,128]{2,1,0:T(8,128)(2,1)S(1)} collective-permute-done((bf16[2,256,128]{2,1,0:T(8,128)(2,1)S(1)}, bf16[2,256,128]{2,1,0:T(8,128)(2,1)S(1)}, u32[]{:S(2)}, u32[]{:S(2)}) %collective-permute-start.23) | collective-permute-done | bytes 131104 | tf_op jit(solution)/shard_map/ppermute | solution.py:102
  181.3 1.1 copy-done.4
  182.4 0.9 shard_map.125.own
  183.4 1.7 collective-permute-done.24.other
  (72 shorter events, 8.8 us)
Async XLA Ops:
  0.6 1.2 copy-start
  0.6 8.2 %copy-start.8 = (s32[128]{0:T(128)S(1)}, s32[128]{0:T(128)}, u32[]{:S(2)}) copy-start(s32[128]{0:T(128)} %param.16) | copy-start | bytes 1540
  0.7 13.1 %copy-start.12 = (bf16[128,128]{1,0:T(8,128)(2,1)S(1)}, bf16[128,128]{1,0:T(8,128)(2,1)}, u32[]{:S(2)}) copy-start(bf16[128,128]{1,0:T(8,128)(2,1)} %param.15) | copy-start | bytes 98308
  0.7 14.9 %copy-start.13 = (s32[1536]{0:T(1024)S(1)}, s32[1536]{0:T(1024)}, u32[]{:S(2)}) copy-start(s32[1536]{0:T(1024)} %param.12) | copy-start | bytes 18436
  5.8 7.9 %collective-permute-start.2 = (bf16[128,768]{1,0:T(8,128)(2,1)S(1)}, bf16[128,768]{1,0:T(8,128)(2,1)S(1)}, u32[]{:S(2)}, u32[]{:S(2)}) collective-permute-start(bf16[128,768]{1,0:T(8,128)(2,1)S(1)} %fusion.4.refs_0_.image), channel_id=1, source_target_pairs={{0,2},{1,3},{2,0},{3,1},{4,6},{5,7},{6,4},{7,5},{8,10},{9,11},{10,... | collective-permute-start | bytes 589832 | tf_op jit(solution)/shard_map/ppermute | solution.py:102
  8.8 11.8 %collective-permute-start.3 = (bf16[128,768]{1,0:T(8,128)(2,1)S(1)}, bf16[128,768]{1,0:T(8,128)(2,1)S(1)}, u32[]{:S(2)}, u32[]{:S(2)}) collective-permute-start(bf16[128,768]{1,0:T(8,128)(2,1)S(1)} %fusion.4.refs_0_.image), channel_id=1, source_target_pairs={{0,1},{1,0},{2,3},{3,2},{4,5},{5,4},{6,7},{7,6},{8,9},{9,8},{10,11... | collective-permute-start | bytes 589832 | tf_op jit(solution)/shard_map/ppermute | solution.py:102
  13.7 6.9 %collective-permute-start.4 = (bf16[128,768]{1,0:T(8,128)(2,1)S(1)}, bf16[128,768]{1,0:T(8,128)(2,1)S(1)}, u32[]{:S(2)}, u32[]{:S(2)}) collective-permute-start(bf16[128,768]{1,0:T(8,128)(2,1)S(1)} %collective-permute-done.2.refs_1_), channel_id=1, source_target_pairs={{0,1},{1,0},{2,3},{3,2},{4,5},{5,4},{6,7},{7,6},{8,9},{9,8},{10,11... | collective-permute-start | bytes 589832 | tf_op jit(solution)/shard_map/ppermute | solution.py:102
  13.8 4.7 %collective-permute-start = (bf16[1,144,128]{2,0,1:T(2,128)(2,1)S(1)}, bf16[1,144,128]{2,0,1:T(2,128)(2,1)S(1)}, u32[]{:S(2)}, u32[]{:S(2)}) collective-permute-start(bf16[1,144,128]{2,0,1:T(2,128)(2,1)S(1)} %copy.21), channel_id=1, source_target_pairs={{0,4},{4,0},{8,12},{12,8},{16,20},{20,16},{24,28},{28,24},{1,5},{5... | collective-permute-start | bytes 110600 | tf_op jit(solution)/shard_map/ppermute | solution.py:102
  18.6 31.3 %copy-start.10 = (bf16[1,144,128]{2,0,1:T(2,128)(2,1)}, bf16[1,144,128]{2,0,1:T(2,128)(2,1)S(1)}, u32[]{:S(2)}) copy-start(bf16[1,144,128]{2,0,1:T(2,128)(2,1)S(1)} %collective-permute-done) | copy-start | bytes 110596
  18.8 31.1 %collective-permute-start.1 = (bf16[2,144,128]{2,0,1:T(2,128)(2,1)S(1)}, bf16[2,144,128]{2,0,1:T(2,128)(2,1)S(1)}, u32[]{:S(2)}, u32[]{:S(2)}) collective-permute-start(bf16[2,144,128]{2,0,1:T(2,128)(2,1)S(1)} %pad_maximum_fusion.4), channel_id=1, source_target_pairs={{0,8},{4,12},{8,0},{12,4},{16,24},{20,28},{24,16},{28,20},{1,9},{5... | collective-permute-start | bytes 221192 | tf_op jit(solution)/shard_map/ppermute | solution.py:102
  49.9 6.0 %copy-start.11 = (bf16[2,144,128]{2,0,1:T(2,128)(2,1)}, bf16[2,144,128]{2,0,1:T(2,128)(2,1)S(1)}, u32[]{:S(2)}) copy-start(bf16[2,144,128]{2,0,1:T(2,128)(2,1)S(1)} %collective-permute-done.1) | copy-start | bytes 221188
  51.7 24.3 %collective-permute-start.5 = (bf16[4,144,128]{2,0,1:T(4,128)(2,1)}, bf16[4,144,128]{2,0,1:T(4,128)(2,1)}, u32[]{:S(2)}, u32[]{:S(2)}) collective-permute-start(bf16[4,144,128]{2,0,1:T(4,128)(2,1)} %pad_maximum_fusion.3), channel_id=1, source_target_pairs={{0,16},{4,20},{8,24},{12,28},{16,0},{20,4},{24,8},{28,12},{1,17},{... | collective-permute-start | bytes 442376 | tf_op jit(solution)/shard_map/ppermute | solution.py:102
  54.4 17.3 %collective-permute-start.6 = (bf16[2,2,128,512]{3,2,1,0:T(8,128)(2,1)S(1)}, bf16[2,2,128,512]{3,2,1,0:T(8,128)(2,1)S(1)}, u32[]{:S(2)}, u32[]{:S(2)}) collective-permute-start(bf16[2,2,128,512]{3,2,1,0:T(8,128)(2,1)S(1)} %get-tuple-element.51), channel_id=1, source_target_pairs={{0,4},{4,0},{8,12},{12,8},{16,20},{20,16},{24,28},{28,24},{1,5},{5... | collective-permute-start | bytes 1572872 | tf_op jit(solution)/shard_map/ppermute | solution.py:102
  55.9 15.8 %collective-permute-start.7 = (bf16[2,2,128,512]{3,2,1,0:T(8,128)(2,1)S(1)}, bf16[2,2,128,512]{3,2,1,0:T(8,128)(2,1)S(1)}, u32[]{:S(2)}, u32[]{:S(2)}) collective-permute-start(bf16[2,2,128,512]{3,2,1,0:T(8,128)(2,1)S(1)} %get-tuple-element.54), channel_id=1, source_target_pairs={{0,8},{4,12},{8,0},{12,4},{16,24},{20,28},{24,16},{28,20},{1,9},{5... | collective-permute-start | bytes 1572872 | tf_op jit(solution)/shard_map/ppermute | solution.py:102
  56.3 1.1 copy-start.5
  70.9 0.8 copy-start.6
  72.6 7.5 %collective-permute-start.8 = (bf16[2,128,512]{2,1,0:T(8,128)(2,1)}, bf16[2,128,512]{2,1,0:T(8,128)(2,1)S(1)}, u32[]{:S(2)}, u32[]{:S(2)}) collective-permute-start(bf16[2,128,512]{2,1,0:T(8,128)(2,1)} %get-tuple-element.56), channel_id=1, source_target_pairs={{0,8},{4,12},{8,0},{12,4},{16,24},{20,28},{24,16},{28,20},{1,9},{5... | collective-permute-start | bytes 786440 | tf_op jit(solution)/shard_map/ppermute | solution.py:102
  74.1 6.7 %collective-permute-start.9 = (bf16[2,128,512]{2,1,0:T(8,128)(2,1)}, bf16[2,128,512]{2,1,0:T(8,128)(2,1)S(1)}, u32[]{:S(2)}, u32[]{:S(2)}) collective-permute-start(bf16[2,128,512]{2,1,0:T(8,128)(2,1)} %get-tuple-element.58), channel_id=1, source_target_pairs={{0,4},{4,0},{8,12},{12,8},{16,20},{20,16},{24,28},{28,24},{1,5},{5... | collective-permute-start | bytes 786440 | tf_op jit(solution)/shard_map/ppermute | solution.py:102
  74.7 6.2 %copy-start.7 = (f32[2,128,512]{2,1,0:T(8,128)S(1)}, f32[2,128,512]{2,1,0:T(8,128)}, u32[]{:S(2)}) copy-start(f32[2,128,512]{2,1,0:T(8,128)} %copy-done.6) | copy-start | bytes 1572868
  77.4 16.5 %copy-start.9 = (bf16[8,144,128]{2,0,1:T(8,128)(2,1)}, bf16[8,144,128]{2,0,1:T(8,128)(2,1)S(1)}, u32[]{:S(2)}) copy-start(bf16[8,144,128]{2,0,1:T(8,128)(2,1)S(1)} %pad_maximum_fusion.2) | copy-start | bytes 884740
  81.6 12.2 %collective-permute-start.10 = (bf16[256,512]{1,0:T(8,128)(2,1)S(1)}, bf16[256,512]{1,0:T(8,128)(2,1)S(1)}, u32[]{:S(2)}, u32[]{:S(2)}) collective-permute-start(bf16[256,512]{1,0:T(8,128)(2,1)S(1)} %get-tuple-element.61), channel_id=1, source_target_pairs={{0,16},{4,20},{8,24},{12,28},{16,0},{20,4},{24,8},{28,12},{1,17},{... | collective-permute-start | bytes 786440 | tf_op jit(solution)/shard_map/ppermute | solution.py:102
  93.8 7.4 %slice-start = ((bf16[8,144,128]{2,0,1:T(8,128)(2,1)}), bf16[8,128,128]{2,0,1:T(8,128)(2,1)S(1)}, s32[]{:S(2)}) async-start(bf16[8,144,128]{2,0,1:T(8,128)(2,1)} %copy-done.9), calls=%async_computation.1 | async-start | bytes 524288 | tf_op jit(solution)/shard_map/slice | solution.py:740
  95.9 29.5 %all-to-all-start = ((bf16[8,128,512]{2,1,0:T(8,128)(2,1)}), bf16[8,128,512]{2,1,0:T(8,128)(2,1)}, u32[]{:S(2)}, u32[]{:S(2)}) async-start(bf16[8,128,512]{2,1,0:T(8,128)(2,1)} %shard_map.116), calls=%async_computation | async-start | bytes 2097152 | tf_op jit(solution)/shard_map/all_to_all | solution.py:764
  134.9 33.4 %copy-start.1 = (bf16[2048,768]{1,0:T(8,128)(2,1)S(1)}, bf16[2048,768]{1,0:T(8,128)(2,1)}, u32[]{:S(2)}) copy-start(bf16[2048,768]{1,0:T(8,128)(2,1)} %w_ref.3) | copy-start | bytes 9437188
  134.9 1.7 collective-permute-start.11
  136.6 1.1 copy-start.3
  138.4 7.0 %collective-permute-start.12 = (bf16[768,128]{1,0:T(8,128)(2,1)S(1)}, bf16[768,128]{1,0:T(8,128)(2,1)S(1)}, u32[]{:S(2)}, u32[]{:S(2)}) collective-permute-start(bf16[768,128]{1,0:T(8,128)(2,1)S(1)} %get-tuple-element.65), channel_id=1, source_target_pairs={{0,2},{1,3},{2,0},{3,1},{4,6},{5,7},{6,4},{7,5},{8,10},{9,11},{10,... | collective-permute-start | bytes 589832 | tf_op jit(solution)/shard_map/ppermute | solution.py:102
  145.6 10.5 %collective-permute-start.13 = (bf16[128,768]{1,0:T(8,128)(2,1)S(1)}, bf16[128,768]{1,0:T(8,128)(2,1)S(1)}, u32[]{:S(2)}, u32[]{:S(2)}) collective-permute-start(bf16[128,768]{1,0:T(8,128)(2,1)S(1)} %shard_map.119.refs_0_), channel_id=1, source_target_pairs={{0,16},{4,20},{8,24},{12,28},{16,0},{20,4},{24,8},{28,12},{1,17},{... | collective-permute-start | bytes 589832 | tf_op jit(solution)/shard_map/ppermute | solution.py:102
  145.7 10.4 %collective-permute-start.14 = (bf16[128,768]{1,0:T(8,128)(2,1)S(1)}, bf16[128,768]{1,0:T(8,128)(2,1)S(1)}, u32[]{:S(2)}, u32[]{:S(2)}) collective-permute-start(bf16[128,768]{1,0:T(8,128)(2,1)S(1)} %shard_map.119.refs_0_), channel_id=1, source_target_pairs={{0,8},{4,12},{8,0},{12,4},{16,24},{20,28},{24,16},{28,20},{1,9},{5... | collective-permute-start | bytes 589832 | tf_op jit(solution)/shard_map/ppermute | solution.py:102
  147.6 8.5 %collective-permute-start.15 = (bf16[128,768]{1,0:T(8,128)(2,1)S(1)}, bf16[128,768]{1,0:T(8,128)(2,1)S(1)}, u32[]{:S(2)}, u32[]{:S(2)}) collective-permute-start(bf16[128,768]{1,0:T(8,128)(2,1)S(1)} %shard_map.119.refs_0_), channel_id=1, source_target_pairs={{0,4},{4,0},{8,12},{12,8},{16,20},{20,16},{24,28},{28,24},{1,5},{5... | collective-permute-start | bytes 589832 | tf_op jit(solution)/shard_map/ppermute | solution.py:102
  156.1 6.8 %collective-permute-start.18 = (bf16[128,768]{1,0:T(8,128)(2,1)S(1)}, bf16[128,768]{1,0:T(8,128)(2,1)S(1)}, u32[]{:S(2)}, u32[]{:S(2)}) collective-permute-start(bf16[128,768]{1,0:T(8,128)(2,1)S(1)} %collective-permute-done.13.refs_4_.refs_0_), channel_id=1, source_target_pairs={{0,8},{4,12},{8,0},{12,4},{16,24},{20,28},{24,16},{28,20},{1,9},{5... | collective-permute-start | bytes 589832 | tf_op jit(solution)/shard_map/ppermute | solution.py:102
  156.3 7.8 %collective-permute-start.16 = (bf16[128,768]{1,0:T(8,128)(2,1)S(1)}, bf16[128,768]{1,0:T(8,128)(2,1)S(1)}, u32[]{:S(2)}, u32[]{:S(2)}) collective-permute-start(bf16[128,768]{1,0:T(8,128)(2,1)S(1)} %collective-permute-done.14.refs_2_), channel_id=1, source_target_pairs={{0,4},{4,0},{8,12},{12,8},{16,20},{20,16},{24,28},{28,24},{1,5},{5... | collective-permute-start | bytes 589832 | tf_op jit(solution)/shard_map/ppermute | solution.py:102
  157.7 10.6 %collective-permute-start.17 = (bf16[128,768]{1,0:T(8,128)(2,1)S(1)}, bf16[128,768]{1,0:T(8,128)(2,1)S(1)}, u32[]{:S(2)}, u32[]{:S(2)}) collective-permute-start(bf16[128,768]{1,0:T(8,128)(2,1)S(1)} %collective-permute-done.13.refs_4_.refs_0_), channel_id=1, source_target_pairs={{0,4},{4,0},{8,12},{12,8},{16,20},{20,16},{24,28},{28,24},{1,5},{5... | collective-permute-start | bytes 589832 | tf_op jit(solution)/shard_map/ppermute | solution.py:102
  162.8 8.5 %collective-permute-start.19 = (bf16[128,768]{1,0:T(8,128)(2,1)S(1)}, bf16[128,768]{1,0:T(8,128)(2,1)S(1)}, u32[]{:S(2)}, u32[]{:S(2)}) collective-permute-start(bf16[128,768]{1,0:T(8,128)(2,1)S(1)} %collective-permute-done.18.refs_6_.refs_2_), channel_id=1, source_target_pairs={{0,4},{4,0},{8,12},{12,8},{16,20},{20,16},{24,28},{28,24},{1,5},{5... | collective-permute-start | bytes 589832 | tf_op jit(solution)/shard_map/ppermute | solution.py:102
  169.4 1.4 collective-permute-start.20
  170.9 10.4 %copy-start.2 = (f32[256,1024]{1,0:T(8,128)S(1)}, f32[256,1024]{1,0:T(8,128)}, u32[]{:S(2)}) copy-start(f32[256,1024]{1,0:T(8,128)} %get-tuple-element.78.a.preact_ref) | copy-start | bytes 3145732
  172.5 1.8 collective-permute-start.22
  172.5 6.4 %collective-permute-start.21 = (bf16[2,256,128]{2,1,0:T(8,128)(2,1)S(1)}, bf16[2,256,128]{2,1,0:T(8,128)(2,1)S(1)}, u32[]{:S(2)}, u32[]{:S(2)}) collective-permute-start(bf16[2,256,128]{2,1,0:T(8,128)(2,1)S(1)} %shard_map.122.refs_4_.p0), channel_id=1, source_target_pairs={{0,2},{1,3},{2,0},{3,1},{4,6},{5,7},{6,4},{7,5},{8,10},{9,11},{10,... | collective-permute-start | bytes 393224 | tf_op jit(solution)/shard_map/ppermute | solution.py:102
  174.3 7.0 %collective-permute-start.23 = (bf16[2,256,128]{2,1,0:T(8,128)(2,1)S(1)}, bf16[2,256,128]{2,1,0:T(8,128)(2,1)S(1)}, u32[]{:S(2)}, u32[]{:S(2)}) collective-permute-start(bf16[2,256,128]{2,1,0:T(8,128)(2,1)S(1)} %shard_map.124.p1), channel_id=1, source_target_pairs={{0,2},{1,3},{2,0},{3,1},{4,6},{5,7},{6,4},{7,5},{8,10},{9,11},{10,... | collective-permute-start | bytes 393224 | tf_op jit(solution)/shard_map/ppermute | solution.py:102
  181.3 1.1 copy-start.4
  183.3 1.8 collective-permute-start.24

commit v8 on v7

--- a/solution.py
+++ b/solution.py
@@ -392,7 +392,8 @@
     )(me, real_labels.reshape(1, -1), syn_labels.reshape(1, -1), *images, records, freq, *extra)
 
 
-def stage_two_send_kernel(ka, ga, kb, gb, after, sa, sb):
+def stage_two_send_kernel(ka, ga, kb, gb, after, sa, sb, token):
+    token[...] = jnp.zeros_like(token)
     sa[...] = (ka[...] + ga[0].astype(F32)).astype(BF)
     sb[...] = (kb[...] + gb[0].astype(F32)).astype(BF)
 
@@ -401,13 +402,14 @@
     return pl.pallas_call(
         stage_two_send_kernel,
         in_specs=[pl.BlockSpec()] * 4 + [pl.BlockSpec(memory_space=pl.ANY)],
-        out_shape=[jax.ShapeDtypeStruct(keep_a.shape, BF)] * 2,
+        out_shape=[jax.ShapeDtypeStruct(keep_a.shape, BF)] * 2 + [jax.ShapeDtypeStruct((8, 128), F32)],
         compiler_params=pltpu.CompilerParams(vmem_limit_bytes=10 * 2**20),
         cost_estimate=pl.CostEstimate(flops=0, bytes_accessed=3 * 2**20, transcendentals=0),
     )(keep_a, got_a, keep_b, got_b, after)
 
 
-def stage_three_kernel(me_ref, na, fa, ga, nb, fb, gb, a, b, c, send, keep):
+def stage_three_kernel(me_ref, na, fa, ga, nb, fb, gb, a, b, c, send, keep, token):
+    token[...] = jnp.zeros_like(token)
     high = me_ref[3]
     half = na.shape[1]
     for flip, out in ((1, send), (0, keep)):
@@ -424,48 +426,50 @@
         num_scalar_prefetch=1,
         grid=(1,),
         in_specs=[whole(x.shape) for x in args] + [pl.BlockSpec(memory_space=pl.ANY)] * 3,
-        out_specs=[whole((2 * half, width))] * 2,
+        out_specs=[whole((2 * half, width))] * 2 + [whole((8, 128))],
     )
     return pl.pallas_call(
         stage_three_kernel,
         grid_spec=spec,
-        out_shape=[jax.ShapeDtypeStruct((2 * half, width), t) for t in (BF, F32)],
+        out_shape=[jax.ShapeDtypeStruct((2 * half, width), t) for t in (BF, F32)]
+        + [jax.ShapeDtypeStruct((8, 128), F32)],
         compiler_params=pltpu.CompilerParams(vmem_limit_bytes=12 * 2**20),
         cost_estimate=pl.CostEstimate(flops=0, bytes_accessed=3 * 2**20, transcendentals=0),
     )(me, *args, *after)
 
 
-def gap_kernel(real_total, me_ref, keep_ref, got_ref, noise_ref, labels_ref, out_ref):
+def gap_kernel(real_total, order, me_ref, keep_ref, got_ref, noise_ref, labels_ref, after, out_ref):
     classes = keep_ref.shape[0]
     rows = labels_ref.shape[1]
     gap = keep_ref[...] + got_ref[...].astype(F32) - noise_ref[...] * (1.0 / real_total)
     gap = (16.0 * gap).astype(BF)
     ids = lax.broadcasted_iota(jnp.int32, (classes, rows), 0)
-    for mask in range(labels_ref.shape[0]):
-        table = jnp.where(ids == labels_ref[mask : mask + 1, :], 1.0, 0.0).astype(BF)
+    for i, mask in enumerate(order):
+        table = jnp.where(ids == labels_ref[i : i + 1, :], 1.0, 0.0).astype(BF)
         out = lax.dot_general(table, gap, (((0,), (0,)), ((), ())), preferred_element_type=F32)
         out_ref[me_ref[4] ^ mask] = out.astype(BF)
 
 
-def gap_rows(me, keep, got, noise, labels, real_total):
+def gap_rows(me, keep, got, noise, labels, real_total, order, after):
     classes, width = keep.shape
     groups, rows = labels.shape
     whole = lambda shape: block(shape, lambda h, me: (0,) * len(shape))
     spec = pltpu.PrefetchScalarGridSpec(
         num_scalar_prefetch=1,
         grid=(1,),
-        in_specs=[whole(x.shape) for x in (keep, got, noise, labels)],
+        in_specs=[whole(x.shape) for x in (keep, got, noise, labels)]
+        + [pl.BlockSpec(memory_space=pl.ANY)],
         out_specs=whole((groups, rows, width)),
     )
     return pl.pallas_call(
-        functools.partial(gap_kernel, real_total),
+        functools.partial(gap_kernel, real_total, order),
         grid_spec=spec,
         out_shape=jax.ShapeDtypeStruct((groups, rows, width), BF),
         compiler_params=pltpu.CompilerParams(vmem_limit_bytes=14 * 2**20),
         cost_estimate=pl.CostEstimate(
             flops=2 * groups * rows * classes * width, bytes_accessed=3 * 2**20, transcendentals=0
         ),
-    )(me, keep, got, noise, labels)
+    )(me, keep, got, noise, labels, after)
 
 
 NT = (((1,), (1,)), ((), ()))
@@ -643,8 +647,8 @@
     acc = None
     for h, (p, q) in enumerate(((p0, q0), (p1, q1))):
         for i in range(2):
-            mask = 4 * h + 2 * i + me_ref[0] % 2
-            at = pl.ds(pl.multiple_of(mask * rows, 128), rows)
+            place = 4 * (me_ref[0] % 2) + 2 * i + h
+            at = pl.ds(pl.multiple_of(place * rows, 128), rows)
             grad = p[i].astype(F32) + q[i].astype(F32)
             grad = jnp.where(preact_ref[:, at] > 0, grad, 0.0).astype(BF)
             d = lax.dot_general(lhs_ref[:, at], grad, NT, preferred_element_type=F32)
@@ -716,27 +720,38 @@
     hidden = jnp.maximum(preact, 0.0).astype(BF)
     own = jnp.tanh(jnp.dot(hidden, w_out, preferred_element_type=F32)).astype(BF)
     far = swap(own, "feat", 2)
-    images = [own, far, swap(own, "feat", 1), swap(far, "feat", 1)]
-
+
+    order = (0, 4, 2, 6, 1, 5, 3, 7)
     label_row = jnp.zeros((16, dz), BF).at[0, :].set(syn_labels.astype(BF))
     packed = jnp.concatenate([latents, label_row], axis=0)[None]
-    packed = jnp.concatenate([packed, swap(packed, "rec", 1)], axis=0)
+    far, pair = tie(far, swap(packed, "rec", 4))
+    images = [own, far, swap(own, "feat", 1), swap(far, "feat", 1)]
+    packed, real_labels = tie(jnp.concatenate([packed, pair], axis=0), real_labels)
     pair = swap(packed, "rec", 2)
+
     masks = (0, 2, 1, 3)
     totals = (real_total, syn_total)
     send_a, keep_a, send_b, keep_b, both, waves, token = feature_sums(
-        False, me, real_labels, syn_labels, masks, images, records, frequencies, classes, totals, packed
+        False, me, real_labels, syn_labels, masks, images, records, frequencies, classes, totals, me
     )
     first_a = swap(send_a, "rec", 1)
     first_b = swap(send_b, "rec", 2)
     pair, token = tie(pair, token)
+    last_a, last_b, waves, token = feature_sums(
+        True, me, real_labels, syn_labels, masks, both, records, frequencies, classes, totals, token, waves
+    )
+
+    send_a, send_b, token = stage_two_send(keep_a, first_a, keep_b, first_b, token)
+    got_a = swap(send_a, "rec", 2)
+    got_b = swap(send_b, "rec", 1)
+    part = frequencies.shape[1] // groups
+    noise = lax.dynamic_slice_in_dim(class_noise, (2 * place + z_high) * part, part, 2)
+    noise = noise.reshape(classes, 2 * part)
+    send, keep, token = stage_three(me, last_a, first_a, got_a, last_b, first_b, got_b, (noise, token, token))
+    got = swap(send, "rec", 4)
+    pair, token = tie(pair, token)
     quad = jnp.concatenate([packed, pair], axis=0)
-    eight = jnp.concatenate([quad, swap(quad, "rec", 4)], axis=0)
-    first_token = token
-    last_a, last_b, waves, token = feature_sums(
-        True, me, real_labels, syn_labels, masks, both, records, frequencies, classes, totals, quad, waves
-    )
-
+    eight = jnp.concatenate([quad, swap(quad, "rec", 1)], axis=0)
     all_latents = eight[:, :rows].reshape(syn_total, dz)
     all_labels = eight[:, rows].reshape(syn_total).astype(jnp.int32)
     all_table = one_hot(all_labels, classes, BF)
@@ -752,15 +767,7 @@
     all_preact = lax.dot_general(w, lhs, (((0,), (0,)), ((), ())), preferred_element_type=F32)
     all_hidden = jnp.maximum(all_preact, 0.0).astype(BF)
 
-    send_a, send_b = stage_two_send(keep_a, first_a, keep_b, first_b, token)
-    got_a = swap(send_a, "rec", 2)
-    got_b = swap(send_b, "rec", 1)
-    part = frequencies.shape[1] // groups
-    noise = lax.dynamic_slice_in_dim(class_noise, (2 * place + z_high) * part, part, 2)
-    noise = noise.reshape(classes, 2 * part)
-    send, keep = stage_three(me, last_a, first_a, got_a, last_b, first_b, got_b, (noise, eight, first_token))
-    got = swap(send, "rec", 4)
-    feat_grad = gap_rows(me, keep, got, noise, all_labels.reshape(groups, rows), real_total)
+    feat_grad = gap_rows(me, keep, got, noise, all_labels.reshape(groups, rows), real_total, order, token)
     feat_grad = lax.all_to_all(feat_grad, "rec", 0, 0, tiled=True)
 
     send, keep = image_grads(
@@ -786,7 +793,7 @@
     send, keep = hidden_grads(me, w_out, [by[i] for i in range(4)], mine, by[5])
     parts = reduced(send, keep)
     parts += reduced(*hidden_grads(me, w_out, [by[4 + i] for i in range(4)], mine, parts[0]))
-    grad_w_out = weight_grads(me, all_hidden, [by[mask] for mask in range(groups)])
+    grad_w_out = weight_grads(me, all_hidden, [by[mask] for mask in order])
     grads = last_grads(me, all_preact, lhs, parts, grad_w_out)
     grad_w_latent, grad_embed = outputs(grads, swap(grads, "feat", 1), dz)
     return grad_w_out, grad_w_latent, grad_embed

time: 186 us -> 182 us (0.978)
  starting transfers between devices: 30.1 us -> 27.5 us
    ppermute x25, starting transfers between devices: 25.6 us -> 23 us  [swap(): return lax.ppermute(x, axis, [(i, i ^ bit) for i in range(n)])]
    unnamed x30 -> x28, local copies, waits for them, and re-layouts: 5.5 us -> 6.92 us
  transfers between devices with their start and end apart: 26 -> 26, of which waited for: 17 -> 19; matrix products, arithmetic and copies ran while one was open for 3% -> 3% of each run, Pallas kernels for 25% -> 25%
where the time goes in v8:
time: 182 us; the launch traced here: 181 us
  waiting for transfers between devices  73.3 us (40%)
  Pallas kernels  63 us (35%)
  starting transfers between devices  27.5 us (15%)
  local copies, waits for them, and re-layouts  10.7 us (6%)
  matrix products  5.33 us (3%)
    ppermute x25, waiting for transfers between devices, swap(): return lax.ppermute(x, axis, [(i, i ^ bit) for i in range(n)])  52.4 us
    pallas_call x2, Pallas kernels, feature_sums(): pl.pallas_call(functools.partial(features_kernel, masks, last, *totals),...  42.6 us
    ppermute x25, starting transfers between devices, swap(): return lax.ppermute(x, axis, [(i, i ^ bit) for i in range(n)])  23 us
    all_to_all x1, waiting for transfers between devices, eight_by_four(): feat_grad = lax.all_to_all(feat_grad, 'rec', 0, 0, tiled=True)  20.8 us
    pallas_call x1, Pallas kernels, image_grads(): pl.pallas_call(image_kernel, grid_spec=spec, out_shape=[jax.ShapeDtypeStr...  9.5 us
    unnamed x28, local copies, waits for them, and re-layouts  6.92 us
    all_to_all x1, starting transfers between devices, eight_by_four(): feat_grad = lax.all_to_all(feat_grad, 'rec', 0, 0, tiled=True)  4.46 us
  transfers between devices with their start and end apart: 26, of which 19 were waited for; matrix products, arithmetic and copies ran while one was open for 3% of the time, Pallas kernels for 25%

profile of v8, /device:TPU:0, one launch (start us, length us, event | category | flops | bytes accessed | tf_op | source)
XLA Modules:
  0.0 181.5 jit_solution(9686606045904537334)
XLA Ops:
  0.7 1.2 copy-done
  1.9 1.0 fusion.12
  2.9 2.9 %fusion.4.refs_0_.image = bf16[128,768]{1,0:T(8,128)(2,1)S(1)} fusion(bf16[2048,768]{1,0:T(8,128)(2,1)} %w_ref.3, f32[128,2048]{1,0:T(8,128)S(1)} %fusion.12, bf16[128,128]{1,0:T(8,128)(2,1)} %param.15, bf16[128,2048]{1,0:T(8,128)(2,1)} %param.17), kind=kOutput, calls=%fused_computation.5 | convolution fusion | flops 470646784 | bytes 4947968 | tf_op jit(solution)/shard_map/dot_general | solution.py:721
  5.8 3.0 %collective-permute-start = (bf16[128,768]{1,0:T(8,128)(2,1)S(1)}, bf16[128,768]{1,0:T(8,128)(2,1)S(1)}, u32[]{:S(2)}, u32[]{:S(2)}) collective-permute-start(bf16[128,768]{1,0:T(8,128)(2,1)S(1)} %fusion.4.refs_0_.image), channel_id=1, source_target_pairs={{0,2},{1,3},{2,0},{3,1},{4,6},{5,7},{6,4},{7,5},{8,10},{9,11},{10,... | collective-permute-start | bytes 589832 | tf_op jit(solution)/shard_map/ppermute | solution.py:102
  8.9 2.7 %collective-permute-start.1 = (bf16[1,144,128]{2,0,1:T(2,128)(2,1)S(1)}, bf16[1,144,128]{2,0,1:T(2,128)(2,1)S(1)}, u32[]{:S(2)}, u32[]{:S(2)}) collective-permute-start(bf16[1,144,128]{2,0,1:T(2,128)(2,1)S(1)} %copy.15), channel_id=1, source_target_pairs={{0,16},{4,20},{8,24},{12,28},{16,0},{20,4},{24,8},{28,12},{1,17},{... | collective-permute-start | bytes 110600 | tf_op jit(solution)/shard_map/ppermute | solution.py:102
  11.6 3.8 %collective-permute-done.1 = bf16[1,144,128]{2,0,1:T(2,128)(2,1)S(1)} collective-permute-done((bf16[1,144,128]{2,0,1:T(2,128)(2,1)S(1)}, bf16[1,144,128]{2,0,1:T(2,128)(2,1)S(1)}, u32[]{:S(2)}, u32[]{:S(2)}) %collective-permute-start.1) | collective-permute-done | bytes 36896 | tf_op jit(solution)/shard_map/ppermute | solution.py:102
  16.8 29.2 %shard_map.112 = (bf16[2,2,128,512]{3,2,1,0:T(8,128)(2,1)S(1)}, f32[2,128,512]{2,1,0:T(8,128)S(1)}, bf16[2,2,128,512]{3,2,1,0:T(8,128)(2,1)S(1)}, f32[2,128,512]...) custom-call(s32[6]{0:T(128)S(1)} %stack.27.me_ref.refs_6_, ...), custom_call_target="tpu_custom_call" | custom-call | flops 18320719872 | bytes 18874368 | tf_op jit(solution)/shard_map/pallas_call | solution.py:381
  46.1 1.5 collective-permute-start.5
  47.6 1.0 collective-permute-start.6
  48.6 1.1 copy-done.5
  49.7 13.4 %shard_map.113 = (f32[2,128,512]{2,1,0:T(8,128)S(1)}, f32[2,128,512]{2,1,0:T(8,128)S(1)}, f32[4,2,128,512]{3,2,1,0:T(8,128)}, f32[8,128]{1,0:T(8,128)S(1)}) custom-call(s32[6]{0:T(128)S(1)} %stack.27.me_ref.refs_6_, s32[1,1536]{1,0:T(1,128)S(1)} %reshape.61.real_labels_ref, s32[1,128]{1,0:T(1,128)S(1)} %bitcast.32, ...), custom_call_target="tpu_custom_call", output_to_operand_aliasing={{2}: (7, {})} | custom-call | flops 6106906624 | bytes 12582912 | tf_op jit(solution)/shard_map/pallas_call | solution.py:381
  63.2 0.8 copy-done.6
  64.0 0.9 shard_map.114
  64.8 1.1 collective-permute-start.7
  66.5 1.2 constant_dynamic-slice_fusion
  67.7 5.2 %collective-permute-done.7.ga = bf16[2,128,512]{2,1,0:T(8,128)(2,1)S(1)} collective-permute-done((bf16[2,128,512]{2,1,0:T(8,128)(2,1)}, bf16[2,128,512]{2,1,0:T(8,128)(2,1)S(1)}, u32[]{:S(2)}, u32[]{:S(2)}) %collective-permute-start.7) | collective-permute-done | bytes 262176 | tf_op jit(solution)/shard_map/ppermute | solution.py:102
  73.6 1.0 copy-done.7
  75.4 2.9 %collective-permute-start.10 = (bf16[256,512]{1,0:T(8,128)(2,1)S(1)}, bf16[256,512]{1,0:T(8,128)(2,1)S(1)}, u32[]{:S(2)}, u32[]{:S(2)}) collective-permute-start(bf16[256,512]{1,0:T(8,128)(2,1)S(1)} %get-tuple-element.76), channel_id=1, source_target_pairs={{0,16},{4,20},{8,24},{12,28},{16,0},{20,4},{24,8},{28,12},{1,17},{... | collective-permute-start | bytes 786440 | tf_op jit(solution)/shard_map/ppermute | solution.py:102
  79.1 4.6 %collective-permute-done.9 = bf16[4,144,128]{2,0,1:T(4,128)(2,1)S(1)} collective-permute-done((bf16[4,144,128]{2,0,1:T(4,128)(2,1)S(1)}, bf16[4,144,128]{2,0,1:T(4,128)(2,1)S(1)}, u32[]{:S(2)}, u32[]{:S(2)}) %collective-permute-start.9) | collective-permute-done | bytes 147488 | tf_op jit(solution)/shard_map/ppermute | solution.py:102
  83.7 5.2 %collective-permute-done.10.got_ref = bf16[256,512]{1,0:T(8,128)(2,1)S(1)} collective-permute-done((bf16[256,512]{1,0:T(8,128)(2,1)S(1)}, bf16[256,512]{1,0:T(8,128)(2,1)S(1)}, u32[]{:S(2)}, u32[]{:S(2)}) %collective-permute-start.10) | collective-permute-done | bytes 262176 | tf_op jit(solution)/shard_map/ppermute | solution.py:102
  88.8 2.1 %shard_map.116 = bf16[8,128,512]{2,1,0:T(8,128)(2,1)} custom-call(s32[6]{0:T(128)S(1)} %stack.27.me_ref.refs_6_, f32[256,512]{1,0:T(8,128)S(1)} %get-tuple-element.75.keep_ref, bf16[256,512]{1,0:T(8,128)(2,1)S(1)} %collective-permute-done.10.got_ref, f32[256,512]{1,0:T(8,128)S(1)} %bitcast.30, s32[8,128]{1,0:T(8,128)S(1)} %get-tuple-element.91.labels_ref, ...), custom_call_target="tpu_custom_call" | custom-call | flops 268435456 | bytes 3145728 | tf_op jit(solution)/shard_map/pallas_call | solution.py:464
  90.9 4.5 %all-to-all-start = ((bf16[8,128,512]{2,1,0:T(8,128)(2,1)}), bf16[8,128,512]{2,1,0:T(8,128)(2,1)}, u32[]{:S(2)}, u32[]{:S(2)}) async-start(bf16[8,128,512]{2,1,0:T(8,128)(2,1)} %shard_map.116), calls=%async_computation | async-start | bytes 2097152 | tf_op jit(solution)/shard_map/all_to_all | solution.py:771
  95.4 1.5 constant_dynamic-slice_fusion.2
  98.7 1.4 maximum_convert_fusion
  100.1 20.8 %all-to-all-done.rows_ref = bf16[8,128,512]{2,1,0:T(8,128)(2,1)} async-done(((bf16[8,128,512]{2,1,0:T(8,128)(2,1)}), bf16[8,128,512]{2,1,0:T(8,128)(2,1)}, u32[]{:S(2)}, u32[]{:S(2)}) %all-to-all-start) | async-done | bytes 1048608 | tf_op jit(solution)/shard_map/all_to_all | solution.py:771
  121.0 9.5 %shard_map.117 = (bf16[2,768,128]{2,1,0:T(8,128)(2,1)S(1)}, f32[2,768,128]{2,1,0:T(8,128)}) custom-call(s32[6]{0:T(128)S(1)} %stack.27.me_ref.refs_6_, f32[4,2,128,512]{3,2,1,0:T(8,128)} %get-tuple-element.74.wave_ref, bf16[8,128,512]{2,1,0:T(8,128)(2,1)} %all-to-all-done.rows_ref, bf16[3072,2048]{1,0:T(8,128)(2,1)} %freq_ref.1, ...), custom_call_target="tpu_custom_call" | custom-call | flops 1610612736 | bytes 12582912 | tf_op jit(solution)/shard_map/pallas_call | solution.py:524
  130.5 1.7 collective-permute-done.11.got_s.got_k
  132.2 1.1 copy-done.3
  134.6 6.4 %collective-permute-done.12.got = bf16[768,128]{1,0:T(8,128)(2,1)S(1)} collective-permute-done((bf16[768,128]{1,0:T(8,128)(2,1)S(1)}, bf16[768,128]{1,0:T(8,128)(2,1)S(1)}, u32[]{:S(2)}, u32[]{:S(2)}) %collective-permute-start.12) | collective-permute-done | bytes 196640 | tf_op jit(solution)/shard_map/ppermute | solution.py:102
  141.2 1.9 %collective-permute-start.14 = (bf16[128,768]{1,0:T(8,128)(2,1)S(1)}, bf16[128,768]{1,0:T(8,128)(2,1)S(1)}, u32[]{:S(2)}, u32[]{:S(2)}) collective-permute-start(bf16[128,768]{1,0:T(8,128)(2,1)S(1)} %shard_map.119.refs_0_), channel_id=1, source_target_pairs={{0,8},{4,12},{8,0},{12,4},{16,24},{20,28},{24,16},{28,20},{1,9},{5... | collective-permute-start | bytes 589832 | tf_op jit(solution)/shard_map/ppermute | solution.py:102
  143.2 1.5 collective-permute-start.15
  144.7 7.0 %collective-permute-done.13.refs_1_.refs_0_ = bf16[128,768]{1,0:T(8,128)(2,1)S(1)} collective-permute-done((bf16[128,768]{1,0:T(8,128)(2,1)S(1)}, bf16[128,768]{1,0:T(8,128)(2,1)S(1)}, u32[]{:S(2)}, u32[]{:S(2)}) %collective-permute-start.13) | collective-permute-done | bytes 196640 | tf_op jit(solution)/shard_map/ppermute | solution.py:102
  151.9 1.4 collective-permute-start.17
  153.9 4.5 %collective-permute-done.16.refs_3_.refs_2_ = bf16[128,768]{1,0:T(8,128)(2,1)S(1)} collective-permute-done((bf16[128,768]{1,0:T(8,128)(2,1)S(1)}, bf16[128,768]{1,0:T(8,128)(2,1)S(1)}, u32[]{:S(2)}, u32[]{:S(2)}) %collective-permute-start.16) | collective-permute-done | bytes 196640 | tf_op jit(solution)/shard_map/ppermute | solution.py:102
  158.4 1.1 collective-permute-start.19
  159.7 4.2 %collective-permute-done.18.refs_6_.refs_3_ = bf16[128,768]{1,0:T(8,128)(2,1)S(1)} collective-permute-done((bf16[128,768]{1,0:T(8,128)(2,1)S(1)}, bf16[128,768]{1,0:T(8,128)(2,1)S(1)}, u32[]{:S(2)}, u32[]{:S(2)}) %collective-permute-start.18) | collective-permute-done | bytes 196640 | tf_op jit(solution)/shard_map/ppermute | solution.py:102
  163.9 1.1 shard_map.121
  165.1 1.3 collective-permute-done.20.b
  166.9 1.1 shard_map.123
  168.7 0.7 collective-permute-done.22.b
  169.5 0.8 collective-permute-start.23
  170.3 2.4 %shard_map.120.after = f32[256,768]{1,0:T(8,128)} custom-call(s32[6]{0:T(128)S(1)} %stack.27.me_ref.refs_6_, bf16[256,1024]{1,0:T(8,128)(2,1)S(1)} %get-tuple-element.93.b.hidden_ref, bf16[128,768]{1,0:T(8,128)(2,1)S(1)} %shard_map.119.refs_0_, bf16[128,768]{1,0:T(8,128)(2,1)S(1)} %collective-permute-done.13.refs_1_.refs_0_, ...), custom_call_target="tpu_custom_call" | custom-call | flops 402653184 | bytes 4194304 | tf_op jit(solution)/shard_map/pallas_call | solution.py:634
  172.7 1.8 collective-permute-done.21.q0
  174.5 2.4 %collective-permute-done.23.q1 = bf16[2,256,128]{2,1,0:T(8,128)(2,1)S(1)} collective-permute-done((bf16[2,256,128]{2,1,0:T(8,128)(2,1)S(1)}, bf16[2,256,128]{2,1,0:T(8,128)(2,1)S(1)}, u32[]{:S(2)}, u32[]{:S(2)}) %collective-permute-start.23) | collective-permute-done | bytes 131104 | tf_op jit(solution)/shard_map/ppermute | solution.py:102
  176.8 1.1 copy-done.4
  178.0 0.9 shard_map.125.own
  179.0 1.7 collective-permute-done.24.other
  180.7 0.8 shard_map.126
  (67 shorter events, 9.9 us)
Async XLA Ops:
  0.6 1.2 copy-start
  0.6 8.2 %copy-start.8 = (s32[128]{0:T(128)S(1)}, s32[128]{0:T(128)}, u32[]{:S(2)}) copy-start(s32[128]{0:T(128)} %param.16) | copy-start | bytes 1540
  0.7 8.2 %copy-start.11 = (bf16[128,128]{1,0:T(8,128)(2,1)S(1)}, bf16[128,128]{1,0:T(8,128)(2,1)}, u32[]{:S(2)}) copy-start(bf16[128,128]{1,0:T(8,128)(2,1)} %param.15) | copy-start | bytes 98308
  2.9 13.4 %copy-start.12 = (s32[1536]{0:T(1024)S(1)}, s32[1536]{0:T(1024)}, u32[]{:S(2)}) copy-start(s32[1536]{0:T(1024)} %param.12) | copy-start | bytes 18436
  5.8 9.6 %collective-permute-start = (bf16[128,768]{1,0:T(8,128)(2,1)S(1)}, bf16[128,768]{1,0:T(8,128)(2,1)S(1)}, u32[]{:S(2)}, u32[]{:S(2)}) collective-permute-start(bf16[128,768]{1,0:T(8,128)(2,1)S(1)} %fusion.4.refs_0_.image), channel_id=1, source_target_pairs={{0,2},{1,3},{2,0},{3,1},{4,6},{5,7},{6,4},{7,5},{8,10},{9,11},{10,... | collective-permute-start | bytes 589832 | tf_op jit(solution)/shard_map/ppermute | solution.py:102
  8.9 6.5 %collective-permute-start.1 = (bf16[1,144,128]{2,0,1:T(2,128)(2,1)S(1)}, bf16[1,144,128]{2,0,1:T(2,128)(2,1)S(1)}, u32[]{:S(2)}, u32[]{:S(2)}) collective-permute-start(bf16[1,144,128]{2,0,1:T(2,128)(2,1)S(1)} %copy.15), channel_id=1, source_target_pairs={{0,16},{4,20},{8,24},{12,28},{16,0},{20,4},{24,8},{28,12},{1,17},{... | collective-permute-start | bytes 110600 | tf_op jit(solution)/shard_map/ppermute | solution.py:102
  11.6 4.7 %collective-permute-start.3 = (bf16[128,768]{1,0:T(8,128)(2,1)S(1)}, bf16[128,768]{1,0:T(8,128)(2,1)S(1)}, u32[]{:S(2)}, u32[]{:S(2)}) collective-permute-start(bf16[128,768]{1,0:T(8,128)(2,1)S(1)} %fusion.4.refs_0_.image), channel_id=1, source_target_pairs={{0,1},{1,0},{2,3},{3,2},{4,5},{5,4},{6,7},{7,6},{8,9},{9,8},{10,11... | collective-permute-start | bytes 589832 | tf_op jit(solution)/shard_map/ppermute | solution.py:102
  15.4 1.4 collective-permute-start.4
  15.7 30.4 %collective-permute-start.2 = (bf16[2,144,128]{2,0,1:T(2,128)(2,1)S(1)}, bf16[2,144,128]{2,0,1:T(2,128)(2,1)S(1)}, u32[]{:S(2)}, u32[]{:S(2)}) collective-permute-start(bf16[2,144,128]{2,0,1:T(2,128)(2,1)S(1)} %pad_maximum_fusion.4), channel_id=1, source_target_pairs={{0,8},{4,12},{8,0},{12,4},{16,24},{20,28},{24,16},{28,20},{1,9},{5... | collective-permute-start | bytes 221192 | tf_op jit(solution)/shard_map/ppermute | solution.py:102
  46.1 17.9 %collective-permute-start.5 = (bf16[2,2,128,512]{3,2,1,0:T(8,128)(2,1)S(1)}, bf16[2,2,128,512]{3,2,1,0:T(8,128)(2,1)S(1)}, u32[]{:S(2)}, u32[]{:S(2)}) collective-permute-start(bf16[2,2,128,512]{3,2,1,0:T(8,128)(2,1)S(1)} %get-tuple-element.63), channel_id=1, source_target_pairs={{0,4},{4,0},{8,12},{12,8},{16,20},{20,16},{24,28},{28,24},{1,5},{5... | collective-permute-start | bytes 1572872 | tf_op jit(solution)/shard_map/ppermute | solution.py:102
  47.6 16.3 %collective-permute-start.6 = (bf16[2,2,128,512]{3,2,1,0:T(8,128)(2,1)S(1)}, bf16[2,2,128,512]{3,2,1,0:T(8,128)(2,1)S(1)}, u32[]{:S(2)}, u32[]{:S(2)}) collective-permute-start(bf16[2,2,128,512]{3,2,1,0:T(8,128)(2,1)S(1)} %get-tuple-element.66), channel_id=1, source_target_pairs={{0,8},{4,12},{8,0},{12,4},{16,24},{20,28},{24,16},{28,20},{1,9},{5... | collective-permute-start | bytes 1572872 | tf_op jit(solution)/shard_map/ppermute | solution.py:102
  48.6 1.1 copy-start.5
  63.2 0.8 copy-start.6
  64.8 8.1 %collective-permute-start.7 = (bf16[2,128,512]{2,1,0:T(8,128)(2,1)}, bf16[2,128,512]{2,1,0:T(8,128)(2,1)S(1)}, u32[]{:S(2)}, u32[]{:S(2)}) collective-permute-start(bf16[2,128,512]{2,1,0:T(8,128)(2,1)} %get-tuple-element.68), channel_id=1, source_target_pairs={{0,8},{4,12},{8,0},{12,4},{16,24},{20,28},{24,16},{28,20},{1,9},{5... | collective-permute-start | bytes 786440 | tf_op jit(solution)/shard_map/ppermute | solution.py:102
  65.9 7.7 %collective-permute-start.8 = (bf16[2,128,512]{2,1,0:T(8,128)(2,1)}, bf16[2,128,512]{2,1,0:T(8,128)(2,1)S(1)}, u32[]{:S(2)}, u32[]{:S(2)}) collective-permute-start(bf16[2,128,512]{2,1,0:T(8,128)(2,1)} %get-tuple-element.70), channel_id=1, source_target_pairs={{0,4},{4,0},{8,12},{12,8},{16,20},{20,16},{24,28},{28,24},{1,5},{5... | collective-permute-start | bytes 786440 | tf_op jit(solution)/shard_map/ppermute | solution.py:102
  73.6 1.0 copy-start.7
  75.4 13.5 %collective-permute-start.10 = (bf16[256,512]{1,0:T(8,128)(2,1)S(1)}, bf16[256,512]{1,0:T(8,128)(2,1)S(1)}, u32[]{:S(2)}, u32[]{:S(2)}) collective-permute-start(bf16[256,512]{1,0:T(8,128)(2,1)S(1)} %get-tuple-element.76), channel_id=1, source_target_pairs={{0,16},{4,20},{8,24},{12,28},{16,0},{20,4},{24,8},{28,12},{1,17},{... | collective-permute-start | bytes 786440 | tf_op jit(solution)/shard_map/ppermute | solution.py:102
  78.4 5.2 %collective-permute-start.9 = (bf16[4,144,128]{2,0,1:T(4,128)(2,1)S(1)}, bf16[4,144,128]{2,0,1:T(4,128)(2,1)S(1)}, u32[]{:S(2)}, u32[]{:S(2)}) collective-permute-start(bf16[4,144,128]{2,0,1:T(4,128)(2,1)S(1)} %pad_maximum_fusion.3), channel_id=1, source_target_pairs={{0,4},{4,0},{8,12},{12,8},{16,20},{20,16},{24,28},{28,24},{1,5},{5... | collective-permute-start | bytes 442376 | tf_op jit(solution)/shard_map/ppermute | solution.py:102
  90.9 30.1 %all-to-all-start = ((bf16[8,128,512]{2,1,0:T(8,128)(2,1)}), bf16[8,128,512]{2,1,0:T(8,128)(2,1)}, u32[]{:S(2)}, u32[]{:S(2)}) async-start(bf16[8,128,512]{2,1,0:T(8,128)(2,1)} %shard_map.116), calls=%async_computation | async-start | bytes 2097152 | tf_op jit(solution)/shard_map/all_to_all | solution.py:771
  97.8 0.9 copy-start.9
  97.8 0.9 copy-start.10
  130.5 33.4 %copy-start.1 = (bf16[2048,768]{1,0:T(8,128)(2,1)S(1)}, bf16[2048,768]{1,0:T(8,128)(2,1)}, u32[]{:S(2)}) copy-start(bf16[2048,768]{1,0:T(8,128)(2,1)} %w_ref.3) | copy-start | bytes 9437188
  130.5 1.7 collective-permute-start.11
  132.2 1.1 copy-start.3
  134.0 7.0 %collective-permute-start.12 = (bf16[768,128]{1,0:T(8,128)(2,1)S(1)}, bf16[768,128]{1,0:T(8,128)(2,1)S(1)}, u32[]{:S(2)}, u32[]{:S(2)}) collective-permute-start(bf16[768,128]{1,0:T(8,128)(2,1)S(1)} %get-tuple-element.81), channel_id=1, source_target_pairs={{0,2},{1,3},{2,0},{3,1},{4,6},{5,7},{6,4},{7,5},{8,10},{9,11},{10,... | collective-permute-start | bytes 589832 | tf_op jit(solution)/shard_map/ppermute | solution.py:102
  141.2 10.5 %collective-permute-start.13 = (bf16[128,768]{1,0:T(8,128)(2,1)S(1)}, bf16[128,768]{1,0:T(8,128)(2,1)S(1)}, u32[]{:S(2)}, u32[]{:S(2)}) collective-permute-start(bf16[128,768]{1,0:T(8,128)(2,1)S(1)} %shard_map.119.refs_0_), channel_id=1, source_target_pairs={{0,16},{4,20},{8,24},{12,28},{16,0},{20,4},{24,8},{28,12},{1,17},{... | collective-permute-start | bytes 589832 | tf_op jit(solution)/shard_map/ppermute | solution.py:102
  141.2 10.4 %collective-permute-start.14 = (bf16[128,768]{1,0:T(8,128)(2,1)S(1)}, bf16[128,768]{1,0:T(8,128)(2,1)S(1)}, u32[]{:S(2)}, u32[]{:S(2)}) collective-permute-start(bf16[128,768]{1,0:T(8,128)(2,1)S(1)} %shard_map.119.refs_0_), channel_id=1, source_target_pairs={{0,8},{4,12},{8,0},{12,4},{16,24},{20,28},{24,16},{28,20},{1,9},{5... | collective-permute-start | bytes 589832 | tf_op jit(solution)/shard_map/ppermute | solution.py:102
  143.2 8.5 %collective-permute-start.15 = (bf16[128,768]{1,0:T(8,128)(2,1)S(1)}, bf16[128,768]{1,0:T(8,128)(2,1)S(1)}, u32[]{:S(2)}, u32[]{:S(2)}) collective-permute-start(bf16[128,768]{1,0:T(8,128)(2,1)S(1)} %shard_map.119.refs_0_), channel_id=1, source_target_pairs={{0,4},{4,0},{8,12},{12,8},{16,20},{20,16},{24,28},{28,24},{1,5},{5... | collective-permute-start | bytes 589832 | tf_op jit(solution)/shard_map/ppermute | solution.py:102
  151.6 6.8 %collective-permute-start.16 = (bf16[128,768]{1,0:T(8,128)(2,1)S(1)}, bf16[128,768]{1,0:T(8,128)(2,1)S(1)}, u32[]{:S(2)}, u32[]{:S(2)}) collective-permute-start(bf16[128,768]{1,0:T(8,128)(2,1)S(1)} %collective-permute-done.13.refs_1_.refs_0_), channel_id=1, source_target_pairs={{0,8},{4,12},{8,0},{12,4},{16,24},{20,28},{24,16},{28,20},{1,9},{5... | collective-permute-start | bytes 589832 | tf_op jit(solution)/shard_map/ppermute | solution.py:102
  151.9 7.8 %collective-permute-start.17 = (bf16[128,768]{1,0:T(8,128)(2,1)S(1)}, bf16[128,768]{1,0:T(8,128)(2,1)S(1)}, u32[]{:S(2)}, u32[]{:S(2)}) collective-permute-start(bf16[128,768]{1,0:T(8,128)(2,1)S(1)} %collective-permute-done.13.refs_1_.refs_0_), channel_id=1, source_target_pairs={{0,4},{4,0},{8,12},{12,8},{16,20},{20,16},{24,28},{28,24},{1,5},{5... | collective-permute-start | bytes 589832 | tf_op jit(solution)/shard_map/ppermute | solution.py:102
  153.3 10.6 %collective-permute-start.18 = (bf16[128,768]{1,0:T(8,128)(2,1)S(1)}, bf16[128,768]{1,0:T(8,128)(2,1)S(1)}, u32[]{:S(2)}, u32[]{:S(2)}) collective-permute-start(bf16[128,768]{1,0:T(8,128)(2,1)S(1)} %collective-permute-done.14.refs_2_), channel_id=1, source_target_pairs={{0,4},{4,0},{8,12},{12,8},{16,20},{20,16},{24,28},{28,24},{1,5},{5... | collective-permute-start | bytes 589832 | tf_op jit(solution)/shard_map/ppermute | solution.py:102
  158.4 8.5 %collective-permute-start.19 = (bf16[128,768]{1,0:T(8,128)(2,1)S(1)}, bf16[128,768]{1,0:T(8,128)(2,1)S(1)}, u32[]{:S(2)}, u32[]{:S(2)}) collective-permute-start(bf16[128,768]{1,0:T(8,128)(2,1)S(1)} %collective-permute-done.16.refs_3_.refs_2_), channel_id=1, source_target_pairs={{0,4},{4,0},{8,12},{12,8},{16,20},{20,16},{24,28},{28,24},{1,5},{5... | collective-permute-start | bytes 589832 | tf_op jit(solution)/shard_map/ppermute | solution.py:102
  165.0 1.4 collective-permute-start.20
  166.5 10.4 %copy-start.2 = (f32[256,1024]{1,0:T(8,128)S(1)}, f32[256,1024]{1,0:T(8,128)}, u32[]{:S(2)}) copy-start(f32[256,1024]{1,0:T(8,128)} %get-tuple-element.94.a.preact_ref) | copy-start | bytes 3145732
  168.0 1.4 collective-permute-start.22
  168.1 6.4 %collective-permute-start.21 = (bf16[2,256,128]{2,1,0:T(8,128)(2,1)S(1)}, bf16[2,256,128]{2,1,0:T(8,128)(2,1)S(1)}, u32[]{:S(2)}, u32[]{:S(2)}) collective-permute-start(bf16[2,256,128]{2,1,0:T(8,128)(2,1)S(1)} %shard_map.122.refs_4_.p0), channel_id=1, source_target_pairs={{0,2},{1,3},{2,0},{3,1},{4,6},{5,7},{6,4},{7,5},{8,10},{9,11},{10,... | collective-permute-start | bytes 393224 | tf_op jit(solution)/shard_map/ppermute | solution.py:102
  169.5 7.4 %collective-permute-start.23 = (bf16[2,256,128]{2,1,0:T(8,128)(2,1)S(1)}, bf16[2,256,128]{2,1,0:T(8,128)(2,1)S(1)}, u32[]{:S(2)}, u32[]{:S(2)}) collective-permute-start(bf16[2,256,128]{2,1,0:T(8,128)(2,1)S(1)} %shard_map.124.p1), channel_id=1, source_target_pairs={{0,2},{1,3},{2,0},{3,1},{4,6},{5,7},{6,4},{7,5},{8,10},{9,11},{10,... | collective-permute-start | bytes 393224 | tf_op jit(solution)/shard_map/ppermute | solution.py:102
  176.8 1.1 copy-start.4
  178.9 1.8 collective-permute-start.24

commit v9 on v8

--- a/solution.py
+++ b/solution.py
@@ -611,9 +611,10 @@
 
 
 def weight_kernel(me_ref, hidden_ref, *refs):
-    out_ref = refs[-1]
+    out_ref, token = refs[-2:]
+    token[...] = jnp.zeros_like(token)
     acc = None
-    for mask, grad in enumerate(refs[:-1]):
+    for mask, grad in enumerate(refs[:-2]):
         rows = grad.shape[0]
         at = slice(mask * rows, (mask + 1) * rows)
         d = jnp.dot(hidden_ref[:, at], grad[...], preferred_element_type=F32)
@@ -629,12 +630,12 @@
         grid=(1,),
         in_specs=[block((mine, total), lambda h, me: (0, 0))]
         + [block((rows, cols), lambda h, me: (0, 0)) for _ in grads],
-        out_specs=block((mine, cols), lambda h, me: (0, 0)),
+        out_specs=[block((mine, cols), lambda h, me: (0, 0)), block((8, 128), lambda h, me: (0, 0))],
     )
     return pl.pallas_call(
         weight_kernel,
         grid_spec=spec,
-        out_shape=pltpu.HBM((mine, cols), F32),
+        out_shape=[pltpu.HBM((mine, cols), F32), jax.ShapeDtypeStruct((8, 128), F32)],
         compiler_params=pltpu.CompilerParams(vmem_limit_bytes=12 * 2**20),
         cost_estimate=pl.CostEstimate(
             flops=2 * mine * total * cols, bytes_accessed=4 * 2**20, transcendentals=0
@@ -642,7 +643,7 @@
     )(me, hidden, *grads)
 
 
-def last_kernel(me_ref, preact_ref, lhs_ref, p0, q0, p1, q1, after, out_ref):
+def last_kernel(me_ref, gate_ref, lhs_ref, p0, q0, p1, q1, after, out_ref):
     rows = p0.shape[2]
     acc = None
     for h, (p, q) in enumerate(((p0, q0), (p1, q1))):
@@ -650,16 +651,16 @@
             place = 4 * (me_ref[0] % 2) + 2 * i + h
             at = pl.ds(pl.multiple_of(place * rows, 128), rows)
             grad = p[i].astype(F32) + q[i].astype(F32)
-            grad = jnp.where(preact_ref[:, at] > 0, grad, 0.0).astype(BF)
+            grad = jnp.where(gate_ref[:, at].astype(F32) > 0, grad, 0.0).astype(BF)
             d = lax.dot_general(lhs_ref[:, at], grad, NT, preferred_element_type=F32)
             acc = d if acc is None else acc + d
     out_ref[...] = acc
 
 
-def last_grads(me, preact, lhs, parts, after):
+def last_grads(me, gate, lhs, parts, after):
     count, total = lhs.shape
-    mine = preact.shape[0]
-    args = (preact, lhs, *parts)
+    mine = gate.shape[0]
+    args = (gate, lhs, *parts)
     whole = lambda shape: block(shape, lambda h, me: (0,) * len(shape))
     spec = pltpu.PrefetchScalarGridSpec(
         num_scalar_prefetch=1,
@@ -766,12 +767,13 @@
     )
     all_preact = lax.dot_general(w, lhs, (((0,), (0,)), ((), ())), preferred_element_type=F32)
     all_hidden = jnp.maximum(all_preact, 0.0).astype(BF)
+    gate = (all_preact > 0).astype(BF)
 
     feat_grad = gap_rows(me, keep, got, noise, all_labels.reshape(groups, rows), real_total, order, token)
     feat_grad = lax.all_to_all(feat_grad, "rec", 0, 0, tiled=True)
 
     send, keep = image_grads(
-        me, waves, feat_grad, frequencies, cols, (all_preact, all_hidden, lhs)
+        me, waves, feat_grad, frequencies, cols, (gate, all_hidden, lhs)
     )
     send, keep = split_y(me, keep, swap(send, "feat", 1))
     out_grad = out_grads(keep, swap(send, "feat", 2), own)
@@ -780,7 +782,7 @@
     by[4] = swap(out_grad, "rec", 4)
     by[2] = swap(out_grad, "rec", 2)
     by[1] = swap(out_grad, "rec", 1)
-    by[4], (by[2], by[1]) = tie(by[4], (by[2], by[1]))
+    by[2], by[1] = tie(by[2], by[1])
     by[3] = swap(by[2], "rec", 1)
     by[6] = swap(by[4], "rec", 2)
     by[5] = swap(by[4], "rec", 1)
@@ -793,8 +795,8 @@
     send, keep = hidden_grads(me, w_out, [by[i] for i in range(4)], mine, by[5])
     parts = reduced(send, keep)
     parts += reduced(*hidden_grads(me, w_out, [by[4 + i] for i in range(4)], mine, parts[0]))
-    grad_w_out = weight_grads(me, all_hidden, [by[mask] for mask in order])
-    grads = last_grads(me, all_preact, lhs, parts, grad_w_out)
+    grad_w_out, token = weight_grads(me, all_hidden, [by[mask] for mask in order])
+    grads = last_grads(me, gate, lhs, parts, token)
     grad_w_latent, grad_embed = outputs(grads, swap(grads, "feat", 1), dz)
     return grad_w_out, grad_w_latent, grad_embed
 

time: 182 us -> 180 us (0.989)
  local copies, waits for them, and re-layouts: 10.7 us -> 6.07 us
  waiting for transfers between devices: 73.3 us -> 75.2 us
    unnamed x28 -> x18, local copies, waits for them, and re-layouts: 6.92 us -> 3.57 us
  transfers between devices with their start and end apart: 26 -> 26, of which waited for: 19 -> 18; matrix products, arithmetic and copies ran while one was open for 3% -> 3% of each run, Pallas kernels for 25% -> 26%
where the time goes in v9:
time: 180 us
  waiting for transfers between devices  75.2 us (42%)
  Pallas kernels  64 us (36%)
  starting transfers between devices  27.2 us (15%)
  local copies, waits for them, and re-layouts  6.07 us (3%)
  matrix products  4.34 us (2%)
    ppermute x25, waiting for transfers between devices, swap(): return lax.ppermute(x, axis, [(i, i ^ bit) for i in range(n)])  52.8 us
    pallas_call x2, Pallas kernels, feature_sums(): pl.pallas_call(functools.partial(features_kernel, masks, last, *totals),...  42.6 us
    ppermute x25, starting transfers between devices, swap(): return lax.ppermute(x, axis, [(i, i ^ bit) for i in range(n)])  22.8 us
    all_to_all x1, waiting for transfers between devices, eight_by_four(): feat_grad = lax.all_to_all(feat_grad, 'rec', 0, 0, tiled=True)  22.5 us
    pallas_call x1, Pallas kernels, image_grads(): pl.pallas_call(image_kernel, grid_spec=spec, out_shape=[jax.ShapeDtypeStr...  9.51 us
    all_to_all x1, starting transfers between devices, eight_by_four(): feat_grad = lax.all_to_all(feat_grad, 'rec', 0, 0, tiled=True)  4.46 us
  transfers between devices with their start and end apart: 26, of which 18 were waited for; matrix products, arithmetic and copies ran while one was open for 3% of the time, Pallas kernels for 26%

profile of v9, /device:TPU:0, one launch (start us, length us, event | category | flops | bytes accessed | tf_op | source)
XLA Modules:
  0.0 179.7 jit_solution(12528714185243453174)
XLA Ops:
  0.7 1.2 copy-done
  1.9 1.0 fusion.12
  2.9 2.9 %fusion.4.refs_0_.image = bf16[128,768]{1,0:T(8,128)(2,1)S(1)} fusion(bf16[2048,768]{1,0:T(8,128)(2,1)} %w_ref.3, f32[128,2048]{1,0:T(8,128)S(1)} %fusion.12, bf16[128,128]{1,0:T(8,128)(2,1)} %param.15, bf16[128,2048]{1,0:T(8,128)(2,1)} %param.17), kind=kOutput, calls=%fused_computation.5 | convolution fusion | flops 470646784 | bytes 4947968 | tf_op jit(solution)/shard_map/dot_general | solution.py:722
  5.8 3.0 %collective-permute-start = (bf16[128,768]{1,0:T(8,128)(2,1)S(1)}, bf16[128,768]{1,0:T(8,128)(2,1)S(1)}, u32[]{:S(2)}, u32[]{:S(2)}) collective-permute-start(bf16[128,768]{1,0:T(8,128)(2,1)S(1)} %fusion.4.refs_0_.image), channel_id=1, source_target_pairs={{0,2},{1,3},{2,0},{3,1},{4,6},{5,7},{6,4},{7,5},{8,10},{9,11},{10,... | collective-permute-start | bytes 589832 | tf_op jit(solution)/shard_map/ppermute | solution.py:102
  8.9 2.7 %collective-permute-start.1 = (bf16[1,144,128]{2,0,1:T(2,128)(2,1)S(1)}, bf16[1,144,128]{2,0,1:T(2,128)(2,1)S(1)}, u32[]{:S(2)}, u32[]{:S(2)}) collective-permute-start(bf16[1,144,128]{2,0,1:T(2,128)(2,1)S(1)} %copy.15), channel_id=1, source_target_pairs={{0,16},{4,20},{8,24},{12,28},{16,0},{20,4},{24,8},{28,12},{1,17},{... | collective-permute-start | bytes 110600 | tf_op jit(solution)/shard_map/ppermute | solution.py:102
  11.6 3.8 %collective-permute-done.1 = bf16[1,144,128]{2,0,1:T(2,128)(2,1)S(1)} collective-permute-done((bf16[1,144,128]{2,0,1:T(2,128)(2,1)S(1)}, bf16[1,144,128]{2,0,1:T(2,128)(2,1)S(1)}, u32[]{:S(2)}, u32[]{:S(2)}) %collective-permute-start.1) | collective-permute-done | bytes 36896 | tf_op jit(solution)/shard_map/ppermute | solution.py:102
  16.8 29.2 %shard_map.112 = (bf16[2,2,128,512]{3,2,1,0:T(8,128)(2,1)S(1)}, f32[2,128,512]{2,1,0:T(8,128)S(1)}, bf16[2,2,128,512]{3,2,1,0:T(8,128)(2,1)S(1)}, f32[2,128,512]...) custom-call(s32[6]{0:T(128)S(1)} %stack.27.me_ref.refs_6_, ...), custom_call_target="tpu_custom_call" | custom-call | flops 18320719872 | bytes 18874368 | tf_op jit(solution)/shard_map/pallas_call | solution.py:381
  46.1 1.5 collective-permute-start.5
  47.6 1.0 collective-permute-start.6
  48.6 1.1 copy-done.4
  49.7 13.4 %shard_map.113 = (f32[2,128,512]{2,1,0:T(8,128)S(1)}, f32[2,128,512]{2,1,0:T(8,128)S(1)}, f32[4,2,128,512]{3,2,1,0:T(8,128)}, f32[8,128]{1,0:T(8,128)S(1)}) custom-call(s32[6]{0:T(128)S(1)} %stack.27.me_ref.refs_6_, s32[1,1536]{1,0:T(1,128)S(1)} %reshape.61.real_labels_ref, s32[1,128]{1,0:T(1,128)S(1)} %bitcast.32, ...), custom_call_target="tpu_custom_call", output_to_operand_aliasing={{2}: (7, {})} | custom-call | flops 6106906624 | bytes 12582912 | tf_op jit(solution)/shard_map/pallas_call | solution.py:381
  63.1 0.9 shard_map.114
  64.0 1.1 collective-permute-start.7
  65.7 1.2 constant_dynamic-slice_fusion
  66.9 5.3 %collective-permute-done.7.ga = bf16[2,128,512]{2,1,0:T(8,128)(2,1)} collective-permute-done((bf16[2,128,512]{2,1,0:T(8,128)(2,1)}, bf16[2,128,512]{2,1,0:T(8,128)(2,1)}, u32[]{:S(2)}, u32[]{:S(2)}) %collective-permute-start.7) | collective-permute-done | bytes 262176 | tf_op jit(solution)/shard_map/ppermute | solution.py:102
  72.2 0.7 collective-permute-done.8.gb
  72.9 1.7 shard_map.115
  74.6 2.9 %collective-permute-start.10 = (bf16[256,512]{1,0:T(8,128)(2,1)S(1)}, bf16[256,512]{1,0:T(8,128)(2,1)S(1)}, u32[]{:S(2)}, u32[]{:S(2)}) collective-permute-start(bf16[256,512]{1,0:T(8,128)(2,1)S(1)} %get-tuple-element.77), channel_id=1, source_target_pairs={{0,16},{4,20},{8,24},{12,28},{16,0},{20,4},{24,8},{28,12},{1,17},{... | collective-permute-start | bytes 786440 | tf_op jit(solution)/shard_map/ppermute | solution.py:102
  78.3 4.6 %collective-permute-done.9 = bf16[4,144,128]{2,0,1:T(4,128)(2,1)S(1)} collective-permute-done((bf16[4,144,128]{2,0,1:T(4,128)(2,1)S(1)}, bf16[4,144,128]{2,0,1:T(4,128)(2,1)S(1)}, u32[]{:S(2)}, u32[]{:S(2)}) %collective-permute-start.9) | collective-permute-done | bytes 147488 | tf_op jit(solution)/shard_map/ppermute | solution.py:102
  82.9 5.2 %collective-permute-done.10.got_ref = bf16[256,512]{1,0:T(8,128)(2,1)S(1)} collective-permute-done((bf16[256,512]{1,0:T(8,128)(2,1)S(1)}, bf16[256,512]{1,0:T(8,128)(2,1)S(1)}, u32[]{:S(2)}, u32[]{:S(2)}) %collective-permute-start.10) | collective-permute-done | bytes 262176 | tf_op jit(solution)/shard_map/ppermute | solution.py:102
  88.1 2.1 %shard_map.116 = bf16[8,128,512]{2,1,0:T(8,128)(2,1)} custom-call(s32[6]{0:T(128)S(1)} %stack.27.me_ref.refs_6_, f32[256,512]{1,0:T(8,128)S(1)} %get-tuple-element.76.keep_ref, bf16[256,512]{1,0:T(8,128)(2,1)S(1)} %collective-permute-done.10.got_ref, f32[256,512]{1,0:T(8,128)S(1)} %bitcast.30, s32[8,128]{1,0:T(8,128)S(1)} %get-tuple-element.93.labels_ref, ...), custom_call_target="tpu_custom_call" | custom-call | flops 268435456 | bytes 3145728 | tf_op jit(solution)/shard_map/pallas_call | solution.py:464
  90.2 4.5 %all-to-all-start = ((bf16[8,128,512]{2,1,0:T(8,128)(2,1)}), bf16[8,128,512]{2,1,0:T(8,128)(2,1)}, u32[]{:S(2)}, u32[]{:S(2)}) async-start(bf16[8,128,512]{2,1,0:T(8,128)(2,1)} %shard_map.116), calls=%async_computation | async-start | bytes 2097152 | tf_op jit(solution)/shard_map/all_to_all | solution.py:773
  94.6 0.8 constant_dynamic-slice_fusion.2
  96.2 1.0 fusion.7.c.lhs_ref
  97.7 22.5 %all-to-all-done.rows_ref = bf16[8,128,512]{2,1,0:T(8,128)(2,1)} async-done(((bf16[8,128,512]{2,1,0:T(8,128)(2,1)}), bf16[8,128,512]{2,1,0:T(8,128)(2,1)}, u32[]{:S(2)}, u32[]{:S(2)}) %all-to-all-start) | async-done | bytes 1048608 | tf_op jit(solution)/shard_map/all_to_all | solution.py:773
  120.2 9.5 %shard_map.117 = (bf16[2,768,128]{2,1,0:T(8,128)(2,1)S(1)}, f32[2,768,128]{2,1,0:T(8,128)}) custom-call(s32[6]{0:T(128)S(1)} %stack.27.me_ref.refs_6_, f32[4,2,128,512]{3,2,1,0:T(8,128)} %get-tuple-element.75.wave_ref, bf16[8,128,512]{2,1,0:T(8,128)(2,1)} %all-to-all-done.rows_ref, bf16[3072,2048]{1,0:T(8,128)(2,1)} %freq_ref.1, ...), custom_call_target="tpu_custom_call" | custom-call | flops 1610612736 | bytes 12582912 | tf_op jit(solution)/shard_map/pallas_call | solution.py:524
  129.8 1.7 collective-permute-done.11.got_s.got_k
  131.5 1.1 copy-done.3
  133.8 6.5 %collective-permute-done.12.got = bf16[768,128]{1,0:T(8,128)(2,1)S(1)} collective-permute-done((bf16[768,128]{1,0:T(8,128)(2,1)S(1)}, bf16[768,128]{1,0:T(8,128)(2,1)S(1)}, u32[]{:S(2)}, u32[]{:S(2)}) %collective-permute-start.12) | collective-permute-done | bytes 196640 | tf_op jit(solution)/shard_map/ppermute | solution.py:102
  140.5 1.9 %collective-permute-start.14 = (bf16[128,768]{1,0:T(8,128)(2,1)S(1)}, bf16[128,768]{1,0:T(8,128)(2,1)S(1)}, u32[]{:S(2)}, u32[]{:S(2)}) collective-permute-start(bf16[128,768]{1,0:T(8,128)(2,1)S(1)} %shard_map.119.refs_0_), channel_id=1, source_target_pairs={{0,8},{4,12},{8,0},{12,4},{16,24},{20,28},{24,16},{28,20},{1,9},{5... | collective-permute-start | bytes 589832 | tf_op jit(solution)/shard_map/ppermute | solution.py:102
  142.5 1.5 collective-permute-start.15
  143.9 7.0 %collective-permute-done.13.refs_1_.refs_0_ = bf16[128,768]{1,0:T(8,128)(2,1)S(1)} collective-permute-done((bf16[128,768]{1,0:T(8,128)(2,1)S(1)}, bf16[128,768]{1,0:T(8,128)(2,1)S(1)}, u32[]{:S(2)}, u32[]{:S(2)}) %collective-permute-start.13) | collective-permute-done | bytes 196640 | tf_op jit(solution)/shard_map/ppermute | solution.py:102
  150.9 1.4 collective-permute-start.17
  152.4 0.7 collective-permute-start.18
  153.0 4.7 %collective-permute-done.16.refs_3_.refs_2_ = bf16[128,768]{1,0:T(8,128)(2,1)S(1)} collective-permute-done((bf16[128,768]{1,0:T(8,128)(2,1)S(1)}, bf16[128,768]{1,0:T(8,128)(2,1)S(1)}, u32[]{:S(2)}, u32[]{:S(2)}) %collective-permute-start.16) | collective-permute-done | bytes 196640 | tf_op jit(solution)/shard_map/ppermute | solution.py:102
  157.7 1.1 collective-permute-start.19
  158.8 4.1 %collective-permute-done.18.refs_6_.refs_3_ = bf16[128,768]{1,0:T(8,128)(2,1)S(1)} collective-permute-done((bf16[128,768]{1,0:T(8,128)(2,1)S(1)}, bf16[128,768]{1,0:T(8,128)(2,1)S(1)}, u32[]{:S(2)}, u32[]{:S(2)}) %collective-permute-start.18) | collective-permute-done | bytes 196640 | tf_op jit(solution)/shard_map/ppermute | solution.py:102
  163.0 1.1 shard_map.121
  164.2 1.3 collective-permute-done.20.b
  166.2 1.1 shard_map.123
  167.9 0.8 collective-permute-done.22.b
  168.8 0.8 collective-permute-start.23
  169.6 2.4 %shard_map.120 = (f32[256,768]{1,0:T(8,128)}, f32[8,128]{1,0:T(8,128)S(1)}) custom-call(s32[6]{0:T(128)S(1)} %stack.27.me_ref.refs_6_, bf16[256,1024]{1,0:T(8,128)(2,1)S(1)} %get-tuple-element.95.b.hidden_ref, bf16[128,768]{1,0:T(8,128)(2,1)S(1)} %shard_map.119.refs_0_, bf16[128,768]{1,0:T(8,128)(2,1)S(1)} %collective-permute-done.13.refs_1_.refs_0_, ...), custom_call_target="tpu_custom_call" | custom-call | flops 402653184 | bytes 4194304 | tf_op jit(solution)/shard_map/pallas_call | solution.py:635
  172.0 1.8 collective-permute-done.21.q0
  173.7 2.4 %collective-permute-done.23.q1 = bf16[2,256,128]{2,1,0:T(8,128)(2,1)S(1)} collective-permute-done((bf16[2,256,128]{2,1,0:T(8,128)(2,1)S(1)}, bf16[2,256,128]{2,1,0:T(8,128)(2,1)S(1)}, u32[]{:S(2)}, u32[]{:S(2)}) %collective-permute-start.23) | collective-permute-done | bytes 131104 | tf_op jit(solution)/shard_map/ppermute | solution.py:102
  176.1 1.0 shard_map.125.own
  177.2 1.7 collective-permute-done.24.other
  178.9 0.8 shard_map.126
  (58 shorter events, 7.1 us)
Async XLA Ops:
  0.6 1.2 copy-start
  0.6 8.2 %copy-start.5 = (s32[128]{0:T(128)S(1)}, s32[128]{0:T(128)}, u32[]{:S(2)}) copy-start(s32[128]{0:T(128)} %param.16) | copy-start | bytes 1540
  0.7 8.2 %copy-start.6 = (bf16[128,128]{1,0:T(8,128)(2,1)S(1)}, bf16[128,128]{1,0:T(8,128)(2,1)}, u32[]{:S(2)}) copy-start(bf16[128,128]{1,0:T(8,128)(2,1)} %param.15) | copy-start | bytes 98308
  2.9 13.4 %copy-start.7 = (s32[1536]{0:T(1024)S(1)}, s32[1536]{0:T(1024)}, u32[]{:S(2)}) copy-start(s32[1536]{0:T(1024)} %param.12) | copy-start | bytes 18436
  5.8 9.6 %collective-permute-start = (bf16[128,768]{1,0:T(8,128)(2,1)S(1)}, bf16[128,768]{1,0:T(8,128)(2,1)S(1)}, u32[]{:S(2)}, u32[]{:S(2)}) collective-permute-start(bf16[128,768]{1,0:T(8,128)(2,1)S(1)} %fusion.4.refs_0_.image), channel_id=1, source_target_pairs={{0,2},{1,3},{2,0},{3,1},{4,6},{5,7},{6,4},{7,5},{8,10},{9,11},{10,... | collective-permute-start | bytes 589832 | tf_op jit(solution)/shard_map/ppermute | solution.py:102
  8.9 6.5 %collective-permute-start.1 = (bf16[1,144,128]{2,0,1:T(2,128)(2,1)S(1)}, bf16[1,144,128]{2,0,1:T(2,128)(2,1)S(1)}, u32[]{:S(2)}, u32[]{:S(2)}) collective-permute-start(bf16[1,144,128]{2,0,1:T(2,128)(2,1)S(1)} %copy.15), channel_id=1, source_target_pairs={{0,16},{4,20},{8,24},{12,28},{16,0},{20,4},{24,8},{28,12},{1,17},{... | collective-permute-start | bytes 110600 | tf_op jit(solution)/shard_map/ppermute | solution.py:102
  11.6 4.7 %collective-permute-start.3 = (bf16[128,768]{1,0:T(8,128)(2,1)S(1)}, bf16[128,768]{1,0:T(8,128)(2,1)S(1)}, u32[]{:S(2)}, u32[]{:S(2)}) collective-permute-start(bf16[128,768]{1,0:T(8,128)(2,1)S(1)} %fusion.4.refs_0_.image), channel_id=1, source_target_pairs={{0,1},{1,0},{2,3},{3,2},{4,5},{5,4},{6,7},{7,6},{8,9},{9,8},{10,11... | collective-permute-start | bytes 589832 | tf_op jit(solution)/shard_map/ppermute | solution.py:102
  15.4 1.4 collective-permute-start.4
  15.7 30.4 %collective-permute-start.2 = (bf16[2,144,128]{2,0,1:T(2,128)(2,1)S(1)}, bf16[2,144,128]{2,0,1:T(2,128)(2,1)S(1)}, u32[]{:S(2)}, u32[]{:S(2)}) collective-permute-start(bf16[2,144,128]{2,0,1:T(2,128)(2,1)S(1)} %pad_maximum_fusion.4), channel_id=1, source_target_pairs={{0,8},{4,12},{8,0},{12,4},{16,24},{20,28},{24,16},{28,20},{1,9},{5... | collective-permute-start | bytes 221192 | tf_op jit(solution)/shard_map/ppermute | solution.py:102
  46.1 17.1 %collective-permute-start.5 = (bf16[2,2,128,512]{3,2,1,0:T(8,128)(2,1)S(1)}, bf16[2,2,128,512]{3,2,1,0:T(8,128)(2,1)S(1)}, u32[]{:S(2)}, u32[]{:S(2)}) collective-permute-start(bf16[2,2,128,512]{3,2,1,0:T(8,128)(2,1)S(1)} %get-tuple-element.64), channel_id=1, source_target_pairs={{0,4},{4,0},{8,12},{12,8},{16,20},{20,16},{24,28},{28,24},{1,5},{5... | collective-permute-start | bytes 1572872 | tf_op jit(solution)/shard_map/ppermute | solution.py:102
  47.6 15.5 %collective-permute-start.6 = (bf16[2,2,128,512]{3,2,1,0:T(8,128)(2,1)S(1)}, bf16[2,2,128,512]{3,2,1,0:T(8,128)(2,1)S(1)}, u32[]{:S(2)}, u32[]{:S(2)}) collective-permute-start(bf16[2,2,128,512]{3,2,1,0:T(8,128)(2,1)S(1)} %get-tuple-element.67), channel_id=1, source_target_pairs={{0,8},{4,12},{8,0},{12,4},{16,24},{20,28},{24,16},{28,20},{1,9},{5... | collective-permute-start | bytes 1572872 | tf_op jit(solution)/shard_map/ppermute | solution.py:102
  48.6 1.1 copy-start.4
  64.0 8.2 %collective-permute-start.7 = (bf16[2,128,512]{2,1,0:T(8,128)(2,1)}, bf16[2,128,512]{2,1,0:T(8,128)(2,1)}, u32[]{:S(2)}, u32[]{:S(2)}) collective-permute-start(bf16[2,128,512]{2,1,0:T(8,128)(2,1)} %get-tuple-element.69), channel_id=1, source_target_pairs={{0,8},{4,12},{8,0},{12,4},{16,24},{20,28},{24,16},{28,20},{1,9},{5... | collective-permute-start | bytes 786440 | tf_op jit(solution)/shard_map/ppermute | solution.py:102
  65.1 7.8 %collective-permute-start.8 = (bf16[2,128,512]{2,1,0:T(8,128)(2,1)}, bf16[2,128,512]{2,1,0:T(8,128)(2,1)}, u32[]{:S(2)}, u32[]{:S(2)}) collective-permute-start(bf16[2,128,512]{2,1,0:T(8,128)(2,1)} %get-tuple-element.71), channel_id=1, source_target_pairs={{0,4},{4,0},{8,12},{12,8},{16,20},{20,16},{24,28},{28,24},{1,5},{5... | collective-permute-start | bytes 786440 | tf_op jit(solution)/shard_map/ppermute | solution.py:102
  74.6 13.5 %collective-permute-start.10 = (bf16[256,512]{1,0:T(8,128)(2,1)S(1)}, bf16[256,512]{1,0:T(8,128)(2,1)S(1)}, u32[]{:S(2)}, u32[]{:S(2)}) collective-permute-start(bf16[256,512]{1,0:T(8,128)(2,1)S(1)} %get-tuple-element.77), channel_id=1, source_target_pairs={{0,16},{4,20},{8,24},{12,28},{16,0},{20,4},{24,8},{28,12},{1,17},{... | collective-permute-start | bytes 786440 | tf_op jit(solution)/shard_map/ppermute | solution.py:102
  77.7 5.2 %collective-permute-start.9 = (bf16[4,144,128]{2,0,1:T(4,128)(2,1)S(1)}, bf16[4,144,128]{2,0,1:T(4,128)(2,1)S(1)}, u32[]{:S(2)}, u32[]{:S(2)}) collective-permute-start(bf16[4,144,128]{2,0,1:T(4,128)(2,1)S(1)} %pad_maximum_fusion.3), channel_id=1, source_target_pairs={{0,4},{4,0},{8,12},{12,8},{16,20},{20,16},{24,28},{28,24},{1,5},{5... | collective-permute-start | bytes 442376 | tf_op jit(solution)/shard_map/ppermute | solution.py:102
  90.2 30.1 %all-to-all-start = ((bf16[8,128,512]{2,1,0:T(8,128)(2,1)}), bf16[8,128,512]{2,1,0:T(8,128)(2,1)}, u32[]{:S(2)}, u32[]{:S(2)}) async-start(bf16[8,128,512]{2,1,0:T(8,128)(2,1)} %shard_map.116), calls=%async_computation | async-start | bytes 2097152 | tf_op jit(solution)/shard_map/all_to_all | solution.py:773
  129.8 33.2 %copy-start.1 = (bf16[2048,768]{1,0:T(8,128)(2,1)S(1)}, bf16[2048,768]{1,0:T(8,128)(2,1)}, u32[]{:S(2)}) copy-start(bf16[2048,768]{1,0:T(8,128)(2,1)} %w_ref.3) | copy-start | bytes 9437188
  129.8 1.7 collective-permute-start.11
  131.5 1.1 copy-start.3
  133.3 7.0 %collective-permute-start.12 = (bf16[768,128]{1,0:T(8,128)(2,1)S(1)}, bf16[768,128]{1,0:T(8,128)(2,1)S(1)}, u32[]{:S(2)}, u32[]{:S(2)}) collective-permute-start(bf16[768,128]{1,0:T(8,128)(2,1)S(1)} %get-tuple-element.82), channel_id=1, source_target_pairs={{0,2},{1,3},{2,0},{3,1},{4,6},{5,7},{6,4},{7,5},{8,10},{9,11},{10,... | collective-permute-start | bytes 589832 | tf_op jit(solution)/shard_map/ppermute | solution.py:102
  140.4 10.5 %collective-permute-start.13 = (bf16[128,768]{1,0:T(8,128)(2,1)S(1)}, bf16[128,768]{1,0:T(8,128)(2,1)S(1)}, u32[]{:S(2)}, u32[]{:S(2)}) collective-permute-start(bf16[128,768]{1,0:T(8,128)(2,1)S(1)} %shard_map.119.refs_0_), channel_id=1, source_target_pairs={{0,16},{4,20},{8,24},{12,28},{16,0},{20,4},{24,8},{28,12},{1,17},{... | collective-permute-start | bytes 589832 | tf_op jit(solution)/shard_map/ppermute | solution.py:102
  140.5 10.4 %collective-permute-start.14 = (bf16[128,768]{1,0:T(8,128)(2,1)S(1)}, bf16[128,768]{1,0:T(8,128)(2,1)S(1)}, u32[]{:S(2)}, u32[]{:S(2)}) collective-permute-start(bf16[128,768]{1,0:T(8,128)(2,1)S(1)} %shard_map.119.refs_0_), channel_id=1, source_target_pairs={{0,8},{4,12},{8,0},{12,4},{16,24},{20,28},{24,16},{28,20},{1,9},{5... | collective-permute-start | bytes 589832 | tf_op jit(solution)/shard_map/ppermute | solution.py:102
  142.5 8.5 %collective-permute-start.15 = (bf16[128,768]{1,0:T(8,128)(2,1)S(1)}, bf16[128,768]{1,0:T(8,128)(2,1)S(1)}, u32[]{:S(2)}, u32[]{:S(2)}) collective-permute-start(bf16[128,768]{1,0:T(8,128)(2,1)S(1)} %shard_map.119.refs_0_), channel_id=1, source_target_pairs={{0,4},{4,0},{8,12},{12,8},{16,20},{20,16},{24,28},{28,24},{1,5},{5... | collective-permute-start | bytes 589832 | tf_op jit(solution)/shard_map/ppermute | solution.py:102
  150.9 6.8 %collective-permute-start.16 = (bf16[128,768]{1,0:T(8,128)(2,1)S(1)}, bf16[128,768]{1,0:T(8,128)(2,1)S(1)}, u32[]{:S(2)}, u32[]{:S(2)}) collective-permute-start(bf16[128,768]{1,0:T(8,128)(2,1)S(1)} %collective-permute-done.13.refs_1_.refs_0_), channel_id=1, source_target_pairs={{0,8},{4,12},{8,0},{12,4},{16,24},{20,28},{24,16},{28,20},{1,9},{5... | collective-permute-start | bytes 589832 | tf_op jit(solution)/shard_map/ppermute | solution.py:102
  150.9 7.9 %collective-permute-start.17 = (bf16[128,768]{1,0:T(8,128)(2,1)S(1)}, bf16[128,768]{1,0:T(8,128)(2,1)S(1)}, u32[]{:S(2)}, u32[]{:S(2)}) collective-permute-start(bf16[128,768]{1,0:T(8,128)(2,1)S(1)} %collective-permute-done.13.refs_1_.refs_0_), channel_id=1, source_target_pairs={{0,4},{4,0},{8,12},{12,8},{16,20},{20,16},{24,28},{28,24},{1,5},{5... | collective-permute-start | bytes 589832 | tf_op jit(solution)/shard_map/ppermute | solution.py:102
  152.4 10.6 %collective-permute-start.18 = (bf16[128,768]{1,0:T(8,128)(2,1)S(1)}, bf16[128,768]{1,0:T(8,128)(2,1)S(1)}, u32[]{:S(2)}, u32[]{:S(2)}) collective-permute-start(bf16[128,768]{1,0:T(8,128)(2,1)S(1)} %collective-permute-done.14.refs_2_), channel_id=1, source_target_pairs={{0,4},{4,0},{8,12},{12,8},{16,20},{20,16},{24,28},{28,24},{1,5},{5... | collective-permute-start | bytes 589832 | tf_op jit(solution)/shard_map/ppermute | solution.py:102
  157.7 8.5 %collective-permute-start.19 = (bf16[128,768]{1,0:T(8,128)(2,1)S(1)}, bf16[128,768]{1,0:T(8,128)(2,1)S(1)}, u32[]{:S(2)}, u32[]{:S(2)}) collective-permute-start(bf16[128,768]{1,0:T(8,128)(2,1)S(1)} %collective-permute-done.16.refs_3_.refs_2_), channel_id=1, source_target_pairs={{0,4},{4,0},{8,12},{12,8},{16,20},{20,16},{24,28},{28,24},{1,5},{5... | collective-permute-start | bytes 589832 | tf_op jit(solution)/shard_map/ppermute | solution.py:102
  164.1 1.4 collective-permute-start.20
  165.5 10.6 %copy-start.2 = (bf16[384,1024]{1,0:T(8,128)(2,1)S(1)}, bf16[384,1024]{1,0:T(8,128)(2,1)}, u32[]{:S(2)}) copy-start(bf16[384,1024]{1,0:T(8,128)(2,1)} %fusion.7.c.lhs_ref) | copy-start | bytes 2359300
  167.3 1.4 collective-permute-start.22
  167.4 6.4 %collective-permute-start.21 = (bf16[2,256,128]{2,1,0:T(8,128)(2,1)S(1)}, bf16[2,256,128]{2,1,0:T(8,128)(2,1)S(1)}, u32[]{:S(2)}, u32[]{:S(2)}) collective-permute-start(bf16[2,256,128]{2,1,0:T(8,128)(2,1)S(1)} %shard_map.122.refs_4_.p0), channel_id=1, source_target_pairs={{0,2},{1,3},{2,0},{3,1},{4,6},{5,7},{6,4},{7,5},{8,10},{9,11},{10,... | collective-permute-start | bytes 393224 | tf_op jit(solution)/shard_map/ppermute | solution.py:102
  168.8 7.3 %collective-permute-start.23 = (bf16[2,256,128]{2,1,0:T(8,128)(2,1)S(1)}, bf16[2,256,128]{2,1,0:T(8,128)(2,1)S(1)}, u32[]{:S(2)}, u32[]{:S(2)}) collective-permute-start(bf16[2,256,128]{2,1,0:T(8,128)(2,1)S(1)} %shard_map.124.p1), channel_id=1, source_target_pairs={{0,2},{1,3},{2,0},{3,1},{4,6},{5,7},{6,4},{7,5},{8,10},{9,11},{10,... | collective-permute-start | bytes 393224 | tf_op jit(solution)/shard_map/ppermute | solution.py:102
  177.1 1.8 collective-permute-start.24

commit v10 on v9

--- a/solution.py
+++ b/solution.py
@@ -475,12 +475,11 @@
 NT = (((1,), (1,)), ((), ()))
 
 
-def image_kernel(me_ref, wave_ref, rows_ref, freq_ref, a, b, c, send_ref, keep_ref, pre_ref):
-    step = pl.program_id(0)
+def sent_kernel(me_ref, wave_ref, rows_ref, freq_ref, a, b, c, send_ref, pre_ref):
     tile = wave_ref.shape[3]
     part = tile // 2
 
-    @pl.when(step == 0)
+    @pl.when(pl.program_id(0) == 0)
     def _():
         for place in range(4):
             for h in range(2):
@@ -492,78 +491,79 @@
                 pre_ref[:, at : at + part] = pre.astype(BF)
 
     out = lax.dot_general(freq_ref[...], pre_ref[...], NT, preferred_element_type=F32)
-
-    @pl.when(step < 2)
-    def _():
-        send_ref[0] = out.astype(BF)
-
-    @pl.when(step >= 2)
-    def _():
-        keep_ref[0] = out
-
-
-def image_grads(me, waves, feat_rows, freq, cols, after):
+    send_ref[0] = out.astype(BF)
+
+
+def kept_kernel(me_ref, pre_ref, freq_ref, keep_ref):
+    keep_ref[0] = lax.dot_general(freq_ref[...], pre_ref[...], NT, preferred_element_type=F32)
+
+
+def image_grads(me, freq, cols, arrays, after, kept=None):
     k, n = freq.shape
-    owners, rows, width = feat_rows.shape
+    sent = kept is None
+    rows = arrays[1].shape[1] if sent else arrays[0].shape[0]
+    count = 2 if sent else 1
     whole = lambda shape: block(shape, lambda s, me: (0,) * len(shape))
 
     def source(s, me):
-        return 2 * (s % 2) + ((me[0] % 2) ^ (1 - s // 2)), 0
-
+        return (me[0] ^ (2 * (1 - s)) ^ 1, 0) if sent else (me[0] ^ (2 * (1 - kept)), 0)
+
+    out = block((1, cols, rows), lambda s, me: (s, 0, 0))
+    shape = jax.ShapeDtypeStruct((count, cols, rows), BF if sent else F32)
+    pre = jax.ShapeDtypeStruct((rows, n), BF)
     spec = pltpu.PrefetchScalarGridSpec(
         num_scalar_prefetch=1,
-        grid=(4,),
-        in_specs=[whole(waves.shape), whole(feat_rows.shape), block((cols, n), source)]
-        + [pl.BlockSpec(memory_space=pl.ANY)] * 3,
-        out_specs=[
-            block((1, cols, rows), lambda s, me: (jnp.minimum(s, 1), 0, 0)),
-            block((1, cols, rows), lambda s, me: (jnp.maximum(s - 2, 0), 0, 0)),
-        ],
-        scratch_shapes=[pltpu.VMEM((rows, n), BF)],
-    )
-    return pl.pallas_call(
-        image_kernel,
+        grid=(count,),
+        in_specs=[whole(x.shape) for x in arrays]
+        + [block((cols, n), source)]
+        + [pl.BlockSpec(memory_space=pl.ANY)] * len(after),
+        out_specs=[out, whole(pre.shape)] if sent else out,
+    )
+    return pl.pallas_call(
+        sent_kernel if sent else kept_kernel,
         grid_spec=spec,
-        out_shape=[jax.ShapeDtypeStruct((2, cols, rows), BF), pltpu.HBM((2, cols, rows), F32)],
+        out_shape=[shape, pre] if sent else shape,
         compiler_params=pltpu.CompilerParams(vmem_limit_bytes=52 * 2**20),
-        cost_estimate=pl.CostEstimate(flops=2 * k * n * rows, bytes_accessed=2 * k * n, transcendentals=0),
-    )(me, waves, feat_rows, freq, *after)
-
-
-def split_y_kernel(me_ref, keep_s, keep_k, got_s, got_k, send, keep):
-    send[...] = (keep_s[0] + got_s[0].astype(F32)).astype(BF)
-    keep[...] = keep_k[0] + got_k[0].astype(F32)
-
-
-def split_y(me, keep, got):
+        cost_estimate=pl.CostEstimate(flops=k * n * rows, bytes_accessed=k * n, transcendentals=0),
+    )(me, *arrays, freq, *after)
+
+
+def first_add_kernel(a, b, out):
+    out[...] = (a[0] + b[0].astype(F32)).astype(BF)
+
+
+def first_add(keep, got):
     _, cols, rows = keep.shape
-    at = lambda flip: block((1, cols, rows), lambda h, me: ((me[0] // 2) ^ flip, 0, 0))
-    out = block((cols, rows), lambda h, me: (0, 0))
-    spec = pltpu.PrefetchScalarGridSpec(
-        num_scalar_prefetch=1, grid=(1,), in_specs=[at(1), at(0)] * 2, out_specs=[out, out]
-    )
-    return pl.pallas_call(
-        split_y_kernel,
-        grid_spec=spec,
-        out_shape=[jax.ShapeDtypeStruct((cols, rows), t) for t in (BF, F32)],
+    one = block((1, cols, rows), lambda h: (0, 0, 0))
+    return pl.pallas_call(
+        first_add_kernel,
+        grid=(1,),
+        in_specs=[one, one],
+        out_specs=block((cols, rows), lambda h: (0, 0)),
+        out_shape=jax.ShapeDtypeStruct((cols, rows), BF),
         compiler_params=pltpu.CompilerParams(vmem_limit_bytes=8 * 2**20),
         cost_estimate=pl.CostEstimate(flops=0, bytes_accessed=2**20, transcendentals=0),
-    )(me, keep, keep, got, got)
-
-
-def out_kernel(keep, got, image, out):
-    grad = (keep[...] + got[...].astype(F32)).T
+    )(keep, got)
+
+
+def out_kernel(keep, near, far, image, out):
+    grad = (keep[0] + near[0].astype(F32) + far[...].astype(F32)).T
     grad = grad * (1.0 - jnp.square(image[...].astype(F32)))
     out[...] = grad.astype(BF)
 
 
-def out_grads(keep, got, image):
+def out_grads(keep, near, far, image):
+    _, cols, rows = keep.shape
+    one = lambda i: block((1, cols, rows), lambda h: (i, 0, 0))
     return pl.pallas_call(
         out_kernel,
+        grid=(1,),
+        in_specs=[one(0), one(1), block((cols, rows), lambda h: (0, 0)), block((rows, cols), lambda h: (0, 0))],
+        out_specs=block((rows, cols), lambda h: (0, 0)),
         out_shape=jax.ShapeDtypeStruct(image.shape, BF),
         compiler_params=pltpu.CompilerParams(vmem_limit_bytes=8 * 2**20),
         cost_estimate=pl.CostEstimate(flops=0, bytes_accessed=2**20, transcendentals=0),
-    )(keep, got, image)
+    )(keep, near, far, image)
 
 
 def hidden_kernel(me_ref, w_ref, *refs):
@@ -772,11 +772,14 @@
     feat_grad = gap_rows(me, keep, got, noise, all_labels.reshape(groups, rows), real_total, order, token)
     feat_grad = lax.all_to_all(feat_grad, "rec", 0, 0, tiled=True)
 
-    send, keep = image_grads(
-        me, waves, feat_grad, frequencies, cols, (gate, all_hidden, lhs)
-    )
-    send, keep = split_y(me, keep, swap(send, "feat", 1))
-    out_grad = out_grads(keep, swap(send, "feat", 2), own)
+    send, pre_grad = image_grads(
+        me, frequencies, cols, (waves, feat_grad), (gate, all_hidden, lhs)
+    )
+    near = swap(send, "feat", 1)
+    keep = image_grads(me, frequencies, cols, (pre_grad,), (), 0)
+    far = swap(first_add(keep, near), "feat", 2)
+    keep = image_grads(me, frequencies, cols, (pre_grad,), (), 1)
+    out_grad = out_grads(keep, near, far, own)
 
     by = {0: out_grad}
     by[4] = swap(out_grad, "rec", 4)

time: 180 us -> 177 us (0.983)
  waiting for transfers between devices: 75.2 us -> 70.6 us
  Pallas kernels: 64 us -> 66.5 us
    ppermute x25, waiting for transfers between devices: 52.8 us -> 48.1 us  [swap(): return lax.ppermute(x, axis, [(i, i ^ bit) for i in range(n)])]
    pallas_call x3 -> x5, Pallas kernels: 10.3 us -> 12.9 us  [the longest x3 12.6 us: image_grads(): pl.pallas_call(sent_kernel if sent else kept_kernel, grid_spec=spec, out_...]
  transfers between devices with their start and end apart: 26 -> 26, of which waited for: 18 -> 17; matrix products, arithmetic and copies ran while one was open for 3% -> 3% of each run, Pallas kernels for 26% -> 30%
where the time goes in v10:
time: 177 us; the launch traced here: 176 us
  waiting for transfers between devices  70.6 us (40%)
  Pallas kernels  66.5 us (38%)
  starting transfers between devices  27.3 us (15%)
  local copies, waits for them, and re-layouts  4.93 us (3%)
  matrix products  4.34 us (2%)
  other arithmetic  1.8 us (1%)
    ppermute x25, waiting for transfers between devices, swap(): return lax.ppermute(x, axis, [(i, i ^ bit) for i in range(n)])  48.1 us
    pallas_call x2, Pallas kernels, feature_sums(): pl.pallas_call(functools.partial(features_kernel, masks, last, *totals),...  42.6 us
    ppermute x25, starting transfers between devices, swap(): return lax.ppermute(x, axis, [(i, i ^ bit) for i in range(n)])  22.9 us
    all_to_all x1, waiting for transfers between devices, eight_by_four(): feat_grad = lax.all_to_all(feat_grad, 'rec', 0, 0, tiled=True)  22.5 us
    pallas_call x3, Pallas kernels, image_grads(): pl.pallas_call(sent_kernel if sent else kept_kernel, grid_spec=spec, out_...  12.6 us
    all_to_all x1, starting transfers between devices, eight_by_four(): feat_grad = lax.all_to_all(feat_grad, 'rec', 0, 0, tiled=True)  4.46 us
  transfers between devices with their start and end apart: 26, of which 17 were waited for; matrix products, arithmetic and copies ran while one was open for 3% of the time, Pallas kernels for 30%

profile of v10, /device:TPU:0, one launch (start us, length us, event | category | flops | bytes accessed | tf_op | source)
XLA Modules:
  0.0 176.5 jit_solution(3297382888950268373)
XLA Ops:
  0.7 1.2 copy-done
  1.9 1.0 fusion.12
  2.9 2.9 %fusion.4.refs_0_.image = bf16[128,768]{1,0:T(8,128)(2,1)S(1)} fusion(bf16[2048,768]{1,0:T(8,128)(2,1)} %w_ref.3, f32[128,2048]{1,0:T(8,128)S(1)} %fusion.12, bf16[128,128]{1,0:T(8,128)(2,1)} %param.15, bf16[128,2048]{1,0:T(8,128)(2,1)} %param.17), kind=kOutput, calls=%fused_computation.5 | convolution fusion | flops 470646784 | bytes 4947968 | tf_op jit(solution)/shard_map/dot_general | solution.py:722
  5.8 3.0 %collective-permute-start = (bf16[128,768]{1,0:T(8,128)(2,1)S(1)}, bf16[128,768]{1,0:T(8,128)(2,1)S(1)}, u32[]{:S(2)}, u32[]{:S(2)}) collective-permute-start(bf16[128,768]{1,0:T(8,128)(2,1)S(1)} %fusion.4.refs_0_.image), channel_id=1, source_target_pairs={{0,2},{1,3},{2,0},{3,1},{4,6},{5,7},{6,4},{7,5},{8,10},{9,11},{10,... | collective-permute-start | bytes 589832 | tf_op jit(solution)/shard_map/ppermute | solution.py:102
  8.9 2.7 %collective-permute-start.1 = (bf16[1,144,128]{2,0,1:T(2,128)(2,1)S(1)}, bf16[1,144,128]{2,0,1:T(2,128)(2,1)S(1)}, u32[]{:S(2)}, u32[]{:S(2)}) collective-permute-start(bf16[1,144,128]{2,0,1:T(2,128)(2,1)S(1)} %copy.15), channel_id=1, source_target_pairs={{0,16},{4,20},{8,24},{12,28},{16,0},{20,4},{24,8},{28,12},{1,17},{... | collective-permute-start | bytes 110600 | tf_op jit(solution)/shard_map/ppermute | solution.py:102
  11.6 3.8 %collective-permute-done.1 = bf16[1,144,128]{2,0,1:T(2,128)(2,1)S(1)} collective-permute-done((bf16[1,144,128]{2,0,1:T(2,128)(2,1)S(1)}, bf16[1,144,128]{2,0,1:T(2,128)(2,1)S(1)}, u32[]{:S(2)}, u32[]{:S(2)}) %collective-permute-start.1) | collective-permute-done | bytes 36896 | tf_op jit(solution)/shard_map/ppermute | solution.py:102
  16.8 29.2 %shard_map.112 = (bf16[2,2,128,512]{3,2,1,0:T(8,128)(2,1)S(1)}, f32[2,128,512]{2,1,0:T(8,128)S(1)}, bf16[2,2,128,512]{3,2,1,0:T(8,128)(2,1)S(1)}, f32[2,128,512]...) custom-call(s32[6]{0:T(128)S(1)} %stack.27.me_ref.refs_6_, ...), custom_call_target="tpu_custom_call" | custom-call | flops 18320719872 | bytes 18874368 | tf_op jit(solution)/shard_map/pallas_call | solution.py:381
  46.1 1.6 collective-permute-start.5
  47.6 1.0 collective-permute-start.6
  48.6 1.1 copy-done.3
  49.7 13.4 %shard_map.113 = (f32[2,128,512]{2,1,0:T(8,128)S(1)}, f32[2,128,512]{2,1,0:T(8,128)S(1)}, f32[4,2,128,512]{3,2,1,0:T(8,128)}, f32[8,128]{1,0:T(8,128)S(1)}) custom-call(s32[6]{0:T(128)S(1)} %stack.27.me_ref.refs_6_, s32[1,1536]{1,0:T(1,128)S(1)} %reshape.61.real_labels_ref, s32[1,128]{1,0:T(1,128)S(1)} %bitcast.32, ...), custom_call_target="tpu_custom_call", output_to_operand_aliasing={{2}: (7, {})} | custom-call | flops 6106906624 | bytes 12582912 | tf_op jit(solution)/shard_map/pallas_call | solution.py:381
  63.2 0.9 shard_map.114
  64.0 1.1 collective-permute-start.7
  65.6 1.2 constant_dynamic-slice_fusion
  66.9 5.3 %collective-permute-done.7.ga = bf16[2,128,512]{2,1,0:T(8,128)(2,1)} collective-permute-done((bf16[2,128,512]{2,1,0:T(8,128)(2,1)}, bf16[2,128,512]{2,1,0:T(8,128)(2,1)}, u32[]{:S(2)}, u32[]{:S(2)}) %collective-permute-start.7) | collective-permute-done | bytes 262176 | tf_op jit(solution)/shard_map/ppermute | solution.py:102
  72.2 0.7 collective-permute-done.8.gb
  72.9 1.7 shard_map.115
  74.6 2.9 %collective-permute-start.10 = (bf16[256,512]{1,0:T(8,128)(2,1)S(1)}, bf16[256,512]{1,0:T(8,128)(2,1)S(1)}, u32[]{:S(2)}, u32[]{:S(2)}) collective-permute-start(bf16[256,512]{1,0:T(8,128)(2,1)S(1)} %get-tuple-element.75), channel_id=1, source_target_pairs={{0,16},{4,20},{8,24},{12,28},{16,0},{20,4},{24,8},{28,12},{1,17},{... | collective-permute-start | bytes 786440 | tf_op jit(solution)/shard_map/ppermute | solution.py:102
  78.3 4.6 %collective-permute-done.9 = bf16[4,144,128]{2,0,1:T(4,128)(2,1)S(1)} collective-permute-done((bf16[4,144,128]{2,0,1:T(4,128)(2,1)S(1)}, bf16[4,144,128]{2,0,1:T(4,128)(2,1)S(1)}, u32[]{:S(2)}, u32[]{:S(2)}) %collective-permute-start.9) | collective-permute-done | bytes 147488 | tf_op jit(solution)/shard_map/ppermute | solution.py:102
  82.9 5.2 %collective-permute-done.10.got_ref = bf16[256,512]{1,0:T(8,128)(2,1)S(1)} collective-permute-done((bf16[256,512]{1,0:T(8,128)(2,1)S(1)}, bf16[256,512]{1,0:T(8,128)(2,1)S(1)}, u32[]{:S(2)}, u32[]{:S(2)}) %collective-permute-start.10) | collective-permute-done | bytes 262176 | tf_op jit(solution)/shard_map/ppermute | solution.py:102
  88.1 2.1 %shard_map.116 = bf16[8,128,512]{2,1,0:T(8,128)(2,1)} custom-call(s32[6]{0:T(128)S(1)} %stack.27.me_ref.refs_6_, f32[256,512]{1,0:T(8,128)S(1)} %get-tuple-element.74.keep_ref, bf16[256,512]{1,0:T(8,128)(2,1)S(1)} %collective-permute-done.10.got_ref, f32[256,512]{1,0:T(8,128)S(1)} %bitcast.30, s32[8,128]{1,0:T(8,128)S(1)} %get-tuple-element.89.labels_ref, ...), custom_call_target="tpu_custom_call" | custom-call | flops 268435456 | bytes 3145728 | tf_op jit(solution)/shard_map/pallas_call | solution.py:464
  90.2 4.5 %all-to-all-start = ((bf16[8,128,512]{2,1,0:T(8,128)(2,1)}), bf16[8,128,512]{2,1,0:T(8,128)(2,1)}, u32[]{:S(2)}, u32[]{:S(2)}) async-start(bf16[8,128,512]{2,1,0:T(8,128)(2,1)} %shard_map.116), calls=%async_computation | async-start | bytes 2097152 | tf_op jit(solution)/shard_map/all_to_all | solution.py:773
  94.6 0.8 constant_dynamic-slice_fusion.2
  96.2 1.0 fusion.7.c.lhs_ref
  97.8 22.5 %all-to-all-done.rows_ref = bf16[8,128,512]{2,1,0:T(8,128)(2,1)} async-done(((bf16[8,128,512]{2,1,0:T(8,128)(2,1)}), bf16[8,128,512]{2,1,0:T(8,128)(2,1)}, u32[]{:S(2)}, u32[]{:S(2)}) %all-to-all-start) | async-done | bytes 1048608 | tf_op jit(solution)/shard_map/all_to_all | solution.py:773
  120.2 5.5 %shard_map.117 = (bf16[2,768,128]{2,1,0:T(8,128)(2,1)S(1)}, bf16[128,2048]{1,0:T(8,128)(2,1)S(1)}) custom-call(s32[6]{0:T(128)S(1)} %stack.27.me_ref.refs_6_, f32[4,2,128,512]{3,2,1,0:T(8,128)} %get-tuple-element.73.wave_ref, bf16[8,128,512]{2,1,0:T(8,128)(2,1)} %all-to-all-done.rows_ref, bf16[3072,2048]{1,0:T(8,128)(2,1)} %freq_ref.5, ...), custom_call_target="tpu_custom_call" | custom-call | flops 805306368 | bytes 6291456 | tf_op jit(solution)/shard_map/pallas_call | solution.py:522
  125.9 3.4 %shard_map.119.a = f32[1,768,128]{2,1,0:T(8,128)S(1)} custom-call(s32[6]{0:T(128)S(1)} %stack.27.me_ref.refs_6_, bf16[128,2048]{1,0:T(8,128)(2,1)S(1)} %get-tuple-element.77.pre_ref, bf16[3072,2048]{1,0:T(8,128)(2,1)} %freq_ref.5), custom_call_target="tpu_custom_call" | custom-call | flops 805306368 | bytes 6291456 | tf_op jit(solution)/shard_map/pallas_call | solution.py:522
  129.9 3.7 %shard_map.118.keep = f32[1,768,128]{2,1,0:T(8,128)S(1)} custom-call(s32[6]{0:T(128)S(1)} %stack.27.me_ref.refs_6_, bf16[128,2048]{1,0:T(8,128)(2,1)S(1)} %get-tuple-element.77.pre_ref, bf16[3072,2048]{1,0:T(8,128)(2,1)} %freq_ref.5), custom_call_target="tpu_custom_call" | custom-call | flops 805306368 | bytes 6291456 | tf_op jit(solution)/shard_map/pallas_call | solution.py:522
  133.6 3.1 %collective-permute-done.12.far = bf16[768,128]{1,0:T(8,128)(2,1)S(1)} collective-permute-done((bf16[768,128]{1,0:T(8,128)(2,1)S(1)}, bf16[768,128]{1,0:T(8,128)(2,1)S(1)}, u32[]{:S(2)}, u32[]{:S(2)}) %collective-permute-start.12) | collective-permute-done | bytes 196640 | tf_op jit(solution)/shard_map/ppermute | solution.py:102
  137.0 1.9 %collective-permute-start.14 = (bf16[128,768]{1,0:T(8,128)(2,1)S(1)}, bf16[128,768]{1,0:T(8,128)(2,1)S(1)}, u32[]{:S(2)}, u32[]{:S(2)}) collective-permute-start(bf16[128,768]{1,0:T(8,128)(2,1)S(1)} %shard_map.121.refs_0_), channel_id=1, source_target_pairs={{0,8},{4,12},{8,0},{12,4},{16,24},{20,28},{24,16},{28,20},{1,9},{5... | collective-permute-start | bytes 589832 | tf_op jit(solution)/shard_map/ppermute | solution.py:102
  138.9 1.5 collective-permute-start.15
  140.4 7.4 %collective-permute-done.13.refs_1_.refs_0_ = bf16[128,768]{1,0:T(8,128)(2,1)S(1)} collective-permute-done((bf16[128,768]{1,0:T(8,128)(2,1)S(1)}, bf16[128,768]{1,0:T(8,128)(2,1)S(1)}, u32[]{:S(2)}, u32[]{:S(2)}) %collective-permute-start.13) | collective-permute-done | bytes 196640 | tf_op jit(solution)/shard_map/ppermute | solution.py:102
  147.8 1.4 collective-permute-start.17
  149.2 0.7 collective-permute-start.18
  149.9 4.7 %collective-permute-done.16.refs_3_.refs_2_ = bf16[128,768]{1,0:T(8,128)(2,1)S(1)} collective-permute-done((bf16[128,768]{1,0:T(8,128)(2,1)S(1)}, bf16[128,768]{1,0:T(8,128)(2,1)S(1)}, u32[]{:S(2)}, u32[]{:S(2)}) %collective-permute-start.16) | collective-permute-done | bytes 196640 | tf_op jit(solution)/shard_map/ppermute | solution.py:102
  154.5 1.1 collective-permute-start.19
  155.7 4.1 %collective-permute-done.18.refs_6_.refs_3_ = bf16[128,768]{1,0:T(8,128)(2,1)S(1)} collective-permute-done((bf16[128,768]{1,0:T(8,128)(2,1)S(1)}, bf16[128,768]{1,0:T(8,128)(2,1)S(1)}, u32[]{:S(2)}, u32[]{:S(2)}) %collective-permute-start.18) | collective-permute-done | bytes 196640 | tf_op jit(solution)/shard_map/ppermute | solution.py:102
  159.8 1.1 shard_map.123
  161.0 1.3 collective-permute-done.20.b
  163.0 1.1 shard_map.125
  164.8 0.8 collective-permute-done.22.b
  165.6 0.8 collective-permute-start.23
  166.4 2.4 %shard_map.122 = (f32[256,768]{1,0:T(8,128)}, f32[8,128]{1,0:T(8,128)S(1)}) custom-call(s32[6]{0:T(128)S(1)} %stack.27.me_ref.refs_6_, bf16[256,1024]{1,0:T(8,128)(2,1)S(1)} %get-tuple-element.91.b.hidden_ref, bf16[128,768]{1,0:T(8,128)(2,1)S(1)} %shard_map.121.refs_0_, bf16[128,768]{1,0:T(8,128)(2,1)S(1)} %collective-permute-done.13.refs_1_.refs_0_, ...), custom_call_target="tpu_custom_call" | custom-call | flops 402653184 | bytes 4194304 | tf_op jit(solution)/shard_map/pallas_call | solution.py:635
  168.8 1.8 %collective-permute-done.21.q0 = bf16[2,256,128]{2,1,0:T(8,128)(2,1)S(1)} collective-permute-done((bf16[2,256,128]{2,1,0:T(8,128)(2,1)S(1)}, bf16[2,256,128]{2,1,0:T(8,128)(2,1)S(1)}, u32[]{:S(2)}, u32[]{:S(2)}) %collective-permute-start.21) | collective-permute-done | bytes 131104 | tf_op jit(solution)/shard_map/ppermute | solution.py:102
  170.6 2.4 %collective-permute-done.23.q1 = bf16[2,256,128]{2,1,0:T(8,128)(2,1)S(1)} collective-permute-done((bf16[2,256,128]{2,1,0:T(8,128)(2,1)S(1)}, bf16[2,256,128]{2,1,0:T(8,128)(2,1)S(1)}, u32[]{:S(2)}, u32[]{:S(2)}) %collective-permute-start.23) | collective-permute-done | bytes 131104 | tf_op jit(solution)/shard_map/ppermute | solution.py:102
  173.0 0.9 shard_map.127.own
  174.0 1.7 collective-permute-done.24.other
  175.7 0.8 shard_map.128
  (58 shorter events, 6.6 us)
Async XLA Ops:
  0.6 1.2 copy-start
  0.6 8.2 %copy-start.4 = (s32[128]{0:T(128)S(1)}, s32[128]{0:T(128)}, u32[]{:S(2)}) copy-start(s32[128]{0:T(128)} %param.16) | copy-start | bytes 1540
  0.7 8.2 %copy-start.5 = (bf16[128,128]{1,0:T(8,128)(2,1)S(1)}, bf16[128,128]{1,0:T(8,128)(2,1)}, u32[]{:S(2)}) copy-start(bf16[128,128]{1,0:T(8,128)(2,1)} %param.15) | copy-start | bytes 98308
  2.9 13.4 %copy-start.6 = (s32[1536]{0:T(1024)S(1)}, s32[1536]{0:T(1024)}, u32[]{:S(2)}) copy-start(s32[1536]{0:T(1024)} %param.12) | copy-start | bytes 18436
  5.8 9.6 %collective-permute-start = (bf16[128,768]{1,0:T(8,128)(2,1)S(1)}, bf16[128,768]{1,0:T(8,128)(2,1)S(1)}, u32[]{:S(2)}, u32[]{:S(2)}) collective-permute-start(bf16[128,768]{1,0:T(8,128)(2,1)S(1)} %fusion.4.refs_0_.image), channel_id=1, source_target_pairs={{0,2},{1,3},{2,0},{3,1},{4,6},{5,7},{6,4},{7,5},{8,10},{9,11},{10,... | collective-permute-start | bytes 589832 | tf_op jit(solution)/shard_map/ppermute | solution.py:102
  8.9 6.5 %collective-permute-start.1 = (bf16[1,144,128]{2,0,1:T(2,128)(2,1)S(1)}, bf16[1,144,128]{2,0,1:T(2,128)(2,1)S(1)}, u32[]{:S(2)}, u32[]{:S(2)}) collective-permute-start(bf16[1,144,128]{2,0,1:T(2,128)(2,1)S(1)} %copy.15), channel_id=1, source_target_pairs={{0,16},{4,20},{8,24},{12,28},{16,0},{20,4},{24,8},{28,12},{1,17},{... | collective-permute-start | bytes 110600 | tf_op jit(solution)/shard_map/ppermute | solution.py:102
  11.6 4.7 %collective-permute-start.3 = (bf16[128,768]{1,0:T(8,128)(2,1)S(1)}, bf16[128,768]{1,0:T(8,128)(2,1)S(1)}, u32[]{:S(2)}, u32[]{:S(2)}) collective-permute-start(bf16[128,768]{1,0:T(8,128)(2,1)S(1)} %fusion.4.refs_0_.image), channel_id=1, source_target_pairs={{0,1},{1,0},{2,3},{3,2},{4,5},{5,4},{6,7},{7,6},{8,9},{9,8},{10,11... | collective-permute-start | bytes 589832 | tf_op jit(solution)/shard_map/ppermute | solution.py:102
  15.4 1.4 collective-permute-start.4
  15.7 30.4 %collective-permute-start.2 = (bf16[2,144,128]{2,0,1:T(2,128)(2,1)S(1)}, bf16[2,144,128]{2,0,1:T(2,128)(2,1)S(1)}, u32[]{:S(2)}, u32[]{:S(2)}) collective-permute-start(bf16[2,144,128]{2,0,1:T(2,128)(2,1)S(1)} %pad_maximum_fusion.4), channel_id=1, source_target_pairs={{0,8},{4,12},{8,0},{12,4},{16,24},{20,28},{24,16},{28,20},{1,9},{5... | collective-permute-start | bytes 221192 | tf_op jit(solution)/shard_map/ppermute | solution.py:102
  46.1 17.1 %collective-permute-start.5 = (bf16[2,2,128,512]{3,2,1,0:T(8,128)(2,1)S(1)}, bf16[2,2,128,512]{3,2,1,0:T(8,128)(2,1)S(1)}, u32[]{:S(2)}, u32[]{:S(2)}) collective-permute-start(bf16[2,2,128,512]{3,2,1,0:T(8,128)(2,1)S(1)} %get-tuple-element.62), channel_id=1, source_target_pairs={{0,4},{4,0},{8,12},{12,8},{16,20},{20,16},{24,28},{28,24},{1,5},{5... | collective-permute-start | bytes 1572872 | tf_op jit(solution)/shard_map/ppermute | solution.py:102
  47.6 15.5 %collective-permute-start.6 = (bf16[2,2,128,512]{3,2,1,0:T(8,128)(2,1)S(1)}, bf16[2,2,128,512]{3,2,1,0:T(8,128)(2,1)S(1)}, u32[]{:S(2)}, u32[]{:S(2)}) collective-permute-start(bf16[2,2,128,512]{3,2,1,0:T(8,128)(2,1)S(1)} %get-tuple-element.65), channel_id=1, source_target_pairs={{0,8},{4,12},{8,0},{12,4},{16,24},{20,28},{24,16},{28,20},{1,9},{5... | collective-permute-start | bytes 1572872 | tf_op jit(solution)/shard_map/ppermute | solution.py:102
  48.6 1.1 copy-start.3
  64.0 8.2 %collective-permute-start.7 = (bf16[2,128,512]{2,1,0:T(8,128)(2,1)}, bf16[2,128,512]{2,1,0:T(8,128)(2,1)}, u32[]{:S(2)}, u32[]{:S(2)}) collective-permute-start(bf16[2,128,512]{2,1,0:T(8,128)(2,1)} %get-tuple-element.67), channel_id=1, source_target_pairs={{0,8},{4,12},{8,0},{12,4},{16,24},{20,28},{24,16},{28,20},{1,9},{5... | collective-permute-start | bytes 786440 | tf_op jit(solution)/shard_map/ppermute | solution.py:102
  65.1 7.8 %collective-permute-start.8 = (bf16[2,128,512]{2,1,0:T(8,128)(2,1)}, bf16[2,128,512]{2,1,0:T(8,128)(2,1)}, u32[]{:S(2)}, u32[]{:S(2)}) collective-permute-start(bf16[2,128,512]{2,1,0:T(8,128)(2,1)} %get-tuple-element.69), channel_id=1, source_target_pairs={{0,4},{4,0},{8,12},{12,8},{16,20},{20,16},{24,28},{28,24},{1,5},{5... | collective-permute-start | bytes 786440 | tf_op jit(solution)/shard_map/ppermute | solution.py:102
  74.6 13.5 %collective-permute-start.10 = (bf16[256,512]{1,0:T(8,128)(2,1)S(1)}, bf16[256,512]{1,0:T(8,128)(2,1)S(1)}, u32[]{:S(2)}, u32[]{:S(2)}) collective-permute-start(bf16[256,512]{1,0:T(8,128)(2,1)S(1)} %get-tuple-element.75), channel_id=1, source_target_pairs={{0,16},{4,20},{8,24},{12,28},{16,0},{20,4},{24,8},{28,12},{1,17},{... | collective-permute-start | bytes 786440 | tf_op jit(solution)/shard_map/ppermute | solution.py:102
  77.7 5.2 %collective-permute-start.9 = (bf16[4,144,128]{2,0,1:T(4,128)(2,1)S(1)}, bf16[4,144,128]{2,0,1:T(4,128)(2,1)S(1)}, u32[]{:S(2)}, u32[]{:S(2)}) collective-permute-start(bf16[4,144,128]{2,0,1:T(4,128)(2,1)S(1)} %pad_maximum_fusion.3), channel_id=1, source_target_pairs={{0,4},{4,0},{8,12},{12,8},{16,20},{20,16},{24,28},{28,24},{1,5},{5... | collective-permute-start | bytes 442376 | tf_op jit(solution)/shard_map/ppermute | solution.py:102
  90.2 30.1 %all-to-all-start = ((bf16[8,128,512]{2,1,0:T(8,128)(2,1)}), bf16[8,128,512]{2,1,0:T(8,128)(2,1)}, u32[]{:S(2)}, u32[]{:S(2)}) async-start(bf16[8,128,512]{2,1,0:T(8,128)(2,1)} %shard_map.116), calls=%async_computation | async-start | bytes 2097152 | tf_op jit(solution)/shard_map/all_to_all | solution.py:773
  125.8 3.5 %collective-permute-start.11 = (bf16[2,768,128]{2,1,0:T(8,128)(2,1)S(1)}, bf16[2,768,128]{2,1,0:T(8,128)(2,1)S(1)}, u32[]{:S(2)}, u32[]{:S(2)}) collective-permute-start(bf16[2,768,128]{2,1,0:T(8,128)(2,1)S(1)} %get-tuple-element.78), channel_id=1, source_target_pairs={{0,1},{1,0},{2,3},{3,2},{4,5},{5,4},{6,7},{7,6},{8,9},{9,8},{10,11... | collective-permute-start | bytes 1179656 | tf_op jit(solution)/shard_map/ppermute | solution.py:102
  129.3 7.4 %collective-permute-start.12 = (bf16[768,128]{1,0:T(8,128)(2,1)S(1)}, bf16[768,128]{1,0:T(8,128)(2,1)S(1)}, u32[]{:S(2)}, u32[]{:S(2)}) collective-permute-start(bf16[768,128]{1,0:T(8,128)(2,1)S(1)} %shard_map.120), channel_id=1, source_target_pairs={{0,2},{1,3},{2,0},{3,1},{4,6},{5,7},{6,4},{7,5},{8,10},{9,11},{10,... | collective-permute-start | bytes 589832 | tf_op jit(solution)/shard_map/ppermute | solution.py:102
  129.9 29.9 %copy-start.1 = (bf16[2048,768]{1,0:T(8,128)(2,1)S(1)}, bf16[2048,768]{1,0:T(8,128)(2,1)}, u32[]{:S(2)}) copy-start(bf16[2048,768]{1,0:T(8,128)(2,1)} %w_ref.3) | copy-start | bytes 9437188
  136.9 10.9 %collective-permute-start.13 = (bf16[128,768]{1,0:T(8,128)(2,1)S(1)}, bf16[128,768]{1,0:T(8,128)(2,1)S(1)}, u32[]{:S(2)}, u32[]{:S(2)}) collective-permute-start(bf16[128,768]{1,0:T(8,128)(2,1)S(1)} %shard_map.121.refs_0_), channel_id=1, source_target_pairs={{0,16},{4,20},{8,24},{12,28},{16,0},{20,4},{24,8},{28,12},{1,17},{... | collective-permute-start | bytes 589832 | tf_op jit(solution)/shard_map/ppermute | solution.py:102
  137.0 10.8 %collective-permute-start.14 = (bf16[128,768]{1,0:T(8,128)(2,1)S(1)}, bf16[128,768]{1,0:T(8,128)(2,1)S(1)}, u32[]{:S(2)}, u32[]{:S(2)}) collective-permute-start(bf16[128,768]{1,0:T(8,128)(2,1)S(1)} %shard_map.121.refs_0_), channel_id=1, source_target_pairs={{0,8},{4,12},{8,0},{12,4},{16,24},{20,28},{24,16},{28,20},{1,9},{5... | collective-permute-start | bytes 589832 | tf_op jit(solution)/shard_map/ppermute | solution.py:102
  138.9 8.9 %collective-permute-start.15 = (bf16[128,768]{1,0:T(8,128)(2,1)S(1)}, bf16[128,768]{1,0:T(8,128)(2,1)S(1)}, u32[]{:S(2)}, u32[]{:S(2)}) collective-permute-start(bf16[128,768]{1,0:T(8,128)(2,1)S(1)} %shard_map.121.refs_0_), channel_id=1, source_target_pairs={{0,4},{4,0},{8,12},{12,8},{16,20},{20,16},{24,28},{28,24},{1,5},{5... | collective-permute-start | bytes 589832 | tf_op jit(solution)/shard_map/ppermute | solution.py:102
  147.8 6.8 %collective-permute-start.16 = (bf16[128,768]{1,0:T(8,128)(2,1)S(1)}, bf16[128,768]{1,0:T(8,128)(2,1)S(1)}, u32[]{:S(2)}, u32[]{:S(2)}) collective-permute-start(bf16[128,768]{1,0:T(8,128)(2,1)S(1)} %collective-permute-done.13.refs_1_.refs_0_), channel_id=1, source_target_pairs={{0,8},{4,12},{8,0},{12,4},{16,24},{20,28},{24,16},{28,20},{1,9},{5... | collective-permute-start | bytes 589832 | tf_op jit(solution)/shard_map/ppermute | solution.py:102
  147.8 7.9 %collective-permute-start.17 = (bf16[128,768]{1,0:T(8,128)(2,1)S(1)}, bf16[128,768]{1,0:T(8,128)(2,1)S(1)}, u32[]{:S(2)}, u32[]{:S(2)}) collective-permute-start(bf16[128,768]{1,0:T(8,128)(2,1)S(1)} %collective-permute-done.13.refs_1_.refs_0_), channel_id=1, source_target_pairs={{0,4},{4,0},{8,12},{12,8},{16,20},{20,16},{24,28},{28,24},{1,5},{5... | collective-permute-start | bytes 589832 | tf_op jit(solution)/shard_map/ppermute | solution.py:102
  149.2 10.6 %collective-permute-start.18 = (bf16[128,768]{1,0:T(8,128)(2,1)S(1)}, bf16[128,768]{1,0:T(8,128)(2,1)S(1)}, u32[]{:S(2)}, u32[]{:S(2)}) collective-permute-start(bf16[128,768]{1,0:T(8,128)(2,1)S(1)} %collective-permute-done.14.refs_2_), channel_id=1, source_target_pairs={{0,4},{4,0},{8,12},{12,8},{16,20},{20,16},{24,28},{28,24},{1,5},{5... | collective-permute-start | bytes 589832 | tf_op jit(solution)/shard_map/ppermute | solution.py:102
  154.5 8.5 %collective-permute-start.19 = (bf16[128,768]{1,0:T(8,128)(2,1)S(1)}, bf16[128,768]{1,0:T(8,128)(2,1)S(1)}, u32[]{:S(2)}, u32[]{:S(2)}) collective-permute-start(bf16[128,768]{1,0:T(8,128)(2,1)S(1)} %collective-permute-done.16.refs_3_.refs_2_), channel_id=1, source_target_pairs={{0,4},{4,0},{8,12},{12,8},{16,20},{20,16},{24,28},{28,24},{1,5},{5... | collective-permute-start | bytes 589832 | tf_op jit(solution)/shard_map/ppermute | solution.py:102
  160.9 1.4 collective-permute-start.20
  162.4 10.6 %copy-start.2 = (bf16[384,1024]{1,0:T(8,128)(2,1)S(1)}, bf16[384,1024]{1,0:T(8,128)(2,1)}, u32[]{:S(2)}) copy-start(bf16[384,1024]{1,0:T(8,128)(2,1)} %fusion.7.c.lhs_ref) | copy-start | bytes 2359300
  164.2 1.4 collective-permute-start.22
  164.2 6.4 %collective-permute-start.21 = (bf16[2,256,128]{2,1,0:T(8,128)(2,1)S(1)}, bf16[2,256,128]{2,1,0:T(8,128)(2,1)S(1)}, u32[]{:S(2)}, u32[]{:S(2)}) collective-permute-start(bf16[2,256,128]{2,1,0:T(8,128)(2,1)S(1)} %shard_map.124.refs_4_.p0), channel_id=1, source_target_pairs={{0,2},{1,3},{2,0},{3,1},{4,6},{5,7},{6,4},{7,5},{8,10},{9,11},{10,... | collective-permute-start | bytes 393224 | tf_op jit(solution)/shard_map/ppermute | solution.py:102
  165.6 7.4 %collective-permute-start.23 = (bf16[2,256,128]{2,1,0:T(8,128)(2,1)S(1)}, bf16[2,256,128]{2,1,0:T(8,128)(2,1)S(1)}, u32[]{:S(2)}, u32[]{:S(2)}) collective-permute-start(bf16[2,256,128]{2,1,0:T(8,128)(2,1)S(1)} %shard_map.126.p1), channel_id=1, source_target_pairs={{0,2},{1,3},{2,0},{3,1},{4,6},{5,7},{6,4},{7,5},{8,10},{9,11},{10,... | collective-permute-start | bytes 393224 | tf_op jit(solution)/shard_map/ppermute | solution.py:102
  173.9 1.8 %collective-permute-start.24 = (f32[384,256]{1,0:T(8,128)S(1)}, f32[384,256]{1,0:T(8,128)S(1)}, u32[]{:S(2)}, u32[]{:S(2)}) collective-permute-start(f32[384,256]{1,0:T(8,128)S(1)} %shard_map.127.own), channel_id=1, source_target_pairs={{0,1},{1,0},{2,3},{3,2},{4,5},{5,4},{6,7},{7,6},{8,9},{9,8},{10,11... | collective-permute-start | bytes 1179656 | tf_op jit(solution)/shard_map/ppermute | solution.py:102

commit v11 on v10

--- a/solution.py
+++ b/solution.py
@@ -354,7 +354,7 @@
         images = (images,)
         extra = (after, waves)
     else:
-        shapes = [sent, kept, sent, kept, pltpu.HBM(both, BF)] + shapes
+        shapes = [sent, kept, sent, kept, jax.ShapeDtypeStruct(both, BF)] + shapes
         specs = [
             block((1, 2, half, tile), lambda j, me: (jnp.minimum(j, 1), 0, 0, 0)),
             whole(kept.shape),

time: 177 us -> 176 us (level)
  no operation moved by 1% of the time
where the time goes in v11:
time: 176 us; the launch traced here: 175 us
  waiting for transfers between devices  70.6 us (40%)
  Pallas kernels  66.2 us (38%)
  starting transfers between devices  27.4 us (16%)
  matrix products  4.34 us (2%)
  local copies, waits for them, and re-layouts  3.8 us (2%)
  other arithmetic  1.78 us (1%)
    ppermute x25, waiting for transfers between devices, swap(): return lax.ppermute(x, axis, [(i, i ^ bit) for i in range(n)])  48.1 us
    pallas_call x2, Pallas kernels, feature_sums(): pl.pallas_call(functools.partial(features_kernel, masks, last, *totals),...  42.4 us
    ppermute x25, starting transfers between devices, swap(): return lax.ppermute(x, axis, [(i, i ^ bit) for i in range(n)])  22.9 us
    all_to_all x1, waiting for transfers between devices, eight_by_four(): feat_grad = lax.all_to_all(feat_grad, 'rec', 0, 0, tiled=True)  22.5 us
    pallas_call x3, Pallas kernels, image_grads(): pl.pallas_call(sent_kernel if sent else kept_kernel, grid_spec=spec, out_...  12.6 us
    all_to_all x1, starting transfers between devices, eight_by_four(): feat_grad = lax.all_to_all(feat_grad, 'rec', 0, 0, tiled=True)  4.47 us
  transfers between devices with their start and end apart: 26, of which 17 were waited for; matrix products, arithmetic and copies ran while one was open for 3% of the time, Pallas kernels for 30%

profile of v11, /device:TPU:0, one launch (start us, length us, event | category | flops | bytes accessed | tf_op | source)
XLA Modules:
  0.0 175.1 jit_solution(1986785229782309681)
XLA Ops:
  0.7 1.2 copy-done
  1.9 1.0 fusion.12
  2.9 2.9 %fusion.4.refs_0_.image = bf16[128,768]{1,0:T(8,128)(2,1)S(1)} fusion(bf16[2048,768]{1,0:T(8,128)(2,1)} %w_ref.3, f32[128,2048]{1,0:T(8,128)S(1)} %fusion.12, bf16[128,128]{1,0:T(8,128)(2,1)} %param.15, bf16[128,2048]{1,0:T(8,128)(2,1)} %param.17), kind=kOutput, calls=%fused_computation.5 | convolution fusion | flops 470646784 | bytes 4947968 | tf_op jit(solution)/shard_map/dot_general | solution.py:722
  5.8 3.0 %collective-permute-start = (bf16[128,768]{1,0:T(8,128)(2,1)S(1)}, bf16[128,768]{1,0:T(8,128)(2,1)S(1)}, u32[]{:S(2)}, u32[]{:S(2)}) collective-permute-start(bf16[128,768]{1,0:T(8,128)(2,1)S(1)} %fusion.4.refs_0_.image), channel_id=1, source_target_pairs={{0,2},{1,3},{2,0},{3,1},{4,6},{5,7},{6,4},{7,5},{8,10},{9,11},{10,... | collective-permute-start | bytes 589832 | tf_op jit(solution)/shard_map/ppermute | solution.py:102
  8.9 2.7 %collective-permute-start.1 = (bf16[1,144,128]{2,0,1:T(2,128)(2,1)S(1)}, bf16[1,144,128]{2,0,1:T(2,128)(2,1)S(1)}, u32[]{:S(2)}, u32[]{:S(2)}) collective-permute-start(bf16[1,144,128]{2,0,1:T(2,128)(2,1)S(1)} %copy.15), channel_id=1, source_target_pairs={{0,16},{4,20},{8,24},{12,28},{16,0},{20,4},{24,8},{28,12},{1,17},{... | collective-permute-start | bytes 110600 | tf_op jit(solution)/shard_map/ppermute | solution.py:102
  11.6 3.8 %collective-permute-done.1 = bf16[1,144,128]{2,0,1:T(2,128)(2,1)S(1)} collective-permute-done((bf16[1,144,128]{2,0,1:T(2,128)(2,1)S(1)}, bf16[1,144,128]{2,0,1:T(2,128)(2,1)S(1)}, u32[]{:S(2)}, u32[]{:S(2)}) %collective-permute-start.1) | collective-permute-done | bytes 36896 | tf_op jit(solution)/shard_map/ppermute | solution.py:102
  16.8 28.9 %shard_map.112 = (bf16[2,2,128,512]{3,2,1,0:T(8,128)(2,1)S(1)}, f32[2,128,512]{2,1,0:T(8,128)S(1)}, bf16[2,2,128,512]{3,2,1,0:T(8,128)(2,1)S(1)}, f32[2,128,512]...) custom-call(s32[6]{0:T(128)S(1)} %stack.27.me_ref.refs_6_, ...), custom_call_target="tpu_custom_call" | custom-call | flops 18320719872 | bytes 18874368 | tf_op jit(solution)/shard_map/pallas_call | solution.py:381
  45.8 1.5 collective-permute-start.5
  47.3 1.0 collective-permute-start.6
  48.3 13.4 %shard_map.113 = (f32[2,128,512]{2,1,0:T(8,128)S(1)}, f32[2,128,512]{2,1,0:T(8,128)S(1)}, f32[4,2,128,512]{3,2,1,0:T(8,128)}, f32[8,128]{1,0:T(8,128)S(1)}) custom-call(s32[6]{0:T(128)S(1)} %stack.27.me_ref.refs_6_, s32[1,1536]{1,0:T(1,128)S(1)} %reshape.61.real_labels_ref, s32[1,128]{1,0:T(1,128)S(1)} %bitcast.32, ...), custom_call_target="tpu_custom_call", output_to_operand_aliasing={{2}: (7, {})} | custom-call | flops 6106906624 | bytes 12582912 | tf_op jit(solution)/shard_map/pallas_call | solution.py:381
  61.7 0.9 shard_map.114
  62.6 1.1 collective-permute-start.7
  64.2 1.2 constant_dynamic-slice_fusion
  65.5 5.3 %collective-permute-done.7.ga = bf16[2,128,512]{2,1,0:T(8,128)(2,1)} collective-permute-done((bf16[2,128,512]{2,1,0:T(8,128)(2,1)}, bf16[2,128,512]{2,1,0:T(8,128)(2,1)}, u32[]{:S(2)}, u32[]{:S(2)}) %collective-permute-start.7) | collective-permute-done | bytes 262176 | tf_op jit(solution)/shard_map/ppermute | solution.py:102
  70.8 0.7 collective-permute-done.8.gb
  71.5 1.7 shard_map.115
  73.2 2.9 %collective-permute-start.10 = (bf16[256,512]{1,0:T(8,128)(2,1)S(1)}, bf16[256,512]{1,0:T(8,128)(2,1)S(1)}, u32[]{:S(2)}, u32[]{:S(2)}) collective-permute-start(bf16[256,512]{1,0:T(8,128)(2,1)S(1)} %get-tuple-element.75), channel_id=1, source_target_pairs={{0,16},{4,20},{8,24},{12,28},{16,0},{20,4},{24,8},{28,12},{1,17},{... | collective-permute-start | bytes 786440 | tf_op jit(solution)/shard_map/ppermute | solution.py:102
  76.9 4.6 %collective-permute-done.9 = bf16[4,144,128]{2,0,1:T(4,128)(2,1)S(1)} collective-permute-done((bf16[4,144,128]{2,0,1:T(4,128)(2,1)S(1)}, bf16[4,144,128]{2,0,1:T(4,128)(2,1)S(1)}, u32[]{:S(2)}, u32[]{:S(2)}) %collective-permute-start.9) | collective-permute-done | bytes 147488 | tf_op jit(solution)/shard_map/ppermute | solution.py:102
  81.5 5.2 %collective-permute-done.10.got_ref = bf16[256,512]{1,0:T(8,128)(2,1)S(1)} collective-permute-done((bf16[256,512]{1,0:T(8,128)(2,1)S(1)}, bf16[256,512]{1,0:T(8,128)(2,1)S(1)}, u32[]{:S(2)}, u32[]{:S(2)}) %collective-permute-start.10) | collective-permute-done | bytes 262176 | tf_op jit(solution)/shard_map/ppermute | solution.py:102
  86.7 2.1 %shard_map.116 = bf16[8,128,512]{2,1,0:T(8,128)(2,1)} custom-call(s32[6]{0:T(128)S(1)} %stack.27.me_ref.refs_6_, f32[256,512]{1,0:T(8,128)S(1)} %get-tuple-element.74.keep_ref, bf16[256,512]{1,0:T(8,128)(2,1)S(1)} %collective-permute-done.10.got_ref, f32[256,512]{1,0:T(8,128)S(1)} %bitcast.30, s32[8,128]{1,0:T(8,128)S(1)} %get-tuple-element.89.labels_ref, ...), custom_call_target="tpu_custom_call" | custom-call | flops 268435456 | bytes 3145728 | tf_op jit(solution)/shard_map/pallas_call | solution.py:464
  88.8 4.5 %all-to-all-start = ((bf16[8,128,512]{2,1,0:T(8,128)(2,1)}), bf16[8,128,512]{2,1,0:T(8,128)(2,1)}, u32[]{:S(2)}, u32[]{:S(2)}) async-start(bf16[8,128,512]{2,1,0:T(8,128)(2,1)} %shard_map.116), calls=%async_computation | async-start | bytes 2097152 | tf_op jit(solution)/shard_map/all_to_all | solution.py:773
  93.2 0.8 constant_dynamic-slice_fusion.2
  94.8 1.0 fusion.7.c.lhs_ref
  96.4 22.5 %all-to-all-done.rows_ref = bf16[8,128,512]{2,1,0:T(8,128)(2,1)} async-done(((bf16[8,128,512]{2,1,0:T(8,128)(2,1)}), bf16[8,128,512]{2,1,0:T(8,128)(2,1)}, u32[]{:S(2)}, u32[]{:S(2)}) %all-to-all-start) | async-done | bytes 1048608 | tf_op jit(solution)/shard_map/all_to_all | solution.py:773
  118.9 5.5 %shard_map.117 = (bf16[2,768,128]{2,1,0:T(8,128)(2,1)S(1)}, bf16[128,2048]{1,0:T(8,128)(2,1)S(1)}) custom-call(s32[6]{0:T(128)S(1)} %stack.27.me_ref.refs_6_, f32[4,2,128,512]{3,2,1,0:T(8,128)} %get-tuple-element.73.wave_ref, bf16[8,128,512]{2,1,0:T(8,128)(2,1)} %all-to-all-done.rows_ref, bf16[3072,2048]{1,0:T(8,128)(2,1)} %freq_ref.5, ...), custom_call_target="tpu_custom_call" | custom-call | flops 805306368 | bytes 6291456 | tf_op jit(solution)/shard_map/pallas_call | solution.py:522
  124.5 3.4 %shard_map.119.a = f32[1,768,128]{2,1,0:T(8,128)S(1)} custom-call(s32[6]{0:T(128)S(1)} %stack.27.me_ref.refs_6_, bf16[128,2048]{1,0:T(8,128)(2,1)S(1)} %get-tuple-element.77.pre_ref, bf16[3072,2048]{1,0:T(8,128)(2,1)} %freq_ref.5), custom_call_target="tpu_custom_call" | custom-call | flops 805306368 | bytes 6291456 | tf_op jit(solution)/shard_map/pallas_call | solution.py:522
  128.5 3.7 %shard_map.118.keep = f32[1,768,128]{2,1,0:T(8,128)S(1)} custom-call(s32[6]{0:T(128)S(1)} %stack.27.me_ref.refs_6_, bf16[128,2048]{1,0:T(8,128)(2,1)S(1)} %get-tuple-element.77.pre_ref, bf16[3072,2048]{1,0:T(8,128)(2,1)} %freq_ref.5), custom_call_target="tpu_custom_call" | custom-call | flops 805306368 | bytes 6291456 | tf_op jit(solution)/shard_map/pallas_call | solution.py:522
  132.2 3.1 %collective-permute-done.12.far = bf16[768,128]{1,0:T(8,128)(2,1)S(1)} collective-permute-done((bf16[768,128]{1,0:T(8,128)(2,1)S(1)}, bf16[768,128]{1,0:T(8,128)(2,1)S(1)}, u32[]{:S(2)}, u32[]{:S(2)}) %collective-permute-start.12) | collective-permute-done | bytes 196640 | tf_op jit(solution)/shard_map/ppermute | solution.py:102
  135.6 1.9 %collective-permute-start.14 = (bf16[128,768]{1,0:T(8,128)(2,1)S(1)}, bf16[128,768]{1,0:T(8,128)(2,1)S(1)}, u32[]{:S(2)}, u32[]{:S(2)}) collective-permute-start(bf16[128,768]{1,0:T(8,128)(2,1)S(1)} %shard_map.121.refs_0_), channel_id=1, source_target_pairs={{0,8},{4,12},{8,0},{12,4},{16,24},{20,28},{24,16},{28,20},{1,9},{5... | collective-permute-start | bytes 589832 | tf_op jit(solution)/shard_map/ppermute | solution.py:102
  137.6 1.5 collective-permute-start.15
  139.0 7.4 %collective-permute-done.13.refs_1_.refs_0_ = bf16[128,768]{1,0:T(8,128)(2,1)S(1)} collective-permute-done((bf16[128,768]{1,0:T(8,128)(2,1)S(1)}, bf16[128,768]{1,0:T(8,128)(2,1)S(1)}, u32[]{:S(2)}, u32[]{:S(2)}) %collective-permute-start.13) | collective-permute-done | bytes 196640 | tf_op jit(solution)/shard_map/ppermute | solution.py:102
  146.4 1.4 collective-permute-start.17
  147.8 0.7 collective-permute-start.18
  148.5 4.7 %collective-permute-done.16.refs_3_.refs_2_ = bf16[128,768]{1,0:T(8,128)(2,1)S(1)} collective-permute-done((bf16[128,768]{1,0:T(8,128)(2,1)S(1)}, bf16[128,768]{1,0:T(8,128)(2,1)S(1)}, u32[]{:S(2)}, u32[]{:S(2)}) %collective-permute-start.16) | collective-permute-done | bytes 196640 | tf_op jit(solution)/shard_map/ppermute | solution.py:102
  153.2 1.1 collective-permute-start.19
  154.3 4.1 %collective-permute-done.18.refs_6_.refs_3_ = bf16[128,768]{1,0:T(8,128)(2,1)S(1)} collective-permute-done((bf16[128,768]{1,0:T(8,128)(2,1)S(1)}, bf16[128,768]{1,0:T(8,128)(2,1)S(1)}, u32[]{:S(2)}, u32[]{:S(2)}) %collective-permute-start.18) | collective-permute-done | bytes 196640 | tf_op jit(solution)/shard_map/ppermute | solution.py:102
  158.5 1.1 shard_map.123
  159.7 1.3 collective-permute-done.20.b
  161.0 0.6 collective-permute-done.19.refs_7_.refs_3_
  161.7 1.1 shard_map.125
  163.4 0.8 collective-permute-done.22.b
  164.2 0.8 collective-permute-start.23
  165.1 2.4 %shard_map.122 = (f32[256,768]{1,0:T(8,128)}, f32[8,128]{1,0:T(8,128)S(1)}) custom-call(s32[6]{0:T(128)S(1)} %stack.27.me_ref.refs_6_, bf16[256,1024]{1,0:T(8,128)(2,1)S(1)} %get-tuple-element.91.b.hidden_ref, bf16[128,768]{1,0:T(8,128)(2,1)S(1)} %shard_map.121.refs_0_, bf16[128,768]{1,0:T(8,128)(2,1)S(1)} %collective-permute-done.13.refs_1_.refs_0_, ...), custom_call_target="tpu_custom_call" | custom-call | flops 402653184 | bytes 4194304 | tf_op jit(solution)/shard_map/pallas_call | solution.py:635
  167.4 1.8 %collective-permute-done.21.q0 = bf16[2,256,128]{2,1,0:T(8,128)(2,1)S(1)} collective-permute-done((bf16[2,256,128]{2,1,0:T(8,128)(2,1)S(1)}, bf16[2,256,128]{2,1,0:T(8,128)(2,1)S(1)}, u32[]{:S(2)}, u32[]{:S(2)}) %collective-permute-start.21) | collective-permute-done | bytes 131104 | tf_op jit(solution)/shard_map/ppermute | solution.py:102
  169.2 2.4 %collective-permute-done.23.q1 = bf16[2,256,128]{2,1,0:T(8,128)(2,1)S(1)} collective-permute-done((bf16[2,256,128]{2,1,0:T(8,128)(2,1)S(1)}, bf16[2,256,128]{2,1,0:T(8,128)(2,1)S(1)}, u32[]{:S(2)}, u32[]{:S(2)}) %collective-permute-start.23) | collective-permute-done | bytes 131104 | tf_op jit(solution)/shard_map/ppermute | solution.py:102
  171.6 0.9 shard_map.127.own
  172.6 1.7 collective-permute-done.24.other
  174.3 0.8 shard_map.128
  (56 shorter events, 6.0 us)
Async XLA Ops:
  0.6 1.2 copy-start
  0.6 8.2 %copy-start.3 = (s32[128]{0:T(128)S(1)}, s32[128]{0:T(128)}, u32[]{:S(2)}) copy-start(s32[128]{0:T(128)} %param.16) | copy-start | bytes 1540
  0.7 8.2 %copy-start.4 = (bf16[128,128]{1,0:T(8,128)(2,1)S(1)}, bf16[128,128]{1,0:T(8,128)(2,1)}, u32[]{:S(2)}) copy-start(bf16[128,128]{1,0:T(8,128)(2,1)} %param.15) | copy-start | bytes 98308
  2.9 13.4 %copy-start.5 = (s32[1536]{0:T(1024)S(1)}, s32[1536]{0:T(1024)}, u32[]{:S(2)}) copy-start(s32[1536]{0:T(1024)} %param.12) | copy-start | bytes 18436
  5.8 9.6 %collective-permute-start = (bf16[128,768]{1,0:T(8,128)(2,1)S(1)}, bf16[128,768]{1,0:T(8,128)(2,1)S(1)}, u32[]{:S(2)}, u32[]{:S(2)}) collective-permute-start(bf16[128,768]{1,0:T(8,128)(2,1)S(1)} %fusion.4.refs_0_.image), channel_id=1, source_target_pairs={{0,2},{1,3},{2,0},{3,1},{4,6},{5,7},{6,4},{7,5},{8,10},{9,11},{10,... | collective-permute-start | bytes 589832 | tf_op jit(solution)/shard_map/ppermute | solution.py:102
  8.9 6.5 %collective-permute-start.1 = (bf16[1,144,128]{2,0,1:T(2,128)(2,1)S(1)}, bf16[1,144,128]{2,0,1:T(2,128)(2,1)S(1)}, u32[]{:S(2)}, u32[]{:S(2)}) collective-permute-start(bf16[1,144,128]{2,0,1:T(2,128)(2,1)S(1)} %copy.15), channel_id=1, source_target_pairs={{0,16},{4,20},{8,24},{12,28},{16,0},{20,4},{24,8},{28,12},{1,17},{... | collective-permute-start | bytes 110600 | tf_op jit(solution)/shard_map/ppermute | solution.py:102
  11.6 4.7 %collective-permute-start.3 = (bf16[128,768]{1,0:T(8,128)(2,1)S(1)}, bf16[128,768]{1,0:T(8,128)(2,1)S(1)}, u32[]{:S(2)}, u32[]{:S(2)}) collective-permute-start(bf16[128,768]{1,0:T(8,128)(2,1)S(1)} %fusion.4.refs_0_.image), channel_id=1, source_target_pairs={{0,1},{1,0},{2,3},{3,2},{4,5},{5,4},{6,7},{7,6},{8,9},{9,8},{10,11... | collective-permute-start | bytes 589832 | tf_op jit(solution)/shard_map/ppermute | solution.py:102
  15.4 1.4 collective-permute-start.4
  15.7 30.1 %collective-permute-start.2 = (bf16[2,144,128]{2,0,1:T(2,128)(2,1)S(1)}, bf16[2,144,128]{2,0,1:T(2,128)(2,1)S(1)}, u32[]{:S(2)}, u32[]{:S(2)}) collective-permute-start(bf16[2,144,128]{2,0,1:T(2,128)(2,1)S(1)} %pad_maximum_fusion.4), channel_id=1, source_target_pairs={{0,8},{4,12},{8,0},{12,4},{16,24},{20,28},{24,16},{28,20},{1,9},{5... | collective-permute-start | bytes 221192 | tf_op jit(solution)/shard_map/ppermute | solution.py:102
  45.8 15.9 %collective-permute-start.5 = (bf16[2,2,128,512]{3,2,1,0:T(8,128)(2,1)S(1)}, bf16[2,2,128,512]{3,2,1,0:T(8,128)(2,1)S(1)}, u32[]{:S(2)}, u32[]{:S(2)}) collective-permute-start(bf16[2,2,128,512]{3,2,1,0:T(8,128)(2,1)S(1)} %get-tuple-element.62), channel_id=1, source_target_pairs={{0,4},{4,0},{8,12},{12,8},{16,20},{20,16},{24,28},{28,24},{1,5},{5... | collective-permute-start | bytes 1572872 | tf_op jit(solution)/shard_map/ppermute | solution.py:102
  47.3 14.4 %collective-permute-start.6 = (bf16[2,2,128,512]{3,2,1,0:T(8,128)(2,1)S(1)}, bf16[2,2,128,512]{3,2,1,0:T(8,128)(2,1)S(1)}, u32[]{:S(2)}, u32[]{:S(2)}) collective-permute-start(bf16[2,2,128,512]{3,2,1,0:T(8,128)(2,1)S(1)} %get-tuple-element.65), channel_id=1, source_target_pairs={{0,8},{4,12},{8,0},{12,4},{16,24},{20,28},{24,16},{28,20},{1,9},{5... | collective-permute-start | bytes 1572872 | tf_op jit(solution)/shard_map/ppermute | solution.py:102
  62.6 8.2 %collective-permute-start.7 = (bf16[2,128,512]{2,1,0:T(8,128)(2,1)}, bf16[2,128,512]{2,1,0:T(8,128)(2,1)}, u32[]{:S(2)}, u32[]{:S(2)}) collective-permute-start(bf16[2,128,512]{2,1,0:T(8,128)(2,1)} %get-tuple-element.67), channel_id=1, source_target_pairs={{0,8},{4,12},{8,0},{12,4},{16,24},{20,28},{24,16},{28,20},{1,9},{5... | collective-permute-start | bytes 786440 | tf_op jit(solution)/shard_map/ppermute | solution.py:102
  63.7 7.8 %collective-permute-start.8 = (bf16[2,128,512]{2,1,0:T(8,128)(2,1)}, bf16[2,128,512]{2,1,0:T(8,128)(2,1)}, u32[]{:S(2)}, u32[]{:S(2)}) collective-permute-start(bf16[2,128,512]{2,1,0:T(8,128)(2,1)} %get-tuple-element.69), channel_id=1, source_target_pairs={{0,4},{4,0},{8,12},{12,8},{16,20},{20,16},{24,28},{28,24},{1,5},{5... | collective-permute-start | bytes 786440 | tf_op jit(solution)/shard_map/ppermute | solution.py:102
  73.2 13.5 %collective-permute-start.10 = (bf16[256,512]{1,0:T(8,128)(2,1)S(1)}, bf16[256,512]{1,0:T(8,128)(2,1)S(1)}, u32[]{:S(2)}, u32[]{:S(2)}) collective-permute-start(bf16[256,512]{1,0:T(8,128)(2,1)S(1)} %get-tuple-element.75), channel_id=1, source_target_pairs={{0,16},{4,20},{8,24},{12,28},{16,0},{20,4},{24,8},{28,12},{1,17},{... | collective-permute-start | bytes 786440 | tf_op jit(solution)/shard_map/ppermute | solution.py:102
  76.3 5.2 %collective-permute-start.9 = (bf16[4,144,128]{2,0,1:T(4,128)(2,1)S(1)}, bf16[4,144,128]{2,0,1:T(4,128)(2,1)S(1)}, u32[]{:S(2)}, u32[]{:S(2)}) collective-permute-start(bf16[4,144,128]{2,0,1:T(4,128)(2,1)S(1)} %pad_maximum_fusion.3), channel_id=1, source_target_pairs={{0,4},{4,0},{8,12},{12,8},{16,20},{20,16},{24,28},{28,24},{1,5},{5... | collective-permute-start | bytes 442376 | tf_op jit(solution)/shard_map/ppermute | solution.py:102
  88.8 30.1 %all-to-all-start = ((bf16[8,128,512]{2,1,0:T(8,128)(2,1)}), bf16[8,128,512]{2,1,0:T(8,128)(2,1)}, u32[]{:S(2)}, u32[]{:S(2)}) async-start(bf16[8,128,512]{2,1,0:T(8,128)(2,1)} %shard_map.116), calls=%async_computation | async-start | bytes 2097152 | tf_op jit(solution)/shard_map/all_to_all | solution.py:773
  124.4 3.5 %collective-permute-start.11 = (bf16[2,768,128]{2,1,0:T(8,128)(2,1)S(1)}, bf16[2,768,128]{2,1,0:T(8,128)(2,1)S(1)}, u32[]{:S(2)}, u32[]{:S(2)}) collective-permute-start(bf16[2,768,128]{2,1,0:T(8,128)(2,1)S(1)} %get-tuple-element.78), channel_id=1, source_target_pairs={{0,1},{1,0},{2,3},{3,2},{4,5},{5,4},{6,7},{7,6},{8,9},{9,8},{10,11... | collective-permute-start | bytes 1179656 | tf_op jit(solution)/shard_map/ppermute | solution.py:102
  128.0 7.4 %collective-permute-start.12 = (bf16[768,128]{1,0:T(8,128)(2,1)S(1)}, bf16[768,128]{1,0:T(8,128)(2,1)S(1)}, u32[]{:S(2)}, u32[]{:S(2)}) collective-permute-start(bf16[768,128]{1,0:T(8,128)(2,1)S(1)} %shard_map.120), channel_id=1, source_target_pairs={{0,2},{1,3},{2,0},{3,1},{4,6},{5,7},{6,4},{7,5},{8,10},{9,11},{10,... | collective-permute-start | bytes 589832 | tf_op jit(solution)/shard_map/ppermute | solution.py:102
  128.5 29.9 %copy-start.1 = (bf16[2048,768]{1,0:T(8,128)(2,1)S(1)}, bf16[2048,768]{1,0:T(8,128)(2,1)}, u32[]{:S(2)}) copy-start(bf16[2048,768]{1,0:T(8,128)(2,1)} %w_ref.3) | copy-start | bytes 9437188
  135.5 10.9 %collective-permute-start.13 = (bf16[128,768]{1,0:T(8,128)(2,1)S(1)}, bf16[128,768]{1,0:T(8,128)(2,1)S(1)}, u32[]{:S(2)}, u32[]{:S(2)}) collective-permute-start(bf16[128,768]{1,0:T(8,128)(2,1)S(1)} %shard_map.121.refs_0_), channel_id=1, source_target_pairs={{0,16},{4,20},{8,24},{12,28},{16,0},{20,4},{24,8},{28,12},{1,17},{... | collective-permute-start | bytes 589832 | tf_op jit(solution)/shard_map/ppermute | solution.py:102
  135.6 10.8 %collective-permute-start.14 = (bf16[128,768]{1,0:T(8,128)(2,1)S(1)}, bf16[128,768]{1,0:T(8,128)(2,1)S(1)}, u32[]{:S(2)}, u32[]{:S(2)}) collective-permute-start(bf16[128,768]{1,0:T(8,128)(2,1)S(1)} %shard_map.121.refs_0_), channel_id=1, source_target_pairs={{0,8},{4,12},{8,0},{12,4},{16,24},{20,28},{24,16},{28,20},{1,9},{5... | collective-permute-start | bytes 589832 | tf_op jit(solution)/shard_map/ppermute | solution.py:102
  137.6 8.9 %collective-permute-start.15 = (bf16[128,768]{1,0:T(8,128)(2,1)S(1)}, bf16[128,768]{1,0:T(8,128)(2,1)S(1)}, u32[]{:S(2)}, u32[]{:S(2)}) collective-permute-start(bf16[128,768]{1,0:T(8,128)(2,1)S(1)} %shard_map.121.refs_0_), channel_id=1, source_target_pairs={{0,4},{4,0},{8,12},{12,8},{16,20},{20,16},{24,28},{28,24},{1,5},{5... | collective-permute-start | bytes 589832 | tf_op jit(solution)/shard_map/ppermute | solution.py:102
  146.4 6.8 %collective-permute-start.16 = (bf16[128,768]{1,0:T(8,128)(2,1)S(1)}, bf16[128,768]{1,0:T(8,128)(2,1)S(1)}, u32[]{:S(2)}, u32[]{:S(2)}) collective-permute-start(bf16[128,768]{1,0:T(8,128)(2,1)S(1)} %collective-permute-done.13.refs_1_.refs_0_), channel_id=1, source_target_pairs={{0,8},{4,12},{8,0},{12,4},{16,24},{20,28},{24,16},{28,20},{1,9},{5... | collective-permute-start | bytes 589832 | tf_op jit(solution)/shard_map/ppermute | solution.py:102
  146.4 7.9 %collective-permute-start.17 = (bf16[128,768]{1,0:T(8,128)(2,1)S(1)}, bf16[128,768]{1,0:T(8,128)(2,1)S(1)}, u32[]{:S(2)}, u32[]{:S(2)}) collective-permute-start(bf16[128,768]{1,0:T(8,128)(2,1)S(1)} %collective-permute-done.13.refs_1_.refs_0_), channel_id=1, source_target_pairs={{0,4},{4,0},{8,12},{12,8},{16,20},{20,16},{24,28},{28,24},{1,5},{5... | collective-permute-start | bytes 589832 | tf_op jit(solution)/shard_map/ppermute | solution.py:102
  147.8 10.6 %collective-permute-start.18 = (bf16[128,768]{1,0:T(8,128)(2,1)S(1)}, bf16[128,768]{1,0:T(8,128)(2,1)S(1)}, u32[]{:S(2)}, u32[]{:S(2)}) collective-permute-start(bf16[128,768]{1,0:T(8,128)(2,1)S(1)} %collective-permute-done.14.refs_2_), channel_id=1, source_target_pairs={{0,4},{4,0},{8,12},{12,8},{16,20},{20,16},{24,28},{28,24},{1,5},{5... | collective-permute-start | bytes 589832 | tf_op jit(solution)/shard_map/ppermute | solution.py:102
  153.2 8.5 %collective-permute-start.19 = (bf16[128,768]{1,0:T(8,128)(2,1)S(1)}, bf16[128,768]{1,0:T(8,128)(2,1)S(1)}, u32[]{:S(2)}, u32[]{:S(2)}) collective-permute-start(bf16[128,768]{1,0:T(8,128)(2,1)S(1)} %collective-permute-done.16.refs_3_.refs_2_), channel_id=1, source_target_pairs={{0,4},{4,0},{8,12},{12,8},{16,20},{20,16},{24,28},{28,24},{1,5},{5... | collective-permute-start | bytes 589832 | tf_op jit(solution)/shard_map/ppermute | solution.py:102
  159.6 1.4 collective-permute-start.20
  161.0 10.6 %copy-start.2 = (bf16[384,1024]{1,0:T(8,128)(2,1)S(1)}, bf16[384,1024]{1,0:T(8,128)(2,1)}, u32[]{:S(2)}) copy-start(bf16[384,1024]{1,0:T(8,128)(2,1)} %fusion.7.c.lhs_ref) | copy-start | bytes 2359300
  162.8 1.4 collective-permute-start.22
  162.9 6.4 %collective-permute-start.21 = (bf16[2,256,128]{2,1,0:T(8,128)(2,1)S(1)}, bf16[2,256,128]{2,1,0:T(8,128)(2,1)S(1)}, u32[]{:S(2)}, u32[]{:S(2)}) collective-permute-start(bf16[2,256,128]{2,1,0:T(8,128)(2,1)S(1)} %shard_map.124.refs_4_.p0), channel_id=1, source_target_pairs={{0,2},{1,3},{2,0},{3,1},{4,6},{5,7},{6,4},{7,5},{8,10},{9,11},{10,... | collective-permute-start | bytes 393224 | tf_op jit(solution)/shard_map/ppermute | solution.py:102
  164.2 7.4 %collective-permute-start.23 = (bf16[2,256,128]{2,1,0:T(8,128)(2,1)S(1)}, bf16[2,256,128]{2,1,0:T(8,128)(2,1)S(1)}, u32[]{:S(2)}, u32[]{:S(2)}) collective-permute-start(bf16[2,256,128]{2,1,0:T(8,128)(2,1)S(1)} %shard_map.126.p1), channel_id=1, source_target_pairs={{0,2},{1,3},{2,0},{3,1},{4,6},{5,7},{6,4},{7,5},{8,10},{9,11},{10,... | collective-permute-start | bytes 393224 | tf_op jit(solution)/shard_map/ppermute | solution.py:102
  172.6 1.8 %collective-permute-start.24 = (f32[384,256]{1,0:T(8,128)S(1)}, f32[384,256]{1,0:T(8,128)S(1)}, u32[]{:S(2)}, u32[]{:S(2)}) collective-permute-start(f32[384,256]{1,0:T(8,128)S(1)} %shard_map.127.own), channel_id=1, source_target_pairs={{0,1},{1,0},{2,3},{3,2},{4,5},{5,4},{6,7},{7,6},{8,9},{9,8},{10,11... | collective-permute-start | bytes 1179656 | tf_op jit(solution)/shard_map/ppermute | solution.py:102

commit v12 on v11

--- a/solution.py
+++ b/solution.py
@@ -502,20 +502,21 @@
     k, n = freq.shape
     sent = kept is None
     rows = arrays[1].shape[1] if sent else arrays[0].shape[0]
-    count = 2 if sent else 1
+    count = 2
     whole = lambda shape: block(shape, lambda s, me: (0,) * len(shape))
 
     def source(s, me):
-        return (me[0] ^ (2 * (1 - s)) ^ 1, 0) if sent else (me[0] ^ (2 * (1 - kept)), 0)
-
-    out = block((1, cols, rows), lambda s, me: (s, 0, 0))
-    shape = jax.ShapeDtypeStruct((count, cols, rows), BF if sent else F32)
+        return (me[0] ^ (2 * (1 - s)) ^ 1, 0) if sent else (2 * (me[0] ^ (2 * (1 - kept))) + s, 0)
+
+    size = cols if sent else cols // 2
+    out = block((1, size, rows), (lambda s, me: (s, 0, 0)) if sent else (lambda s, me: (0, s, 0)))
+    shape = jax.ShapeDtypeStruct((2 if sent else 1, cols, rows), BF if sent else F32)
     pre = jax.ShapeDtypeStruct((rows, n), BF)
     spec = pltpu.PrefetchScalarGridSpec(
         num_scalar_prefetch=1,
         grid=(count,),
         in_specs=[whole(x.shape) for x in arrays]
-        + [block((cols, n), source)]
+        + [block((size, n), source)]
         + [pl.BlockSpec(memory_space=pl.ANY)] * len(after),
         out_specs=[out, whole(pre.shape)] if sent else out,
     )

time: 176 us -> 175 us (level)
  no operation moved by 1% of the time
where the time goes in v12:
time: 175 us
  waiting for transfers between devices  70.9 us (41%)
  Pallas kernels  65.7 us (38%)
  starting transfers between devices  27.3 us (16%)
  matrix products  4.34 us (2%)
  local copies, waits for them, and re-layouts  3.8 us (2%)
  other arithmetic  1.78 us (1%)
    ppermute x25, waiting for transfers between devices, swap(): return lax.ppermute(x, axis, [(i, i ^ bit) for i in range(n)])  48.4 us
    pallas_call x2, Pallas kernels, feature_sums(): pl.pallas_call(functools.partial(features_kernel, masks, last, *totals),...  42.4 us
    ppermute x25, starting transfers between devices, swap(): return lax.ppermute(x, axis, [(i, i ^ bit) for i in range(n)])  22.9 us
    all_to_all x1, waiting for transfers between devices, eight_by_four(): feat_grad = lax.all_to_all(feat_grad, 'rec', 0, 0, tiled=True)  22.5 us
    pallas_call x3, Pallas kernels, image_grads(): pl.pallas_call(sent_kernel if sent else kept_kernel, grid_spec=spec, out_...  12.1 us
    all_to_all x1, starting transfers between devices, eight_by_four(): feat_grad = lax.all_to_all(feat_grad, 'rec', 0, 0, tiled=True)  4.47 us
  transfers between devices with their start and end apart: 26, of which 17 were waited for; matrix products, arithmetic and copies ran while one was open for 3% of the time, Pallas kernels for 30%

profile of v12, /device:TPU:0, one launch (start us, length us, event | category | flops | bytes accessed | tf_op | source)
XLA Modules:
  0.0 174.8 jit_solution(12508897606925801254)
XLA Ops:
  0.7 1.2 copy-done
  1.9 1.0 fusion.12
  2.9 2.9 %fusion.4.refs_0_.image = bf16[128,768]{1,0:T(8,128)(2,1)S(1)} fusion(bf16[2048,768]{1,0:T(8,128)(2,1)} %w_ref.3, f32[128,2048]{1,0:T(8,128)S(1)} %fusion.12, bf16[128,128]{1,0:T(8,128)(2,1)} %param.15, bf16[128,2048]{1,0:T(8,128)(2,1)} %param.17), kind=kOutput, calls=%fused_computation.5 | convolution fusion | flops 470646784 | bytes 4947968 | tf_op jit(solution)/shard_map/dot_general | solution.py:723
  5.8 3.0 %collective-permute-start = (bf16[128,768]{1,0:T(8,128)(2,1)S(1)}, bf16[128,768]{1,0:T(8,128)(2,1)S(1)}, u32[]{:S(2)}, u32[]{:S(2)}) collective-permute-start(bf16[128,768]{1,0:T(8,128)(2,1)S(1)} %fusion.4.refs_0_.image), channel_id=1, source_target_pairs={{0,2},{1,3},{2,0},{3,1},{4,6},{5,7},{6,4},{7,5},{8,10},{9,11},{10,... | collective-permute-start | bytes 589832 | tf_op jit(solution)/shard_map/ppermute | solution.py:102
  8.9 2.7 %collective-permute-start.1 = (bf16[1,144,128]{2,0,1:T(2,128)(2,1)S(1)}, bf16[1,144,128]{2,0,1:T(2,128)(2,1)S(1)}, u32[]{:S(2)}, u32[]{:S(2)}) collective-permute-start(bf16[1,144,128]{2,0,1:T(2,128)(2,1)S(1)} %copy.15), channel_id=1, source_target_pairs={{0,16},{4,20},{8,24},{12,28},{16,0},{20,4},{24,8},{28,12},{1,17},{... | collective-permute-start | bytes 110600 | tf_op jit(solution)/shard_map/ppermute | solution.py:102
  11.6 3.8 %collective-permute-done.1 = bf16[1,144,128]{2,0,1:T(2,128)(2,1)S(1)} collective-permute-done((bf16[1,144,128]{2,0,1:T(2,128)(2,1)S(1)}, bf16[1,144,128]{2,0,1:T(2,128)(2,1)S(1)}, u32[]{:S(2)}, u32[]{:S(2)}) %collective-permute-start.1) | collective-permute-done | bytes 36896 | tf_op jit(solution)/shard_map/ppermute | solution.py:102
  16.8 28.9 %shard_map.112 = (bf16[2,2,128,512]{3,2,1,0:T(8,128)(2,1)S(1)}, f32[2,128,512]{2,1,0:T(8,128)S(1)}, bf16[2,2,128,512]{3,2,1,0:T(8,128)(2,1)S(1)}, f32[2,128,512]...) custom-call(s32[6]{0:T(128)S(1)} %stack.27.me_ref.refs_6_, ...), custom_call_target="tpu_custom_call" | custom-call | flops 18320719872 | bytes 18874368 | tf_op jit(solution)/shard_map/pallas_call | solution.py:381
  45.8 1.5 collective-permute-start.5
  47.3 1.0 collective-permute-start.6
  48.3 13.4 %shard_map.113 = (f32[2,128,512]{2,1,0:T(8,128)S(1)}, f32[2,128,512]{2,1,0:T(8,128)S(1)}, f32[4,2,128,512]{3,2,1,0:T(8,128)}, f32[8,128]{1,0:T(8,128)S(1)}) custom-call(s32[6]{0:T(128)S(1)} %stack.27.me_ref.refs_6_, s32[1,1536]{1,0:T(1,128)S(1)} %reshape.61.real_labels_ref, s32[1,128]{1,0:T(1,128)S(1)} %bitcast.32, ...), custom_call_target="tpu_custom_call", output_to_operand_aliasing={{2}: (7, {})} | custom-call | flops 6106906624 | bytes 12582912 | tf_op jit(solution)/shard_map/pallas_call | solution.py:381
  61.7 0.9 shard_map.114
  62.6 1.1 collective-permute-start.7
  64.2 1.2 constant_dynamic-slice_fusion
  65.5 5.3 %collective-permute-done.7.ga = bf16[2,128,512]{2,1,0:T(8,128)(2,1)} collective-permute-done((bf16[2,128,512]{2,1,0:T(8,128)(2,1)}, bf16[2,128,512]{2,1,0:T(8,128)(2,1)}, u32[]{:S(2)}, u32[]{:S(2)}) %collective-permute-start.7) | collective-permute-done | bytes 262176 | tf_op jit(solution)/shard_map/ppermute | solution.py:102
  70.8 0.7 collective-permute-done.8.gb
  71.5 1.7 shard_map.115
  73.2 2.9 %collective-permute-start.10 = (bf16[256,512]{1,0:T(8,128)(2,1)S(1)}, bf16[256,512]{1,0:T(8,128)(2,1)S(1)}, u32[]{:S(2)}, u32[]{:S(2)}) collective-permute-start(bf16[256,512]{1,0:T(8,128)(2,1)S(1)} %get-tuple-element.75), channel_id=1, source_target_pairs={{0,16},{4,20},{8,24},{12,28},{16,0},{20,4},{24,8},{28,12},{1,17},{... | collective-permute-start | bytes 786440 | tf_op jit(solution)/shard_map/ppermute | solution.py:102
  76.9 4.6 %collective-permute-done.9 = bf16[4,144,128]{2,0,1:T(4,128)(2,1)S(1)} collective-permute-done((bf16[4,144,128]{2,0,1:T(4,128)(2,1)S(1)}, bf16[4,144,128]{2,0,1:T(4,128)(2,1)S(1)}, u32[]{:S(2)}, u32[]{:S(2)}) %collective-permute-start.9) | collective-permute-done | bytes 147488 | tf_op jit(solution)/shard_map/ppermute | solution.py:102
  81.5 5.2 %collective-permute-done.10.got_ref = bf16[256,512]{1,0:T(8,128)(2,1)S(1)} collective-permute-done((bf16[256,512]{1,0:T(8,128)(2,1)S(1)}, bf16[256,512]{1,0:T(8,128)(2,1)S(1)}, u32[]{:S(2)}, u32[]{:S(2)}) %collective-permute-start.10) | collective-permute-done | bytes 262176 | tf_op jit(solution)/shard_map/ppermute | solution.py:102
  86.7 2.1 %shard_map.116 = bf16[8,128,512]{2,1,0:T(8,128)(2,1)} custom-call(s32[6]{0:T(128)S(1)} %stack.27.me_ref.refs_6_, f32[256,512]{1,0:T(8,128)S(1)} %get-tuple-element.74.keep_ref, bf16[256,512]{1,0:T(8,128)(2,1)S(1)} %collective-permute-done.10.got_ref, f32[256,512]{1,0:T(8,128)S(1)} %bitcast.30, s32[8,128]{1,0:T(8,128)S(1)} %get-tuple-element.89.labels_ref, ...), custom_call_target="tpu_custom_call" | custom-call | flops 268435456 | bytes 3145728 | tf_op jit(solution)/shard_map/pallas_call | solution.py:464
  88.8 4.5 %all-to-all-start = ((bf16[8,128,512]{2,1,0:T(8,128)(2,1)}), bf16[8,128,512]{2,1,0:T(8,128)(2,1)}, u32[]{:S(2)}, u32[]{:S(2)}) async-start(bf16[8,128,512]{2,1,0:T(8,128)(2,1)} %shard_map.116), calls=%async_computation | async-start | bytes 2097152 | tf_op jit(solution)/shard_map/all_to_all | solution.py:774
  93.2 0.8 constant_dynamic-slice_fusion.2
  94.8 1.0 fusion.7.c.lhs_ref
  96.4 22.5 %all-to-all-done.rows_ref = bf16[8,128,512]{2,1,0:T(8,128)(2,1)} async-done(((bf16[8,128,512]{2,1,0:T(8,128)(2,1)}), bf16[8,128,512]{2,1,0:T(8,128)(2,1)}, u32[]{:S(2)}, u32[]{:S(2)}) %all-to-all-start) | async-done | bytes 1048608 | tf_op jit(solution)/shard_map/all_to_all | solution.py:774
  118.9 5.5 %shard_map.117 = (bf16[2,768,128]{2,1,0:T(8,128)(2,1)S(1)}, bf16[128,2048]{1,0:T(8,128)(2,1)S(1)}) custom-call(s32[6]{0:T(128)S(1)} %stack.27.me_ref.refs_6_, f32[4,2,128,512]{3,2,1,0:T(8,128)} %get-tuple-element.73.wave_ref, bf16[8,128,512]{2,1,0:T(8,128)(2,1)} %all-to-all-done.rows_ref, bf16[3072,2048]{1,0:T(8,128)(2,1)} %freq_ref.5, ...), custom_call_target="tpu_custom_call" | custom-call | flops 805306368 | bytes 6291456 | tf_op jit(solution)/shard_map/pallas_call | solution.py:523
  124.5 3.1 %shard_map.119.a = f32[1,768,128]{2,1,0:T(8,128)S(1)} custom-call(s32[6]{0:T(128)S(1)} %stack.27.me_ref.refs_6_, bf16[128,2048]{1,0:T(8,128)(2,1)S(1)} %get-tuple-element.77.pre_ref, bf16[3072,2048]{1,0:T(8,128)(2,1)} %freq_ref.5), custom_call_target="tpu_custom_call" | custom-call | flops 805306368 | bytes 6291456 | tf_op jit(solution)/shard_map/pallas_call | solution.py:523
  128.3 3.4 %shard_map.118.keep = f32[1,768,128]{2,1,0:T(8,128)S(1)} custom-call(s32[6]{0:T(128)S(1)} %stack.27.me_ref.refs_6_, bf16[128,2048]{1,0:T(8,128)(2,1)S(1)} %get-tuple-element.77.pre_ref, bf16[3072,2048]{1,0:T(8,128)(2,1)} %freq_ref.5), custom_call_target="tpu_custom_call" | custom-call | flops 805306368 | bytes 6291456 | tf_op jit(solution)/shard_map/pallas_call | solution.py:523
  131.7 3.4 %collective-permute-done.12.far = bf16[768,128]{1,0:T(8,128)(2,1)S(1)} collective-permute-done((bf16[768,128]{1,0:T(8,128)(2,1)S(1)}, bf16[768,128]{1,0:T(8,128)(2,1)S(1)}, u32[]{:S(2)}, u32[]{:S(2)}) %collective-permute-start.12) | collective-permute-done | bytes 196640 | tf_op jit(solution)/shard_map/ppermute | solution.py:102
  135.3 1.9 %collective-permute-start.14 = (bf16[128,768]{1,0:T(8,128)(2,1)S(1)}, bf16[128,768]{1,0:T(8,128)(2,1)S(1)}, u32[]{:S(2)}, u32[]{:S(2)}) collective-permute-start(bf16[128,768]{1,0:T(8,128)(2,1)S(1)} %shard_map.121.refs_0_), channel_id=1, source_target_pairs={{0,8},{4,12},{8,0},{12,4},{16,24},{20,28},{24,16},{28,20},{1,9},{5... | collective-permute-start | bytes 589832 | tf_op jit(solution)/shard_map/ppermute | solution.py:102
  137.3 1.5 collective-permute-start.15
  138.7 7.4 %collective-permute-done.13.refs_1_.refs_0_ = bf16[128,768]{1,0:T(8,128)(2,1)S(1)} collective-permute-done((bf16[128,768]{1,0:T(8,128)(2,1)S(1)}, bf16[128,768]{1,0:T(8,128)(2,1)S(1)}, u32[]{:S(2)}, u32[]{:S(2)}) %collective-permute-start.13) | collective-permute-done | bytes 196640 | tf_op jit(solution)/shard_map/ppermute | solution.py:102
  146.1 1.4 collective-permute-start.17
  147.6 0.7 collective-permute-start.18
  148.2 4.7 %collective-permute-done.16.refs_3_.refs_2_ = bf16[128,768]{1,0:T(8,128)(2,1)S(1)} collective-permute-done((bf16[128,768]{1,0:T(8,128)(2,1)S(1)}, bf16[128,768]{1,0:T(8,128)(2,1)S(1)}, u32[]{:S(2)}, u32[]{:S(2)}) %collective-permute-start.16) | collective-permute-done | bytes 196640 | tf_op jit(solution)/shard_map/ppermute | solution.py:102
  152.9 1.1 collective-permute-start.19
  154.0 4.1 %collective-permute-done.18.refs_6_.refs_3_ = bf16[128,768]{1,0:T(8,128)(2,1)S(1)} collective-permute-done((bf16[128,768]{1,0:T(8,128)(2,1)S(1)}, bf16[128,768]{1,0:T(8,128)(2,1)S(1)}, u32[]{:S(2)}, u32[]{:S(2)}) %collective-permute-start.18) | collective-permute-done | bytes 196640 | tf_op jit(solution)/shard_map/ppermute | solution.py:102
  158.2 1.1 shard_map.123
  159.4 1.3 collective-permute-done.20.b
  160.8 0.6 collective-permute-done.19.refs_7_.refs_3_
  161.4 1.1 shard_map.125
  163.2 0.8 collective-permute-done.22.b
  164.0 0.8 collective-permute-start.23
  164.8 2.4 %shard_map.122 = (f32[256,768]{1,0:T(8,128)}, f32[8,128]{1,0:T(8,128)S(1)}) custom-call(s32[6]{0:T(128)S(1)} %stack.27.me_ref.refs_6_, bf16[256,1024]{1,0:T(8,128)(2,1)S(1)} %get-tuple-element.91.b.hidden_ref, bf16[128,768]{1,0:T(8,128)(2,1)S(1)} %shard_map.121.refs_0_, bf16[128,768]{1,0:T(8,128)(2,1)S(1)} %collective-permute-done.13.refs_1_.refs_0_, ...), custom_call_target="tpu_custom_call" | custom-call | flops 402653184 | bytes 4194304 | tf_op jit(solution)/shard_map/pallas_call | solution.py:636
  167.2 1.8 %collective-permute-done.21.q0 = bf16[2,256,128]{2,1,0:T(8,128)(2,1)S(1)} collective-permute-done((bf16[2,256,128]{2,1,0:T(8,128)(2,1)S(1)}, bf16[2,256,128]{2,1,0:T(8,128)(2,1)S(1)}, u32[]{:S(2)}, u32[]{:S(2)}) %collective-permute-start.21) | collective-permute-done | bytes 131104 | tf_op jit(solution)/shard_map/ppermute | solution.py:102
  169.0 2.4 %collective-permute-done.23.q1 = bf16[2,256,128]{2,1,0:T(8,128)(2,1)S(1)} collective-permute-done((bf16[2,256,128]{2,1,0:T(8,128)(2,1)S(1)}, bf16[2,256,128]{2,1,0:T(8,128)(2,1)S(1)}, u32[]{:S(2)}, u32[]{:S(2)}) %collective-permute-start.23) | collective-permute-done | bytes 131104 | tf_op jit(solution)/shard_map/ppermute | solution.py:102
  171.3 0.9 shard_map.127.own
  172.3 1.7 collective-permute-done.24.other
  174.1 0.8 shard_map.128
  (56 shorter events, 6.0 us)
Async XLA Ops:
  0.6 1.2 copy-start
  0.6 8.2 %copy-start.3 = (s32[128]{0:T(128)S(1)}, s32[128]{0:T(128)}, u32[]{:S(2)}) copy-start(s32[128]{0:T(128)} %param.16) | copy-start | bytes 1540
  0.7 8.2 %copy-start.4 = (bf16[128,128]{1,0:T(8,128)(2,1)S(1)}, bf16[128,128]{1,0:T(8,128)(2,1)}, u32[]{:S(2)}) copy-start(bf16[128,128]{1,0:T(8,128)(2,1)} %param.15) | copy-start | bytes 98308
  2.9 13.4 %copy-start.5 = (s32[1536]{0:T(1024)S(1)}, s32[1536]{0:T(1024)}, u32[]{:S(2)}) copy-start(s32[1536]{0:T(1024)} %param.12) | copy-start | bytes 18436
  5.8 9.6 %collective-permute-start = (bf16[128,768]{1,0:T(8,128)(2,1)S(1)}, bf16[128,768]{1,0:T(8,128)(2,1)S(1)}, u32[]{:S(2)}, u32[]{:S(2)}) collective-permute-start(bf16[128,768]{1,0:T(8,128)(2,1)S(1)} %fusion.4.refs_0_.image), channel_id=1, source_target_pairs={{0,2},{1,3},{2,0},{3,1},{4,6},{5,7},{6,4},{7,5},{8,10},{9,11},{10,... | collective-permute-start | bytes 589832 | tf_op jit(solution)/shard_map/ppermute | solution.py:102
  8.9 6.5 %collective-permute-start.1 = (bf16[1,144,128]{2,0,1:T(2,128)(2,1)S(1)}, bf16[1,144,128]{2,0,1:T(2,128)(2,1)S(1)}, u32[]{:S(2)}, u32[]{:S(2)}) collective-permute-start(bf16[1,144,128]{2,0,1:T(2,128)(2,1)S(1)} %copy.15), channel_id=1, source_target_pairs={{0,16},{4,20},{8,24},{12,28},{16,0},{20,4},{24,8},{28,12},{1,17},{... | collective-permute-start | bytes 110600 | tf_op jit(solution)/shard_map/ppermute | solution.py:102
  11.6 4.7 %collective-permute-start.3 = (bf16[128,768]{1,0:T(8,128)(2,1)S(1)}, bf16[128,768]{1,0:T(8,128)(2,1)S(1)}, u32[]{:S(2)}, u32[]{:S(2)}) collective-permute-start(bf16[128,768]{1,0:T(8,128)(2,1)S(1)} %fusion.4.refs_0_.image), channel_id=1, source_target_pairs={{0,1},{1,0},{2,3},{3,2},{4,5},{5,4},{6,7},{7,6},{8,9},{9,8},{10,11... | collective-permute-start | bytes 589832 | tf_op jit(solution)/shard_map/ppermute | solution.py:102
  15.4 1.4 collective-permute-start.4
  15.7 30.1 %collective-permute-start.2 = (bf16[2,144,128]{2,0,1:T(2,128)(2,1)S(1)}, bf16[2,144,128]{2,0,1:T(2,128)(2,1)S(1)}, u32[]{:S(2)}, u32[]{:S(2)}) collective-permute-start(bf16[2,144,128]{2,0,1:T(2,128)(2,1)S(1)} %pad_maximum_fusion.4), channel_id=1, source_target_pairs={{0,8},{4,12},{8,0},{12,4},{16,24},{20,28},{24,16},{28,20},{1,9},{5... | collective-permute-start | bytes 221192 | tf_op jit(solution)/shard_map/ppermute | solution.py:102
  45.8 15.9 %collective-permute-start.5 = (bf16[2,2,128,512]{3,2,1,0:T(8,128)(2,1)S(1)}, bf16[2,2,128,512]{3,2,1,0:T(8,128)(2,1)S(1)}, u32[]{:S(2)}, u32[]{:S(2)}) collective-permute-start(bf16[2,2,128,512]{3,2,1,0:T(8,128)(2,1)S(1)} %get-tuple-element.62), channel_id=1, source_target_pairs={{0,4},{4,0},{8,12},{12,8},{16,20},{20,16},{24,28},{28,24},{1,5},{5... | collective-permute-start | bytes 1572872 | tf_op jit(solution)/shard_map/ppermute | solution.py:102
  47.3 14.4 %collective-permute-start.6 = (bf16[2,2,128,512]{3,2,1,0:T(8,128)(2,1)S(1)}, bf16[2,2,128,512]{3,2,1,0:T(8,128)(2,1)S(1)}, u32[]{:S(2)}, u32[]{:S(2)}) collective-permute-start(bf16[2,2,128,512]{3,2,1,0:T(8,128)(2,1)S(1)} %get-tuple-element.65), channel_id=1, source_target_pairs={{0,8},{4,12},{8,0},{12,4},{16,24},{20,28},{24,16},{28,20},{1,9},{5... | collective-permute-start | bytes 1572872 | tf_op jit(solution)/shard_map/ppermute | solution.py:102
  62.6 8.2 %collective-permute-start.7 = (bf16[2,128,512]{2,1,0:T(8,128)(2,1)}, bf16[2,128,512]{2,1,0:T(8,128)(2,1)}, u32[]{:S(2)}, u32[]{:S(2)}) collective-permute-start(bf16[2,128,512]{2,1,0:T(8,128)(2,1)} %get-tuple-element.67), channel_id=1, source_target_pairs={{0,8},{4,12},{8,0},{12,4},{16,24},{20,28},{24,16},{28,20},{1,9},{5... | collective-permute-start | bytes 786440 | tf_op jit(solution)/shard_map/ppermute | solution.py:102
  63.7 7.8 %collective-permute-start.8 = (bf16[2,128,512]{2,1,0:T(8,128)(2,1)}, bf16[2,128,512]{2,1,0:T(8,128)(2,1)}, u32[]{:S(2)}, u32[]{:S(2)}) collective-permute-start(bf16[2,128,512]{2,1,0:T(8,128)(2,1)} %get-tuple-element.69), channel_id=1, source_target_pairs={{0,4},{4,0},{8,12},{12,8},{16,20},{20,16},{24,28},{28,24},{1,5},{5... | collective-permute-start | bytes 786440 | tf_op jit(solution)/shard_map/ppermute | solution.py:102
  73.2 13.5 %collective-permute-start.10 = (bf16[256,512]{1,0:T(8,128)(2,1)S(1)}, bf16[256,512]{1,0:T(8,128)(2,1)S(1)}, u32[]{:S(2)}, u32[]{:S(2)}) collective-permute-start(bf16[256,512]{1,0:T(8,128)(2,1)S(1)} %get-tuple-element.75), channel_id=1, source_target_pairs={{0,16},{4,20},{8,24},{12,28},{16,0},{20,4},{24,8},{28,12},{1,17},{... | collective-permute-start | bytes 786440 | tf_op jit(solution)/shard_map/ppermute | solution.py:102
  76.3 5.2 %collective-permute-start.9 = (bf16[4,144,128]{2,0,1:T(4,128)(2,1)S(1)}, bf16[4,144,128]{2,0,1:T(4,128)(2,1)S(1)}, u32[]{:S(2)}, u32[]{:S(2)}) collective-permute-start(bf16[4,144,128]{2,0,1:T(4,128)(2,1)S(1)} %pad_maximum_fusion.3), channel_id=1, source_target_pairs={{0,4},{4,0},{8,12},{12,8},{16,20},{20,16},{24,28},{28,24},{1,5},{5... | collective-permute-start | bytes 442376 | tf_op jit(solution)/shard_map/ppermute | solution.py:102
  88.8 30.1 %all-to-all-start = ((bf16[8,128,512]{2,1,0:T(8,128)(2,1)}), bf16[8,128,512]{2,1,0:T(8,128)(2,1)}, u32[]{:S(2)}, u32[]{:S(2)}) async-start(bf16[8,128,512]{2,1,0:T(8,128)(2,1)} %shard_map.116), calls=%async_computation | async-start | bytes 2097152 | tf_op jit(solution)/shard_map/all_to_all | solution.py:774
  124.4 3.2 %collective-permute-start.11 = (bf16[2,768,128]{2,1,0:T(8,128)(2,1)S(1)}, bf16[2,768,128]{2,1,0:T(8,128)(2,1)S(1)}, u32[]{:S(2)}, u32[]{:S(2)}) collective-permute-start(bf16[2,768,128]{2,1,0:T(8,128)(2,1)S(1)} %get-tuple-element.78), channel_id=1, source_target_pairs={{0,1},{1,0},{2,3},{3,2},{4,5},{5,4},{6,7},{7,6},{8,9},{9,8},{10,11... | collective-permute-start | bytes 1179656 | tf_op jit(solution)/shard_map/ppermute | solution.py:102
  127.7 7.4 %collective-permute-start.12 = (bf16[768,128]{1,0:T(8,128)(2,1)S(1)}, bf16[768,128]{1,0:T(8,128)(2,1)S(1)}, u32[]{:S(2)}, u32[]{:S(2)}) collective-permute-start(bf16[768,128]{1,0:T(8,128)(2,1)S(1)} %shard_map.120), channel_id=1, source_target_pairs={{0,2},{1,3},{2,0},{3,1},{4,6},{5,7},{6,4},{7,5},{8,10},{9,11},{10,... | collective-permute-start | bytes 589832 | tf_op jit(solution)/shard_map/ppermute | solution.py:102
  128.3 29.9 %copy-start.1 = (bf16[2048,768]{1,0:T(8,128)(2,1)S(1)}, bf16[2048,768]{1,0:T(8,128)(2,1)}, u32[]{:S(2)}) copy-start(bf16[2048,768]{1,0:T(8,128)(2,1)} %w_ref.3) | copy-start | bytes 9437188
  135.2 10.9 %collective-permute-start.13 = (bf16[128,768]{1,0:T(8,128)(2,1)S(1)}, bf16[128,768]{1,0:T(8,128)(2,1)S(1)}, u32[]{:S(2)}, u32[]{:S(2)}) collective-permute-start(bf16[128,768]{1,0:T(8,128)(2,1)S(1)} %shard_map.121.refs_0_), channel_id=1, source_target_pairs={{0,16},{4,20},{8,24},{12,28},{16,0},{20,4},{24,8},{28,12},{1,17},{... | collective-permute-start | bytes 589832 | tf_op jit(solution)/shard_map/ppermute | solution.py:102
  135.3 10.8 %collective-permute-start.14 = (bf16[128,768]{1,0:T(8,128)(2,1)S(1)}, bf16[128,768]{1,0:T(8,128)(2,1)S(1)}, u32[]{:S(2)}, u32[]{:S(2)}) collective-permute-start(bf16[128,768]{1,0:T(8,128)(2,1)S(1)} %shard_map.121.refs_0_), channel_id=1, source_target_pairs={{0,8},{4,12},{8,0},{12,4},{16,24},{20,28},{24,16},{28,20},{1,9},{5... | collective-permute-start | bytes 589832 | tf_op jit(solution)/shard_map/ppermute | solution.py:102
  137.3 8.9 %collective-permute-start.15 = (bf16[128,768]{1,0:T(8,128)(2,1)S(1)}, bf16[128,768]{1,0:T(8,128)(2,1)S(1)}, u32[]{:S(2)}, u32[]{:S(2)}) collective-permute-start(bf16[128,768]{1,0:T(8,128)(2,1)S(1)} %shard_map.121.refs_0_), channel_id=1, source_target_pairs={{0,4},{4,0},{8,12},{12,8},{16,20},{20,16},{24,28},{28,24},{1,5},{5... | collective-permute-start | bytes 589832 | tf_op jit(solution)/shard_map/ppermute | solution.py:102
  146.1 6.8 %collective-permute-start.16 = (bf16[128,768]{1,0:T(8,128)(2,1)S(1)}, bf16[128,768]{1,0:T(8,128)(2,1)S(1)}, u32[]{:S(2)}, u32[]{:S(2)}) collective-permute-start(bf16[128,768]{1,0:T(8,128)(2,1)S(1)} %collective-permute-done.13.refs_1_.refs_0_), channel_id=1, source_target_pairs={{0,8},{4,12},{8,0},{12,4},{16,24},{20,28},{24,16},{28,20},{1,9},{5... | collective-permute-start | bytes 589832 | tf_op jit(solution)/shard_map/ppermute | solution.py:102
  146.1 7.9 %collective-permute-start.17 = (bf16[128,768]{1,0:T(8,128)(2,1)S(1)}, bf16[128,768]{1,0:T(8,128)(2,1)S(1)}, u32[]{:S(2)}, u32[]{:S(2)}) collective-permute-start(bf16[128,768]{1,0:T(8,128)(2,1)S(1)} %collective-permute-done.13.refs_1_.refs_0_), channel_id=1, source_target_pairs={{0,4},{4,0},{8,12},{12,8},{16,20},{20,16},{24,28},{28,24},{1,5},{5... | collective-permute-start | bytes 589832 | tf_op jit(solution)/shard_map/ppermute | solution.py:102
  147.6 10.6 %collective-permute-start.18 = (bf16[128,768]{1,0:T(8,128)(2,1)S(1)}, bf16[128,768]{1,0:T(8,128)(2,1)S(1)}, u32[]{:S(2)}, u32[]{:S(2)}) collective-permute-start(bf16[128,768]{1,0:T(8,128)(2,1)S(1)} %collective-permute-done.14.refs_2_), channel_id=1, source_target_pairs={{0,4},{4,0},{8,12},{12,8},{16,20},{20,16},{24,28},{28,24},{1,5},{5... | collective-permute-start | bytes 589832 | tf_op jit(solution)/shard_map/ppermute | solution.py:102
  152.9 8.5 %collective-permute-start.19 = (bf16[128,768]{1,0:T(8,128)(2,1)S(1)}, bf16[128,768]{1,0:T(8,128)(2,1)S(1)}, u32[]{:S(2)}, u32[]{:S(2)}) collective-permute-start(bf16[128,768]{1,0:T(8,128)(2,1)S(1)} %collective-permute-done.16.refs_3_.refs_2_), channel_id=1, source_target_pairs={{0,4},{4,0},{8,12},{12,8},{16,20},{20,16},{24,28},{28,24},{1,5},{5... | collective-permute-start | bytes 589832 | tf_op jit(solution)/shard_map/ppermute | solution.py:102
  159.3 1.4 collective-permute-start.20
  160.7 10.6 %copy-start.2 = (bf16[384,1024]{1,0:T(8,128)(2,1)S(1)}, bf16[384,1024]{1,0:T(8,128)(2,1)}, u32[]{:S(2)}) copy-start(bf16[384,1024]{1,0:T(8,128)(2,1)} %fusion.7.c.lhs_ref) | copy-start | bytes 2359300
  162.5 1.4 collective-permute-start.22
  162.6 6.4 %collective-permute-start.21 = (bf16[2,256,128]{2,1,0:T(8,128)(2,1)S(1)}, bf16[2,256,128]{2,1,0:T(8,128)(2,1)S(1)}, u32[]{:S(2)}, u32[]{:S(2)}) collective-permute-start(bf16[2,256,128]{2,1,0:T(8,128)(2,1)S(1)} %shard_map.124.refs_4_.p0), channel_id=1, source_target_pairs={{0,2},{1,3},{2,0},{3,1},{4,6},{5,7},{6,4},{7,5},{8,10},{9,11},{10,... | collective-permute-start | bytes 393224 | tf_op jit(solution)/shard_map/ppermute | solution.py:102
  164.0 7.4 %collective-permute-start.23 = (bf16[2,256,128]{2,1,0:T(8,128)(2,1)S(1)}, bf16[2,256,128]{2,1,0:T(8,128)(2,1)S(1)}, u32[]{:S(2)}, u32[]{:S(2)}) collective-permute-start(bf16[2,256,128]{2,1,0:T(8,128)(2,1)S(1)} %shard_map.126.p1), channel_id=1, source_target_pairs={{0,2},{1,3},{2,0},{3,1},{4,6},{5,7},{6,4},{7,5},{8,10},{9,11},{10,... | collective-permute-start | bytes 393224 | tf_op jit(solution)/shard_map/ppermute | solution.py:102
  172.3 1.8 %collective-permute-start.24 = (f32[384,256]{1,0:T(8,128)S(1)}, f32[384,256]{1,0:T(8,128)S(1)}, u32[]{:S(2)}, u32[]{:S(2)}) collective-permute-start(f32[384,256]{1,0:T(8,128)S(1)} %shard_map.127.own), channel_id=1, source_target_pairs={{0,1},{1,0},{2,3},{3,2},{4,5},{5,4},{6,7},{7,6},{8,9},{9,8},{10,11... | collective-permute-start | bytes 1179656 | tf_op jit(solution)/shard_map/ppermute | solution.py:102

commit v13 on v12

--- a/solution.py
+++ b/solution.py
@@ -502,14 +502,14 @@
     k, n = freq.shape
     sent = kept is None
     rows = arrays[1].shape[1] if sent else arrays[0].shape[0]
-    count = 2
+    count = 4 if sent else 2
     whole = lambda shape: block(shape, lambda s, me: (0,) * len(shape))
 
     def source(s, me):
-        return (me[0] ^ (2 * (1 - s)) ^ 1, 0) if sent else (2 * (me[0] ^ (2 * (1 - kept))) + s, 0)
-
-    size = cols if sent else cols // 2
-    out = block((1, size, rows), (lambda s, me: (s, 0, 0)) if sent else (lambda s, me: (0, s, 0)))
+        return (2 * (me[0] ^ (2 * (1 - s // 2)) ^ 1) + s % 2, 0) if sent else (2 * (me[0] ^ (2 * (1 - kept))) + s, 0)
+
+    size = cols // 2
+    out = block((1, size, rows), lambda s, me: (s // 2, s % 2, 0))
     shape = jax.ShapeDtypeStruct((2 if sent else 1, cols, rows), BF if sent else F32)
     pre = jax.ShapeDtypeStruct((rows, n), BF)
     spec = pltpu.PrefetchScalarGridSpec(

time: 175 us -> 176 us (level)
  no operation moved by 1% of the time
where the time goes in v13:
time: 176 us
  waiting for transfers between devices  70.9 us (40%)
  Pallas kernels  66.6 us (38%)
  starting transfers between devices  27.4 us (16%)
  matrix products  4.34 us (2%)
  local copies, waits for them, and re-layouts  3.8 us (2%)
  other arithmetic  1.78 us (1%)
    ppermute x25, waiting for transfers between devices, swap(): return lax.ppermute(x, axis, [(i, i ^ bit) for i in range(n)])  48.4 us
    pallas_call x2, Pallas kernels, feature_sums(): pl.pallas_call(functools.partial(features_kernel, masks, last, *totals),...  42.4 us
    ppermute x25, starting transfers between devices, swap(): return lax.ppermute(x, axis, [(i, i ^ bit) for i in range(n)])  22.9 us
    all_to_all x1, waiting for transfers between devices, eight_by_four(): feat_grad = lax.all_to_all(feat_grad, 'rec', 0, 0, tiled=True)  22.5 us
    pallas_call x3, Pallas kernels, image_grads(): pl.pallas_call(sent_kernel if sent else kept_kernel, grid_spec=spec, out_...  13 us
    all_to_all x1, starting transfers between devices, eight_by_four(): feat_grad = lax.all_to_all(feat_grad, 'rec', 0, 0, tiled=True)  4.47 us
  transfers between devices with their start and end apart: 26, of which 17 were waited for; matrix products, arithmetic and copies ran while one was open for 3% of the time, Pallas kernels for 30%

profile of v13, /device:TPU:0, one launch (start us, length us, event | category | flops | bytes accessed | tf_op | source)
XLA Modules:
  0.0 175.8 jit_solution(7492511179155172735)
XLA Ops:
  0.7 1.2 copy-done
  1.9 1.0 fusion.12
  2.9 2.9 %fusion.4.refs_0_.image = bf16[128,768]{1,0:T(8,128)(2,1)S(1)} fusion(bf16[2048,768]{1,0:T(8,128)(2,1)} %w_ref.3, f32[128,2048]{1,0:T(8,128)S(1)} %fusion.12, bf16[128,128]{1,0:T(8,128)(2,1)} %param.15, bf16[128,2048]{1,0:T(8,128)(2,1)} %param.17), kind=kOutput, calls=%fused_computation.5 | convolution fusion | flops 470646784 | bytes 4947968 | tf_op jit(solution)/shard_map/dot_general | solution.py:723
  5.8 3.0 %collective-permute-start = (bf16[128,768]{1,0:T(8,128)(2,1)S(1)}, bf16[128,768]{1,0:T(8,128)(2,1)S(1)}, u32[]{:S(2)}, u32[]{:S(2)}) collective-permute-start(bf16[128,768]{1,0:T(8,128)(2,1)S(1)} %fusion.4.refs_0_.image), channel_id=1, source_target_pairs={{0,2},{1,3},{2,0},{3,1},{4,6},{5,7},{6,4},{7,5},{8,10},{9,11},{10,... | collective-permute-start | bytes 589832 | tf_op jit(solution)/shard_map/ppermute | solution.py:102
  8.9 2.7 %collective-permute-start.1 = (bf16[1,144,128]{2,0,1:T(2,128)(2,1)S(1)}, bf16[1,144,128]{2,0,1:T(2,128)(2,1)S(1)}, u32[]{:S(2)}, u32[]{:S(2)}) collective-permute-start(bf16[1,144,128]{2,0,1:T(2,128)(2,1)S(1)} %copy.15), channel_id=1, source_target_pairs={{0,16},{4,20},{8,24},{12,28},{16,0},{20,4},{24,8},{28,12},{1,17},{... | collective-permute-start | bytes 110600 | tf_op jit(solution)/shard_map/ppermute | solution.py:102
  11.6 3.8 %collective-permute-done.1 = bf16[1,144,128]{2,0,1:T(2,128)(2,1)S(1)} collective-permute-done((bf16[1,144,128]{2,0,1:T(2,128)(2,1)S(1)}, bf16[1,144,128]{2,0,1:T(2,128)(2,1)S(1)}, u32[]{:S(2)}, u32[]{:S(2)}) %collective-permute-start.1) | collective-permute-done | bytes 36896 | tf_op jit(solution)/shard_map/ppermute | solution.py:102
  16.8 28.9 %shard_map.112 = (bf16[2,2,128,512]{3,2,1,0:T(8,128)(2,1)S(1)}, f32[2,128,512]{2,1,0:T(8,128)S(1)}, bf16[2,2,128,512]{3,2,1,0:T(8,128)(2,1)S(1)}, f32[2,128,512]...) custom-call(s32[6]{0:T(128)S(1)} %stack.27.me_ref.refs_6_, ...), custom_call_target="tpu_custom_call" | custom-call | flops 18320719872 | bytes 18874368 | tf_op jit(solution)/shard_map/pallas_call | solution.py:381
  45.8 1.5 collective-permute-start.5
  47.3 1.0 collective-permute-start.6
  48.3 13.4 %shard_map.113 = (f32[2,128,512]{2,1,0:T(8,128)S(1)}, f32[2,128,512]{2,1,0:T(8,128)S(1)}, f32[4,2,128,512]{3,2,1,0:T(8,128)}, f32[8,128]{1,0:T(8,128)S(1)}) custom-call(s32[6]{0:T(128)S(1)} %stack.27.me_ref.refs_6_, s32[1,1536]{1,0:T(1,128)S(1)} %reshape.61.real_labels_ref, s32[1,128]{1,0:T(1,128)S(1)} %bitcast.32, ...), custom_call_target="tpu_custom_call", output_to_operand_aliasing={{2}: (7, {})} | custom-call | flops 6106906624 | bytes 12582912 | tf_op jit(solution)/shard_map/pallas_call | solution.py:381
  61.7 0.9 shard_map.114
  62.6 1.1 collective-permute-start.7
  64.2 1.2 constant_dynamic-slice_fusion
  65.5 5.3 %collective-permute-done.7.ga = bf16[2,128,512]{2,1,0:T(8,128)(2,1)} collective-permute-done((bf16[2,128,512]{2,1,0:T(8,128)(2,1)}, bf16[2,128,512]{2,1,0:T(8,128)(2,1)}, u32[]{:S(2)}, u32[]{:S(2)}) %collective-permute-start.7) | collective-permute-done | bytes 262176 | tf_op jit(solution)/shard_map/ppermute | solution.py:102
  70.8 0.7 collective-permute-done.8.gb
  71.5 1.7 shard_map.115
  73.2 2.9 %collective-permute-start.10 = (bf16[256,512]{1,0:T(8,128)(2,1)S(1)}, bf16[256,512]{1,0:T(8,128)(2,1)S(1)}, u32[]{:S(2)}, u32[]{:S(2)}) collective-permute-start(bf16[256,512]{1,0:T(8,128)(2,1)S(1)} %get-tuple-element.75), channel_id=1, source_target_pairs={{0,16},{4,20},{8,24},{12,28},{16,0},{20,4},{24,8},{28,12},{1,17},{... | collective-permute-start | bytes 786440 | tf_op jit(solution)/shard_map/ppermute | solution.py:102
  76.9 4.6 %collective-permute-done.9 = bf16[4,144,128]{2,0,1:T(4,128)(2,1)S(1)} collective-permute-done((bf16[4,144,128]{2,0,1:T(4,128)(2,1)S(1)}, bf16[4,144,128]{2,0,1:T(4,128)(2,1)S(1)}, u32[]{:S(2)}, u32[]{:S(2)}) %collective-permute-start.9) | collective-permute-done | bytes 147488 | tf_op jit(solution)/shard_map/ppermute | solution.py:102
  81.5 5.2 %collective-permute-done.10.got_ref = bf16[256,512]{1,0:T(8,128)(2,1)S(1)} collective-permute-done((bf16[256,512]{1,0:T(8,128)(2,1)S(1)}, bf16[256,512]{1,0:T(8,128)(2,1)S(1)}, u32[]{:S(2)}, u32[]{:S(2)}) %collective-permute-start.10) | collective-permute-done | bytes 262176 | tf_op jit(solution)/shard_map/ppermute | solution.py:102
  86.7 2.1 %shard_map.116 = bf16[8,128,512]{2,1,0:T(8,128)(2,1)} custom-call(s32[6]{0:T(128)S(1)} %stack.27.me_ref.refs_6_, f32[256,512]{1,0:T(8,128)S(1)} %get-tuple-element.74.keep_ref, bf16[256,512]{1,0:T(8,128)(2,1)S(1)} %collective-permute-done.10.got_ref, f32[256,512]{1,0:T(8,128)S(1)} %bitcast.30, s32[8,128]{1,0:T(8,128)S(1)} %get-tuple-element.89.labels_ref, ...), custom_call_target="tpu_custom_call" | custom-call | flops 268435456 | bytes 3145728 | tf_op jit(solution)/shard_map/pallas_call | solution.py:464
  88.8 4.5 %all-to-all-start = ((bf16[8,128,512]{2,1,0:T(8,128)(2,1)}), bf16[8,128,512]{2,1,0:T(8,128)(2,1)}, u32[]{:S(2)}, u32[]{:S(2)}) async-start(bf16[8,128,512]{2,1,0:T(8,128)(2,1)} %shard_map.116), calls=%async_computation | async-start | bytes 2097152 | tf_op jit(solution)/shard_map/all_to_all | solution.py:774
  93.2 0.8 constant_dynamic-slice_fusion.2
  94.8 1.0 fusion.7.c.lhs_ref
  96.4 22.5 %all-to-all-done.rows_ref = bf16[8,128,512]{2,1,0:T(8,128)(2,1)} async-done(((bf16[8,128,512]{2,1,0:T(8,128)(2,1)}), bf16[8,128,512]{2,1,0:T(8,128)(2,1)}, u32[]{:S(2)}, u32[]{:S(2)}) %all-to-all-start) | async-done | bytes 1048608 | tf_op jit(solution)/shard_map/all_to_all | solution.py:774
  118.9 6.5 %shard_map.117 = (bf16[2,768,128]{2,1,0:T(8,128)(2,1)S(1)}, bf16[128,2048]{1,0:T(8,128)(2,1)S(1)}) custom-call(s32[6]{0:T(128)S(1)} %stack.27.me_ref.refs_6_, f32[4,2,128,512]{3,2,1,0:T(8,128)} %get-tuple-element.73.wave_ref, bf16[8,128,512]{2,1,0:T(8,128)(2,1)} %all-to-all-done.rows_ref, bf16[3072,2048]{1,0:T(8,128)(2,1)} %freq_ref.5, ...), custom_call_target="tpu_custom_call" | custom-call | flops 805306368 | bytes 6291456 | tf_op jit(solution)/shard_map/pallas_call | solution.py:523
  125.4 3.1 %shard_map.119.a = f32[1,768,128]{2,1,0:T(8,128)S(1)} custom-call(s32[6]{0:T(128)S(1)} %stack.27.me_ref.refs_6_, bf16[128,2048]{1,0:T(8,128)(2,1)S(1)} %get-tuple-element.77.pre_ref, bf16[3072,2048]{1,0:T(8,128)(2,1)} %freq_ref.5), custom_call_target="tpu_custom_call" | custom-call | flops 805306368 | bytes 6291456 | tf_op jit(solution)/shard_map/pallas_call | solution.py:523
  129.2 3.4 %shard_map.118.keep = f32[1,768,128]{2,1,0:T(8,128)S(1)} custom-call(s32[6]{0:T(128)S(1)} %stack.27.me_ref.refs_6_, bf16[128,2048]{1,0:T(8,128)(2,1)S(1)} %get-tuple-element.77.pre_ref, bf16[3072,2048]{1,0:T(8,128)(2,1)} %freq_ref.5), custom_call_target="tpu_custom_call" | custom-call | flops 805306368 | bytes 6291456 | tf_op jit(solution)/shard_map/pallas_call | solution.py:523
  132.6 3.4 %collective-permute-done.12.far = bf16[768,128]{1,0:T(8,128)(2,1)S(1)} collective-permute-done((bf16[768,128]{1,0:T(8,128)(2,1)S(1)}, bf16[768,128]{1,0:T(8,128)(2,1)S(1)}, u32[]{:S(2)}, u32[]{:S(2)}) %collective-permute-start.12) | collective-permute-done | bytes 196640 | tf_op jit(solution)/shard_map/ppermute | solution.py:102
  136.3 1.9 %collective-permute-start.14 = (bf16[128,768]{1,0:T(8,128)(2,1)S(1)}, bf16[128,768]{1,0:T(8,128)(2,1)S(1)}, u32[]{:S(2)}, u32[]{:S(2)}) collective-permute-start(bf16[128,768]{1,0:T(8,128)(2,1)S(1)} %shard_map.121.refs_0_), channel_id=1, source_target_pairs={{0,8},{4,12},{8,0},{12,4},{16,24},{20,28},{24,16},{28,20},{1,9},{5... | collective-permute-start | bytes 589832 | tf_op jit(solution)/shard_map/ppermute | solution.py:102
  138.2 1.5 collective-permute-start.15
  139.7 7.4 %collective-permute-done.13.refs_1_.refs_0_ = bf16[128,768]{1,0:T(8,128)(2,1)S(1)} collective-permute-done((bf16[128,768]{1,0:T(8,128)(2,1)S(1)}, bf16[128,768]{1,0:T(8,128)(2,1)S(1)}, u32[]{:S(2)}, u32[]{:S(2)}) %collective-permute-start.13) | collective-permute-done | bytes 196640 | tf_op jit(solution)/shard_map/ppermute | solution.py:102
  147.1 1.4 collective-permute-start.17
  148.5 0.7 collective-permute-start.18
  149.2 4.7 %collective-permute-done.16.refs_3_.refs_2_ = bf16[128,768]{1,0:T(8,128)(2,1)S(1)} collective-permute-done((bf16[128,768]{1,0:T(8,128)(2,1)S(1)}, bf16[128,768]{1,0:T(8,128)(2,1)S(1)}, u32[]{:S(2)}, u32[]{:S(2)}) %collective-permute-start.16) | collective-permute-done | bytes 196640 | tf_op jit(solution)/shard_map/ppermute | solution.py:102
  153.8 1.2 collective-permute-start.19
  155.0 4.1 %collective-permute-done.18.refs_6_.refs_3_ = bf16[128,768]{1,0:T(8,128)(2,1)S(1)} collective-permute-done((bf16[128,768]{1,0:T(8,128)(2,1)S(1)}, bf16[128,768]{1,0:T(8,128)(2,1)S(1)}, u32[]{:S(2)}, u32[]{:S(2)}) %collective-permute-start.18) | collective-permute-done | bytes 196640 | tf_op jit(solution)/shard_map/ppermute | solution.py:102
  159.1 1.1 shard_map.123
  160.3 1.3 collective-permute-done.20.b
  161.7 0.6 collective-permute-done.19.refs_7_.refs_3_
  162.3 1.1 shard_map.125
  164.1 0.8 collective-permute-done.22.b
  164.9 0.8 collective-permute-start.23
  165.7 2.4 %shard_map.122 = (f32[256,768]{1,0:T(8,128)}, f32[8,128]{1,0:T(8,128)S(1)}) custom-call(s32[6]{0:T(128)S(1)} %stack.27.me_ref.refs_6_, bf16[256,1024]{1,0:T(8,128)(2,1)S(1)} %get-tuple-element.91.b.hidden_ref, bf16[128,768]{1,0:T(8,128)(2,1)S(1)} %shard_map.121.refs_0_, bf16[128,768]{1,0:T(8,128)(2,1)S(1)} %collective-permute-done.13.refs_1_.refs_0_, ...), custom_call_target="tpu_custom_call" | custom-call | flops 402653184 | bytes 4194304 | tf_op jit(solution)/shard_map/pallas_call | solution.py:636
  168.1 1.8 %collective-permute-done.21.q0 = bf16[2,256,128]{2,1,0:T(8,128)(2,1)S(1)} collective-permute-done((bf16[2,256,128]{2,1,0:T(8,128)(2,1)S(1)}, bf16[2,256,128]{2,1,0:T(8,128)(2,1)S(1)}, u32[]{:S(2)}, u32[]{:S(2)}) %collective-permute-start.21) | collective-permute-done | bytes 131104 | tf_op jit(solution)/shard_map/ppermute | solution.py:102
  169.9 2.4 %collective-permute-done.23.q1 = bf16[2,256,128]{2,1,0:T(8,128)(2,1)S(1)} collective-permute-done((bf16[2,256,128]{2,1,0:T(8,128)(2,1)S(1)}, bf16[2,256,128]{2,1,0:T(8,128)(2,1)S(1)}, u32[]{:S(2)}, u32[]{:S(2)}) %collective-permute-start.23) | collective-permute-done | bytes 131104 | tf_op jit(solution)/shard_map/ppermute | solution.py:102
  172.3 0.9 shard_map.127.own
  173.3 1.7 collective-permute-done.24.other
  175.0 0.8 shard_map.128
  (56 shorter events, 6.0 us)
Async XLA Ops:
  0.6 1.2 copy-start
  0.6 8.2 %copy-start.3 = (s32[128]{0:T(128)S(1)}, s32[128]{0:T(128)}, u32[]{:S(2)}) copy-start(s32[128]{0:T(128)} %param.16) | copy-start | bytes 1540
  0.7 8.2 %copy-start.4 = (bf16[128,128]{1,0:T(8,128)(2,1)S(1)}, bf16[128,128]{1,0:T(8,128)(2,1)}, u32[]{:S(2)}) copy-start(bf16[128,128]{1,0:T(8,128)(2,1)} %param.15) | copy-start | bytes 98308
  2.9 13.4 %copy-start.5 = (s32[1536]{0:T(1024)S(1)}, s32[1536]{0:T(1024)}, u32[]{:S(2)}) copy-start(s32[1536]{0:T(1024)} %param.12) | copy-start | bytes 18436
  5.8 9.6 %collective-permute-start = (bf16[128,768]{1,0:T(8,128)(2,1)S(1)}, bf16[128,768]{1,0:T(8,128)(2,1)S(1)}, u32[]{:S(2)}, u32[]{:S(2)}) collective-permute-start(bf16[128,768]{1,0:T(8,128)(2,1)S(1)} %fusion.4.refs_0_.image), channel_id=1, source_target_pairs={{0,2},{1,3},{2,0},{3,1},{4,6},{5,7},{6,4},{7,5},{8,10},{9,11},{10,... | collective-permute-start | bytes 589832 | tf_op jit(solution)/shard_map/ppermute | solution.py:102
  8.9 6.5 %collective-permute-start.1 = (bf16[1,144,128]{2,0,1:T(2,128)(2,1)S(1)}, bf16[1,144,128]{2,0,1:T(2,128)(2,1)S(1)}, u32[]{:S(2)}, u32[]{:S(2)}) collective-permute-start(bf16[1,144,128]{2,0,1:T(2,128)(2,1)S(1)} %copy.15), channel_id=1, source_target_pairs={{0,16},{4,20},{8,24},{12,28},{16,0},{20,4},{24,8},{28,12},{1,17},{... | collective-permute-start | bytes 110600 | tf_op jit(solution)/shard_map/ppermute | solution.py:102
  11.6 4.7 %collective-permute-start.3 = (bf16[128,768]{1,0:T(8,128)(2,1)S(1)}, bf16[128,768]{1,0:T(8,128)(2,1)S(1)}, u32[]{:S(2)}, u32[]{:S(2)}) collective-permute-start(bf16[128,768]{1,0:T(8,128)(2,1)S(1)} %fusion.4.refs_0_.image), channel_id=1, source_target_pairs={{0,1},{1,0},{2,3},{3,2},{4,5},{5,4},{6,7},{7,6},{8,9},{9,8},{10,11... | collective-permute-start | bytes 589832 | tf_op jit(solution)/shard_map/ppermute | solution.py:102
  15.4 1.4 collective-permute-start.4
  15.7 30.1 %collective-permute-start.2 = (bf16[2,144,128]{2,0,1:T(2,128)(2,1)S(1)}, bf16[2,144,128]{2,0,1:T(2,128)(2,1)S(1)}, u32[]{:S(2)}, u32[]{:S(2)}) collective-permute-start(bf16[2,144,128]{2,0,1:T(2,128)(2,1)S(1)} %pad_maximum_fusion.4), channel_id=1, source_target_pairs={{0,8},{4,12},{8,0},{12,4},{16,24},{20,28},{24,16},{28,20},{1,9},{5... | collective-permute-start | bytes 221192 | tf_op jit(solution)/shard_map/ppermute | solution.py:102
  45.8 15.9 %collective-permute-start.5 = (bf16[2,2,128,512]{3,2,1,0:T(8,128)(2,1)S(1)}, bf16[2,2,128,512]{3,2,1,0:T(8,128)(2,1)S(1)}, u32[]{:S(2)}, u32[]{:S(2)}) collective-permute-start(bf16[2,2,128,512]{3,2,1,0:T(8,128)(2,1)S(1)} %get-tuple-element.62), channel_id=1, source_target_pairs={{0,4},{4,0},{8,12},{12,8},{16,20},{20,16},{24,28},{28,24},{1,5},{5... | collective-permute-start | bytes 1572872 | tf_op jit(solution)/shard_map/ppermute | solution.py:102
  47.3 14.4 %collective-permute-start.6 = (bf16[2,2,128,512]{3,2,1,0:T(8,128)(2,1)S(1)}, bf16[2,2,128,512]{3,2,1,0:T(8,128)(2,1)S(1)}, u32[]{:S(2)}, u32[]{:S(2)}) collective-permute-start(bf16[2,2,128,512]{3,2,1,0:T(8,128)(2,1)S(1)} %get-tuple-element.65), channel_id=1, source_target_pairs={{0,8},{4,12},{8,0},{12,4},{16,24},{20,28},{24,16},{28,20},{1,9},{5... | collective-permute-start | bytes 1572872 | tf_op jit(solution)/shard_map/ppermute | solution.py:102
  62.6 8.2 %collective-permute-start.7 = (bf16[2,128,512]{2,1,0:T(8,128)(2,1)}, bf16[2,128,512]{2,1,0:T(8,128)(2,1)}, u32[]{:S(2)}, u32[]{:S(2)}) collective-permute-start(bf16[2,128,512]{2,1,0:T(8,128)(2,1)} %get-tuple-element.67), channel_id=1, source_target_pairs={{0,8},{4,12},{8,0},{12,4},{16,24},{20,28},{24,16},{28,20},{1,9},{5... | collective-permute-start | bytes 786440 | tf_op jit(solution)/shard_map/ppermute | solution.py:102
  63.7 7.8 %collective-permute-start.8 = (bf16[2,128,512]{2,1,0:T(8,128)(2,1)}, bf16[2,128,512]{2,1,0:T(8,128)(2,1)}, u32[]{:S(2)}, u32[]{:S(2)}) collective-permute-start(bf16[2,128,512]{2,1,0:T(8,128)(2,1)} %get-tuple-element.69), channel_id=1, source_target_pairs={{0,4},{4,0},{8,12},{12,8},{16,20},{20,16},{24,28},{28,24},{1,5},{5... | collective-permute-start | bytes 786440 | tf_op jit(solution)/shard_map/ppermute | solution.py:102
  73.2 13.5 %collective-permute-start.10 = (bf16[256,512]{1,0:T(8,128)(2,1)S(1)}, bf16[256,512]{1,0:T(8,128)(2,1)S(1)}, u32[]{:S(2)}, u32[]{:S(2)}) collective-permute-start(bf16[256,512]{1,0:T(8,128)(2,1)S(1)} %get-tuple-element.75), channel_id=1, source_target_pairs={{0,16},{4,20},{8,24},{12,28},{16,0},{20,4},{24,8},{28,12},{1,17},{... | collective-permute-start | bytes 786440 | tf_op jit(solution)/shard_map/ppermute | solution.py:102
  76.3 5.2 %collective-permute-start.9 = (bf16[4,144,128]{2,0,1:T(4,128)(2,1)S(1)}, bf16[4,144,128]{2,0,1:T(4,128)(2,1)S(1)}, u32[]{:S(2)}, u32[]{:S(2)}) collective-permute-start(bf16[4,144,128]{2,0,1:T(4,128)(2,1)S(1)} %pad_maximum_fusion.3), channel_id=1, source_target_pairs={{0,4},{4,0},{8,12},{12,8},{16,20},{20,16},{24,28},{28,24},{1,5},{5... | collective-permute-start | bytes 442376 | tf_op jit(solution)/shard_map/ppermute | solution.py:102
  88.8 30.1 %all-to-all-start = ((bf16[8,128,512]{2,1,0:T(8,128)(2,1)}), bf16[8,128,512]{2,1,0:T(8,128)(2,1)}, u32[]{:S(2)}, u32[]{:S(2)}) async-start(bf16[8,128,512]{2,1,0:T(8,128)(2,1)} %shard_map.116), calls=%async_computation | async-start | bytes 2097152 | tf_op jit(solution)/shard_map/all_to_all | solution.py:774
  125.4 3.2 %collective-permute-start.11 = (bf16[2,768,128]{2,1,0:T(8,128)(2,1)S(1)}, bf16[2,768,128]{2,1,0:T(8,128)(2,1)S(1)}, u32[]{:S(2)}, u32[]{:S(2)}) collective-permute-start(bf16[2,768,128]{2,1,0:T(8,128)(2,1)S(1)} %get-tuple-element.78), channel_id=1, source_target_pairs={{0,1},{1,0},{2,3},{3,2},{4,5},{5,4},{6,7},{7,6},{8,9},{9,8},{10,11... | collective-permute-start | bytes 1179656 | tf_op jit(solution)/shard_map/ppermute | solution.py:102
  128.6 7.4 %collective-permute-start.12 = (bf16[768,128]{1,0:T(8,128)(2,1)S(1)}, bf16[768,128]{1,0:T(8,128)(2,1)S(1)}, u32[]{:S(2)}, u32[]{:S(2)}) collective-permute-start(bf16[768,128]{1,0:T(8,128)(2,1)S(1)} %shard_map.120), channel_id=1, source_target_pairs={{0,2},{1,3},{2,0},{3,1},{4,6},{5,7},{6,4},{7,5},{8,10},{9,11},{10,... | collective-permute-start | bytes 589832 | tf_op jit(solution)/shard_map/ppermute | solution.py:102
  129.2 29.9 %copy-start.1 = (bf16[2048,768]{1,0:T(8,128)(2,1)S(1)}, bf16[2048,768]{1,0:T(8,128)(2,1)}, u32[]{:S(2)}) copy-start(bf16[2048,768]{1,0:T(8,128)(2,1)} %w_ref.3) | copy-start | bytes 9437188
  136.2 10.9 %collective-permute-start.13 = (bf16[128,768]{1,0:T(8,128)(2,1)S(1)}, bf16[128,768]{1,0:T(8,128)(2,1)S(1)}, u32[]{:S(2)}, u32[]{:S(2)}) collective-permute-start(bf16[128,768]{1,0:T(8,128)(2,1)S(1)} %shard_map.121.refs_0_), channel_id=1, source_target_pairs={{0,16},{4,20},{8,24},{12,28},{16,0},{20,4},{24,8},{28,12},{1,17},{... | collective-permute-start | bytes 589832 | tf_op jit(solution)/shard_map/ppermute | solution.py:102
  136.3 10.8 %collective-permute-start.14 = (bf16[128,768]{1,0:T(8,128)(2,1)S(1)}, bf16[128,768]{1,0:T(8,128)(2,1)S(1)}, u32[]{:S(2)}, u32[]{:S(2)}) collective-permute-start(bf16[128,768]{1,0:T(8,128)(2,1)S(1)} %shard_map.121.refs_0_), channel_id=1, source_target_pairs={{0,8},{4,12},{8,0},{12,4},{16,24},{20,28},{24,16},{28,20},{1,9},{5... | collective-permute-start | bytes 589832 | tf_op jit(solution)/shard_map/ppermute | solution.py:102
  138.2 8.9 %collective-permute-start.15 = (bf16[128,768]{1,0:T(8,128)(2,1)S(1)}, bf16[128,768]{1,0:T(8,128)(2,1)S(1)}, u32[]{:S(2)}, u32[]{:S(2)}) collective-permute-start(bf16[128,768]{1,0:T(8,128)(2,1)S(1)} %shard_map.121.refs_0_), channel_id=1, source_target_pairs={{0,4},{4,0},{8,12},{12,8},{16,20},{20,16},{24,28},{28,24},{1,5},{5... | collective-permute-start | bytes 589832 | tf_op jit(solution)/shard_map/ppermute | solution.py:102
  147.1 6.8 %collective-permute-start.16 = (bf16[128,768]{1,0:T(8,128)(2,1)S(1)}, bf16[128,768]{1,0:T(8,128)(2,1)S(1)}, u32[]{:S(2)}, u32[]{:S(2)}) collective-permute-start(bf16[128,768]{1,0:T(8,128)(2,1)S(1)} %collective-permute-done.13.refs_1_.refs_0_), channel_id=1, source_target_pairs={{0,8},{4,12},{8,0},{12,4},{16,24},{20,28},{24,16},{28,20},{1,9},{5... | collective-permute-start | bytes 589832 | tf_op jit(solution)/shard_map/ppermute | solution.py:102
  147.1 7.9 %collective-permute-start.17 = (bf16[128,768]{1,0:T(8,128)(2,1)S(1)}, bf16[128,768]{1,0:T(8,128)(2,1)S(1)}, u32[]{:S(2)}, u32[]{:S(2)}) collective-permute-start(bf16[128,768]{1,0:T(8,128)(2,1)S(1)} %collective-permute-done.13.refs_1_.refs_0_), channel_id=1, source_target_pairs={{0,4},{4,0},{8,12},{12,8},{16,20},{20,16},{24,28},{28,24},{1,5},{5... | collective-permute-start | bytes 589832 | tf_op jit(solution)/shard_map/ppermute | solution.py:102
  148.5 10.6 %collective-permute-start.18 = (bf16[128,768]{1,0:T(8,128)(2,1)S(1)}, bf16[128,768]{1,0:T(8,128)(2,1)S(1)}, u32[]{:S(2)}, u32[]{:S(2)}) collective-permute-start(bf16[128,768]{1,0:T(8,128)(2,1)S(1)} %collective-permute-done.14.refs_2_), channel_id=1, source_target_pairs={{0,4},{4,0},{8,12},{12,8},{16,20},{20,16},{24,28},{28,24},{1,5},{5... | collective-permute-start | bytes 589832 | tf_op jit(solution)/shard_map/ppermute | solution.py:102
  153.8 8.5 %collective-permute-start.19 = (bf16[128,768]{1,0:T(8,128)(2,1)S(1)}, bf16[128,768]{1,0:T(8,128)(2,1)S(1)}, u32[]{:S(2)}, u32[]{:S(2)}) collective-permute-start(bf16[128,768]{1,0:T(8,128)(2,1)S(1)} %collective-permute-done.16.refs_3_.refs_2_), channel_id=1, source_target_pairs={{0,4},{4,0},{8,12},{12,8},{16,20},{20,16},{24,28},{28,24},{1,5},{5... | collective-permute-start | bytes 589832 | tf_op jit(solution)/shard_map/ppermute | solution.py:102
  160.2 1.4 collective-permute-start.20
  161.7 10.6 %copy-start.2 = (bf16[384,1024]{1,0:T(8,128)(2,1)S(1)}, bf16[384,1024]{1,0:T(8,128)(2,1)}, u32[]{:S(2)}) copy-start(bf16[384,1024]{1,0:T(8,128)(2,1)} %fusion.7.c.lhs_ref) | copy-start | bytes 2359300
  163.5 1.4 collective-permute-start.22
  163.5 6.4 %collective-permute-start.21 = (bf16[2,256,128]{2,1,0:T(8,128)(2,1)S(1)}, bf16[2,256,128]{2,1,0:T(8,128)(2,1)S(1)}, u32[]{:S(2)}, u32[]{:S(2)}) collective-permute-start(bf16[2,256,128]{2,1,0:T(8,128)(2,1)S(1)} %shard_map.124.refs_4_.p0), channel_id=1, source_target_pairs={{0,2},{1,3},{2,0},{3,1},{4,6},{5,7},{6,4},{7,5},{8,10},{9,11},{10,... | collective-permute-start | bytes 393224 | tf_op jit(solution)/shard_map/ppermute | solution.py:102
  164.9 7.4 %collective-permute-start.23 = (bf16[2,256,128]{2,1,0:T(8,128)(2,1)S(1)}, bf16[2,256,128]{2,1,0:T(8,128)(2,1)S(1)}, u32[]{:S(2)}, u32[]{:S(2)}) collective-permute-start(bf16[2,256,128]{2,1,0:T(8,128)(2,1)S(1)} %shard_map.126.p1), channel_id=1, source_target_pairs={{0,2},{1,3},{2,0},{3,1},{4,6},{5,7},{6,4},{7,5},{8,10},{9,11},{10,... | collective-permute-start | bytes 393224 | tf_op jit(solution)/shard_map/ppermute | solution.py:102
  173.2 1.8 %collective-permute-start.24 = (f32[384,256]{1,0:T(8,128)S(1)}, f32[384,256]{1,0:T(8,128)S(1)}, u32[]{:S(2)}, u32[]{:S(2)}) collective-permute-start(f32[384,256]{1,0:T(8,128)S(1)} %shard_map.127.own), channel_id=1, source_target_pairs={{0,1},{1,0},{2,3},{3,2},{4,5},{5,4},{6,7},{7,6},{8,9},{9,8},{10,11... | collective-permute-start | bytes 1179656 | tf_op jit(solution)/shard_map/ppermute | solution.py:102
